TPU v7x, 32 devices: a whole 2x2x4 slice. The times are simulated.
32 devices in a mesh: fsdp: 4 (over x, core), ctx: 2 (over y), tp: 4 (over z).
Axes of the slice: x: 2, y: 2, z: 4, core: 2. Of those that a mesh axis runs over, the one named last changes fastest.
Arguments:
- tokens: bfloat16 [4, 512, 2048], P('fsdp', 'ctx'), may hold values from -6 to 6
- cotangent: bfloat16 [4, 512, 2048], P('fsdp', 'ctx'), may hold values from -6 to 6
- doc_lengths: int32 [4, 5], P('fsdp'), may hold values from 1 to 508, as said below
- norm_gains: bfloat16 [2, 2, 2048], P(None, None, ('fsdp', 'ctx')), may hold values from 0.5 to 1.5
- norm_biases: bfloat16 [2, 2, 2048], P(None, None, ('fsdp', 'ctx')), may hold values from -3 to 3
- qkv_weight: bfloat16 [2, 2048, 3, 2048], P(None, ('fsdp', 'ctx'), None, 'tp'), may hold values from -0.125 to 0.125
- qkv_bias: bfloat16 [2, 3, 2048], P(None, None, ('fsdp', 'ctx')), may hold values from -3 to 3
- out_weight: bfloat16 [2, 2048, 2048], P(None, 'tp', ('fsdp', 'ctx')), may hold values from -1 to 1
- gate_up_weight: bfloat16 [2, 2048, 2, 5632], P(None, ('fsdp', 'ctx'), None, 'tp'), may hold values from -0.125 to 0.125
- down_weight: bfloat16 [2, 5632, 2048], P(None, 'tp', ('fsdp', 'ctx')), may hold values from -0.078125 to 0.078125
Outputs:
- output: bfloat16 [4, 512, 2048], P('fsdp', 'ctx')
- grad_input: float32 [4, 512, 2048], P('fsdp', 'ctx')
- grad_norm_gains: float32 [2, 2, 2048], P(None, None, ('fsdp', 'ctx'))
- grad_norm_biases: float32 [2, 2, 2048], P(None, None, ('fsdp', 'ctx'))
- grad_qkv_weight: float32 [2, 2048, 3, 2048], P(None, ('fsdp', 'ctx'), None, 'tp')
- grad_qkv_bias: float32 [2, 3, 2048], P(None, None, ('fsdp', 'ctx'))
- grad_out_weight: float32 [2, 2048, 2048], P(None, 'tp', ('fsdp', 'ctx'))
- grad_gate_up: float32 [2, 2048, 2, 5632], P(None, ('fsdp', 'ctx'), None, 'tp')
- grad_down: float32 [2, 5632, 2048], P(None, 'tp', ('fsdp', 'ctx'))
Inputs may be any that keep to these rules, and one draw needn't show every extreme that they name: `doc_lengths`: each row holds the lengths of 5 documents packed in order into one sequence of 512 tokens and sums to 512; the first two together and the last two together hold at most 255 tokens each, so the middle document starts among the first 256 tokens and ends among the last 256; in one row the first two and the last two hold 2 tokens each.
All inputs are finite; a program needn't handle non-finite values.
Results may differ from a plain program's by a relative error of at most 0.028.
Values may be sent and summed in bfloat16 or wider, within the bound.
No kernel may reach another device: no remote copies, remote signals or barrier semaphores. Data moves between devices by JAX's collectives and lax.ppermute only.
A program may use at most 256 MiB of HBM per device.

v0:
```python
import jax
import jax.numpy as jnp
from jax import lax
from jax.sharding import PartitionSpec as P

HD = 64
ROT = 16


def layout(lengths, first_row, row_count):
    token_index = first_row + jnp.arange(row_count, dtype=jnp.int32)
    doc_ends = jnp.cumsum(lengths)
    starts = doc_ends - lengths
    segment = jnp.sum(
        (token_index[:, None] >= doc_ends[None, :]).astype(jnp.int32), axis=1, dtype=jnp.int32
    )
    doc_begin = jnp.max(
        jnp.where(token_index[:, None] >= starts[None, :], starts[None, :], 0), axis=1
    )
    return (segment, token_index - doc_begin, token_index)


def rotary_tables(position):
    frequency = 10000.0 ** (-jnp.arange(0, ROT, 2, dtype=jnp.float32) / ROT)
    angles = position.astype(jnp.float32)[:, None] * frequency[None, :]
    return (jnp.cos(angles), jnp.sin(angles))


def rotate(field, cos_table, sin_table):
    half_rot = cos_table.shape[1]
    cos_part = cos_table[:, None, :]
    sin_part = sin_table[:, None, :]
    lower = field[..., :half_rot]
    upper = field[..., half_rot : 2 * half_rot]
    return jnp.concatenate(
        [
            lower * cos_part - upper * sin_part,
            upper * cos_part + lower * sin_part,
            field[..., 2 * half_rot :],
        ],
        axis=-1,
    )


def layer_norm(stream, gain_row, shift_row):
    centered = stream - jnp.mean(stream, axis=-1, keepdims=True)
    variance = jnp.mean(centered * centered, axis=-1, keepdims=True)
    return centered * lax.rsqrt(variance + 1e-05) * gain_row + shift_row


def gated(gate_part, up_part):
    return jax.nn.silu(gate_part) * up_part


def branch_sum(partial_out):
    return lax.psum(partial_out.astype(jnp.bfloat16), "tp").astype(jnp.float32)


def split_heads(rows_flat, heads_here):
    return rows_flat.reshape(rows_flat.shape[0], heads_here, HD).transpose(1, 0, 2)


def attend(queries, key_values, allowed):
    seq_rows = queries.shape[0]
    heads_here = queries.shape[1]
    query_heads = queries.transpose(1, 0, 2)
    key_heads = split_heads(key_values[0], heads_here)
    value_heads = split_heads(key_values[1], heads_here)

    def one_head(inputs):
        query_head, key_head, value_head = inputs
        scores = jnp.einsum(
            "qd,kd->qk", query_head, key_head, preferred_element_type=jnp.float32
        ) * (1.0 / HD**0.5)
        scores = jnp.where(allowed, scores, -1e30)
        row_max = jnp.max(scores, axis=1, keepdims=True)
        exponent = jnp.exp(scores - row_max)
        row_total = jnp.sum(exponent, axis=1, keepdims=True)
        probs = exponent / row_total
        result = jnp.dot(probs.astype(jnp.bfloat16), value_head, preferred_element_type=jnp.float32)
        return (result, (row_max + jnp.log(row_total))[:, 0])

    results, log_total = lax.map(one_head, (query_heads, key_heads, value_heads))
    return (results.transpose(1, 0, 2).reshape(seq_rows, heads_here * HD), log_total)


def attend_back(queries, key_values, d_mixed, log_total, allowed):
    heads_here = queries.shape[1]
    query_heads = queries.transpose(1, 0, 2)
    key_heads = split_heads(key_values[0], heads_here)
    value_heads = split_heads(key_values[1], heads_here)
    grad_heads = split_heads(d_mixed, heads_here)

    def one_head(inputs):
        query_head, key_head, value_head, grad_head, total_head = inputs
        scores = jnp.einsum(
            "qd,kd->qk", query_head, key_head, preferred_element_type=jnp.float32
        ) * (1.0 / HD**0.5)
        scores = jnp.where(allowed, scores, -1e30)
        probs = jnp.exp(scores - total_head[:, None])
        d_probs = jnp.einsum("qd,kd->qk", grad_head, value_head, preferred_element_type=jnp.float32)
        delta = jnp.sum(probs * d_probs, axis=1, keepdims=True)
        d_scores = (probs * (d_probs - delta)).astype(jnp.bfloat16)
        d_query = jnp.dot(d_scores, key_head, preferred_element_type=jnp.float32) * (1.0 / HD**0.5)
        d_key = jnp.einsum(
            "qk,qd->kd", d_scores, query_head, preferred_element_type=jnp.float32
        ) * (1.0 / HD**0.5)
        d_value = jnp.einsum(
            "qk,qd->kd", probs.astype(jnp.bfloat16), grad_head, preferred_element_type=jnp.float32
        )
        return (d_query, d_key, d_value)

    d_query, d_key, d_value = lax.map(
        one_head, (query_heads, key_heads, value_heads, grad_heads, log_total)
    )
    key_count = d_key.shape[1]
    return (
        d_query.transpose(1, 0, 2),
        d_key.transpose(1, 0, 2).reshape(key_count, heads_here * HD),
        d_value.transpose(1, 0, 2).reshape(key_count, heads_here * HD),
    )


def local(
    tokens,
    cotangent,
    doc_lengths,
    norm_gains,
    norm_biases,
    qkv_weight,
    qkv_bias,
    out_weight,
    gate_up_weight,
    down_weight,
):
    seq_rows = tokens.shape[1]
    width = tokens.shape[2]
    local_width = qkv_weight.shape[3]
    local_heads = local_width // HD
    layers = norm_gains.shape[0]
    total_rows = seq_rows * lax.axis_size("ctx")
    tensor_rank = lax.axis_index("tp")
    lengths = doc_lengths[0]
    seg_query, pos_query, index_query = layout(lengths, lax.axis_index("ctx") * seq_rows, seq_rows)
    seg_key, pos_key, index_key = layout(lengths, jnp.int32(0), total_rows)
    allowed = (seg_query[:, None] == seg_key[None, :]) & (
        index_query[:, None] >= index_key[None, :]
    )
    cos_table, sin_table = rotary_tables(pos_query)

    def unpack(gathered):
        bias_local = lax.dynamic_slice_in_dim(
            gathered[3], tensor_rank * local_width, local_width, 1
        ).astype(jnp.float32)
        return (
            gathered[0].astype(jnp.float32),
            gathered[1].astype(jnp.float32),
            gathered[2],
            bias_local,
            gathered[4],
            gathered[5],
            gathered[6],
        )

    stream = tokens[0].astype(jnp.float32)
    saved = []
    for layer_index in range(layers):
        gathered = (
            lax.all_gather(norm_gains[layer_index], ("fsdp", "ctx"), axis=1, tiled=True),
            lax.all_gather(norm_biases[layer_index], ("fsdp", "ctx"), axis=1, tiled=True),
            lax.all_gather(qkv_weight[layer_index], ("fsdp", "ctx"), axis=0, tiled=True),
            lax.all_gather(qkv_bias[layer_index], ("fsdp", "ctx"), axis=1, tiled=True),
            lax.all_gather(out_weight[layer_index], ("fsdp", "ctx"), axis=1, tiled=True),
            lax.all_gather(gate_up_weight[layer_index], ("fsdp", "ctx"), axis=0, tiled=True),
            lax.all_gather(down_weight[layer_index], ("fsdp", "ctx"), axis=1, tiled=True),
        )
        gain_pair, shifts, w_qkv, b_qkv, w_out, w_gate_up, w_down = unpack(gathered)
        first_in = layer_norm(stream, gain_pair[0], shifts[0]).astype(jnp.bfloat16)
        qkv = (
            jnp.einsum("sd,dch->sch", first_in, w_qkv, preferred_element_type=jnp.float32)
            + b_qkv[None]
        )
        queries = rotate(qkv[:, 0].reshape(seq_rows, local_heads, HD), cos_table, sin_table).astype(
            jnp.bfloat16
        )
        key_rows = rotate(
            qkv[:, 1].reshape(seq_rows, local_heads, HD), cos_table, sin_table
        ).astype(jnp.bfloat16)
        local_kv = jnp.stack(
            [key_rows.reshape(seq_rows, local_width), qkv[:, 2].astype(jnp.bfloat16)]
        )
        key_values = lax.all_gather(local_kv, "ctx", axis=1, tiled=True)
        mixed, log_total = attend(queries, key_values, allowed)
        mixed = mixed.astype(jnp.bfloat16)
        stream_mid = stream + branch_sum(jnp.dot(mixed, w_out, preferred_element_type=jnp.float32))
        second_in = layer_norm(stream_mid, gain_pair[1], shifts[1]).astype(jnp.bfloat16)
        gate_up = jnp.einsum(
            "sd,dcf->scf", second_in, w_gate_up, preferred_element_type=jnp.float32
        )
        hidden = gated(gate_up[:, 0], gate_up[:, 1]).astype(jnp.bfloat16)
        stream_next = stream_mid + branch_sum(
            jnp.dot(hidden, w_down, preferred_element_type=jnp.float32)
        )
        saved.append(
            (stream, stream_mid, queries, local_kv, key_values, mixed, log_total, gate_up, gathered)
        )
        stream = stream_next
    output = stream.astype(jnp.bfloat16)[None]
    grad_stream = cotangent[0].astype(jnp.float32)
    per_layer = [None] * layers
    for layer_index in reversed(range(layers)):
        (
            stream_in,
            stream_mid,
            queries,
            local_kv,
            key_values,
            mixed,
            log_total,
            gate_up,
            gathered,
        ) = saved[layer_index]
        weight_set = (
            lax.all_gather(norm_gains[layer_index], ("fsdp", "ctx"), axis=1, tiled=True),
            lax.all_gather(norm_biases[layer_index], ("fsdp", "ctx"), axis=1, tiled=True),
            lax.all_gather(qkv_weight[layer_index], ("fsdp", "ctx"), axis=0, tiled=True),
            lax.all_gather(qkv_bias[layer_index], ("fsdp", "ctx"), axis=1, tiled=True),
            lax.all_gather(out_weight[layer_index], ("fsdp", "ctx"), axis=1, tiled=True),
            lax.all_gather(gate_up_weight[layer_index], ("fsdp", "ctx"), axis=0, tiled=True),
            lax.all_gather(down_weight[layer_index], ("fsdp", "ctx"), axis=1, tiled=True),
        )
        gain_pair, shifts, w_qkv, b_qkv, w_out, w_gate_up, w_down = unpack(weight_set)
        d_mlp = grad_stream.astype(jnp.bfloat16)
        hidden, gated_back = jax.vjp(gated, gate_up[:, 0], gate_up[:, 1])
        grad_down = jnp.einsum(
            "sf,sd->fd", hidden.astype(jnp.bfloat16), d_mlp, preferred_element_type=jnp.float32
        )
        d_gate, d_up = gated_back(
            jnp.einsum("sd,fd->sf", d_mlp, w_down, preferred_element_type=jnp.float32)
        )
        d_gate_up = jnp.stack([d_gate, d_up], axis=1).astype(jnp.bfloat16)
        second_in, norm_back_two = jax.vjp(layer_norm, stream_mid, gain_pair[1], shifts[1])
        grad_gate_up = jnp.einsum(
            "sd,scf->dcf",
            second_in.astype(jnp.bfloat16),
            d_gate_up,
            preferred_element_type=jnp.float32,
        )
        d_second = lax.psum(
            jnp.einsum(
                "scf,dcf->sd", d_gate_up, w_gate_up, preferred_element_type=jnp.float32
            ).astype(jnp.bfloat16),
            "tp",
        ).astype(jnp.float32)
        back_input, gain_two, shift_two = norm_back_two(d_second)
        grad_mid = grad_stream + back_input
        d_attn = grad_mid.astype(jnp.bfloat16)
        grad_out = jnp.einsum("sh,sd->hd", mixed, d_attn, preferred_element_type=jnp.float32)
        d_mixed = jnp.einsum("sd,hd->sh", d_attn, w_out, preferred_element_type=jnp.float32).astype(
            jnp.bfloat16
        )
        d_query, d_key_all, d_value_all = attend_back(
            queries, key_values, d_mixed, log_total, allowed
        )
        d_key, d_value = (
            lax.psum_scatter(
                d_key_all.astype(jnp.bfloat16), "ctx", scatter_dimension=0, tiled=True
            ).astype(jnp.float32),
            lax.psum_scatter(
                d_value_all.astype(jnp.bfloat16), "ctx", scatter_dimension=0, tiled=True
            ).astype(jnp.float32),
        )
        d_query_back = rotate(d_query, cos_table, -sin_table).reshape(seq_rows, local_width)
        d_key_back = rotate(
            d_key.reshape(seq_rows, local_heads, HD), cos_table, -sin_table
        ).reshape(seq_rows, local_width)
        d_qkv = jnp.stack([d_query_back, d_key_back, d_value], axis=1).astype(jnp.bfloat16)
        first_in, norm_back_one = jax.vjp(layer_norm, stream_in, gain_pair[0], shifts[0])
        grad_qkv = jnp.einsum(
            "sd,sch->dch", first_in.astype(jnp.bfloat16), d_qkv, preferred_element_type=jnp.float32
        )
        bias_term = lax.dynamic_update_slice_in_dim(
            jnp.zeros((3, width), jnp.float32),
            jnp.sum(d_qkv, axis=0, dtype=jnp.float32),
            tensor_rank * local_width,
            1,
        )
        d_first, grad_bias = (
            lax.psum(
                jnp.einsum("sch,dch->sd", d_qkv, w_qkv, preferred_element_type=jnp.float32).astype(
                    jnp.bfloat16
                ),
                "tp",
            ).astype(jnp.float32),
            lax.psum(bias_term.astype(jnp.bfloat16), "tp").astype(jnp.float32),
        )
        back_input, gain_one, shift_one = norm_back_one(d_first)
        grad_stream = grad_mid + back_input
        weight_terms = (
            jnp.stack([gain_one, gain_two]),
            jnp.stack([shift_one, shift_two]),
            grad_qkv,
            grad_bias,
            grad_out,
            grad_gate_up,
            grad_down,
        )
        per_layer[layer_index] = (
            lax.psum_scatter(
                weight_terms[0].astype(jnp.bfloat16),
                ("fsdp", "ctx"),
                scatter_dimension=1,
                tiled=True,
            ).astype(jnp.float32),
            lax.psum_scatter(
                weight_terms[1].astype(jnp.bfloat16),
                ("fsdp", "ctx"),
                scatter_dimension=1,
                tiled=True,
            ).astype(jnp.float32),
            lax.psum_scatter(
                weight_terms[2].astype(jnp.bfloat16),
                ("fsdp", "ctx"),
                scatter_dimension=0,
                tiled=True,
            ).astype(jnp.float32),
            lax.psum_scatter(
                weight_terms[3].astype(jnp.bfloat16),
                ("fsdp", "ctx"),
                scatter_dimension=1,
                tiled=True,
            ).astype(jnp.float32),
            lax.psum_scatter(
                weight_terms[4].astype(jnp.bfloat16),
                ("fsdp", "ctx"),
                scatter_dimension=1,
                tiled=True,
            ).astype(jnp.float32),
            lax.psum_scatter(
                weight_terms[5].astype(jnp.bfloat16),
                ("fsdp", "ctx"),
                scatter_dimension=0,
                tiled=True,
            ).astype(jnp.float32),
            lax.psum_scatter(
                weight_terms[6].astype(jnp.bfloat16),
                ("fsdp", "ctx"),
                scatter_dimension=1,
                tiled=True,
            ).astype(jnp.float32),
        )
    stacked = tuple(
        (jnp.stack([layer_terms[member] for layer_terms in per_layer]) for member in range(7))
    )
    return (
        output,
        grad_stream[None],
        stacked[0],
        stacked[1],
        stacked[2],
        stacked[3],
        stacked[4],
        stacked[5],
        stacked[6],
    )


def solution(mesh):
    return jax.shard_map(
        local,
        mesh=mesh,
        in_specs=(
            P("fsdp", "ctx", None),
            P("fsdp", "ctx", None),
            P("fsdp", None),
            P(None, None, ("fsdp", "ctx")),
            P(None, None, ("fsdp", "ctx")),
            P(None, ("fsdp", "ctx"), None, "tp"),
            P(None, None, ("fsdp", "ctx")),
            P(None, "tp", ("fsdp", "ctx")),
            P(None, ("fsdp", "ctx"), None, "tp"),
            P(None, "tp", ("fsdp", "ctx")),
        ),
        out_specs=(
            P("fsdp", "ctx", None),
            P("fsdp", "ctx", None),
            P(None, None, ("fsdp", "ctx")),
            P(None, None, ("fsdp", "ctx")),
            P(None, ("fsdp", "ctx"), None, "tp"),
            P(None, None, ("fsdp", "ctx")),
            P(None, "tp", ("fsdp", "ctx")),
            P(None, ("fsdp", "ctx"), None, "tp"),
            P(None, "tp", ("fsdp", "ctx")),
        ),
        check_vma=False,
    )
```

profile of v0, /device:TPU:0, one launch (start us, length us, event | category | flops | bytes accessed | tf_op | source)
XLA Modules:
  0.0 1912.0 jit_solution(14423031224862704756)
XLA Ops:
  10.2 14.3 all-gather.3
  24.7 14.0 all-gather
  38.6 14.3 all-gather.1
  67.3 19.3 %all-gather.25.cloned.1.call-done = bf16[2,512,512]{2,1,0:T(8,128)(2,1)} async-done(((bf16[2,256,512]{2,1,0:T(8,128)(2,1)}), bf16[2,512,512]{2,1,0:T(8,128)(2,1)}) %all-gather.25.cloned.1.call-update) | async-done | bytes 1048592 | tf_op jit(solution)/shard_map/all_gather | solution.py:192
  90.2 21.6 %while.56 = (s32[]{:T(128)}, bf16[8,256,64]{1,2,0:T(8,128)(2,1)S(1)}, f32[8,256]{1,0:T(8,128)S(1)}, bf16[8,256,64]{2,1,0:T(8,128)(2,1)}, bf16[8,512,64]{2,1,0:T(...) while((s32[]{:T(128)}, ...), condition=%wide.region_9.10_spmd.clone, body=%wide.region_6.9_spmd.clone.sunk | while | flops 34995968 | bytes 1982577 | solution.py:83
  128.6 44.0 %all-reduce.10.cloned.1.call-done = bf16[256,2048]{1,0:T(8,128)(2,1)} async-done(((bf16[256,2048]{1,0:T(8,128)(2,1)}), bf16[256,2048]{1,0:T(8,128)(2,1)}) %all-reduce.10.cloned.1.call-update) | async-done | bytes 1048592 | tf_op jit(solution)/shard_map/psum | solution.py:56
  174.8 67.4 %all-gather.33.cloned.1.call-done = bf16[1,2048,2,1408]{3,1,2,0:T(8,128)(2,1)} async-done(((bf16[1,256,2,1408]{3,1,2,0:T(8,128)(2,1)}), bf16[1,2048,2,1408]{3,1,2,0:T(8,128)(2,1)}) %all-gather.33.cloned.1.call-update) | async-done | bytes 11534352 | tf_op jit(solution)/shard_map/all_gather | solution.py:174
  250.6 37.9 %all-gather.35.cloned.1.call-done = bf16[1,1408,2048]{2,1,0:T(8,128)(2,1)} async-done(((bf16[1,1408,256]{2,1,0:T(8,128)(2,1)}), bf16[1,1408,2048]{2,1,0:T(8,128)(2,1)}) %all-gather.35.cloned.1.call-update) | async-done | bytes 5767184 | tf_op jit(solution)/shard_map/all_gather | solution.py:175
  294.7 12.9 all-gather.10
  307.6 14.3 all-gather.7
  322.0 13.6 all-gather.8
  335.6 10.2 all-reduce.12.cloned.1.call-done
  348.3 45.0 %all-gather.37.cloned.1.call-done = bf16[1,2048,3,512]{3,1,2,0:T(8,128)(2,1)} async-done(((bf16[1,256,3,512]{3,1,2,0:T(8,128)(2,1)}), bf16[1,2048,3,512]{3,1,2,0:T(8,128)(2,1)}) %all-gather.37.cloned.1.call-update) | async-done | bytes 6291472 | tf_op jit(solution)/shard_map/all_gather | solution.py:171
  411.3 18.7 all-gather.27.cloned.1.call-done
  441.1 30.1 %while.57 = (s32[]{:T(128)}, bf16[8,256,64]{1,2,0:T(8,128)(2,1)S(1)}, f32[8,256]{1,0:T(8,128)S(1)}, bf16[8,256,64]{2,1,0:T(8,128)(2,1)}, bf16[8,512,64]{2,1,0:T(...) while((s32[]{:T(128)}, ...), condition=%wide.region_19.20_spmd.clone, body=%wide.region_16.19_spmd.clone.sunk | while | flops 34995968 | bytes 4079757 | solution.py:83
  478.0 48.5 %all-reduce.14.cloned.1.call-done = bf16[256,2048]{1,0:T(8,128)(2,1)} async-done(((bf16[256,2048]{1,0:T(8,128)(2,1)}), bf16[256,2048]{1,0:T(8,128)(2,1)}) %all-reduce.14.cloned.1.call-update) | async-done | bytes 1048592 | tf_op jit(solution)/shard_map/psum | solution.py:56
  529.7 66.4 %all-gather.41.cloned.1.call-done = bf16[1,2048,2,1408]{3,1,2,0:T(8,128)(2,1)} async-done(((bf16[1,256,2,1408]{3,1,2,0:T(8,128)(2,1)}), bf16[1,2048,2,1408]{3,1,2,0:T(8,128)(2,1)}) %all-gather.41.cloned.1.call-update) | async-done | bytes 11534352 | tf_op jit(solution)/shard_map/all_gather | solution.py:174
  596.1 9.8 fusion.98
  605.8 36.7 %all-gather.43.cloned.1.call-done = bf16[1,1408,2048]{2,1,0:T(8,128)(2,1)} async-done(((bf16[1,1408,256]{2,1,0:T(8,128)(2,1)}), bf16[1,1408,2048]{2,1,0:T(8,128)(2,1)}) %all-gather.43.cloned.1.call-update) | async-done | bytes 5767184 | tf_op jit(solution)/shard_map/all_gather | solution.py:175
  649.6 8.4 fusion.138
  658.1 51.9 %all-reduce.16.cloned.1.call-done = bf16[256,2048]{1,0:T(8,128)(2,1)} async-done(((bf16[256,2048]{1,0:T(8,128)(2,1)}), bf16[256,2048]{1,0:T(8,128)(2,1)}) %all-reduce.16.cloned.1.call-update) | async-done | bytes 1048592 | tf_op jit(solution)/shard_map/psum | solution.py:249
  722.4 61.4 %while.58 = (s32[]{:T(128)}, f32[8,256,64]{1,2,0:T(8,128)}, bf16[8,512,64]{1,2,0:T(8,128)(2,1)}, bf16[8,512,64]{1,2,0:T(8,128)(2,1)}, bf16[8,256,64]{2,1,0:T(8,1...) while((s32[]{:T(128)}, f32[8,256,64]{1,2,0:T(8,128)}, ...), condition=%wide.region_29.30_spmd.clone, body=%wide.region_27.29_spmd.clone.sunk | while | flops 85507840 | bytes 4864129 | solution.py:113
  787.8 10.1 reduce-scatter.31.cloned.1.call-done
  806.1 9.1 reduce-scatter.33.cloned.1.call-done
  821.2 51.9 %all-reduce.18.cloned.1.call-done = bf16[256,2048]{1,0:T(8,128)(2,1)} async-done(((bf16[256,2048]{1,0:T(8,128)(2,1)}), bf16[256,2048]{1,0:T(8,128)(2,1)}) %all-reduce.18.cloned.1.call-update) | async-done | bytes 1048592 | tf_op jit(solution)/shard_map/psum | solution.py:289
  878.5 6.9 fusion.219
  891.9 51.1 %all-reduce.20.cloned.1.call-done = bf16[256,2048]{1,0:T(8,128)(2,1)} async-done(((bf16[256,2048]{1,0:T(8,128)(2,1)}), bf16[256,2048]{1,0:T(8,128)(2,1)}) %all-reduce.20.cloned.1.call-update) | async-done | bytes 1048592 | tf_op jit(solution)/shard_map/psum | solution.py:249
  955.2 67.0 %while.59 = (s32[]{:T(128)}, f32[8,256,64]{1,2,0:T(8,128)}, bf16[8,512,64]{1,2,0:T(8,128)(2,1)}, bf16[8,512,64]{1,2,0:T(8,128)(2,1)}, bf16[8,256,64]{2,1,0:T(8,1...) while((s32[]{:T(128)}, f32[8,256,64]{1,2,0:T(8,128)}, ...), condition=%wide.region_40.41_spmd.clone, body=%wide.region_38.40_spmd.clone.sunk | while | flops 85507840 | bytes 4864129 | solution.py:113
  1024.3 6.4 fusion.153
  1078.8 67.3 %all-reduce.22.cloned.1.call-done = (bf16[256,2048]{1,0:T(8,128)(2,1)}, bf16[256,2048]{1,0:T(8,128)(2,1)}) async-done(((bf16[256,2048]{1,0:T(8,128)(2,1)}, bf16[256,2048]{1,0:T(8,128)(2,1)}), (bf16[256,2048]{1,0:T(8,128)(2,1)}, bf16[256,2048]{1,0:T(8,128)(2,1)})) %all-reduce.22.cloned.1.call-update) | async-done | bytes 2097168 | tf_op jit(solution)/shard_map/psum | solution.py:56
  1152.8 6.4 convolution_convert_fusion.2
  1179.4 7.5 convolution_convert_fusion
  1187.6 9.6 convolution_convert_fusion.1
  1198.1 21.8 %reduce-scatter.61.cloned.1.call-done = bf16[256,2]{1,0:T(8,128)(2,1)} async-done(((bf16[2048,2]{1,0:T(8,128)(2,1)}), bf16[256,2]{1,0:T(8,128)(2,1)}) %reduce-scatter.61.cloned.1.call-update) | async-done | bytes 1040
  1220.8 36.5 %reduce-scatter.57.cloned.1.call-done = bf16[256,2]{1,0:T(8,128)(2,1)} async-done(((bf16[2048,2]{1,0:T(8,128)(2,1)}), bf16[256,2]{1,0:T(8,128)(2,1)}) %reduce-scatter.57.cloned.1.call-update) | async-done | bytes 1040
  1258.2 36.3 %reduce-scatter.63.cloned.1.call-done = bf16[256,3]{1,0:T(8,128)(2,1)} async-done(((bf16[2048,3]{1,0:T(8,128)(2,1)}), bf16[256,3]{1,0:T(8,128)(2,1)}) %reduce-scatter.63.cloned.1.call-update) | async-done | bytes 1552
  1295.4 11.7 all-reduce
  1307.7 31.5 %reduce-scatter.45.cloned.1.call-done = bf16[512,256]{1,0:T(8,128)(2,1)} async-done(((bf16[512,2048]{1,0:T(8,128)(2,1)}), bf16[512,256]{1,0:T(8,128)(2,1)}) %reduce-scatter.45.cloned.1.call-update) | async-done | bytes 262160 | tf_op jit(solution)/shard_map/reduce_scatter | solution.py:333
  1339.2 44.4 %reduce-scatter.43.cloned.1.call-done = bf16[512,256]{1,0:T(8,128)(2,1)} async-done(((bf16[512,2048]{1,0:T(8,128)(2,1)}), bf16[512,256]{1,0:T(8,128)(2,1)}) %reduce-scatter.43.cloned.1.call-update) | async-done | bytes 262160 | tf_op jit(solution)/shard_map/reduce_scatter | solution.py:333
  1390.1 31.0 %reduce-scatter.59.cloned.1.call-done = bf16[256,2]{1,0:T(8,128)(2,1)} async-done(((bf16[2048,2]{1,0:T(8,128)(2,1)}), bf16[256,2]{1,0:T(8,128)(2,1)}) %reduce-scatter.59.cloned.1.call-update) | async-done | bytes 1040
  1422.1 36.3 %reduce-scatter.55.cloned.1.call-done = bf16[256,2]{1,0:T(8,128)(2,1)} async-done(((bf16[2048,2]{1,0:T(8,128)(2,1)}), bf16[256,2]{1,0:T(8,128)(2,1)}) %reduce-scatter.55.cloned.1.call-update) | async-done | bytes 1040
  1460.5 61.2 %reduce-scatter.53.cloned.1.call-done = bf16[1408,256]{1,0:T(8,128)(2,1)} async-done(((bf16[1408,2048]{1,0:T(8,128)(2,1)}), bf16[1408,256]{1,0:T(8,128)(2,1)}) %reduce-scatter.53.cloned.1.call-update) | async-done | bytes 720912 | tf_op jit(solution)/shard_map/reduce_scatter | solution.py:345
  1521.7 62.5 %reduce-scatter.51.cloned.1.call-done = bf16[1408,256]{1,0:T(8,128)(2,1)} async-done(((bf16[1408,2048]{1,0:T(8,128)(2,1)}), bf16[1408,256]{1,0:T(8,128)(2,1)}) %reduce-scatter.51.cloned.1.call-update) | async-done | bytes 720912 | tf_op jit(solution)/shard_map/reduce_scatter | solution.py:345
  1587.3 62.4 %reduce-scatter.41.cloned.1.call-done = bf16[256,3,512]{2,0,1:T(8,128)(2,1)} async-done(((bf16[2048,3,512]{2,0,1:T(8,128)(2,1)}), bf16[256,3,512]{2,0,1:T(8,128)(2,1)}) %reduce-scatter.41.cloned.1.call-update) | async-done | bytes 786448 | tf_op jit(solution)/shard_map/reduce_scatter | solution.py:321
  1649.8 65.0 %reduce-scatter.39.cloned.1.call-done = bf16[256,3,512]{2,0,1:T(8,128)(2,1)} async-done(((bf16[2048,3,512]{2,0,1:T(8,128)(2,1)}), bf16[256,3,512]{2,0,1:T(8,128)(2,1)}) %reduce-scatter.39.cloned.1.call-update) | async-done | bytes 786448 | tf_op jit(solution)/shard_map/reduce_scatter | solution.py:321
  1718.0 87.5 %reduce-scatter.49.cloned.1.call-done = bf16[256,2,1408]{2,0,1:T(8,128)(2,1)} async-done(((bf16[2048,2,1408]{2,0,1:T(8,128)(2,1)}), bf16[256,2,1408]{2,0,1:T(8,128)(2,1)}) %reduce-scatter.49.cloned.1.call-update) | async-done | bytes 1441808 | tf_op jit(solution)/shard_map/reduce_scatter | solution.py:339
  1805.5 90.7 %reduce-scatter.47.cloned.1.call-done = bf16[256,2,1408]{2,0,1:T(8,128)(2,1)} async-done(((bf16[2048,2,1408]{2,0,1:T(8,128)(2,1)}), bf16[256,2,1408]{2,0,1:T(8,128)(2,1)}) %reduce-scatter.47.cloned.1.call-update) | async-done | bytes 1441808 | tf_op jit(solution)/shard_map/reduce_scatter | solution.py:339
  1898.3 7.0 copy.176
  (631 shorter events, 436.1 us)
Async XLA Ops:
  7.2 51.6 %all-gather.29.cloned.1.call-start = ((), (), s32[]{:S(2)}) async-start(), calls=%async_computation.38 | async-start | bytes 7077888 | tf_op jit(solution)/shard_map/all_gather | solution.py:171
  10.1 76.5 %all-gather.25.cloned.1.call-start = ((), (), s32[]{:S(2)}) async-start(), calls=%async_computation.18 | async-start | bytes 1572864 | tf_op jit(solution)/shard_map/all_gather | solution.py:192
  55.1 187.1 %copy-start.62 = (f32[1,1,2048]{2,1,0:T(1,128)}, f32[1,1,2048]{2,1,0:T(1,128)S(1)}, u32[]{:S(2)}) copy-start(f32[1,1,2048]{2,1,0:T(1,128)S(1)} %get-tuple-element.633) | copy-start | bytes 24580
  65.2 52.1 %all-gather.31.cloned.1.call-start = ((), (), s32[]{:S(2)}) async-start(), calls=%async_computation.39 | async-start | bytes 2359296 | tf_op jit(solution)/shard_map/all_gather | solution.py:173
  66.1 106.5 %all-reduce.10.cloned.1.call-start = ((), (), s32[]{:S(2)}) async-start(), calls=%async_computation.19 | async-start | bytes 2097152 | tf_op jit(solution)/shard_map/psum | solution.py:56
  120.7 121.5 %all-gather.33.cloned.1.call-start = ((), (), s32[]{:S(2)}) async-start(), calls=%async_computation.40 | async-start | bytes 12976128 | tf_op jit(solution)/shard_map/all_gather | solution.py:174
  126.6 161.8 %all-gather.35.cloned.1.call-start = ((), (), s32[]{:S(2)}) async-start(), calls=%async_computation.41 | async-start | bytes 6488064 | tf_op jit(solution)/shard_map/all_gather | solution.py:175
  128.6 217.3 %all-reduce.12.cloned.1.call-start = ((), (), s32[]{:S(2)}) async-start(), calls=%async_computation.20 | async-start | bytes 2097152 | tf_op jit(solution)/shard_map/psum | solution.py:56
  174.8 73.8 %copy-start.48 = (f32[256]{0:T(256)}, f32[256]{0:T(256)S(1)}, u32[]{:S(2)}) copy-start(f32[256]{0:T(256)S(1)} %multiply_reduce_fusion.4) | copy-start | bytes 3076
  174.8 73.8 %copy-start.59 = (f32[256]{0:T(256)}, f32[256]{0:T(256)S(1)}, u32[]{:S(2)}) copy-start(f32[256]{0:T(256)S(1)} %fusion.229) | copy-start | bytes 3076
  293.9 99.4 %all-gather.37.cloned.1.call-start = ((), (), s32[]{:S(2)}) async-start(), calls=%async_computation.42 | async-start | bytes 7077888 | tf_op jit(solution)/shard_map/all_gather | solution.py:171
  294.6 135.4 %all-gather.27.cloned.1.call-start = ((), (), s32[]{:S(2)}) async-start(), calls=%async_computation.21 | async-start | bytes 1572864 | tf_op jit(solution)/shard_map/all_gather | solution.py:192
  335.6 57.6 %copy-start.66 = (f32[1,1,2048]{2,1,0:T(1,128)}, f32[1,1,2048]{2,1,0:T(1,128)S(1)}, u32[]{:S(2)}) copy-start(f32[1,1,2048]{2,1,0:T(1,128)S(1)} %get-tuple-element.630) | copy-start | bytes 24580
  348.2 49.7 %copy-start.50 = (f32[256]{0:T(256)}, f32[256]{0:T(256)S(1)}, u32[]{:S(2)}) copy-start(f32[256]{0:T(256)S(1)} %multiply_reduce_fusion.3) | copy-start | bytes 3076
  348.3 49.7 %copy-start.52 = (f32[256]{0:T(256)}, f32[256]{0:T(256)S(1)}, u32[]{:S(2)}) copy-start(f32[256]{0:T(256)S(1)} %fusion.230) | copy-start | bytes 3076
  408.5 62.7 %all-gather.39.cloned.1.call-start = ((), (), s32[]{:S(2)}) async-start(), calls=%async_computation.43 | async-start | bytes 2359296 | tf_op jit(solution)/shard_map/all_gather | solution.py:173
  409.1 117.4 %all-reduce.14.cloned.1.call-start = ((), (), s32[]{:S(2)}) async-start(), calls=%async_computation.22 | async-start | bytes 2097152 | tf_op jit(solution)/shard_map/psum | solution.py:56
  474.5 121.6 %all-gather.41.cloned.1.call-start = ((), (), s32[]{:S(2)}) async-start(), calls=%async_computation.44 | async-start | bytes 12976128 | tf_op jit(solution)/shard_map/all_gather | solution.py:174
  477.2 165.3 %all-gather.43.cloned.1.call-start = ((), (), s32[]{:S(2)}) async-start(), calls=%async_computation.45 | async-start | bytes 6488064 | tf_op jit(solution)/shard_map/all_gather | solution.py:175
  478.0 232.1 %all-reduce.16.cloned.1.call-start = ((), (), s32[]{:S(2)}) async-start(), calls=%async_computation.23 | async-start | bytes 2097152 | tf_op jit(solution)/shard_map/psum | solution.py:249
  529.7 183.8 %copy-start.42 = (f32[256]{0:T(256)}, f32[256]{0:T(256)S(1)}, u32[]{:S(2)}) copy-start(f32[256]{0:T(256)S(1)} %fusion.231) | copy-start | bytes 3076
  658.1 139.8 %reduce-scatter.31.cloned.1.call-start = ((), (), s32[]{:S(2)}) async-start(), calls=%async_computation.24 | async-start | bytes 786432 | tf_op jit(solution)/shard_map/reduce_scatter | solution.py:266
  783.8 31.4 %reduce-scatter.33.cloned.1.call-start = ((), (), s32[]{:S(2)}) async-start(), calls=%async_computation.25 | async-start | bytes 786432 | tf_op jit(solution)/shard_map/reduce_scatter | solution.py:269
  785.9 87.2 %all-reduce.18.cloned.1.call-start = ((), (), s32[]{:S(2)}) async-start(), calls=%async_computation.26 | async-start | bytes 2097152 | tf_op jit(solution)/shard_map/psum | solution.py:289
  821.1 53.8 %copy-start.51 = (f32[256]{0:T(256)S(1)}, f32[256]{0:T(256)}, u32[]{:S(2)}) copy-start(f32[256]{0:T(256)} %copy-done.50) | copy-start | bytes 3076
  821.1 53.8 %copy-start.53 = (f32[256]{0:T(256)S(1)}, f32[256]{0:T(256)}, u32[]{:S(2)}) copy-start(f32[256]{0:T(256)} %copy-done.52) | copy-start | bytes 3076
  821.1 121.9 %all-reduce.20.cloned.1.call-start = ((), (), s32[]{:S(2)}) async-start(), calls=%async_computation.27 | async-start | bytes 2097152 | tf_op jit(solution)/shard_map/psum | solution.py:249
  891.7 53.7 %copy-start.49 = (f32[256]{0:T(256)S(1)}, f32[256]{0:T(256)}, u32[]{:S(2)}) copy-start(f32[256]{0:T(256)} %copy-done.48) | copy-start | bytes 3076
  891.7 53.8 %copy-start.60 = (f32[256]{0:T(256)S(1)}, f32[256]{0:T(256)}, u32[]{:S(2)}) copy-start(f32[256]{0:T(256)} %copy-done.59) | copy-start | bytes 3076
  891.7 144.6 %reduce-scatter.35.cloned.1.call-start = ((), (), s32[]{:S(2)}) async-start(), calls=%async_computation.28 | async-start | bytes 786432 | tf_op jit(solution)/shard_map/reduce_scatter | solution.py:266
  1022.2 30.9 %reduce-scatter.37.cloned.1.call-start = ((), (), s32[]{:S(2)}) async-start(), calls=%async_computation.29 | async-start | bytes 786432 | tf_op jit(solution)/shard_map/reduce_scatter | solution.py:269
  1024.3 121.8 %all-reduce.22.cloned.1.call-start = ((), (), s32[]{:S(2)}) async-start(), calls=%async_computation.52 | async-start | bytes 4194304 | tf_op jit(solution)/shard_map/psum | solution.py:56
  1058.9 138.3 %reduce-scatter.65.cloned.1.call-start = ((), (), s32[]{:S(2)}) async-start(), calls=%async_computation.51 | async-start | bytes 589824
  1062.7 157.1 %reduce-scatter.61.cloned.1.call-start = ((), (), s32[]{:S(2)}) async-start(), calls=%async_computation.49 | async-start | bytes 589824
  1065.3 191.9 %reduce-scatter.57.cloned.1.call-start = ((), (), s32[]{:S(2)}) async-start(), calls=%async_computation.47 | async-start | bytes 589824
  1066.5 228.0 %reduce-scatter.63.cloned.1.call-start = ((), (), s32[]{:S(2)}) async-start(), calls=%async_computation.50 | async-start | bytes 589824
  1068.9 270.3 %reduce-scatter.45.cloned.1.call-start = ((), (), s32[]{:S(2)}) async-start(), calls=%async_computation.33 | async-start | bytes 2359296 | tf_op jit(solution)/shard_map/reduce_scatter | solution.py:333
  1072.2 311.4 %reduce-scatter.43.cloned.1.call-start = ((), (), s32[]{:S(2)}) async-start(), calls=%async_computation.32 | async-start | bytes 2359296 | tf_op jit(solution)/shard_map/reduce_scatter | solution.py:333
  1076.9 344.3 %reduce-scatter.59.cloned.1.call-start = ((), (), s32[]{:S(2)}) async-start(), calls=%async_computation.48 | async-start | bytes 589824
  1078.7 71.8 %copy-start.56 = (f32[256]{0:T(256)S(1)}, f32[256]{0:T(256)}, u32[]{:S(2)}) copy-start(f32[256]{0:T(256)} %copy-done.55) | copy-start | bytes 3076
  1078.7 71.8 %copy-start.58 = (f32[256]{0:T(256)S(1)}, f32[256]{0:T(256)}, u32[]{:S(2)}) copy-start(f32[256]{0:T(256)} %copy-done.57) | copy-start | bytes 3076
  1151.6 306.8 %reduce-scatter.55.cloned.1.call-start = ((), (), s32[]{:S(2)}) async-start(), calls=%async_computation.46 | async-start | bytes 589824
  1152.8 369.0 %reduce-scatter.53.cloned.1.call-start = ((), (), s32[]{:S(2)}) async-start(), calls=%async_computation.37 | async-start | bytes 6488064 | tf_op jit(solution)/shard_map/reduce_scatter | solution.py:345
  1159.3 424.9 %reduce-scatter.51.cloned.1.call-start = ((), (), s32[]{:S(2)}) async-start(), calls=%async_computation.36 | async-start | bytes 6488064 | tf_op jit(solution)/shard_map/reduce_scatter | solution.py:345
  1165.3 484.4 %reduce-scatter.41.cloned.1.call-start = ((), (), s32[]{:S(2)}) async-start(), calls=%async_computation.31 | async-start | bytes 7077888 | tf_op jit(solution)/shard_map/reduce_scatter | solution.py:321
  1172.0 542.7 %reduce-scatter.39.cloned.1.call-start = ((), (), s32[]{:S(2)}) async-start(), calls=%async_computation.30 | async-start | bytes 7077888 | tf_op jit(solution)/shard_map/reduce_scatter | solution.py:321
  1177.8 627.7 %reduce-scatter.49.cloned.1.call-start = ((), (), s32[]{:S(2)}) async-start(), calls=%async_computation.35 | async-start | bytes 12976128 | tf_op jit(solution)/shard_map/reduce_scatter | solution.py:339
  1186.9 709.3 %reduce-scatter.47.cloned.1.call-start = ((), (), s32[]{:S(2)}) async-start(), calls=%async_computation.34 | async-start | bytes 12976128 | tf_op jit(solution)/shard_map/reduce_scatter | solution.py:339
  (76 other events, 386.0 us)
Sparse Core Ops, SparseCore 0:
  10.5 48.2 all-gather.28
  65.3 21.2 all-gather.24
  89.1 28.1 all-gather.30
  120.7 51.7 all-reduce.9
  175.1 67.0 all-gather.32
  244.1 44.3 all-gather.34
  294.0 51.7 all-reduce.11
  348.3 44.8 all-gather.36
  408.6 21.3 all-gather.26
  431.7 28.2 all-gather.38
  474.7 51.7 all-reduce.13
  529.0 67.0 all-gather.40
  598.1 44.3 all-gather.42
  658.2 51.7 all-reduce.15
  783.9 13.9 reduce-scatter.30
  800.6 14.5 reduce-scatter.32
  821.2 51.7 all-reduce.17
  891.8 51.1 all-reduce.19
  1022.3 13.9 reduce-scatter.34
  1038.4 14.5 reduce-scatter.36
  1059.0 87.0 all-reduce.21
  1149.5 33.1 reduce-scatter.64
  1185.7 34.1 reduce-scatter.60
  1223.1 34.1 reduce-scatter.56
  1260.3 34.1 reduce-scatter.62
  1298.0 41.2 reduce-scatter.44
  1342.4 41.2 reduce-scatter.42
  1387.0 34.1 reduce-scatter.58
  1424.3 34.1 reduce-scatter.54
  1462.7 59.0 reduce-scatter.52
  1525.2 59.0 reduce-scatter.50
  1588.0 61.7 reduce-scatter.40
  1653.0 61.7 reduce-scatter.38
  1718.7 86.7 reduce-scatter.48
  1809.4 86.7 reduce-scatter.46
where the time goes:
time: 1930 us; the launch traced here: 1910 us
  waiting for transfers between devices  1320 us (68%)
  matrix products  293 us (15%)
  local copies, waits for them, and re-layouts  114 us (6%)
  blocking collectives  95.1 us (5%)
  other arithmetic  66.9 us (3%)
    reduce_scatter x2, waiting for transfers between devices, local(): lax.psum_scatter(weight_terms[5].astype(jnp.bfloat16), ('fsdp', 'ctx'), s...  178 us
    psum x4, waiting for transfers between devices, branch_sum(): return lax.psum(partial_out.astype(jnp.bfloat16), 'tp').astype(jnp.float32)  170 us
    unnamed x41, waiting for transfers between devices  164 us
    all_gather x2, waiting for transfers between devices, local(): lax.all_gather(gate_up_weight[layer_index], ('fsdp', 'ctx'), axis=0, tile...  134 us
    reduce_scatter x2, waiting for transfers between devices, local(): lax.psum_scatter(weight_terms[2].astype(jnp.bfloat16), ('fsdp', 'ctx'), s...  127 us
    reduce_scatter x2, waiting for transfers between devices, local(): lax.psum_scatter(weight_terms[6].astype(jnp.bfloat16), ('fsdp', 'ctx'), s...  124 us
    psum x2, waiting for transfers between devices, local(): lax.psum(jnp.einsum('scf,dcf->sd', d_gate_up, w_gate_up, preferred_elemen...  103 us
    reduce_scatter x2, waiting for transfers between devices, local(): lax.psum_scatter(weight_terms[4].astype(jnp.bfloat16), ('fsdp', 'ctx'), s...  75.9 us
  transfers between devices with their start and end apart: 35, of which 33 were waited for; matrix products, arithmetic and copies ran while one was open for 11% of the time, Pallas kernels for 0%

commit v1 on v0

v1 whole, which is shorter than its diff:
```python
import functools

import jax
import jax.numpy as jnp
from jax import lax
from jax.experimental import pallas as pl
from jax.experimental.pallas import tpu as pltpu
from jax.sharding import PartitionSpec as P

HD = 64
ROT = 16
LANES = 128
VMEM_LIMIT = 48 * 1024 * 1024
NN = (((1,), (0,)), ((), ()))
NT = (((1,), (1,)), ((), ()))
TN = (((0,), (0,)), ((), ()))
BF = jnp.bfloat16
F32 = jnp.float32


def mm(lhs, rhs, dims):
    return lax.dot_general(lhs, rhs, dims, preferred_element_type=F32)


def spec_vmem():
    return pl.BlockSpec(memory_space=pltpu.VMEM)


def spec_any():
    return pl.BlockSpec(memory_space=pl.ANY)


def spec_smem():
    return pl.BlockSpec(memory_space=pltpu.SMEM)


def call(body, outs, args, specs, scratch, flops, name, out_specs=None):
    moved = sum(a.size * a.dtype.itemsize for a in args) + sum(
        o.size * jnp.dtype(o.dtype).itemsize for o in outs
    )
    return pl.pallas_call(
        body,
        out_shape=outs,
        in_specs=specs,
        out_specs=out_specs if out_specs is not None else [spec_vmem()] * len(outs),
        scratch_shapes=scratch,
        compiler_params=pltpu.CompilerParams(vmem_limit_bytes=VMEM_LIMIT),
        cost_estimate=pl.CostEstimate(flops=flops, bytes_accessed=moved, transcendentals=0),
        name=name,
    )(*args)


def shape(dims, dtype):
    return jax.ShapeDtypeStruct(tuple(dims), dtype)


def weight_copies(offs, pieces, held, sems, matrices):
    copies = []
    for slot, matrix in enumerate(matrices):
        row = []
        for index, piece in enumerate(pieces):
            start = pl.multiple_of(offs[index], LANES)
            row.append(
                pltpu.make_async_copy(
                    piece.at[matrix],
                    held.at[slot, pl.ds(start, piece.shape[1]), :],
                    sems.at[slot, index],
                )
            )
        copies.append(row)
    for row in copies:
        for copy in row:
            copy.start()
    return copies


def finish(copies):
    for copy in copies:
        copy.wait()


def normalized(v):
    centered = v - jnp.mean(v, axis=1, keepdims=True)
    variance = jnp.mean(centered * centered, axis=1, keepdims=True)
    scale = lax.rsqrt(variance + 1e-05)
    return centered * scale, scale


def norm_back(v, cot, gain):
    n, scale = normalized(v)
    e = cot * gain
    grad = scale * (
        e - jnp.mean(e, axis=1, keepdims=True) - n * jnp.mean(e * n, axis=1, keepdims=True)
    )
    return grad, n


def turn(tile, tables, sign):
    return (
        tile * tables[0]
        + sign * (pltpu.roll(tile, 8, 1) * tables[1] + pltpu.roll(tile, LANES - 8, 1) * tables[2])
    )


def turn_wide(wide, tables, sign):
    tabs = (tables[0], tables[1], tables[2])
    return jnp.concatenate(
        [
            turn(wide[:, at : at + LANES], tabs, sign)
            for at in range(0, wide.shape[1], LANES)
        ],
        axis=1,
    )


def qkv_body(n_pieces, has_delta, *refs):
    refs = list(refs)
    offs = refs.pop(0)
    base = refs.pop(0)
    delta = refs.pop(0) if has_delta else None
    gain, shift, bias, tables = refs[:4]
    pieces = refs[4 : 4 + n_pieces]
    rest = refs[4 + n_pieces :]
    if has_delta:
        stream_out = rest.pop(0)
    first_out, q_out, k_out, v_out, held, sems = rest
    copies = weight_copies(offs, pieces, held, sems, (0, 1, 2))
    stream = base[...].astype(F32)
    if has_delta:
        stream = stream + delta[...].astype(F32)
        stream_out[...] = stream
    n, _ = normalized(stream)
    first_out[...] = (n * gain[...] + shift[...]).astype(BF)
    for index, out in enumerate((q_out, k_out, v_out)):
        finish(copies[index])
        part = mm(first_out[...], held[index], NN) + bias[index : index + 1, :]
        if index < 2:
            part = turn_wide(part, tables, 1.0)
        out[...] = part.astype(BF)


def attend_body(n_pieces, n_blocks, *refs):
    offs, q_ref = refs[:2]
    ks = refs[2 : 2 + n_blocks]
    vs = refs[2 + n_blocks : 2 + 2 * n_blocks]
    masks = refs[2 + 2 * n_blocks : 2 + 3 * n_blocks]
    pieces = refs[2 + 3 * n_blocks : 2 + 3 * n_blocks + n_pieces]
    mixed_out, total_out, part_out, held, sems = refs[2 + 3 * n_blocks + n_pieces :]
    copies = weight_copies(offs, pieces, held, sems, (3,))
    for head in range(q_ref.shape[1] // HD):
        span = slice(head * HD, (head + 1) * HD)
        query = q_ref[:, span]
        scores = [
            mm(k[:, span], query, NT) * (1.0 / HD**0.5) + mask[...]
            for k, mask in zip(ks, masks, strict=True)
        ]
        top = functools.reduce(
            jnp.maximum, [jnp.max(s, axis=0, keepdims=True) for s in scores]
        )
        exps = [jnp.exp(s - top) for s in scores]
        total = functools.reduce(jnp.add, [jnp.sum(e, axis=0, keepdims=True) for e in exps])
        inverse = 1.0 / total
        result = functools.reduce(
            jnp.add,
            [mm((e * inverse).astype(BF), v[:, span], TN) for e, v in zip(exps, vs, strict=True)],
        )
        total_out[head : head + 1, :] = top + jnp.log(total)
        mixed_out[:, span] = result.astype(BF)
    finish(copies[0])
    part_out[...] = mm(mixed_out[...], held[0], NT).astype(BF)


def mlp_body(n_pieces, *refs):
    offs, base, delta, gain, shift = refs[:5]
    pieces = refs[5 : 5 + n_pieces]
    mid_out, second_out, gate_out, up_out, hidden_out, part_out, held, sems = refs[5 + n_pieces :]
    copies = weight_copies(offs, pieces, held, sems, (0, 1, 2))
    stream = base[...].astype(F32) + delta[...].astype(F32)
    mid_out[...] = stream
    n, _ = normalized(stream)
    second_out[...] = (n * gain[...] + shift[...]).astype(BF)
    finish(copies[0])
    gate = mm(second_out[...], held[0], NN)
    gate_out[...] = gate.astype(BF)
    act = gate * jax.nn.sigmoid(gate)
    finish(copies[1])
    up = mm(second_out[...], held[1], NN)
    up_out[...] = up.astype(BF)
    hidden_out[...] = (act * up).astype(BF)
    finish(copies[2])
    part_out[...] = mm(hidden_out[...], held[2], NT).astype(BF)


def mlp_back_body(n_pieces, *refs):
    offs, grad_in, gate_ref, up_ref = refs[:4]
    pieces = refs[4 : 4 + n_pieces]
    d_mlp_out, d_gate_out, d_up_out, part_out, held, sems = refs[4 + n_pieces :]
    copies = weight_copies(offs, pieces, held, sems, (2, 0, 1))
    d_mlp_out[...] = grad_in[...].astype(BF)
    gate = gate_ref[...].astype(F32)
    sig = jax.nn.sigmoid(gate)
    finish(copies[0])
    d_hidden = mm(d_mlp_out[...], held[0], NN)
    d_up_out[...] = (d_hidden * (gate * sig)).astype(BF)
    d_gate_out[...] = (
        d_hidden * up_ref[...].astype(F32) * (sig * (1.0 + gate * (1.0 - sig)))
    ).astype(BF)
    finish(copies[1])
    part = mm(d_gate_out[...], held[1], NT)
    finish(copies[2])
    part_out[...] = (part + mm(d_up_out[...], held[2], NT)).astype(BF)


def attend_back_body(n_pieces, n_blocks, *refs):
    offs, mid, cot, gain, grad_in, tables, q_ref, total_ref = refs[:8]
    at = 8
    ks = refs[at : at + n_blocks]
    vs = refs[at + n_blocks : at + 2 * n_blocks]
    masks = refs[at + 2 * n_blocks : at + 3 * n_blocks]
    at += 3 * n_blocks
    pieces = refs[at : at + n_pieces]
    at += n_pieces
    grad_out, d_attn_out, sums_out, dq_out = refs[at : at + 4]
    dkv_outs = refs[at + 4 : at + 4 + n_blocks]
    held, d_mixed, sems = refs[at + 4 + n_blocks :]
    copies = weight_copies(offs, pieces, held, sems, (3,))
    c = cot[...].astype(F32)
    grad, n = norm_back(mid[...], c, gain[...])
    sums_out[0:1, :] = jnp.sum(n * c, axis=0, keepdims=True)
    sums_out[1:2, :] = jnp.sum(c, axis=0, keepdims=True)
    grad = grad_in[...].astype(F32) + grad
    grad_out[...] = grad
    d_attn_out[...] = grad.astype(BF)
    finish(copies[0])
    d_mixed[...] = mm(d_attn_out[...], held[0], NN).astype(BF)
    d_queries = []
    for head in range(q_ref.shape[1] // HD):
        span = slice(head * HD, (head + 1) * HD)
        query = q_ref[:, span]
        d_out = d_mixed[:, span]
        log_total = total_ref[head : head + 1, :]
        probs = [
            jnp.exp(mm(k[:, span], query, NT) * (1.0 / HD**0.5) + mask[...] - log_total)
            for k, mask in zip(ks, masks, strict=True)
        ]
        d_probs = [mm(v[:, span], d_out, NT) for v in vs]
        delta = functools.reduce(
            jnp.add,
            [
                jnp.sum(p * dp, axis=0, keepdims=True)
                for p, dp in zip(probs, d_probs, strict=True)
            ],
        )
        d_scores = [
            (p * (dp - delta)).astype(BF) for p, dp in zip(probs, d_probs, strict=True)
        ]
        d_query = functools.reduce(
            jnp.add, [mm(ds, k[:, span], TN) for ds, k in zip(d_scores, ks, strict=True)]
        )
        d_queries.append(d_query * (1.0 / HD**0.5))
        for ds, p, dkv in zip(d_scores, probs, dkv_outs, strict=True):
            dkv[0, :, span] = (mm(ds, query, NN) * (1.0 / HD**0.5)).astype(dkv.dtype)
            dkv[1, :, span] = mm(p.astype(BF), d_out, NN).astype(dkv.dtype)
    dq_out[...] = turn_wide(jnp.concatenate(d_queries, axis=1), tables, -1.0).astype(BF)


def qkv_back_body(n_pieces, has_other, *refs):
    refs = list(refs)
    offs, dq_ref, own = refs[:3]
    refs = refs[3:]
    other = refs.pop(0) if has_other else None
    tables, stream, n_ref_unused = refs[:3]
    pieces = refs[3 : 3 + n_pieces]
    d_qkv_out, bias_out, part_out, sums_out, held, sems = refs[3 + n_pieces :]
    copies = weight_copies(offs, pieces, held, sems, (0, 1, 2))
    d_key = own[0].astype(F32)
    d_value = own[1].astype(F32)
    if has_other:
        d_key = d_key + other[0].astype(F32)
        d_value = d_value + other[1].astype(F32)
    d_qkv_out[0] = dq_ref[...]
    d_qkv_out[1] = turn_wide(d_key, tables, -1.0).astype(BF)
    d_qkv_out[2] = d_value.astype(BF)
    for index in range(3):
        bias_out[index : index + 1, :] = jnp.sum(
            d_qkv_out[index].astype(F32), axis=0, keepdims=True
        )
    part = None
    for index in range(3):
        finish(copies[index])
        term = mm(d_qkv_out[index], held[index], NT)
        part = term if part is None else part + term
    part_out[...] = part.astype(BF)
    n, _ = normalized(stream[...].astype(F32))
    sums_out[0:1, :] = jnp.sum(n * part, axis=0, keepdims=True)
    sums_out[1:2, :] = jnp.sum(part, axis=0, keepdims=True)


def norm_back_body(stream, cot, gain, grad_in, grad_out):
    grad, _ = norm_back(stream[...].astype(F32), cot[...].astype(F32), gain[...])
    grad_out[...] = grad_in[...] + grad


def weight_grad_body(n_left, n_right, pairs, *refs):
    ids = refs[0]
    n_in = n_left + n_right
    own = refs[1 : 1 + n_in]
    peer = refs[1 + n_in : 1 + 2 * n_in]
    outs = refs[1 + 2 * n_in : 6 + 2 * n_in]
    held = refs[6 + 2 * n_in : 6 + 3 * n_in]
    stage, in_sems, out_sems = refs[6 + 3 * n_in :]
    rows = own[0].shape[0]
    loads = []
    for index in range(n_in):
        for part, source in enumerate((own[index], peer[index])):
            copy = pltpu.make_async_copy(
                source,
                held[index].at[pl.ds(part * rows, rows), :],
                in_sems.at[index, part],
            )
            copy.start()
            loads.append(copy)
    finish(loads)
    half = stage.shape[2]
    own_out, x1, y1, x2, y2 = outs
    targets = (
        (x1.at[0], y1.at[0]),
        (x1.at[1], x2),
        (y2, y1.at[1]),
        (own_out.at[0], own_out.at[1]),
    )
    stores = []
    for block in range(4):
        start = pl.multiple_of(ids[block], LANES)
        for matrix, (left, right) in enumerate(pairs):
            lhs = held[left][:, pl.ds(start, 2 * half)]
            result = mm(lhs, held[n_left + right][...], TN).astype(BF)
            stage[2 * block, matrix] = result[:half]
            stage[2 * block + 1, matrix] = result[half:]
        for part in range(2):
            copy = pltpu.make_async_copy(
                stage.at[2 * block + part], targets[block][part], out_sems.at[block, part]
            )
            copy.start()
            stores.append(copy)
    finish(stores)


def pairs_of(axis, bit):
    return [(index, index ^ bit) for index in range(lax.axis_size(axis))]


def swap_x(array):
    return lax.ppermute(array, "fsdp", pairs_of("fsdp", 2))


def swap_core(array):
    return lax.ppermute(array, "fsdp", pairs_of("fsdp", 1))


def swap_y(array):
    return lax.ppermute(array, "ctx", pairs_of("ctx", 1))


def place():
    fsdp = lax.axis_index("fsdp")
    return fsdp // 2, fsdp % 2, lax.axis_index("ctx")


def gather_pieces(shard, fast):
    if not fast:
        whole = lax.all_gather(shard, ("fsdp", "ctx"), axis=1, tiled=True)
        return [whole], jnp.zeros((1,), jnp.int32)
    rows = shard.shape[1]
    half = rows // 2
    from_x = swap_x(shard)
    from_y = swap_y(shard)
    far_low = swap_x(from_y[:, :half])
    far_high = swap_y(from_x[:, half:])
    mine = [shard, from_x, from_y, far_low, far_high]
    peers = [swap_core(piece) for piece in mine]
    x, core, y = place()

    def row(x_at, core_at, y_at):
        return ((x_at * 2 + core_at) * 2 + y_at) * rows

    offs = []
    for core_at in (core, 1 - core):
        offs += [
            row(x, core_at, y),
            row(1 - x, core_at, y),
            row(x, core_at, 1 - y),
            row(1 - x, core_at, 1 - y),
            row(1 - x, core_at, 1 - y) + half,
        ]
    return mine + peers, jnp.stack(offs).astype(jnp.int32)


def gather_small(packed, fast):
    if not fast:
        return lax.all_gather(packed, ("fsdp", "ctx"), axis=1, tiled=True)
    x, core, y = place()

    def join(array, other, bit):
        return jnp.where(
            bit == 0, jnp.stack([array, other]), jnp.stack([other, array])
        )

    held = join(packed, swap_y(packed), y)
    held = join(held, swap_core(held), core)
    held = join(held, swap_x(held), x)
    rows, cols = packed.shape
    return held.reshape(8, rows, cols).transpose(1, 0, 2).reshape(rows, 8 * cols)


def reduce_small(sums, fast):
    if not fast:
        part = lax.psum_scatter(sums, ("fsdp", "ctx"), scatter_dimension=1, tiled=True)
        return lax.psum(part, "tp")
    x, core, y = place()
    rows, width = sums.shape
    held = sums.reshape(rows, 2, 2, 2, width // 8).transpose(1, 2, 3, 0, 4)
    for bit, swap in ((x, swap_x), (core, swap_core), (y, swap_y)):
        keep = jnp.where(bit == 0, held[0], held[1])
        send = jnp.where(bit == 0, held[1], held[0])
        held = keep + swap(send)
    tensor_size = lax.axis_size("tp")
    step = 1
    while step < tensor_size:
        held = held + lax.ppermute(held, "tp", pairs_of("tp", step))
        step *= 2
    return held


def tensor_sum(part):
    return lax.psum(part, "tp")


def weight_grads(lefts, rights, pairs, fast, name):
    n_left, n_right = len(lefts), len(rights)
    columns = rights[0].shape[1]
    tokens, width = lefts[0].shape
    if not fast:
        whole = jnp.stack([mm(lefts[a], rights[b], TN).astype(BF) for a, b in pairs])
        return lax.psum_scatter(
            whole, ("fsdp", "ctx"), scatter_dimension=1, tiled=True
        ).astype(F32)
    own = list(lefts) + list(rights)
    peer = [swap_core(array) for array in own]
    rows = width // 8
    half = rows // 2
    x, core, y = place()
    ids = jnp.stack(
        [
            ((x_at * 2 + core) * 2 + y_at) * rows
            for x_at, y_at in ((1 - x, 1 - y), (1 - x, y), (x, 1 - y), (x, y))
        ]
    ).astype(jnp.int32)
    k = len(pairs)
    block = (k, half, columns)
    outs = [
        shape((2,) + block, BF),
        shape((2,) + block, BF),
        shape((2,) + block, BF),
        shape(block, BF),
        shape(block, BF),
    ]
    scratch = [pltpu.VMEM((2 * tokens, array.shape[1]), BF) for array in own]
    scratch += [
        pltpu.VMEM((8,) + block, BF),
        pltpu.SemaphoreType.DMA((n_left + n_right, 2)),
        pltpu.SemaphoreType.DMA((4, 2)),
    ]
    own_sum, x1, y1, x2, y2 = call(
        functools.partial(weight_grad_body, n_left, n_right, pairs),
        outs,
        [ids] + own + peer,
        [spec_smem()] + [spec_any()] * (2 * len(own)),
        scratch,
        2 * 2 * tokens * (4 * rows) * columns * k,
        name,
        [spec_any()] * 5,
    )
    got_x1 = swap_x(x1)
    got_y1 = swap_y(y1)
    got_x2 = swap_x((x2.astype(F32) + got_y1[0].astype(F32)).astype(BF))
    got_y2 = swap_y((y2.astype(F32) + got_x1[0].astype(F32)).astype(BF))
    low = own_sum[0].astype(F32) + got_x1[1].astype(F32) + got_y2.astype(F32)
    high = own_sum[1].astype(F32) + got_y1[1].astype(F32) + got_x2.astype(F32)
    return jnp.concatenate([low, high], axis=1)


def layout(lengths, first_row, row_count):
    token_index = first_row + jnp.arange(row_count, dtype=jnp.int32)
    doc_ends = jnp.cumsum(lengths)
    starts = doc_ends - lengths
    segment = jnp.sum(
        (token_index[:, None] >= doc_ends[None, :]).astype(jnp.int32), axis=1, dtype=jnp.int32
    )
    doc_begin = jnp.max(
        jnp.where(token_index[:, None] >= starts[None, :], starts[None, :], 0), axis=1
    )
    return (segment, token_index - doc_begin, token_index)


def rotary_tables(position):
    frequency = 10000.0 ** (-jnp.arange(0, ROT, 2, dtype=F32) / ROT)
    angles = position.astype(F32)[:, None] * frequency[None, :]
    cos, sin = jnp.cos(angles), jnp.sin(angles)
    rows = position.shape[0]
    blank = jnp.zeros((rows, ROT // 2), F32)
    rest = HD - ROT
    keep = jnp.concatenate([cos, cos, jnp.ones((rows, rest), F32)], axis=1)
    below = jnp.concatenate([blank, sin, jnp.zeros((rows, rest), F32)], axis=1)
    above = jnp.concatenate([-sin, blank, jnp.zeros((rows, rest), F32)], axis=1)
    return jnp.stack([jnp.tile(t, (1, LANES // HD)) for t in (keep, below, above)])


def local(
    tokens,
    cotangent,
    doc_lengths,
    norm_gains,
    norm_biases,
    qkv_weight,
    qkv_bias,
    out_weight,
    gate_up_weight,
    down_weight,
):
    rows = tokens.shape[1]
    width = tokens.shape[2]
    heads_width = qkv_weight.shape[3]
    hidden_width = gate_up_weight.shape[3]
    heads = heads_width // HD
    layers = norm_gains.shape[0]
    ctx_size = lax.axis_size("ctx")
    fast = lax.axis_size("fsdp") == 4 and ctx_size == 2
    ctx_rank = lax.axis_index("ctx")
    tensor_rank = lax.axis_index("tp")

    small = jnp.concatenate(
        [
            norm_gains.reshape(2 * layers, -1),
            norm_biases.reshape(2 * layers, -1),
            qkv_bias.reshape(3 * layers, -1),
        ]
    )
    small = gather_small(small, fast).astype(F32)
    gains = small[: 2 * layers].reshape(layers, 2, width)
    shifts = small[2 * layers : 4 * layers].reshape(layers, 2, width)
    biases = lax.dynamic_slice_in_dim(
        small[4 * layers :], tensor_rank * heads_width, heads_width, 1
    ).reshape(layers, 3, heads_width)
    attn_groups, mlp_groups = [], []
    for layer in range(layers):
        attn_groups.append(
            gather_pieces(
                jnp.concatenate(
                    [qkv_weight[layer].transpose(1, 0, 2), out_weight[layer].T[None]]
                ),
                fast,
            )
        )
        mlp_groups.append(
            gather_pieces(
                jnp.concatenate(
                    [gate_up_weight[layer].transpose(1, 0, 2), down_weight[layer].T[None]]
                ),
                fast,
            )
        )

    lengths = doc_lengths[0]
    seg_query, pos_query, index_query = layout(lengths, ctx_rank * rows, rows)
    tables = rotary_tables(pos_query)

    def mask_of(first, count, usable):
        seg_key, _, index_key = layout(lengths, first, count)
        allowed = (seg_query[None, :] == seg_key[:, None]) & (
            index_query[None, :] >= index_key[:, None]
        )
        return jnp.where(allowed & usable, 0.0, -1e30).astype(F32)

    if fast:
        masks = [
            mask_of(jnp.int32(0), rows, ctx_rank > 0),
            mask_of(ctx_rank * rows, rows, True),
        ]
    else:
        masks = [mask_of(jnp.int32(0), rows * ctx_size, True)]
    n_blocks = len(masks)

    def weight_scratch(count, columns, n_pieces):
        return [
            pltpu.VMEM((count, width, columns), BF),
            pltpu.SemaphoreType.DMA((count, n_pieces)),
        ]

    base, delta = tokens[0], None
    saved = []
    for layer in range(layers):
        pieces, offs = attn_groups[layer]
        n_pieces = len(pieces)
        args = [offs, base] + ([] if delta is None else [delta])
        args += [gains[layer, 0][None], shifts[layer, 0][None], biases[layer], tables]
        outs = [] if delta is None else [shape((rows, width), F32)]
        outs += [shape((rows, width), BF)] + [shape((rows, heads_width), BF)] * 3
        results = call(
            functools.partial(qkv_body, n_pieces, delta is not None),
            outs,
            args + pieces,
            [spec_smem()] + [spec_vmem()] * (len(args) - 1) + [spec_any()] * n_pieces,
            weight_scratch(3, heads_width, n_pieces),
            2 * rows * width * heads_width * 3,
            "qkv",
        )
        stream = base if delta is None else results[0]
        first_in, queries, keys, values = results[-4:]
        if fast:
            kv = jnp.stack([keys, values])
            prev = lax.ppermute(kv, "ctx", [(0, 1)])
            key_blocks, value_blocks = [prev[0], keys], [prev[1], values]
        else:
            kv = lax.all_gather(jnp.stack([keys, values]), "ctx", axis=1, tiled=True)
            key_blocks, value_blocks = [kv[0]], [kv[1]]
        args = [offs, queries] + key_blocks + value_blocks + masks
        mixed, log_total, part = call(
            functools.partial(attend_body, n_pieces, n_blocks),
            [
                shape((rows, heads_width), BF),
                shape((heads, rows), F32),
                shape((rows, width), BF),
            ],
            args + pieces,
            [spec_smem()] + [spec_vmem()] * (len(args) - 1) + [spec_any()] * n_pieces,
            weight_scratch(1, heads_width, n_pieces),
            2 * rows * width * heads_width + 4 * rows * rows * n_blocks * heads_width,
            "attend",
        )
        delta = tensor_sum(part)
        pieces, offs = mlp_groups[layer]
        n_pieces = len(pieces)
        args = [offs, stream, delta, gains[layer, 1][None], shifts[layer, 1][None]]
        mid, second_in, gate, up, hidden, part = call(
            functools.partial(mlp_body, n_pieces),
            [
                shape((rows, width), F32),
                shape((rows, width), BF),
                shape((rows, hidden_width), BF),
                shape((rows, hidden_width), BF),
                shape((rows, hidden_width), BF),
                shape((rows, width), BF),
            ],
            args + pieces,
            [spec_smem()] + [spec_vmem()] * 4 + [spec_any()] * n_pieces,
            weight_scratch(3, hidden_width, n_pieces),
            2 * rows * width * hidden_width * 3,
            "mlp",
        )
        delta = tensor_sum(part)
        saved.append(
            (stream, first_in, queries, key_blocks, value_blocks, mixed, log_total)
            + (mid, second_in, gate, up, hidden)
        )
        base = mid
    output = (base + delta.astype(F32)).astype(BF)[None]

    grad_stream = cotangent[0]
    grads = [None] * layers
    sums = [None] * layers
    on_first = (tensor_rank == 0).astype(F32)
    for layer in reversed(range(layers)):
        (stream, first_in, queries, key_blocks, value_blocks, mixed, log_total) = saved[layer][:7]
        (mid, second_in, gate, up, hidden) = saved[layer][7:]
        pieces, offs = mlp_groups[layer]
        n_pieces = len(pieces)
        d_mlp, d_gate, d_up, part = call(
            functools.partial(mlp_back_body, n_pieces),
            [
                shape((rows, width), BF),
                shape((rows, hidden_width), BF),
                shape((rows, hidden_width), BF),
                shape((rows, width), BF),
            ],
            [offs, grad_stream, gate, up] + pieces,
            [spec_smem()] + [spec_vmem()] * 3 + [spec_any()] * n_pieces,
            weight_scratch(3, hidden_width, n_pieces),
            2 * rows * width * hidden_width * 3,
            "mlp_back",
        )
        d_second = tensor_sum(part)
        mlp_grad = weight_grads(
            [second_in, d_mlp], [d_gate, d_up, hidden], ((0, 0), (0, 1), (1, 2)), fast, "mlp_grads"
        )
        pieces, offs = attn_groups[layer]
        n_pieces = len(pieces)
        args = [offs, mid, d_second, gains[layer, 1][None], grad_stream, tables, queries]
        args += [log_total] + key_blocks + value_blocks + masks
        kv_outs = [shape((2,) + block.shape, BF) for block in key_blocks]
        if fast:
            kv_outs[-1] = shape((2, rows, heads_width), F32)
        results = call(
            functools.partial(attend_back_body, n_pieces, n_blocks),
            [
                shape((rows, width), F32),
                shape((rows, width), BF),
                shape((2, width), F32),
                shape((rows, heads_width), BF),
            ]
            + kv_outs,
            args + pieces,
            [spec_smem()] + [spec_vmem()] * (len(args) - 1) + [spec_any()] * n_pieces,
            weight_scratch(1, heads_width, n_pieces)[:1]
            + [pltpu.VMEM((rows, heads_width), BF)]
            + weight_scratch(1, heads_width, n_pieces)[1:],
            2 * rows * width * heads_width + 10 * rows * rows * n_blocks * heads_width,
            "attend_back",
        )
        grad_mid, d_attn, sums_two, d_query = results[:4]
        if fast:
            own = results[5]
            other = [lax.ppermute(results[4], "ctx", [(1, 0)])]
        else:
            own = lax.psum_scatter(results[4], "ctx", scatter_dimension=1, tiled=True)
            other = []
        args = [offs, d_query, own] + other + [tables, stream, gains[layer, 0][None]]
        d_qkv, bias_sums, part, sums_one = call(
            functools.partial(qkv_back_body, n_pieces, fast),
            [
                shape((3, rows, heads_width), BF),
                shape((3, heads_width), F32),
                shape((rows, width), BF),
                shape((2, width), F32),
            ],
            args + pieces,
            [spec_smem()] + [spec_vmem()] * (len(args) - 1) + [spec_any()] * n_pieces,
            weight_scratch(3, heads_width, n_pieces),
            2 * rows * width * heads_width * 3,
            "qkv_back",
        )
        d_first = tensor_sum(part)
        attn_grad = weight_grads(
            [first_in, d_attn],
            [d_qkv[0], d_qkv[1], d_qkv[2], mixed],
            ((0, 0), (0, 1), (0, 2), (1, 3)),
            fast,
            "attn_grads",
        )
        (grad_stream,) = call(
            norm_back_body,
            [shape((rows, width), F32)],
            [stream, d_first, gains[layer, 0][None], grad_mid],
            [spec_vmem()] * 4,
            [],
            20 * rows * width,
            "norm_back",
        )
        bias_rows = lax.dynamic_update_slice_in_dim(
            jnp.zeros((3, width), F32), bias_sums, tensor_rank * heads_width, 1
        )
        sums[layer] = jnp.concatenate(
            [
                sums_one[0:1],
                sums_two[0:1] * on_first,
                sums_one[1:2],
                sums_two[1:2] * on_first,
                bias_rows,
            ]
        )
        grads[layer] = (
            attn_grad[:3].transpose(1, 0, 2),
            attn_grad[3].T,
            mlp_grad[:2].transpose(1, 0, 2),
            mlp_grad[2].T,
        )
    totals = reduce_small(jnp.concatenate(sums), fast).reshape(layers, 7, -1)
    stacked = [jnp.stack([terms[member] for terms in grads]) for member in range(4)]
    return (
        output,
        grad_stream[None],
        totals[:, 0:2],
        totals[:, 2:4],
        stacked[0],
        totals[:, 4:7],
        stacked[1],
        stacked[2],
        stacked[3],
    )


def solution(mesh):
    return jax.shard_map(
        local,
        mesh=mesh,
        in_specs=(
            P("fsdp", "ctx", None),
            P("fsdp", "ctx", None),
            P("fsdp", None),
            P(None, None, ("fsdp", "ctx")),
            P(None, None, ("fsdp", "ctx")),
            P(None, ("fsdp", "ctx"), None, "tp"),
            P(None, None, ("fsdp", "ctx")),
            P(None, "tp", ("fsdp", "ctx")),
            P(None, ("fsdp", "ctx"), None, "tp"),
            P(None, "tp", ("fsdp", "ctx")),
        ),
        out_specs=(
            P("fsdp", "ctx", None),
            P("fsdp", "ctx", None),
            P(None, None, ("fsdp", "ctx")),
            P(None, None, ("fsdp", "ctx")),
            P(None, ("fsdp", "ctx"), None, "tp"),
            P(None, None, ("fsdp", "ctx")),
            P(None, "tp", ("fsdp", "ctx")),
            P(None, ("fsdp", "ctx"), None, "tp"),
            P(None, "tp", ("fsdp", "ctx")),
        ),
        check_vma=False,
    )
```

time: 1930 us -> 938 us (0.49)
  waiting for transfers between devices: 1320 us -> 530 us
  matrix products: 293 us -> 0 us
  Pallas kernels: 0 us -> 149 us
  blocking collectives: 95.1 us -> 0 us
  starting transfers between devices: 2.76 us -> 64.2 us
    reduce_scatter x12 -> x0, waiting for transfers between devices: 535 us -> none  [the longest x2 178 us: local(): lax.psum_scatter(weight_terms[5].astype(jnp.bfloat16), ('fsdp', 'ctx'), s...]
    all_gather x10 -> x0, waiting for transfers between devices: 301 us -> none  [the longest x2 134 us: local(): lax.all_gather(gate_up_weight[layer_index], ('fsdp', 'ctx'), axis=0, tile...]
    dot_general x136 -> x0, matrix products: 293 us -> none  [the longest x32 41.7 us: one_head(): jnp.einsum('qd,kd->qk', query_head, key_head, preferred_element_type=jnp....]
    ppermute x0 -> x86, waiting for transfers between devices: none -> 282 us  [the longest x18 130 us: swap_y(): return lax.ppermute(array, 'ctx', pairs_of('ctx', 1))]
    unnamed x41 -> x7, waiting for transfers between devices: 164 us -> 0.12 us
    pallas_call x0 -> x18, Pallas kernels: none -> 149 us  [call(): pl.pallas_call(body, out_shape=outs, in_specs=specs, out_specs=out_specs...]
    all_gather x6 -> x0, blocking collectives: 83.4 us -> none  [the longest x2 28.3 us: local(): lax.all_gather(norm_gains[layer_index], ('fsdp', 'ctx'), axis=1, tiled=True)]
    psum x7, waiting for transfers between devices: 325 us -> 248 us  [tensor_sum(): return lax.psum(part, 'tp')]
  transfers between devices with their start and end apart: 35 -> 93, of which waited for: 33 -> 30; matrix products, arithmetic and copies ran while one was open for 11% -> 10% of each run, Pallas kernels for 0% -> 14%
where the time goes in v1:
time: 938 us; the launch traced here: 929 us
  waiting for transfers between devices  530 us (57%)
  Pallas kernels  149 us (16%)
  local copies, waits for them, and re-layouts  111 us (12%)
  starting transfers between devices  64.2 us (7%)
  other arithmetic  58.2 us (6%)
  between operations  16.2 us (2%)
    psum x7, waiting for transfers between devices, tensor_sum(): return lax.psum(part, 'tp')  248 us
    pallas_call x18, Pallas kernels, call(): pl.pallas_call(body, out_shape=outs, in_specs=specs, out_specs=out_specs...  149 us
    ppermute x18, waiting for transfers between devices, swap_y(): return lax.ppermute(array, 'ctx', pairs_of('ctx', 1))  130 us
    ppermute x18, waiting for transfers between devices, swap_x(): return lax.ppermute(array, 'fsdp', pairs_of('fsdp', 2))  94.2 us
    unnamed x304, local copies, waits for them, and re-layouts  76.1 us
    ppermute x2, waiting for transfers between devices, local(): other = [lax.ppermute(results[4], 'ctx', [(1, 0)])]  33.4 us
    ppermute x18, starting transfers between devices, swap_x(): return lax.ppermute(array, 'fsdp', pairs_of('fsdp', 2))  21.2 us
    ppermute x2, waiting for transfers between devices, local(): prev = lax.ppermute(kv, 'ctx', [(0, 1)])  19.9 us
  transfers between devices with their start and end apart: 93, of which 30 were waited for; matrix products, arithmetic and copies ran while one was open for 10% of the time, Pallas kernels for 14%

profile of v1, /device:TPU:0, one launch (start us, length us, event | category | flops | bytes accessed | tf_op | source)
XLA Modules:
  0.0 929.0 jit_solution(14584250650942522868)
XLA Ops:
  10.0 3.0 collective-permute-start.4
  14.5 4.6 fusion.30
  23.9 3.2 pad_maximum_fusion.3.refs_5_.refs_4_
  29.5 53.3 %collective-permute-done = bf16[14,256]{1,0:T(8,128)(2,1)S(1)} collective-permute-done((bf16[14,256]{1,0:T(8,128)(2,1)S(1)}, bf16[14,256]{1,0:T(8,128)(2,1)S(1)}, u32[]{:S(2)}, u32[]{:S(2)}) %collective-permute-start) | collective-permute-done | bytes 7200 | tf_op jit(solution)/shard_map/ppermute | solution.py:362
  90.3 54.2 %collective-permute-done.2 = bf16[2,2,14,256]{3,2,1,0:T(8,128)(2,1)S(1)} collective-permute-done((bf16[2,2,14,256]{3,2,1,0:T(8,128)(2,1)S(1)}, bf16[2,2,14,256]{3,2,1,0:T(8,128)(2,1)S(1)}, u32[]{:S(2)}, u32[]{:S(2)}) %collective-permute-start.2) | collective-permute-done | bytes 28704 | tf_op jit(solution)/shard_map/ppermute | solution.py:354
  148.0 10.2 %collective-permute-done.6.refs_10_.refs_12_.refs_18_.refs_11_ = bf16[4,128,512]{2,1,0:T(8,128)(2,1)S(1)} collective-permute-done((bf16[4,128,512]{2,1,0:T(8,128)(2,1)}, bf16[4,128,512]{2,1,0:T(8,128)(2,1)S(1)}, u32[]{:S(2)}, u32[]{:S(2)}) %collective-permute-start.6) | collective-permute-done | bytes 524320 | tf_op jit(solution)/shard_map/ppermute | solution.py:362
  181.3 13.5 %collective-permute-done.15.refs_8_.refs_7_ = bf16[3,128,1408]{2,1,0:T(8,128)(2,1)} collective-permute-done((bf16[3,128,1408]{2,1,0:T(8,128)(2,1)}, bf16[3,128,1408]{2,1,0:T(8,128)(2,1)}, u32[]{:S(2)}, u32[]{:S(2)}) %collective-permute-start.15) | collective-permute-done | bytes 1081376 | tf_op jit(solution)/shard_map/ppermute | solution.py:354
  195.4 6.8 qkv.2
  204.0 4.7 collective-permute-start.12
  208.6 8.0 collective-permute-done.22.refs_8_.refs_9_.refs_15_
  220.7 3.1 pad_maximum_fusion.4.refs_5_.refs_4_
  223.8 8.6 collective-permute-done.12
  241.3 5.9 attend.2
  254.4 47.4 %all-reduce.9.cloned.1.call-done.refs_2_ = bf16[256,2048]{1,0:T(8,128)(2,1)} async-done(((bf16[256,2048]{1,0:T(8,128)(2,1)}), bf16[256,2048]{1,0:T(8,128)(2,1)}) %all-reduce.9.cloned.1.call-update) | async-done | bytes 1048592 | tf_op jit(solution)/shard_map/psum | solution.py:436
  301.8 10.6 %mlp.2 = (f32[256,2048]{1,0:T(8,128)}, bf16[256,2048]{1,0:T(8,128)(2,1)}, bf16[256,1408]{1,0:T(8,128)(2,1)S(1)}, bf16[256,1408]{1,0:T(8,128)(2,1)S(1)}, bf16[256...) custom-call(s32[10]{0:T(128)S(1)} %copy-done.64, bf16[256,2048]{1,0:T(8,128)(2,1)S(1)} %bitcast.238, ...), custom_call_target="tpu_custom_call" | custom-call | flops 4429185024 | bytes 25772072 | tf_op jit(solution)/shard_map/mlp/pallas_call | solution.py:41
  323.7 42.4 %all-reduce.11.cloned.1.call-done.refs_2_ = bf16[256,2048]{1,0:T(8,128)(2,1)} async-done(((bf16[256,2048]{1,0:T(8,128)(2,1)}), bf16[256,2048]{1,0:T(8,128)(2,1)}) %all-reduce.11.cloned.1.call-update) | async-done | bytes 1048592 | tf_op jit(solution)/shard_map/psum | solution.py:436
  367.3 8.7 qkv.3
  376.1 3.6 collective-permute-start.31
  379.8 11.2 %collective-permute-done.31 = bf16[2,256,512]{2,1,0:T(8,128)(2,1)S(1)} collective-permute-done((bf16[2,256,512]{2,1,0:T(8,128)(2,1)S(1)}, bf16[2,256,512]{2,1,0:T(8,128)(2,1)S(1)}, u32[]{:S(2)}, u32[]{:S(2)}) %collective-permute-start.31) | collective-permute-done | bytes 524320 | tf_op jit(solution)/shard_map/ppermute | solution.py:622
  391.1 6.0 attend.3
  399.7 52.2 %all-reduce.13.cloned.1.call-done.refs_2_ = bf16[256,2048]{1,0:T(8,128)(2,1)} async-done(((bf16[256,2048]{1,0:T(8,128)(2,1)}), bf16[256,2048]{1,0:T(8,128)(2,1)}) %all-reduce.13.cloned.1.call-update) | async-done | bytes 1048592 | tf_op jit(solution)/shard_map/psum | solution.py:436
  455.1 11.3 %mlp.3 = (f32[256,2048]{1,0:T(8,128)}, bf16[256,2048]{1,0:T(8,128)(2,1)S(1)}, bf16[256,1408]{1,0:T(8,128)(2,1)S(1)}, bf16[256,1408]{1,0:T(8,128)(2,1)S(1)}, bf16...) custom-call(s32[10]{0:T(128)S(1)} %copy-done.66, f32[256,2048]{1,0:T(8,128)} %get-tuple-element.90.refs_1_.refs_5_.stream, ...), custom_call_target="tpu_custom_call" | custom-call | flops 4429185024 | bytes 26820648 | tf_op jit(solution)/shard_map/mlp/pallas_call | solution.py:41
  468.2 10.2 %mlp_back.2 = (bf16[256,2048]{1,0:T(8,128)(2,1)S(1)}, bf16[256,1408]{1,0:T(8,128)(2,1)S(1)}, bf16[256,1408]{1,0:T(8,128)(2,1)S(1)}, bf16[256,2048]{1,0:T(8,128)(2,1)S(1)}) custom-call(s32[10]{0:T(128)S(1)} %copy-done.66, bf16[256,2048]{1,0:T(8,128)(2,1)S(1)} %bitcast.241, bf16[256,1408]{1,0:T(8,128)(2,1)S(1)} %get-tuple-element.97.refs_2_, ...), custom_call_target="tpu_custom_call" | custom-call | flops 4429185024 | bytes 23330856 | tf_op jit(solution)/shard_map/mlp_back/pallas_call | solution.py:41
  483.1 50.4 %all-reduce.15.cloned.1.call-done.refs_2_ = bf16[256,2048]{1,0:T(8,128)(2,1)} async-done(((bf16[256,2048]{1,0:T(8,128)(2,1)}), bf16[256,2048]{1,0:T(8,128)(2,1)}) %all-reduce.15.cloned.1.call-update) | async-done | bytes 1048592 | tf_op jit(solution)/shard_map/psum | solution.py:436
  538.4 11.6 %attend_back.2 = (f32[256,2048]{1,0:T(8,128)}, bf16[256,2048]{1,0:T(8,128)(2,1)}, f32[2,2048]{1,0:T(2,128)S(1)}, bf16[256,512]{1,0:T(8,128)(2,1)S(1)}, bf16[2,25...) custom-call(s32[10]{0:T(128)S(1)} %copy-done.67, f32[256,2048]{1,0:T(8,128)} %get-tuple-element.95.refs_1_, ...), custom_call_target="tpu_custom_call" | custom-call | flops 1207959552 | bytes 19824680 | tf_op jit(solution)/shard_map/attend_back/pallas_call | solution.py:41
  553.3 13.1 %collective-permute-done.41.refs_3_ = bf16[2,256,512]{2,1,0:T(8,128)(2,1)S(1)} collective-permute-done((bf16[2,256,512]{2,1,0:T(8,128)(2,1)S(1)}, bf16[2,256,512]{2,1,0:T(8,128)(2,1)S(1)}, u32[]{:S(2)}, u32[]{:S(2)}) %collective-permute-start.41) | collective-permute-done | bytes 524320 | tf_op jit(solution)/shard_map/ppermute | solution.py:723
  567.7 8.0 qkv_back.2
  579.0 9.7 %mlp_grads.3 = (bf16[2,3,128,1408]{3,2,1,0:T(8,128)(2,1)}, bf16[2,3,128,1408]{3,2,1,0:T(8,128)(2,1)}, bf16[2,3,128,1408]{3,2,1,0:T(8,128)(2,1)}, bf16[3,128,1408]{2,1,0:T(8,128)(2,1)}, bf16[3,128,1408]{2,1,0:T(8,128)(2,1)}) custom-call(s32[4]{0:T(128)S(1)} %pad_add_fusion.refs_0_, bf16[256,2048]{1,0:T(8,128)(2,1)S(1)} %copy-done.97, ...), custom_call_target="tpu_custom_call" | custom-call | flops 4429185024 | bytes 17170448 | tf_op jit(solution)/shard_map/mlp_grads/pallas_call | solution.py:41
  599.6 6.1 attn_grads.3
  611.8 28.8 %all-reduce.17.cloned.1.call-done.cot = bf16[256,2048]{1,0:T(8,128)(2,1)} async-done(((bf16[256,2048]{1,0:T(8,128)(2,1)}), bf16[256,2048]{1,0:T(8,128)(2,1)}) %all-reduce.17.cloned.1.call-update) | async-done | bytes 1048592 | tf_op jit(solution)/shard_map/psum | solution.py:436
  641.8 3.0 norm_back.2.refs_1_.refs_4_
  646.2 12.3 %mlp_back.3 = (bf16[256,2048]{1,0:T(8,128)(2,1)}, bf16[256,1408]{1,0:T(8,128)(2,1)}, bf16[256,1408]{1,0:T(8,128)(2,1)}, bf16[256,2048]{1,0:T(8,128)(2,1)}) custom-call(s32[10]{0:T(128)S(1)} %copy-done.69, f32[256,2048]{1,0:T(8,128)} %copy-done, bf16[256,1408]{1,0:T(8,128)(2,1)S(1)} %copy-done.51, bf16[256,1408]{1,0:T(8,128)(2,1)S(1)} %copy-done.53, ...), custom_call_target="tpu_custom_call" | custom-call | flops 4429185024 | bytes 24379432 | tf_op jit(solution)/shard_map/mlp_back/pallas_call | solution.py:41
  670.1 8.8 collective-permute-done.65
  683.0 26.8 %all-reduce.19.cloned.1.call-done.refs_2_ = bf16[256,2048]{1,0:T(8,128)(2,1)} async-done(((bf16[256,2048]{1,0:T(8,128)(2,1)}), bf16[256,2048]{1,0:T(8,128)(2,1)}) %all-reduce.19.cloned.1.call-update) | async-done | bytes 1048592 | tf_op jit(solution)/shard_map/psum | solution.py:436
  714.2 11.9 %attend_back.3 = (f32[256,2048]{1,0:T(8,128)}, bf16[256,2048]{1,0:T(8,128)(2,1)S(1)}, f32[2,2048]{1,0:T(2,128)S(1)}, bf16[256,512]{1,0:T(8,128)(2,1)S(1)}, bf16[...) custom-call(s32[10]{0:T(128)S(1)} %copy-done.70, f32[256,2048]{1,0:T(8,128)} %get-tuple-element.88.refs_1_, ...), custom_call_target="tpu_custom_call" | custom-call | flops 1207959552 | bytes 20873256 | tf_op jit(solution)/shard_map/attend_back/pallas_call | solution.py:41
  733.5 10.6 %mlp_grads.2 = (bf16[2,3,128,1408]{3,2,1,0:T(8,128)(2,1)}, bf16[2,3,128,1408]{3,2,1,0:T(8,128)(2,1)}, bf16[2,3,128,1408]{3,2,1,0:T(8,128)(2,1)}, bf16[3,128,1408]{2,1,0:T(8,128)(2,1)}, bf16[3,128,1408]{2,1,0:T(8,128)(2,1)}) custom-call(s32[4]{0:T(128)S(1)} %copy-done.91, bf16[256,2048]{1,0:T(8,128)(2,1)} %get-tuple-element.139.refs_1_, ...), custom_call_target="tpu_custom_call" | custom-call | flops 4429185024 | bytes 17170448 | tf_op jit(solution)/shard_map/mlp_grads/pallas_call | solution.py:41
  746.0 20.3 %collective-permute-done.42.refs_3_ = bf16[2,256,512]{2,1,0:T(8,128)(2,1)S(1)} collective-permute-done((bf16[2,256,512]{2,1,0:T(8,128)(2,1)S(1)}, bf16[2,256,512]{2,1,0:T(8,128)(2,1)S(1)}, u32[]{:S(2)}, u32[]{:S(2)}) %collective-permute-start.42) | collective-permute-done | bytes 524320 | tf_op jit(solution)/shard_map/ppermute | solution.py:723
  766.3 7.7 qkv_back.3
  784.8 3.8 bitcast_add_fusion
  791.7 6.2 attn_grads.2
  798.7 40.0 %collective-permute-done.45 = f32[14,256]{1,0:T(8,128)S(1)} collective-permute-done((f32[14,256]{1,0:T(8,128)S(1)}, f32[14,256]{1,0:T(8,128)S(1)}, u32[]{:S(2)}, u32[]{:S(2)}) %collective-permute-start.45) | collective-permute-done | bytes 14368 | tf_op jit(solution)/shard_map/ppermute | solution.py:362
  849.3 5.6 collective-permute-done.54
  856.1 10.4 %collective-permute-done.56 = bf16[2,4,128,512]{3,2,1,0:T(8,128)(2,1)} collective-permute-done((bf16[2,4,128,512]{3,2,1,0:T(8,128)(2,1)}, bf16[2,4,128,512]{3,2,1,0:T(8,128)(2,1)}, u32[]{:S(2)}, u32[]{:S(2)}) %collective-permute-start.56) | collective-permute-done | bytes 1048608 | tf_op jit(solution)/shard_map/ppermute | solution.py:362
  877.7 5.1 collective-permute-done.57
  892.4 2.8 norm_back.3
  902.0 2.9 bitcast_add_fusion.2
  908.7 3.5 copy.84
  914.8 7.0 copy.83
  (575 shorter events, 213.6 us)
Async XLA Ops:
  7.2 294.6 %all-reduce.9.cloned.1.call-start = ((), (), s32[]{:S(2)}) async-start(), calls=%async_computation | async-start | bytes 2097152 | tf_op jit(solution)/shard_map/psum | solution.py:436
  10.0 72.9 %collective-permute-start.4 = (bf16[4,256,512]{2,1,0:T(8,128)(2,1)S(1)}, bf16[4,256,512]{2,1,0:T(8,128)(2,1)}, u32[]{:S(2)}, u32[]{:S(2)}) collective-permute-start(bf16[4,256,512]{2,1,0:T(8,128)(2,1)S(1)} %pad_maximum_fusion.7.refs_6_.refs_8_.refs_14_.refs_7_), channel_id=1, source_target_pairs={{0,4},{4,0},{1,5},{5,1},{2,6},{6,2},{3,7},{7,3},{8,12},{12,8},{9,1... | collective-permute-start | bytes 3145736 | tf_op jit(solution)/shard_map/ppermute | solution.py:362
  13.0 74.5 %collective-permute-start.3 = (bf16[4,256,512]{2,1,0:T(8,128)(2,1)S(1)}, bf16[4,256,512]{2,1,0:T(8,128)(2,1)S(1)}, u32[]{:S(2)}, u32[]{:S(2)}) collective-permute-start(bf16[4,256,512]{2,1,0:T(8,128)(2,1)S(1)} %pad_maximum_fusion.7.refs_6_.refs_8_.refs_14_.refs_7_), channel_id=1, source_target_pairs={{0,16},{8,24},{16,0},{24,8},{1,17},{9,25},{17,1},{25,9},{2,18},{10... | collective-permute-start | bytes 3145736 | tf_op jit(solution)/shard_map/ppermute | solution.py:354
  27.1 136.4 %collective-permute-start.14 = (bf16[3,256,1408]{2,1,0:T(8,128)(2,1)}, bf16[3,256,1408]{2,1,0:T(8,128)(2,1)}, u32[]{:S(2)}, u32[]{:S(2)}) collective-permute-start(bf16[3,256,1408]{2,1,0:T(8,128)(2,1)} %pad_maximum_fusion.3.refs_5_.refs_4_), channel_id=1, source_target_pairs={{0,4},{4,0},{1,5},{5,1},{2,6},{6,2},{3,7},{7,3},{8,12},{12,8},{9,1... | collective-permute-start | bytes 6488072 | tf_op jit(solution)/shard_map/ppermute | solution.py:362
  27.6 119.9 %collective-permute-start.7 = (bf16[4,256,512]{2,1,0:T(8,128)(2,1)S(1)}, bf16[4,256,512]{2,1,0:T(8,128)(2,1)}, u32[]{:S(2)}, u32[]{:S(2)}) collective-permute-start(bf16[4,256,512]{2,1,0:T(8,128)(2,1)S(1)} %pad_maximum_fusion.7.refs_6_.refs_8_.refs_14_.refs_7_), channel_id=1, source_target_pairs={{0,8},{8,0},{16,24},{24,16},{1,9},{9,1},{17,25},{25,17},{2,10},{10... | collective-permute-start | bytes 3145736 | tf_op jit(solution)/shard_map/ppermute | solution.py:358
  27.7 55.0 %collective-permute-start = (bf16[14,256]{1,0:T(8,128)(2,1)S(1)}, bf16[14,256]{1,0:T(8,128)(2,1)S(1)}, u32[]{:S(2)}, u32[]{:S(2)}) collective-permute-start(bf16[14,256]{1,0:T(8,128)(2,1)S(1)} %get-tuple-element.246), channel_id=1, source_target_pairs={{0,4},{4,0},{1,5},{5,1},{2,6},{6,2},{3,7},{7,3},{8,12},{12,8},{9,1... | collective-permute-start | bytes 21512 | tf_op jit(solution)/shard_map/ppermute | solution.py:362
  82.9 92.3 %collective-permute-start.13 = (bf16[3,256,1408]{2,1,0:T(8,128)(2,1)}, bf16[3,256,1408]{2,1,0:T(8,128)(2,1)}, u32[]{:S(2)}, u32[]{:S(2)}) collective-permute-start(bf16[3,256,1408]{2,1,0:T(8,128)(2,1)} %pad_maximum_fusion.3.refs_5_.refs_4_), channel_id=1, source_target_pairs={{0,16},{8,24},{16,0},{24,8},{1,17},{9,25},{17,1},{25,9},{2,18},{10... | collective-permute-start | bytes 6488072 | tf_op jit(solution)/shard_map/ppermute | solution.py:354
  86.5 59.7 %collective-permute-start.5 = (bf16[4,128,512]{2,1,0:T(8,128)(2,1)}, bf16[4,128,512]{2,1,0:T(8,128)(2,1)S(1)}, u32[]{:S(2)}, u32[]{:S(2)}) collective-permute-start(bf16[4,128,512]{2,1,0:T(8,128)(2,1)} %slice.377), channel_id=1, source_target_pairs={{0,16},{8,24},{16,0},{24,8},{1,17},{9,25},{17,1},{25,9},{2,18},{10... | collective-permute-start | bytes 1572872 | tf_op jit(solution)/shard_map/ppermute | solution.py:354
  87.5 57.0 %collective-permute-start.2 = (bf16[2,2,14,256]{3,2,1,0:T(8,128)(2,1)S(1)}, bf16[2,2,14,256]{3,2,1,0:T(8,128)(2,1)S(1)}, u32[]{:S(2)}, u32[]{:S(2)}) collective-permute-start(bf16[2,2,14,256]{3,2,1,0:T(8,128)(2,1)S(1)} %maximum_select_fusion.2), channel_id=1, source_target_pairs={{0,16},{8,24},{16,0},{24,8},{1,17},{9,25},{17,1},{25,9},{2,18},{10... | collective-permute-start | bytes 86024 | tf_op jit(solution)/shard_map/ppermute | solution.py:354
  147.5 69.1 %collective-permute-start.17 = (bf16[3,256,1408]{2,1,0:T(8,128)(2,1)}, bf16[3,256,1408]{2,1,0:T(8,128)(2,1)}, u32[]{:S(2)}, u32[]{:S(2)}) collective-permute-start(bf16[3,256,1408]{2,1,0:T(8,128)(2,1)} %pad_maximum_fusion.3.refs_5_.refs_4_), channel_id=1, source_target_pairs={{0,8},{8,0},{16,24},{24,16},{1,9},{9,1},{17,25},{25,17},{2,10},{10... | collective-permute-start | bytes 6488072 | tf_op jit(solution)/shard_map/ppermute | solution.py:358
  175.1 41.5 %collective-permute-start.22 = (bf16[4,256,512]{2,1,0:T(8,128)(2,1)}, bf16[4,256,512]{2,1,0:T(8,128)(2,1)}, u32[]{:S(2)}, u32[]{:S(2)}) collective-permute-start(bf16[4,256,512]{2,1,0:T(8,128)(2,1)} %pad_maximum_fusion.8.refs_7_.refs_8_.refs_14_), channel_id=1, source_target_pairs={{0,16},{8,24},{16,0},{24,8},{1,17},{9,25},{17,1},{25,9},{2,18},{10... | collective-permute-start | bytes 3145736 | tf_op jit(solution)/shard_map/ppermute | solution.py:354
  179.5 55.5 %collective-permute-start.16 = (bf16[3,128,1408]{2,1,0:T(8,128)(2,1)}, bf16[3,128,1408]{2,1,0:T(8,128)(2,1)}, u32[]{:S(2)}, u32[]{:S(2)}) collective-permute-start(bf16[3,128,1408]{2,1,0:T(8,128)(2,1)} %slice.384), channel_id=1, source_target_pairs={{0,4},{4,0},{1,5},{5,1},{2,6},{6,2},{3,7},{7,3},{8,12},{12,8},{9,1... | collective-permute-start | bytes 3244040 | tf_op jit(solution)/shard_map/ppermute | solution.py:362
  232.5 81.8 %collective-permute-start.33 = (bf16[3,256,1408]{2,1,0:T(8,128)(2,1)}, bf16[3,256,1408]{2,1,0:T(8,128)(2,1)}, u32[]{:S(2)}, u32[]{:S(2)}) collective-permute-start(bf16[3,256,1408]{2,1,0:T(8,128)(2,1)} %pad_maximum_fusion.4.refs_5_.refs_4_), channel_id=1, source_target_pairs={{0,4},{4,0},{1,5},{5,1},{2,6},{6,2},{3,7},{7,3},{8,12},{12,8},{9,1... | collective-permute-start | bytes 6488072 | tf_op jit(solution)/shard_map/ppermute | solution.py:362
  235.9 83.1 %collective-permute-start.32 = (bf16[3,256,1408]{2,1,0:T(8,128)(2,1)}, bf16[3,256,1408]{2,1,0:T(8,128)(2,1)}, u32[]{:S(2)}, u32[]{:S(2)}) collective-permute-start(bf16[3,256,1408]{2,1,0:T(8,128)(2,1)} %pad_maximum_fusion.4.refs_5_.refs_4_), channel_id=1, source_target_pairs={{0,16},{8,24},{16,0},{24,8},{1,17},{9,25},{17,1},{25,9},{2,18},{10... | collective-permute-start | bytes 6488072 | tf_op jit(solution)/shard_map/ppermute | solution.py:354
  249.5 116.5 %all-reduce.11.cloned.1.call-start = ((), (), s32[]{:S(2)}) async-start(), calls=%async_computation.1 | async-start | bytes 2097152 | tf_op jit(solution)/shard_map/psum | solution.py:436
  249.6 64.6 %collective-permute-start.26 = (bf16[4,256,512]{2,1,0:T(8,128)(2,1)}, bf16[4,256,512]{2,1,0:T(8,128)(2,1)}, u32[]{:S(2)}, u32[]{:S(2)}) collective-permute-start(bf16[4,256,512]{2,1,0:T(8,128)(2,1)} %pad_maximum_fusion.8.refs_7_.refs_8_.refs_14_), channel_id=1, source_target_pairs={{0,8},{8,0},{16,24},{24,16},{1,9},{9,1},{17,25},{25,17},{2,10},{10... | collective-permute-start | bytes 3145736 | tf_op jit(solution)/shard_map/ppermute | solution.py:358
  252.8 64.7 %collective-permute-start.24 = (bf16[4,128,512]{2,1,0:T(8,128)(2,1)S(1)}, bf16[4,128,512]{2,1,0:T(8,128)(2,1)S(1)}, u32[]{:S(2)}, u32[]{:S(2)}) collective-permute-start(bf16[4,128,512]{2,1,0:T(8,128)(2,1)S(1)} %slice.387), channel_id=1, source_target_pairs={{0,16},{8,24},{16,0},{24,8},{1,17},{9,25},{17,1},{25,9},{2,18},{10... | collective-permute-start | bytes 1572872 | tf_op jit(solution)/shard_map/ppermute | solution.py:354
  254.3 63.2 %collective-permute-start.25 = (bf16[4,128,512]{2,1,0:T(8,128)(2,1)}, bf16[4,128,512]{2,1,0:T(8,128)(2,1)S(1)}, u32[]{:S(2)}, u32[]{:S(2)}) collective-permute-start(bf16[4,128,512]{2,1,0:T(8,128)(2,1)} %slice.388), channel_id=1, source_target_pairs={{0,4},{4,0},{1,5},{5,1},{2,6},{6,2},{3,7},{7,3},{8,12},{12,8},{9,1... | collective-permute-start | bytes 1572872 | tf_op jit(solution)/shard_map/ppermute | solution.py:362
  314.7 137.1 %all-reduce.13.cloned.1.call-start = ((), (), s32[]{:S(2)}) async-start(), calls=%async_computation.2 | async-start | bytes 2097152 | tf_op jit(solution)/shard_map/psum | solution.py:436
  317.6 58.5 %collective-permute-start.34 = (bf16[3,128,1408]{2,1,0:T(8,128)(2,1)}, bf16[3,128,1408]{2,1,0:T(8,128)(2,1)}, u32[]{:S(2)}, u32[]{:S(2)}) collective-permute-start(bf16[3,128,1408]{2,1,0:T(8,128)(2,1)} %slice.393), channel_id=1, source_target_pairs={{0,16},{8,24},{16,0},{24,8},{1,17},{9,25},{17,1},{25,9},{2,18},{10... | collective-permute-start | bytes 3244040 | tf_op jit(solution)/shard_map/ppermute | solution.py:354
  321.5 58.1 %collective-permute-start.35 = (bf16[3,128,1408]{2,1,0:T(8,128)(2,1)}, bf16[3,128,1408]{2,1,0:T(8,128)(2,1)}, u32[]{:S(2)}, u32[]{:S(2)}) collective-permute-start(bf16[3,128,1408]{2,1,0:T(8,128)(2,1)} %slice.394), channel_id=1, source_target_pairs={{0,4},{4,0},{1,5},{5,1},{2,6},{6,2},{3,7},{7,3},{8,12},{12,8},{9,1... | collective-permute-start | bytes 3244040 | tf_op jit(solution)/shard_map/ppermute | solution.py:362
  323.1 76.5 %collective-permute-start.36 = (bf16[3,256,1408]{2,1,0:T(8,128)(2,1)}, bf16[3,256,1408]{2,1,0:T(8,128)(2,1)}, u32[]{:S(2)}, u32[]{:S(2)}) collective-permute-start(bf16[3,256,1408]{2,1,0:T(8,128)(2,1)} %pad_maximum_fusion.4.refs_5_.refs_4_), channel_id=1, source_target_pairs={{0,8},{8,0},{16,24},{24,16},{1,9},{9,1},{17,25},{25,17},{2,10},{10... | collective-permute-start | bytes 6488072 | tf_op jit(solution)/shard_map/ppermute | solution.py:358
  323.1 76.5 %collective-permute-start.37 = (bf16[3,256,1408]{2,1,0:T(8,128)(2,1)}, bf16[3,256,1408]{2,1,0:T(8,128)(2,1)}, u32[]{:S(2)}, u32[]{:S(2)}) collective-permute-start(bf16[3,256,1408]{2,1,0:T(8,128)(2,1)} %collective-permute-done.32.refs_6_.refs_5_), channel_id=1, source_target_pairs={{0,8},{8,0},{16,24},{24,16},{1,9},{9,1},{17,25},{25,17},{2,10},{10... | collective-permute-start | bytes 6488072 | tf_op jit(solution)/shard_map/ppermute | solution.py:358
  323.6 76.0 %collective-permute-start.38 = (bf16[3,256,1408]{2,1,0:T(8,128)(2,1)}, bf16[3,256,1408]{2,1,0:T(8,128)(2,1)}, u32[]{:S(2)}, u32[]{:S(2)}) collective-permute-start(bf16[3,256,1408]{2,1,0:T(8,128)(2,1)} %collective-permute-done.33.refs_7_.refs_6_), channel_id=1, source_target_pairs={{0,8},{8,0},{16,24},{24,16},{1,9},{9,1},{17,25},{25,17},{2,10},{10... | collective-permute-start | bytes 6488072 | tf_op jit(solution)/shard_map/ppermute | solution.py:358
  399.4 134.1 %all-reduce.15.cloned.1.call-start = ((), (), s32[]{:S(2)}) async-start(), calls=%async_computation.3 | async-start | bytes 2097152 | tf_op jit(solution)/shard_map/psum | solution.py:436
  482.2 158.5 %all-reduce.17.cloned.1.call-start = ((), (), s32[]{:S(2)}) async-start(), calls=%async_computation.4 | async-start | bytes 2097152 | tf_op jit(solution)/shard_map/psum | solution.py:436
  482.4 70.3 %collective-permute-start.79 = (bf16[256,1408]{1,0:T(8,128)(2,1)}, bf16[256,1408]{1,0:T(8,128)(2,1)}, u32[]{:S(2)}, u32[]{:S(2)}) collective-permute-start(bf16[256,1408]{1,0:T(8,128)(2,1)} %copy-done.102), channel_id=1, source_target_pairs={{0,8},{8,0},{16,24},{24,16},{1,9},{9,1},{17,25},{25,17},{2,10},{10... | collective-permute-start | bytes 2162696 | tf_op jit(solution)/shard_map/ppermute | solution.py:358
  482.5 70.3 %collective-permute-start.80 = (bf16[256,1408]{1,0:T(8,128)(2,1)}, bf16[256,1408]{1,0:T(8,128)(2,1)}, u32[]{:S(2)}, u32[]{:S(2)}) collective-permute-start(bf16[256,1408]{1,0:T(8,128)(2,1)} %copy-done.104), channel_id=1, source_target_pairs={{0,8},{8,0},{16,24},{24,16},{1,9},{9,1},{17,25},{25,17},{2,10},{10... | collective-permute-start | bytes 2162696 | tf_op jit(solution)/shard_map/ppermute | solution.py:358
  483.0 69.3 %collective-permute-start.63 = (bf16[256,512]{1,0:T(8,128)(2,1)}, bf16[256,512]{1,0:T(8,128)(2,1)}, u32[]{:S(2)}, u32[]{:S(2)}) collective-permute-start(bf16[256,512]{1,0:T(8,128)(2,1)} %copy-done.108), channel_id=1, source_target_pairs={{0,8},{8,0},{16,24},{24,16},{1,9},{9,1},{17,25},{25,17},{2,10},{10... | collective-permute-start | bytes 786440 | tf_op jit(solution)/shard_map/ppermute | solution.py:358
  589.6 77.2 %collective-permute-start.82 = (bf16[2,3,128,1408]{3,2,1,0:T(8,128)(2,1)}, bf16[2,3,128,1408]{3,2,1,0:T(8,128)(2,1)}, u32[]{:S(2)}, u32[]{:S(2)}) collective-permute-start(bf16[2,3,128,1408]{3,2,1,0:T(8,128)(2,1)} %get-tuple-element.155), channel_id=1, source_target_pairs={{0,16},{8,24},{16,0},{24,8},{1,17},{9,25},{17,1},{25,9},{2,18},{10... | collective-permute-start | bytes 6488072 | tf_op jit(solution)/shard_map/ppermute | solution.py:354
  591.1 118.7 %all-reduce.19.cloned.1.call-start = ((), (), s32[]{:S(2)}) async-start(), calls=%async_computation.5 | async-start | bytes 2097152 | tf_op jit(solution)/shard_map/psum | solution.py:436
  592.4 136.2 %collective-permute-start.68 = (bf16[256,2048]{1,0:T(8,128)(2,1)}, bf16[256,2048]{1,0:T(8,128)(2,1)}, u32[]{:S(2)}, u32[]{:S(2)}) collective-permute-start(bf16[256,2048]{1,0:T(8,128)(2,1)} %get-tuple-element.139.refs_1_), channel_id=1, source_target_pairs={{0,8},{8,0},{16,24},{24,16},{1,9},{9,1},{17,25},{25,17},{2,10},{10... | collective-permute-start | bytes 3145736 | tf_op jit(solution)/shard_map/ppermute | solution.py:358
  593.1 77.0 %collective-permute-start.84 = (bf16[2,3,128,1408]{3,2,1,0:T(8,128)(2,1)}, bf16[2,3,128,1408]{3,2,1,0:T(8,128)(2,1)}, u32[]{:S(2)}, u32[]{:S(2)}) collective-permute-start(bf16[2,3,128,1408]{3,2,1,0:T(8,128)(2,1)} %get-tuple-element.157), channel_id=1, source_target_pairs={{0,4},{4,0},{1,5},{5,1},{2,6},{6,2},{3,7},{7,3},{8,12},{12,8},{9,1... | collective-permute-start | bytes 6488072 | tf_op jit(solution)/shard_map/ppermute | solution.py:362
  607.5 54.0 %collective-permute-start.64 = (bf16[2,4,128,512]{3,2,1,0:T(8,128)(2,1)}, bf16[2,4,128,512]{3,2,1,0:T(8,128)(2,1)}, u32[]{:S(2)}, u32[]{:S(2)}) collective-permute-start(bf16[2,4,128,512]{3,2,1,0:T(8,128)(2,1)} %get-tuple-element.135), channel_id=1, source_target_pairs={{0,16},{8,24},{16,0},{24,8},{1,17},{9,25},{17,1},{25,9},{2,18},{10... | collective-permute-start | bytes 3145736 | tf_op jit(solution)/shard_map/ppermute | solution.py:354
  609.3 56.0 %collective-permute-start.66 = (bf16[2,4,128,512]{3,2,1,0:T(8,128)(2,1)}, bf16[2,4,128,512]{3,2,1,0:T(8,128)(2,1)}, u32[]{:S(2)}, u32[]{:S(2)}) collective-permute-start(bf16[2,4,128,512]{3,2,1,0:T(8,128)(2,1)} %get-tuple-element.137), channel_id=1, source_target_pairs={{0,4},{4,0},{1,5},{5,1},{2,6},{6,2},{3,7},{7,3},{8,12},{12,8},{9,1... | collective-permute-start | bytes 3145736 | tf_op jit(solution)/shard_map/ppermute | solution.py:362
  658.5 231.6 %all-reduce.21.cloned.1.call-start = ((), (), s32[]{:S(2)}) async-start(), calls=%async_computation.6 | async-start | bytes 4194304 | tf_op jit(solution)/shard_map/psum | solution.py:436
  661.5 70.4 %collective-permute-start.69 = (bf16[256,2048]{1,0:T(8,128)(2,1)}, bf16[256,2048]{1,0:T(8,128)(2,1)}, u32[]{:S(2)}, u32[]{:S(2)}) collective-permute-start(bf16[256,2048]{1,0:T(8,128)(2,1)} %get-tuple-element.140.refs_2_), channel_id=1, source_target_pairs={{0,8},{8,0},{16,24},{24,16},{1,9},{9,1},{17,25},{25,17},{2,10},{10... | collective-permute-start | bytes 3145736 | tf_op jit(solution)/shard_map/ppermute | solution.py:358
  670.1 58.4 %collective-permute-start.72 = (bf16[256,1408]{1,0:T(8,128)(2,1)}, bf16[256,1408]{1,0:T(8,128)(2,1)}, u32[]{:S(2)}, u32[]{:S(2)}) collective-permute-start(bf16[256,1408]{1,0:T(8,128)(2,1)} %get-tuple-element.143.refs_5_), channel_id=1, source_target_pairs={{0,8},{8,0},{16,24},{24,16},{1,9},{9,1},{17,25},{25,17},{2,10},{10... | collective-permute-start | bytes 2162696 | tf_op jit(solution)/shard_map/ppermute | solution.py:358
  679.0 50.1 %collective-permute-start.70 = (bf16[256,1408]{1,0:T(8,128)(2,1)}, bf16[256,1408]{1,0:T(8,128)(2,1)}, u32[]{:S(2)}, u32[]{:S(2)}) collective-permute-start(bf16[256,1408]{1,0:T(8,128)(2,1)} %get-tuple-element.141.refs_3_), channel_id=1, source_target_pairs={{0,8},{8,0},{16,24},{24,16},{1,9},{9,1},{17,25},{25,17},{2,10},{10... | collective-permute-start | bytes 2162696 | tf_op jit(solution)/shard_map/ppermute | solution.py:358
  680.5 50.0 %collective-permute-start.71 = (bf16[256,1408]{1,0:T(8,128)(2,1)}, bf16[256,1408]{1,0:T(8,128)(2,1)}, u32[]{:S(2)}, u32[]{:S(2)}) collective-permute-start(bf16[256,1408]{1,0:T(8,128)(2,1)} %get-tuple-element.142.refs_4_), channel_id=1, source_target_pairs={{0,8},{8,0},{16,24},{24,16},{1,9},{9,1},{17,25},{25,17},{2,10},{10... | collective-permute-start | bytes 2162696 | tf_op jit(solution)/shard_map/ppermute | solution.py:358
  728.4 55.8 %collective-permute-start.48 = (bf16[256,2048]{1,0:T(8,128)(2,1)}, bf16[256,2048]{1,0:T(8,128)(2,1)}, u32[]{:S(2)}, u32[]{:S(2)}) collective-permute-start(bf16[256,2048]{1,0:T(8,128)(2,1)} %get-tuple-element.121.refs_1_), channel_id=1, source_target_pairs={{0,8},{8,0},{16,24},{24,16},{1,9},{9,1},{17,25},{25,17},{2,10},{10... | collective-permute-start | bytes 3145736 | tf_op jit(solution)/shard_map/ppermute | solution.py:358
  728.6 54.1 %collective-permute-start.53 = (bf16[256,512]{1,0:T(8,128)(2,1)S(1)}, bf16[256,512]{1,0:T(8,128)(2,1)S(1)}, u32[]{:S(2)}, u32[]{:S(2)}) collective-permute-start(bf16[256,512]{1,0:T(8,128)(2,1)S(1)} %copy-done.107), channel_id=1, source_target_pairs={{0,8},{8,0},{16,24},{24,16},{1,9},{9,1},{17,25},{25,17},{2,10},{10... | collective-permute-start | bytes 786440 | tf_op jit(solution)/shard_map/ppermute | solution.py:358
  729.0 55.2 %collective-permute-start.83 = (bf16[3,128,1408]{2,1,0:T(8,128)(2,1)}, bf16[3,128,1408]{2,1,0:T(8,128)(2,1)}, u32[]{:S(2)}, u32[]{:S(2)}) collective-permute-start(bf16[3,128,1408]{2,1,0:T(8,128)(2,1)} %fusion.5), channel_id=1, source_target_pairs={{0,4},{4,0},{1,5},{5,1},{2,6},{6,2},{3,7},{7,3},{8,12},{12,8},{9,1... | collective-permute-start | bytes 3244040 | tf_op jit(solution)/shard_map/ppermute | solution.py:362
  730.5 54.2 %collective-permute-start.85 = (bf16[3,128,1408]{2,1,0:T(8,128)(2,1)}, bf16[3,128,1408]{2,1,0:T(8,128)(2,1)}, u32[]{:S(2)}, u32[]{:S(2)}) collective-permute-start(bf16[3,128,1408]{2,1,0:T(8,128)(2,1)} %fusion.4), channel_id=1, source_target_pairs={{0,16},{8,24},{16,0},{24,8},{1,17},{9,25},{17,1},{25,9},{2,18},{10... | collective-permute-start | bytes 3244040 | tf_op jit(solution)/shard_map/ppermute | solution.py:354
  782.7 85.7 %collective-permute-start.73 = (bf16[2,3,128,1408]{3,2,1,0:T(8,128)(2,1)}, bf16[2,3,128,1408]{3,2,1,0:T(8,128)(2,1)}, u32[]{:S(2)}, u32[]{:S(2)}) collective-permute-start(bf16[2,3,128,1408]{3,2,1,0:T(8,128)(2,1)} %get-tuple-element.145), channel_id=1, source_target_pairs={{0,16},{8,24},{16,0},{24,8},{1,17},{9,25},{17,1},{25,9},{2,18},{10... | collective-permute-start | bytes 6488072 | tf_op jit(solution)/shard_map/ppermute | solution.py:354
  788.7 82.9 %collective-permute-start.75 = (bf16[2,3,128,1408]{3,2,1,0:T(8,128)(2,1)}, bf16[2,3,128,1408]{3,2,1,0:T(8,128)(2,1)}, u32[]{:S(2)}, u32[]{:S(2)}) collective-permute-start(bf16[2,3,128,1408]{3,2,1,0:T(8,128)(2,1)} %get-tuple-element.147), channel_id=1, source_target_pairs={{0,4},{4,0},{1,5},{5,1},{2,6},{6,2},{3,7},{7,3},{8,12},{12,8},{9,1... | collective-permute-start | bytes 6488072 | tf_op jit(solution)/shard_map/ppermute | solution.py:362
  788.7 49.9 %collective-permute-start.45 = (f32[14,256]{1,0:T(8,128)S(1)}, f32[14,256]{1,0:T(8,128)S(1)}, u32[]{:S(2)}, u32[]{:S(2)}) collective-permute-start(f32[14,256]{1,0:T(8,128)S(1)} %bitcast.267), channel_id=1, source_target_pairs={{0,4},{4,0},{1,5},{5,1},{2,6},{6,2},{3,7},{7,3},{8,12},{12,8},{9,1... | collective-permute-start | bytes 43016 | tf_op jit(solution)/shard_map/ppermute | solution.py:362
  797.9 56.9 %collective-permute-start.54 = (bf16[2,4,128,512]{3,2,1,0:T(8,128)(2,1)}, bf16[2,4,128,512]{3,2,1,0:T(8,128)(2,1)}, u32[]{:S(2)}, u32[]{:S(2)}) collective-permute-start(bf16[2,4,128,512]{3,2,1,0:T(8,128)(2,1)} %get-tuple-element.126), channel_id=1, source_target_pairs={{0,16},{8,24},{16,0},{24,8},{1,17},{9,25},{17,1},{25,9},{2,18},{10... | collective-permute-start | bytes 3145736 | tf_op jit(solution)/shard_map/ppermute | solution.py:354
  (190 other events, 2471.7 us)
Sparse Core Ops, SparseCore 0:
  249.7 52.0 all-reduce.8
  314.8 51.1 all-reduce.10
  399.5 52.2 all-reduce.12
  482.3 51.1 all-reduce.14
  591.3 49.3 all-reduce.16
  658.6 51.1 all-reduce.18
  781.5 86.3 all-reduce.20

commit v2 on v1

v2 whole, which is shorter than its diff:
```python
import functools

import jax
import jax.numpy as jnp
from jax import lax
from jax.experimental import pallas as pl
from jax.experimental.pallas import tpu as pltpu
from jax.sharding import PartitionSpec as P

HD = 64
ROT = 16
LANES = 128
SCALE = 1.0 / HD**0.5
VMEM_LIMIT = 50 * 1024 * 1024
NN = (((1,), (0,)), ((), ()))
NT = (((1,), (1,)), ((), ()))
TN = (((0,), (0,)), ((), ()))
BF = jnp.bfloat16
F32 = jnp.float32
EACH = -1
TIMES = {
    "pack": 7.0,
    "qkv": 8.5,
    "attend": 8.0,
    "norm": 3.0,
    "mlp": 11.5,
    "mlp_back": 14.0,
    "norm_back": 3.5,
    "attend_back": 10.0,
    "qkv_back": 9.0,
    "mlp_grads": 10.5,
    "attn_grads": 7.0,
    "mlp_add": 4.0,
    "attn_add": 3.0,
    "mlp_finish": 7.5,
    "attn_finish": 4.5,
    "sum": 3.0,
}


def cost(name):
    return pl.CostEstimate(flops=0, bytes_accessed=int(TIMES[name] * 3.0e6), transcendentals=0)


def mm(lhs, rhs, dims):
    return lax.dot_general(lhs, rhs, dims, preferred_element_type=F32)


def shape(dims, dtype):
    return jax.ShapeDtypeStruct(tuple(dims), dtype)


class Free:
    def __init__(self, array):
        self.array = array


class Io:
    def __init__(self, ins, loads, outs, stores, held, weights, started, extra):
        self.ins, self.loads, self.outs, self.stores = ins, loads, outs, stores
        self.held, self.weights, self.started, self.extra = held, weights, started, extra
        self.there, self.gone = set(), []

    def get(self, index):
        if index not in self.there:
            self.loads[index].wait()
            self.there.add(index)
        return self.ins[index]

    def weight(self, slot):
        for copy in self.weights[slot]:
            copy.wait()
        self.begin(slot + 2)
        return self.held[slot]

    def begin(self, count):
        while self.started < min(count, len(self.weights)):
            for copy in self.weights[self.started]:
                copy.start()
            self.started += 1

    def put(self, index):
        for copy in self.stores[index]:
            copy.start()
            self.gone.append(copy)


def kernel(body, name, spots, loads, outs, slots=(), eager=1, extra=(), reuse=()):
    free = [isinstance(item, Free) for item in loads]
    loads = [item.array if isinstance(item, Free) else item for item in loads]
    loads = [item if isinstance(item, tuple) else (item, None) for item in loads]
    outs = [item if isinstance(item, tuple) else (item, None) for item in outs]
    pieces, place_of = [], {}
    for group, _, _ in slots:
        for piece in group:
            if id(piece) not in place_of:
                place_of[id(piece)] = len(pieces)
                pieces.append(piece)
    slot_at = [([place_of[id(piece)] for piece in group], m, at) for group, m, at in slots]
    out_shapes = [item[0] for item in outs]
    n_in, n_piece, n_reuse = len(loads), len(pieces), len(reuse)

    def part(item):
        return tuple(item[0].shape) if item[1] is None else tuple(item[0].shape[1:])

    def view(ref, index):
        return ref if index is None else ref.at[index]

    def run(*refs):
        refs = list(refs)

        def take(count):
            taken = refs[:count]
            del refs[:count]
            return taken

        starts = take(1)[0]
        in_hbm, piece_hbm, _ = take(n_in), take(n_piece), take(n_reuse)
        out_hbm = take(len(out_shapes))
        ins, results, held = take(n_in), take(len(outs)), take(len(slots))
        in_sems, out_sems = take(2)
        slot_sems = take(len(slots))
        load_copies = [
            pltpu.make_async_copy(view(ref, index), ins[at], in_sems.at[at])
            for at, (ref, (_, index)) in enumerate(zip(in_hbm, loads, strict=True))
        ]
        for copy in load_copies:
            copy.start()
        weight_sets = []
        for slot, (members, matrix, first) in enumerate(slot_at):
            copies = []
            for number, member in enumerate(members):
                piece = piece_hbm[member]
                row = pl.multiple_of(starts[first + number], 64)
                copies.append(
                    pltpu.make_async_copy(
                        piece.at[matrix],
                        held[slot].at[pl.ds(row, piece.shape[1]), :],
                        slot_sems[slot].at[number],
                    )
                )
            weight_sets.append(copies)
        stores = []
        for at, (ref, (_, index)) in enumerate(zip(out_hbm, outs, strict=True)):
            if index == EACH:
                stores.append(
                    [
                        pltpu.make_async_copy(results[at], ref.at[each], out_sems.at[at, each])
                        for each in range(ref.shape[0])
                    ]
                )
            else:
                stores.append(
                    [pltpu.make_async_copy(results[at], view(ref, index), out_sems.at[at, 0])]
                )
        io = Io(ins, load_copies, results, stores, held, weight_sets, 0, refs)
        io.begin(eager)
        body(io)
        for at in range(n_in):
            io.get(at)
        for copy in io.gone:
            copy.wait()

    def in_hbm_now(array):
        return pltpu.with_memory_space_constraint(array, pltpu.HBM)

    args = [spots]
    args += [a if any_place else in_hbm_now(a) for (a, _), any_place in zip(loads, free, strict=True)]
    args += [in_hbm_now(piece) for piece in pieces]
    aliases = {len(args) + at: out for at, (_, out) in enumerate(reuse)}
    args += [in_hbm_now(array) for array, _ in reuse]
    hbm = pl.BlockSpec(memory_space=pltpu.HBM)
    most = max([out.shape[0] for out, index in outs if index == EACH], default=1)
    scratch = [pltpu.VMEM(part(item), item[0].dtype) for item in loads]
    scratch += [pltpu.VMEM(part(item), item[0].dtype) for item in outs]
    scratch += [
        pltpu.VMEM((sum(piece.shape[1] for piece in group), group[0].shape[2]), group[0].dtype)
        for group, _, _ in slots
    ]
    scratch += [
        pltpu.SemaphoreType.DMA((max(n_in, 1),)),
        pltpu.SemaphoreType.DMA((len(outs), most)),
    ]
    scratch += [pltpu.SemaphoreType.DMA((len(group),)) for group, _, _ in slots]
    return pl.pallas_call(
        run,
        out_shape=[pltpu.HBM(out.shape, out.dtype) for out in out_shapes],
        in_specs=[pl.BlockSpec(memory_space=pltpu.SMEM)]
        + [pl.BlockSpec(memory_space=pl.ANY) if any_place else hbm for any_place in free]
        + [hbm] * (n_piece + n_reuse),
        out_specs=[hbm] * len(out_shapes),
        scratch_shapes=scratch + list(extra),
        input_output_aliases=aliases,
        compiler_params=pltpu.CompilerParams(vmem_limit_bytes=VMEM_LIMIT),
        cost_estimate=cost(name),
        name=name,
    )(*args)


def normalized(v):
    centered = v - jnp.mean(v, axis=1, keepdims=True)
    variance = jnp.mean(centered * centered, axis=1, keepdims=True)
    scale = lax.rsqrt(variance + 1e-05)
    return centered * scale, scale


def norm_back(v, cot, gain):
    n, scale = normalized(v)
    e = cot * gain
    grad = scale * (
        e - jnp.mean(e, axis=1, keepdims=True) - n * jnp.mean(e * n, axis=1, keepdims=True)
    )
    return grad, n


def turn_wide(wide, tables, sign):
    keep, below, above = tables[0], tables[1], tables[2]
    turned = []
    for at in range(0, wide.shape[1], LANES):
        tile = wide[:, at : at + LANES]
        moved = pltpu.roll(tile, 8, 1) * below + pltpu.roll(tile, LANES - 8, 1) * above
        turned.append(tile * keep + sign * moved)
    return jnp.concatenate(turned, axis=1)


def total_of(terms):
    return functools.reduce(jnp.add, terms)


def qkv_body(has_norm, io):
    queries, kv = io.outs[:2]
    if has_norm:
        first_in = io.outs[2]
        n, _ = normalized(io.get(4)[...].astype(F32))
        first_in[...] = (n * io.get(2)[...] + io.get(3)[...]).astype(BF)
        io.put(2)
    else:
        first_in = io.get(2)
    bias, tables = io.get(0), io.get(1)
    for slot, index in enumerate((1, 2, 0)):
        part = mm(first_in[...], io.weight(slot)[...], NN) + bias[index : index + 1, :]
        if index < 2:
            part = turn_wide(part, tables, 1.0)
        if index == 0:
            queries[...] = part.astype(BF)
        else:
            kv[index - 1] = part.astype(BF)
    io.put(1)
    io.put(0)


def attend_body(n_blocks, io):
    queries = io.get(0)
    kvs = [io.get(1 + at) for at in range(n_blocks)]
    masks = [io.get(1 + n_blocks + at) for at in range(n_blocks)]
    mixed, log_total, part = io.outs
    for head in range(queries.shape[1] // HD):
        span = slice(head * HD, (head + 1) * HD)
        query = queries[:, span]
        scores = [
            mm(kv[0, :, span], query, NT) * SCALE + mask[...]
            for kv, mask in zip(kvs, masks, strict=True)
        ]
        top = functools.reduce(jnp.maximum, [jnp.max(s, axis=0, keepdims=True) for s in scores])
        exps = [jnp.exp(s - top) for s in scores]
        total = total_of([jnp.sum(e, axis=0, keepdims=True) for e in exps])
        inverse = 1.0 / total
        result = total_of(
            [
                mm((e * inverse).astype(BF), kv[1, :, span], TN)
                for e, kv in zip(exps, kvs, strict=True)
            ]
        )
        log_total[head : head + 1, :] = top + jnp.log(total)
        mixed[:, span] = result.astype(BF)
    io.put(0)
    io.put(1)
    part[...] = mm(mixed[...], io.weight(0)[...], NT).astype(BF)
    io.put(2)


def terms_sum(terms):
    return total_of([terms[at].astype(F32) for at in range(terms.shape[0])])


def norm_body(io):
    stream = terms_sum(io.get(0)) + io.get(1)[...].astype(F32)
    io.outs[0][...] = stream
    io.put(0)
    n, _ = normalized(stream)
    io.outs[1][...] = (n * io.get(2)[...] + io.get(3)[...]).astype(BF)
    io.put(1)


def sum_body(io):
    io.outs[0][...] = (terms_sum(io.get(0)) + io.get(1)[...].astype(F32)).astype(BF)
    io.put(0)


def mlp_body(io):
    gate_out, up_out, hidden, part = io.outs
    second_in = io.get(0)
    gate = mm(second_in[...], io.weight(0)[...], NN)
    gate_out[...] = gate.astype(BF)
    io.put(0)
    act = gate * jax.nn.sigmoid(gate)
    up = mm(second_in[...], io.weight(1)[...], NN)
    up_out[...] = up.astype(BF)
    io.put(1)
    hidden[...] = (act * up).astype(BF)
    io.put(2)
    part[...] = mm(hidden[...], io.weight(2)[...], NT).astype(BF)
    io.put(3)


def mlp_back_body(io):
    d_gate_up, part = io.outs
    d_mlp = io.get(2)
    gate = io.get(0)[...].astype(F32)
    sig = jax.nn.sigmoid(gate)
    d_hidden = mm(d_mlp[...], io.weight(0)[...], NN)
    d_gate_up[1] = (d_hidden * (gate * sig)).astype(BF)
    d_gate_up[0] = (
        d_hidden * io.get(1)[...].astype(F32) * (sig * (1.0 + gate * (1.0 - sig)))
    ).astype(BF)
    io.put(0)
    total = mm(d_gate_up[0], io.weight(1)[...], NT)
    total = total + mm(d_gate_up[1], io.weight(2)[...], NT)
    part[...] = total.astype(BF)
    io.put(1)


def norm_back_body(io):
    c = terms_sum(io.get(0))
    grad, n = norm_back(io.get(1)[...].astype(F32), c, io.get(2)[...])
    grad = io.get(3)[...].astype(F32) + grad
    io.outs[0][...] = grad
    io.put(0)
    io.outs[1][...] = grad.astype(BF)
    io.put(1)
    io.outs[2][0:1, :] = jnp.sum(n * c, axis=0, keepdims=True)
    io.outs[2][1:2, :] = jnp.sum(c, axis=0, keepdims=True)
    io.put(2)


def attend_back_body(n_blocks, io):
    d_query, d_kvs = io.outs[0], io.outs[1:]
    d_mixed = io.extra[0]
    d_mixed[...] = mm(io.get(0)[...], io.weight(0)[...], NN).astype(BF)
    queries, log_total, tables = io.get(1), io.get(2), io.get(3)
    kvs = [io.get(4 + at) for at in range(n_blocks)]
    masks = [io.get(4 + n_blocks + at) for at in range(n_blocks)]
    pair = []
    for head in range(queries.shape[1] // HD):
        span = slice(head * HD, (head + 1) * HD)
        query = queries[:, span]
        d_out = d_mixed[:, span]
        row_log = log_total[head : head + 1, :]
        probs = [
            jnp.exp(mm(kv[0, :, span], query, NT) * SCALE + mask[...] - row_log)
            for kv, mask in zip(kvs, masks, strict=True)
        ]
        d_probs = [mm(kv[1, :, span], d_out, NT) for kv in kvs]
        delta = total_of(
            [jnp.sum(p * dp, axis=0, keepdims=True) for p, dp in zip(probs, d_probs, strict=True)]
        )
        d_scores = [
            (p * (dp - delta)).astype(BF) for p, dp in zip(probs, d_probs, strict=True)
        ]
        pair.append(
            total_of([mm(ds, kv[0, :, span], TN) for ds, kv in zip(d_scores, kvs, strict=True)])
            * SCALE
        )
        if len(pair) == LANES // HD:
            wide = slice((head + 1) * HD - LANES, (head + 1) * HD)
            d_query[:, wide] = turn_wide(jnp.concatenate(pair, axis=1), tables, -1.0).astype(BF)
            pair = []
        for ds, p, d_kv in zip(d_scores, probs, d_kvs, strict=True):
            d_kv[0, :, span] = (mm(ds, query, NN) * SCALE).astype(d_kv.dtype)
            d_kv[1, :, span] = mm(p.astype(BF), d_out, NN).astype(d_kv.dtype)
    for at in range(1 + n_blocks):
        io.put(at)


def qkv_back_body(n_other, io):
    d_qkv, bias, part = io.outs
    tables = io.get(1)
    terms = [io.get(2 + at) for at in range(1 + n_other)]
    d_qkv[0] = io.get(0)[...]
    d_qkv[1] = turn_wide(
        total_of([term[0].astype(F32) for term in terms]), tables, -1.0
    ).astype(BF)
    d_qkv[2] = total_of([term[1].astype(F32) for term in terms]).astype(BF)
    io.put(0)
    for index in range(3):
        bias[index : index + 1, :] = jnp.sum(d_qkv[index].astype(F32), axis=0, keepdims=True)
    io.put(1)
    part[...] = total_of(
        [mm(d_qkv[index], io.weight(index)[...], NT) for index in range(3)]
    ).astype(BF)
    io.put(2)


def pack_body(io):
    gate_up, down = io.get(0), io.get(1)
    for part in range(2):
        io.outs[part][0] = gate_up[:, part, :]
        io.put(part)
    io.outs[2][0] = down[...].T
    io.put(2)


def add_body(io):
    io.outs[0][...] = (io.get(0)[...].astype(F32) + io.get(2)[...].astype(F32)).astype(BF)
    io.put(0)
    io.outs[1][...] = (io.get(1)[...].astype(F32) + io.get(3)[...].astype(F32)).astype(BF)
    io.put(1)


def finish_body(is_mlp, io):
    own, x1, y1, x2, y2 = (io.get(at) for at in range(5))
    half = own.shape[2]
    main, other = io.outs
    matrices = own.shape[1]
    for side, (one, two) in enumerate(((x1, y2), (y1, x2))):
        rows = slice(side * half, (side + 1) * half)
        for matrix in range(matrices):
            whole = (
                own[side, matrix].astype(F32) + one[matrix].astype(F32) + two[matrix].astype(F32)
            )
            if matrix == matrices - 1:
                other[:, rows] = whole.T
            elif is_mlp:
                main[rows, matrix, :] = whole
            else:
                main[matrix, rows, :] = whole
    io.put(0)
    io.put(1)


def weight_grad_body(counts, n_left, pairs, *refs):
    ids = refs[0]
    n_in, n_held = len(counts), sum(counts)
    own = refs[1 : 1 + n_in]
    peer = refs[1 + n_in : 1 + 2 * n_in]
    outs = refs[1 + 2 * n_in : 6 + 2 * n_in]
    held = refs[6 + 2 * n_in : 6 + 2 * n_in + n_held]
    stage, in_sems, out_sems = refs[6 + 2 * n_in + n_held :]
    rows = held[0].shape[0] // 2
    loads = []
    for part, side in enumerate((own, peer)):
        at = 0
        for source, count in zip(side, counts, strict=True):
            for index in range(count):
                copy = pltpu.make_async_copy(
                    source if len(source.shape) == 2 else source.at[index],
                    held[at].at[pl.ds(part * rows, rows), :],
                    in_sems.at[at, part],
                )
                copy.start()
                loads.append(copy)
                at += 1
    for copy in loads:
        copy.wait()
    half = stage.shape[2]
    own_out, x1, y1, x2, y2 = outs
    targets = (
        (x1.at[0], y1.at[0]),
        (x1.at[1], x2),
        (y2, y1.at[1]),
        (own_out.at[0], own_out.at[1]),
    )
    stores = []
    for block in range(4):
        start = pl.multiple_of(ids[block], LANES)
        for matrix, (left, right) in enumerate(pairs):
            lhs = held[left][:, pl.ds(start, 2 * half)]
            result = mm(lhs, held[n_left + right][...], TN).astype(BF)
            stage[2 * block, matrix] = result[:half]
            stage[2 * block + 1, matrix] = result[half:]
        for part in range(2):
            copy = pltpu.make_async_copy(
                stage.at[2 * block + part], targets[block][part], out_sems.at[block, part]
            )
            copy.start()
            stores.append(copy)
    for copy in stores:
        copy.wait()


def after(array, *earlier):
    return lax.optimization_barrier((array,) + earlier)[0]


def pairs_of(axis, bit):
    return [(index, index ^ bit) for index in range(lax.axis_size(axis))]


def swap_x(array):
    return lax.ppermute(array, "fsdp", pairs_of("fsdp", 2))


def swap_core(array):
    return lax.ppermute(array, "fsdp", pairs_of("fsdp", 1))


def swap_y(array):
    return lax.ppermute(array, "ctx", pairs_of("ctx", 1))


def place():
    fsdp = lax.axis_index("fsdp")
    return fsdp // 2, fsdp % 2, lax.axis_index("ctx")


class Gather:
    def __init__(self, shard):
        self.shard = shard
        self.rows = shard.shape[1]

    def near_x(self, wait=()):
        self.from_x = swap_x(after(self.shard, *wait))

    def near_y(self, wait=()):
        self.from_y = swap_y(after(self.shard, *wait))
        self.mine = [self.shard, self.from_x, self.from_y]

    def near(self, wait_x=(), wait_y=()):
        self.near_x(wait_x)
        self.near_y(wait_y)

    def swap(self, *wait):
        self.peers = [swap_core(after(piece, *wait)) for piece in self.mine]

    def far(self, way, wait_x=(), wait_y=()):
        half = self.rows // 2
        self.way = way
        if way == "x":
            self.pieces = [swap_x(after(self.from_y, *wait_x))]
        elif way == "y":
            self.pieces = [swap_y(after(self.from_x, *wait_y))]
        else:
            self.pieces = [
                swap_x(after(self.from_y[:, :half], *wait_x)),
                swap_y(after(self.from_x[:, half:], *wait_y)),
            ]

    def all(self):
        far_peers = [swap_core(piece) for piece in self.pieces]
        return self.mine + self.pieces + self.peers + far_peers


def piece_rows(rows):
    x, core, y = place()

    def row(x_at, core_at, y_at):
        return ((x_at * 2 + core_at) * 2 + y_at) * rows

    offs = []
    for halves in (0, 1):
        for core_at in (core, 1 - core):
            offs += [row(x, core_at, y), row(1 - x, core_at, y), row(x, core_at, 1 - y)]
            offs.append(row(1 - x, core_at, 1 - y))
            if halves:
                offs.append(row(1 - x, core_at, 1 - y) + rows // 2)
    return offs


def gather_whole(shard):
    return [lax.all_gather(shard, ("fsdp", "ctx"), axis=1, tiled=True)]


def gather_small(packed, fast):
    if not fast:
        return lax.all_gather(packed, ("fsdp", "ctx"), axis=1, tiled=True)
    x, core, y = place()

    def join(array, other, bit):
        return jnp.where(bit == 0, jnp.stack([array, other]), jnp.stack([other, array]))

    held = join(packed, swap_core(packed), core)
    held = join(held, swap_x(held), x)
    held = join(held, swap_y(held), y)
    rows, cols = packed.shape
    return held.transpose(3, 1, 2, 0, 4).reshape(rows, 8 * cols)


def reduce_small(sums, fast):
    if not fast:
        part = lax.psum_scatter(sums, ("fsdp", "ctx"), scatter_dimension=1, tiled=True)
        return lax.psum(part, "tp"), part
    x, core, y = place()
    rows, width = sums.shape
    held = sums.reshape(rows, 2, 2, 2, width // 8).transpose(1, 3, 2, 0, 4)
    for bit, swap in ((x, swap_x), (y, swap_y), (core, swap_core)):
        keep = jnp.where(bit == 0, held[0], held[1])
        send = jnp.where(bit == 0, held[1], held[0])
        held = keep + swap(send)
        if swap is swap_y:
            halfway = held
    step = 1
    while step < lax.axis_size("tp"):
        held = held + lax.ppermute(held, "tp", pairs_of("tp", step))
        step *= 2
    return held, halfway


def tensor_scatter(part, *earlier):
    size = lax.axis_size("tp")
    blocks = after(part, *earlier).reshape(size, part.shape[0] // size, part.shape[1])
    return lax.all_to_all(blocks, "tp", 0, 0, tiled=True)


def tensor_gather(copies):
    size, block, width = copies.shape
    return lax.all_to_all(copies, "tp", 0, 0, tiled=True).reshape(size * block, width)


def weight_grads(own, n_left, pairs, earlier, wait, name):
    counts = tuple(1 if array.ndim == 2 else array.shape[0] for array in own)
    columns = own[-1].shape[-1]
    tokens, width = own[0].shape
    peer = [swap_core(after(array, *earlier)) for array in own]
    rows = width // 8
    half = rows // 2
    x, core, y = place()
    ids = jnp.stack(
        [
            ((x_at * 2 + core) * 2 + y_at) * rows
            for x_at, y_at in ((1 - x, 1 - y), (1 - x, y), (x, 1 - y), (x, y))
        ]
    ).astype(jnp.int32)
    block = (len(pairs), half, columns)
    hbm = pl.BlockSpec(memory_space=pltpu.HBM)
    scratch = [
        pltpu.VMEM((2 * tokens, array.shape[-1]), BF)
        for array, count in zip(own, counts, strict=True)
        for _ in range(count)
    ]
    scratch += [
        pltpu.VMEM((8,) + block, BF),
        pltpu.SemaphoreType.DMA((sum(counts), 2)),
        pltpu.SemaphoreType.DMA((4, 2)),
    ]
    own_sum, x1, y1, x2, y2 = pl.pallas_call(
        functools.partial(weight_grad_body, counts, n_left, pairs),
        out_shape=[pltpu.HBM((2,) + block, BF)] * 3 + [pltpu.HBM(block, BF)] * 2,
        in_specs=[pl.BlockSpec(memory_space=pltpu.SMEM)] + [hbm] * (2 * len(own)),
        out_specs=[hbm] * 5,
        scratch_shapes=scratch,
        compiler_params=pltpu.CompilerParams(vmem_limit_bytes=VMEM_LIMIT),
        cost_estimate=cost(name),
        name=name,
    )(ids, *[pltpu.with_memory_space_constraint(a, pltpu.HBM) for a in list(own) + peer])
    return (own_sum, x2, y2), (swap_x(after(x1, *wait)), swap_y(after(y1, *wait)))


def reduce_second(spots, parts, received, earlier_add, earlier_send, name):
    own_sum, x2, y2 = parts
    got_x1, got_y1 = received
    block = shape(x2.shape, BF)
    send_x, send_y = kernel(
        add_body,
        name,
        spots,
        [after(x2, *earlier_add), y2, (got_y1, 0), (got_x1, 0)],
        [block, block],
    )
    far_x = swap_x(after(send_x, *earlier_send))
    far_y = swap_y(after(send_y, *earlier_send))
    return [own_sum, (got_x1, 1), (got_y1, 1), far_x, far_y], send_x


def layout(lengths, first_row, row_count):
    token_index = first_row + jnp.arange(row_count, dtype=jnp.int32)
    doc_ends = jnp.cumsum(lengths)
    starts = doc_ends - lengths
    segment = jnp.sum(
        (token_index[:, None] >= doc_ends[None, :]).astype(jnp.int32), axis=1, dtype=jnp.int32
    )
    doc_begin = jnp.max(
        jnp.where(token_index[:, None] >= starts[None, :], starts[None, :], 0), axis=1
    )
    return (segment, token_index - doc_begin, token_index)


def rotary_tables(position):
    frequency = 10000.0 ** (-jnp.arange(0, ROT, 2, dtype=F32) / ROT)
    angles = position.astype(F32)[:, None] * frequency[None, :]
    cos, sin = jnp.cos(angles), jnp.sin(angles)
    rows = position.shape[0]
    blank = jnp.zeros((rows, ROT // 2), F32)
    rest = HD - ROT
    keep = jnp.concatenate([cos, cos, jnp.ones((rows, rest), F32)], axis=1)
    below = jnp.concatenate([blank, sin, jnp.zeros((rows, rest), F32)], axis=1)
    above = jnp.concatenate([-sin, blank, jnp.zeros((rows, rest), F32)], axis=1)
    return jnp.stack([jnp.tile(t, (1, LANES // HD)) for t in (keep, below, above)])


def local(
    tokens,
    cotangent,
    doc_lengths,
    norm_gains,
    norm_biases,
    qkv_weight,
    qkv_bias,
    out_weight,
    gate_up_weight,
    down_weight,
):
    rows = tokens.shape[1]
    width = tokens.shape[2]
    heads_width = qkv_weight.shape[3]
    hidden_width = gate_up_weight.shape[3]
    heads = heads_width // HD
    layers = norm_gains.shape[0]
    block_rows = qkv_weight.shape[1]
    ctx_size = lax.axis_size("ctx")
    fast = lax.axis_size("fsdp") == 4 and ctx_size == 2
    ctx_rank = lax.axis_index("ctx")
    tensor_rank = lax.axis_index("tp")

    small = jnp.concatenate(
        [
            norm_gains.reshape(2 * layers, -1),
            norm_biases.reshape(2 * layers, -1),
            qkv_bias.reshape(3 * layers, -1),
        ]
    )
    small = gather_small(small, fast).astype(F32)
    gains = small[: 2 * layers].reshape(layers, 2, width)
    shifts = small[2 * layers : 4 * layers].reshape(layers, 2, width)
    biases = lax.dynamic_slice_in_dim(
        small[4 * layers :], tensor_rank * heads_width, heads_width, 1
    ).reshape(layers, 3, heads_width)

    tensor_size = lax.axis_size("tp")
    block = rows // tensor_size
    spots = piece_rows(block_rows) if fast else [jnp.int32(0)]
    spots = jnp.stack([jnp.asarray(spot, jnp.int32) for spot in spots])
    spots_at = {8: 0, 10: 8, 1: 0}

    def slot(pieces, matrix):
        return (pieces, matrix, spots_at[len(pieces)])

    shards = []
    for layer in range(layers):
        if fast:
            mlp_shards = kernel(
                pack_body,
                "pack",
                spots,
                [(gate_up_weight, layer), (down_weight, layer)],
                [shape((1, block_rows, hidden_width), BF)] * 3,
            )
        else:
            mlp_shards = [gate_up_weight[layer][None, :, part] for part in range(2)]
            mlp_shards.append(down_weight[layer].T[None])
        shards.append((qkv_weight[layer].transpose(1, 0, 2), out_weight[layer].T[None], *mlp_shards))

    lengths = doc_lengths[0]
    seg_query, pos_query, index_query = layout(lengths, ctx_rank * rows, rows)
    tables = rotary_tables(pos_query)

    def mask_of(first, count, usable):
        seg_key, _, index_key = layout(lengths, first, count)
        allowed = (seg_query[None, :] == seg_key[:, None]) & (
            index_query[None, :] >= index_key[:, None]
        )
        return jnp.where(allowed & usable, 0.0, -1e30).astype(F32)

    if fast:
        masks = [
            mask_of(jnp.int32(0), rows, ctx_rank > 0),
            mask_of(ctx_rank * rows, rows, True),
        ]
    else:
        masks = [mask_of(jnp.int32(0), rows * ctx_size, True)]
    n_blocks = len(masks)

    wide = shape((rows, width), BF)
    inner = shape((rows, hidden_width), BF)
    headed = shape((rows, heads_width), BF)
    block_f = shape((block, width), F32)
    copies_b = (shape((tensor_size, block, width), BF), EACH)

    stream = lax.dynamic_slice_in_dim(tokens[0], tensor_rank * block, block, 0)
    first_in = None
    saved, groups = [], []
    if fast:
        qkv_g, out_g, gate_g, up_g, down_g = (Gather(shard) for shard in shards[0])
        qkv_g.near()
        qkv_g.swap()
        qkv_g.far("both")
        out_g.near(qkv_g.pieces, qkv_g.pieces)
    for layer in range(layers):
        if fast:
            qkv_pieces = qkv_g.all()
        else:
            qkv_pieces, *others = (gather_whole(shard) for shard in shards[layer])
            out_pieces, gate_pieces, up_pieces, down_pieces = others
        outs = [headed, shape((2, rows, heads_width), BF)]
        if layer == 0:
            args = [biases[0], tables, gains[0, 0][None], shifts[0, 0][None], tokens[0]]
            if fast:
                args[0] = after(args[0], gate_g.shard)
            outs.append(wide)
        else:
            args = [biases[layer], tables, Free(first_in)]
        queries, kv, *normed = kernel(
            functools.partial(qkv_body, layer == 0),
            "qkv",
            spots,
            args,
            outs,
            [slot(qkv_pieces, index) for index in (1, 2, 0)],
        )
        if layer == 0:
            first_in = normed[0]
        if fast:
            prev = lax.ppermute(kv, "ctx", [(0, 1)])
            kv_blocks = [prev, kv]
            out_g.swap(queries)
            if layer == 0:
                out_g.far("x", (queries,))
                gate_g.near((*out_g.pieces, out_g.from_x), (prev,))
            else:
                out_g.far("x", (queries, up_g.from_x))
                gate_g.swap(queries)
                gate_g.far("x", (queries, *out_g.pieces))
                up_g.near_y((prev,))
            out_pieces = out_g.all()
        else:
            kv_blocks = [lax.all_gather(kv, "ctx", axis=1, tiled=True)]
        mixed, log_total, part = kernel(
            functools.partial(attend_body, n_blocks),
            "attend",
            spots,
            [queries] + kv_blocks + masks,
            [headed, shape((heads, rows), F32), wide],
            [slot(out_pieces, 0)],
        )
        terms = tensor_scatter(part)
        if fast:
            if layer == 0:
                up_g.near((part, gate_g.from_x), (part, gate_g.from_y))
                gate_g.swap(part)
                gate_g.far("both", (part,), (part,))
            else:
                down_g.near((part, *gate_g.pieces), (part, up_g.from_y))
                up_g.swap(part)
                up_g.far("both", (part,), (part,))
        mid, normed = kernel(
            norm_body,
            "norm",
            spots,
            [Free(terms), stream, gains[layer, 1][None], shifts[layer, 1][None]],
            [block_f, copies_b],
        )
        second_in = tensor_gather(normed)
        if fast:
            if layer == 0:
                down_g.near((mid, gate_g.pieces[0]), (mid, gate_g.pieces[1]))
                up_g.swap(mid)
                up_g.far("both", (mid,), (mid,))
                down_g.swap()
            else:
                down_g.swap(mid)
            down_g.far("both", (mid, up_g.pieces[0]), (mid, up_g.pieces[1]))
            gate_pieces, up_pieces, down_pieces = gate_g.all(), up_g.all(), down_g.all()
        gate, up, hidden, part = kernel(
            mlp_body,
            "mlp",
            spots,
            [Free(second_in)],
            [inner, inner, inner, wide],
            [slot(gate_pieces, 0), slot(up_pieces, 0), slot(down_pieces, 0)],
        )
        saved.append((stream, first_in, queries, kv_blocks, mixed, log_total, mid))
        saved[-1] += (second_in, gate, up, hidden)
        groups.append((qkv_pieces, out_pieces, gate_pieces, up_pieces, down_pieces))
        if layer == layers - 1:
            break
        terms = tensor_scatter(part)
        if fast:
            sent = down_g.pieces
            qkv_g, out_g, gate_g, up_g, down_g = (Gather(shard) for shard in shards[layer + 1])
            qkv_g.near(sent[:1], sent[1:])
            qkv_g.swap(part)
            qkv_g.far("y", (), (part,))
            out_g.near((qkv_g.from_x, part), (qkv_g.pieces[0],))
            gate_g.near((out_g.from_x,), (out_g.from_y,))
            up_g.near_x((gate_g.from_x,))
            terms = after(terms, gate_g.shard)
        stream, normed = kernel(
            norm_body,
            "norm",
            spots,
            [Free(terms), mid, gains[layer + 1, 0][None], shifts[layer + 1, 0][None]],
            [block_f, copies_b],
        )
        first_in = tensor_gather(normed)
    last_part, last_mid = part, mid

    attn_outs, mlp_outs, pending = None, None, None
    sums = [None] * layers
    plain = [None] * layers
    grad = lax.dynamic_slice_in_dim(cotangent[0], tensor_rank * block, block, 0)
    d_mlp = cotangent[0]
    for layer in reversed(range(layers)):
        (stream, first_in, queries, kv_blocks, mixed, log_total, mid) = saved[layer][:7]
        (second_in, gate, up, hidden) = saved[layer][7:]
        qkv_pieces, out_pieces, gate_pieces, up_pieces, down_pieces = groups[layer]
        d_gate_up, part = kernel(
            mlp_back_body,
            "mlp_back",
            spots,
            [gate, up, Free(d_mlp)],
            [shape((2, rows, hidden_width), BF), wide],
            [slot(down_pieces, 0), slot(gate_pieces, 0), slot(up_pieces, 0)],
        )
        terms = tensor_scatter(part)
        pairs = ((0, 0), (0, 1), (1, 2))
        if fast:
            ready, attn_added = [], ()
            if pending is not None:
                attn_terms, attn_added = reduce_second(spots, *pending, (part,), (), "attn_add")
                attn_added = (attn_added,)
                ready += attn_terms[3:]
            mlp_parts, mlp_sent = weight_grads(
                [second_in, d_mlp, d_gate_up, hidden],
                2,
                pairs,
                (part, *attn_added),
                ready,
                "mlp_grads",
            )
            ready.append(mlp_parts[0])
            terms = after(terms, *ready)
        else:
            mlp_grad = plain_grads(
                [second_in, d_mlp], [d_gate_up[0], d_gate_up[1], hidden], pairs
            )
        grad_mid, normed, sums_two = kernel(
            norm_back_body,
            "norm_back",
            spots,
            [Free(terms), mid, gains[layer, 1][None], grad],
            [block_f, copies_b, shape((2, width), F32)],
        )
        d_attn = tensor_gather(normed)
        if pending is not None:
            attn_terms[0] = after(attn_terms[0], grad_mid)
            attn_outs = attn_finish(spots, attn_outs, attn_terms, layer + 1, layers)
            d_attn = after(d_attn, attn_outs[0])
        if layer == layers - 1:
            (summed,) = kernel(
                sum_body, "sum", spots, [tensor_scatter(last_part, d_attn), last_mid], [copies_b]
            )
        elif layer == layers - 2:
            output = tensor_gather(after(summed, d_attn))
        kv_outs = [shape(kv.shape, BF) for kv in kv_blocks]
        if fast:
            kv_outs[-1] = shape((2, rows, heads_width), F32)
        d_query, *d_kvs = kernel(
            functools.partial(attend_back_body, n_blocks),
            "attend_back",
            spots,
            [Free(d_attn), queries, log_total, tables] + kv_blocks + masks,
            [headed] + kv_outs,
            [slot(out_pieces, 0)],
            extra=[pltpu.VMEM((rows, heads_width), BF)],
        )
        if fast:
            own = d_kvs[1]
            other = [lax.ppermute(after(d_kvs[0], *mlp_sent), "ctx", [(1, 0)])]
            mlp_terms, mlp_added = reduce_second(
                spots, mlp_parts, mlp_sent, (d_kvs[0],), (), "mlp_add"
            )
            own = after(own, mlp_added)
        else:
            own = lax.psum_scatter(d_kvs[0], "ctx", scatter_dimension=1, tiled=True)
            other = []
        d_qkv, bias_sums, part = kernel(
            functools.partial(qkv_back_body, len(other)),
            "qkv_back",
            spots,
            [d_query, tables, own] + other,
            [shape((3, rows, heads_width), BF), shape((3, heads_width), F32), wide],
            [slot(qkv_pieces, index) for index in range(3)],
        )
        terms = tensor_scatter(part)
        if layer == layers - 1:
            terms = after(terms, summed)
        elif layer == layers - 2:
            terms = after(terms, output)
        pairs = ((0, 0), (0, 1), (0, 2), (1, 3))
        if fast:
            pending = weight_grads(
                [first_in, d_attn, d_qkv, mixed], 2, pairs, (part,), (), "attn_grads"
            )
            terms = after(terms, pending[0][0], *mlp_terms[3:])
        else:
            rights = [d_qkv[0], d_qkv[1], d_qkv[2], mixed]
            plain[layer] = (plain_grads([first_in, d_attn], rights, pairs), mlp_grad)
        grad, normed, sums_one = kernel(
            norm_back_body,
            "norm_back",
            spots,
            [Free(terms), stream, gains[layer, 0][None], grad_mid],
            [block_f, copies_b, shape((2, width), F32)],
        )
        d_mlp = tensor_gather(normed)
        if fast:
            mlp_terms[0] = after(mlp_terms[0], grad)
            mlp_outs = kernel(
                functools.partial(finish_body, True),
                "mlp_finish",
                spots,
                mlp_terms,
                [
                    (shape((layers, block_rows, 2, hidden_width), F32), layer),
                    (shape((layers, hidden_width, block_rows), F32), layer),
                ],
                reuse=() if mlp_outs is None else ((mlp_outs[0], 0), (mlp_outs[1], 1)),
            )
            d_mlp = after(d_mlp, mlp_outs[0], *pending[1])
        bias_rows = lax.dynamic_update_slice_in_dim(
            jnp.zeros((3, width), F32), bias_sums, tensor_rank * heads_width, 1
        )
        sums[layer] = jnp.concatenate(
            [sums_one[0:1], sums_two[0:1], sums_one[1:2], sums_two[1:2], bias_rows]
        )
    totals, halfway = reduce_small(jnp.concatenate(sums), fast)
    totals = totals.reshape(layers, 7, -1)
    if fast:
        attn_terms, _ = reduce_second(spots, *pending, (grad,), (), "attn_add")
        attn_outs = attn_finish(spots, attn_outs, attn_terms, 0, layers)
    grad_input = d_mlp.astype(F32)
    if fast:
        grads = (attn_outs[0].transpose(0, 2, 1, 3), attn_outs[1], mlp_outs[0], mlp_outs[1])
    else:
        attn = jnp.stack([pair[0] for pair in plain])
        mlp = jnp.stack([pair[1] for pair in plain])
        grads = (
            attn[:, :3].transpose(0, 2, 1, 3),
            attn[:, 3].transpose(0, 2, 1),
            mlp[:, :2].transpose(0, 2, 1, 3),
            mlp[:, 2].transpose(0, 2, 1),
        )
    return (
        output[None],
        grad_input[None],
        totals[:, 0:2],
        totals[:, 2:4],
        grads[0],
        totals[:, 4:7],
        grads[1],
        grads[2],
        grads[3],
    )


def attn_finish(spots, outs, terms, layer, layers):
    matrices, half, columns = terms[3].shape
    rows = 2 * half
    return kernel(
        functools.partial(finish_body, False),
        "attn_finish",
        spots,
        terms,
        [
            (shape((layers, matrices - 1, rows, columns), F32), layer),
            (shape((layers, columns, rows), F32), layer),
        ],
        reuse=() if outs is None else ((outs[0], 0), (outs[1], 1)),
    )


def plain_grads(lefts, rights, pairs):
    whole = jnp.stack([mm(lefts[a], rights[b], TN).astype(BF) for a, b in pairs])
    return lax.psum_scatter(whole, ("fsdp", "ctx"), scatter_dimension=1, tiled=True).astype(F32)


def solution(mesh):
    return jax.shard_map(
        local,
        mesh=mesh,
        in_specs=(
            P("fsdp", "ctx", None),
            P("fsdp", "ctx", None),
            P("fsdp", None),
            P(None, None, ("fsdp", "ctx")),
            P(None, None, ("fsdp", "ctx")),
            P(None, ("fsdp", "ctx"), None, "tp"),
            P(None, None, ("fsdp", "ctx")),
            P(None, "tp", ("fsdp", "ctx")),
            P(None, ("fsdp", "ctx"), None, "tp"),
            P(None, "tp", ("fsdp", "ctx")),
        ),
        out_specs=(
            P("fsdp", "ctx", None),
            P("fsdp", "ctx", None),
            P(None, None, ("fsdp", "ctx")),
            P(None, None, ("fsdp", "ctx")),
            P(None, ("fsdp", "ctx"), None, "tp"),
            P(None, None, ("fsdp", "ctx")),
            P(None, "tp", ("fsdp", "ctx")),
            P(None, ("fsdp", "ctx"), None, "tp"),
            P(None, "tp", ("fsdp", "ctx")),
        ),
        check_vma=False,
    )
```

time: 938 us -> 801 us (0.85)
  waiting for transfers between devices: 530 us -> 356 us
  Pallas kernels: 149 us -> 235 us
  starting transfers between devices: 64.2 us -> 149 us
  local copies, waits for them, and re-layouts: 111 us -> 44 us
  other arithmetic: 58.2 us -> 4.02 us
  between operations: 16.2 us -> 3.06 us
    psum x7 -> x0, waiting for transfers between devices: 248 us -> none  [tensor_sum(): return lax.psum(part, 'tp')]
    all_to_all x0 -> x16, waiting for transfers between devices: none -> 99.5 us  [the longest x8 53.8 us: tensor_gather(): lax.all_to_all(copies, 'tp', 0, 0, tiled=True).reshape(size * block, width)]
    pallas_call x18 -> x34, Pallas kernels: 149 us -> 235 us  [the longest x30 200 us: kernel(): pl.pallas_call(run, out_shape=[pltpu.HBM(out.shape, out.dtype) for out in...]
    all_to_all x0 -> x16, starting transfers between devices: none -> 70.4 us  [the longest x8 35.6 us: tensor_scatter(): return lax.all_to_all(blocks, 'tp', 0, 0, tiled=True)]
    unnamed x304 -> x203, local copies, waits for them, and re-layouts: 76.1 us -> 22.4 us
    ppermute x18 -> x27, waiting for transfers between devices: 130 us -> 92.1 us  [swap_y(): return lax.ppermute(array, 'ctx', pairs_of('ctx', 1))]
    ppermute x18 -> x29, waiting for transfers between devices: 94.2 us -> 113 us  [swap_x(): return lax.ppermute(array, 'fsdp', pairs_of('fsdp', 2))]
    ppermute x2, waiting for transfers between devices: 33.4 us -> 17.7 us  [local(): other = [lax.ppermute(after(d_kvs[0], *mlp_sent), 'ctx', [(1, 0)])]]
  transfers between devices with their start and end apart: 93 -> 142, of which waited for: 30 -> 55; matrix products, arithmetic and copies ran while one was open for 10% -> 3% of each run, Pallas kernels for 14% -> 20%
where the time goes in v2:
time: 801 us; the launch traced here: 792 us
  waiting for transfers between devices  356 us (44%)
  Pallas kernels  235 us (29%)
  starting transfers between devices  149 us (19%)
  local copies, waits for them, and re-layouts  44 us (5%)
    pallas_call x30, Pallas kernels, kernel(): pl.pallas_call(run, out_shape=[pltpu.HBM(out.shape, out.dtype) for out in...  200 us
    ppermute x29, waiting for transfers between devices, swap_x(): return lax.ppermute(array, 'fsdp', pairs_of('fsdp', 2))  113 us
    ppermute x27, waiting for transfers between devices, swap_y(): return lax.ppermute(array, 'ctx', pairs_of('ctx', 1))  92.1 us
    all_to_all x8, waiting for transfers between devices, tensor_gather(): lax.all_to_all(copies, 'tp', 0, 0, tiled=True).reshape(size * block, width)  53.8 us
    all_to_all x8, waiting for transfers between devices, tensor_scatter(): return lax.all_to_all(blocks, 'tp', 0, 0, tiled=True)  45.7 us
    all_to_all x8, starting transfers between devices, tensor_scatter(): return lax.all_to_all(blocks, 'tp', 0, 0, tiled=True)  35.6 us
    pallas_call x4, Pallas kernels, weight_grads(): pl.pallas_call(functools.partial(weight_grad_body, counts, n_left, pairs)...  34.9 us
    all_to_all x8, starting transfers between devices, tensor_gather(): lax.all_to_all(copies, 'tp', 0, 0, tiled=True).reshape(size * block, width)  34.8 us
  transfers between devices with their start and end apart: 142, of which 55 were waited for; matrix products, arithmetic and copies ran while one was open for 3% of the time, Pallas kernels for 20%

profile of v2, /device:TPU:0, one launch (start us, length us, event | category | flops | bytes accessed | tf_op | source)
XLA Modules:
  0.0 791.7 jit_solution(10350002773880661985)
XLA Ops:
  10.3 6.9 pack.2
  17.8 6.8 collective-permute-done.1
  43.9 9.3 %qkv.2 = (bf16[256,512]{1,0:T(8,128)(2,1)}, bf16[2,256,512]{2,1,0:T(8,128)(2,1)}, bf16[256,2048]{1,0:T(8,128)(2,1)}) custom-call(s32[18]{0:T(128)S(1)} %stack.130.refs_0_, f32[3,512]{1,0:T(4,128)} %get-tuple-element.199.refs_1_, f32[3,256,128]{2,1,0:T(8,128)} %pad_maximum_fusion.refs_2_.refs_4_, f32[1,2048]{1,0:T(1,128)} %get-tuple-element.462.refs_3_, ...), custom_call_target="tpu_custom_call" | custom-call | bytes 25500000 | tf_op jit(solution)/shard_map/qkv/pallas_call | solution.py:185
  62.9 5.5 collective-permute-done.12.refs_2_.refs_5_
  69.2 8.1 %attend.2 = (bf16[256,512]{1,0:T(8,128)(2,1)}, f32[8,256]{1,0:T(8,128)}, bf16[256,2048]{1,0:T(8,128)(2,1)}) custom-call(s32[18]{0:T(128)S(1)} %stack.130.refs_0_, bf16[256,512]{1,0:T(8,128)(2,1)} %get-tuple-element.200.refs_1_.refs_2_, bf16[2,256,512]{2,1,0:T(8,128)(2,1)} %copy-done.37, bf16[2,256,512]{2,1,0:T(8,128)(2,1)} %get-tuple-element.201.refs_3_.refs_6_, ...), custom_call_target="tpu_custom_call" | custom-call | bytes 24000000 | tf_op jit(solution)/shard_map/attend/pallas_call | solution.py:185
  85.2 13.7 %collective-permute-done.20.refs_3_.refs_15_ = bf16[1,256,1408]{2,1,0:T(8,128)(2,1)S(1)} collective-permute-done((bf16[1,256,1408]{2,1,0:T(8,128)(2,1)}, bf16[1,256,1408]{2,1,0:T(8,128)(2,1)S(1)}, u32[]{:S(2)}, u32[]{:S(2)}) %collective-permute-start.20) | collective-permute-done | bytes 720928 | tf_op jit(solution)/shard_map/ppermute | solution.py:500
  104.1 6.6 collective-permute-done.23.refs_6_.refs_18_
  118.2 7.0 collective-permute-done.29.refs_13_.refs_25_
  138.0 18.2 %collective-permute-done.32.refs_16_.refs_28_ = bf16[1,128,1408]{2,1,0:T(8,128)(2,1)} collective-permute-done((bf16[1,128,1408]{2,1,0:T(8,128)(2,1)}, bf16[1,128,1408]{2,1,0:T(8,128)(2,1)}, u32[]{:S(2)}, u32[]{:S(2)}) %collective-permute-start.32) | collective-permute-done | bytes 360480 | tf_op jit(solution)/shard_map/ppermute | solution.py:508
  163.6 8.1 %collective-permute-done.41.refs_26_.refs_8_ = bf16[1,128,1408]{2,1,0:T(8,128)(2,1)S(1)} collective-permute-done((bf16[1,128,1408]{2,1,0:T(8,128)(2,1)S(1)}, bf16[1,128,1408]{2,1,0:T(8,128)(2,1)S(1)}, u32[]{:S(2)}, u32[]{:S(2)}) %collective-permute-start.41) | collective-permute-done | bytes 360480 | tf_op jit(solution)/shard_map/ppermute | solution.py:508
  175.9 11.6 %mlp.2 = (bf16[256,1408]{1,0:T(8,128)(2,1)}, bf16[256,1408]{1,0:T(8,128)(2,1)}, bf16[256,1408]{1,0:T(8,128)(2,1)}, bf16[256,2048]{1,0:T(8,128)(2,1)}) custom-call(s32[18]{0:T(128)S(1)} %stack.130.refs_0_, bf16[256,2048]{1,0:T(8,128)(2,1)S(1)} %bitcast.121, bf16[1,256,1408]{2,1,0:T(8,128)(2,1)} %get-tuple-element.212.refs_2_.refs_14_, ...), custom_call_target="tpu_custom_call" | custom-call | bytes 34500000 | tf_op jit(solution)/shard_map/mlp/pallas_call | solution.py:185
  193.0 18.6 %collective-permute-done.47.refs_5_.refs_6_ = bf16[3,256,512]{2,1,0:T(8,128)(2,1)} collective-permute-done((bf16[3,256,512]{2,1,0:T(8,128)(2,1)S(1)}, bf16[3,256,512]{2,1,0:T(8,128)(2,1)}, u32[]{:S(2)}, u32[]{:S(2)}) %collective-permute-start.47) | collective-permute-done | bytes 786464 | tf_op jit(solution)/shard_map/ppermute | solution.py:500
  212.5 6.8 pack.3
  231.5 8.5 %collective-permute-done.48.refs_6_.refs_7_ = bf16[3,256,512]{2,1,0:T(8,128)(2,1)} collective-permute-done((bf16[3,256,512]{2,1,0:T(8,128)(2,1)S(1)}, bf16[3,256,512]{2,1,0:T(8,128)(2,1)}, u32[]{:S(2)}, u32[]{:S(2)}) %collective-permute-start.48) | collective-permute-done | bytes 786464 | tf_op jit(solution)/shard_map/ppermute | solution.py:508
  240.0 14.9 %collective-permute-done.49.refs_7_.refs_8_ = bf16[3,256,512]{2,1,0:T(8,128)(2,1)} collective-permute-done((bf16[3,256,512]{2,1,0:T(8,128)(2,1)}, bf16[3,256,512]{2,1,0:T(8,128)(2,1)}, u32[]{:S(2)}, u32[]{:S(2)}) %collective-permute-start.49) | collective-permute-done | bytes 786464 | tf_op jit(solution)/shard_map/ppermute | solution.py:508
  259.0 7.3 qkv.3
  266.4 7.3 collective-permute-done.58.refs_11_.refs_23_
  283.1 7.5 collective-permute-done.54.refs_2_.refs_5_
  291.5 8.2 %attend.3 = (bf16[256,512]{1,0:T(8,128)(2,1)}, f32[8,256]{1,0:T(8,128)}, bf16[256,2048]{1,0:T(8,128)(2,1)}) custom-call(s32[18]{0:T(128)S(1)} %stack.130.refs_0_, bf16[256,512]{1,0:T(8,128)(2,1)} %get-tuple-element.238.refs_1_.refs_2_, bf16[2,256,512]{2,1,0:T(8,128)(2,1)} %copy-done.38, bf16[2,256,512]{2,1,0:T(8,128)(2,1)} %get-tuple-element.239.refs_3_.refs_6_, ...), custom_call_target="tpu_custom_call" | custom-call | bytes 24000000 | tf_op jit(solution)/shard_map/attend/pallas_call | solution.py:185
  309.5 11.6 %collective-permute-done.65.refs_5_.refs_17_ = bf16[1,256,1408]{2,1,0:T(8,128)(2,1)S(1)} collective-permute-done((bf16[1,256,1408]{2,1,0:T(8,128)(2,1)}, bf16[1,256,1408]{2,1,0:T(8,128)(2,1)S(1)}, u32[]{:S(2)}, u32[]{:S(2)}) %collective-permute-start.65) | collective-permute-done | bytes 720928 | tf_op jit(solution)/shard_map/ppermute | solution.py:500
  321.1 10.2 %collective-permute-done.72.refs_14_.refs_26_ = bf16[1,128,1408]{2,1,0:T(8,128)(2,1)S(1)} collective-permute-done((bf16[1,128,1408]{2,1,0:T(8,128)(2,1)S(1)}, bf16[1,128,1408]{2,1,0:T(8,128)(2,1)S(1)}, u32[]{:S(2)}, u32[]{:S(2)}) %collective-permute-start.72) | collective-permute-done | bytes 360480 | tf_op jit(solution)/shard_map/ppermute | solution.py:508
  345.2 9.7 %collective-permute-done.71.refs_13_.refs_25_ = bf16[1,128,1408]{2,1,0:T(8,128)(2,1)} collective-permute-done((bf16[1,128,1408]{2,1,0:T(8,128)(2,1)}, bf16[1,128,1408]{2,1,0:T(8,128)(2,1)}, u32[]{:S(2)}, u32[]{:S(2)}) %collective-permute-start.71) | collective-permute-done | bytes 360480 | tf_op jit(solution)/shard_map/ppermute | solution.py:500
  361.2 7.3 collective-permute-done.81.refs_24_.refs_8_
  373.3 11.6 %mlp.3 = (bf16[256,1408]{1,0:T(8,128)(2,1)}, bf16[256,1408]{1,0:T(8,128)(2,1)}, bf16[256,1408]{1,0:T(8,128)(2,1)}, bf16[256,2048]{1,0:T(8,128)(2,1)}) custom-call(s32[18]{0:T(128)S(1)} %stack.130.refs_0_, bf16[256,2048]{1,0:T(8,128)(2,1)S(1)} %bitcast.124, bf16[1,256,1408]{2,1,0:T(8,128)(2,1)} %get-tuple-element.254.refs_2_.refs_14_, ...), custom_call_target="tpu_custom_call" | custom-call | bytes 34500000 | tf_op jit(solution)/shard_map/mlp/pallas_call | solution.py:185
  384.9 14.2 %mlp_back.2 = (bf16[2,256,1408]{2,1,0:T(8,128)(2,1)}, bf16[256,2048]{1,0:T(8,128)(2,1)}) custom-call(s32[18]{0:T(128)S(1)} %stack.130.refs_0_, bf16[256,1408]{1,0:T(8,128)(2,1)} %get-tuple-element.273.refs_1_, bf16[256,1408]{1,0:T(8,128)(2,1)} %get-tuple-element.274.refs_2_, bf16[256,2048]{1,0:T(8,128)(2,1)S(1)} %bitcast.129, ...), custom_call_target="tpu_custom_call" | custom-call | bytes 42000000 | tf_op jit(solution)/shard_map/mlp_back/pallas_call | solution.py:185
  413.8 10.6 %mlp_grads.2 = (bf16[2,3,128,1408]{3,2,1,0:T(8,128)(2,1)}, bf16[2,3,128,1408]{3,2,1,0:T(8,128)(2,1)}, bf16[2,3,128,1408]{3,2,1,0:T(8,128)(2,1)}, bf16[3,128,1408]{2,1,0:T(8,128)(2,1)}, bf16[3,128,1408]{2,1,0:T(8,128)(2,1)}) custom-call(s32[4]{0:T(128)S(1)} %pad_add_fusion.refs_0_, bf16[256,2048]{1,0:T(8,128)(2,1)} %bitcast.126, bf16[256,2048]{1,0:T(8,128)(2,1)} %bitcast.128, ...), custom_call_target="tpu_custom_call" | custom-call | bytes 31500000 | tf_op jit(solution)/shard_map/mlp_grads/pallas_call | solution.py:645
  424.4 5.6 all-to-all-done.6.refs_1_
  439.2 23.5 %all-to-all-done.7 = bf16[4,64,2048]{2,1,0:T(8,128)(2,1)S(1)} async-done(((bf16[4,64,2048]{2,1,0:T(8,128)(2,1)}), bf16[4,64,2048]{2,1,0:T(8,128)(2,1)S(1)}, u32[]{:S(2)}, u32[]{:S(2)}) %all-to-all-start.7) | async-done | bytes 1048608 | tf_op jit(solution)/shard_map/all_to_all | solution.py:616
  466.9 9.9 %attend_back.2 = (bf16[256,512]{1,0:T(8,128)(2,1)}, bf16[2,256,512]{2,1,0:T(8,128)(2,1)}, f32[2,256,512]{2,1,0:T(8,128)}) custom-call(s32[18]{0:T(128)S(1)} %stack.130.refs_0_, bf16[256,2048]{1,0:T(8,128)(2,1)S(1)} %bitcast.118, bf16[256,512]{1,0:T(8,128)(2,1)} %get-tuple-element.238.refs_1_.refs_2_, f32[8,256]{1,0:T(8,128)} %get-tuple-element.287.refs_3_, ...), custom_call_target="tpu_custom_call" | custom-call | bytes 30000000 | tf_op jit(solution)/shard_map/attend_back/pallas_call | solution.py:185
  476.9 9.0 %collective-permute-done.91.refs_3_ = bf16[2,3,128,1408]{3,2,1,0:T(8,128)(2,1)} collective-permute-done((bf16[2,3,128,1408]{3,2,1,0:T(8,128)(2,1)}, bf16[2,3,128,1408]{3,2,1,0:T(8,128)(2,1)}, u32[]{:S(2)}, u32[]{:S(2)}) %collective-permute-start.91) | collective-permute-done | bytes 2162720 | tf_op jit(solution)/shard_map/ppermute | solution.py:508
  492.1 8.3 %collective-permute-done.93.refs_4_ = bf16[2,256,512]{2,1,0:T(8,128)(2,1)S(1)} collective-permute-done((bf16[2,256,512]{2,1,0:T(8,128)(2,1)}, bf16[2,256,512]{2,1,0:T(8,128)(2,1)S(1)}, u32[]{:S(2)}, u32[]{:S(2)}) %collective-permute-start.93) | collective-permute-done | bytes 524320 | tf_op jit(solution)/shard_map/ppermute | solution.py:977
  501.2 8.9 %qkv_back.2 = (bf16[3,256,512]{2,1,0:T(8,128)(2,1)}, f32[3,512]{1,0:T(4,128)}, bf16[256,2048]{1,0:T(8,128)(2,1)}) custom-call(s32[18]{0:T(128)S(1)} %stack.130.refs_0_, bf16[256,512]{1,0:T(8,128)(2,1)} %get-tuple-element.288.refs_1_, f32[3,256,128]{2,1,0:T(8,128)} %pad_maximum_fusion.refs_2_.refs_4_, f32[2,256,512]{2,1,0:T(8,128)} %get-tuple-element.297.refs_3_, ...), custom_call_target="tpu_custom_call" | custom-call | bytes 27000000 | tf_op jit(solution)/shard_map/qkv_back/pallas_call | solution.py:185
  523.4 6.9 attn_grads.2
  530.3 7.6 all-to-all-done.9.refs_1_
  548.5 7.4 mlp_finish.2
  556.0 13.5 %collective-permute-done.100.refs_4_.refs_2_ = bf16[2,4,128,512]{3,2,1,0:T(8,128)(2,1)S(1)} collective-permute-done((bf16[2,4,128,512]{3,2,1,0:T(8,128)(2,1)}, bf16[2,4,128,512]{3,2,1,0:T(8,128)(2,1)S(1)}, u32[]{:S(2)}, u32[]{:S(2)}) %collective-permute-start.100) | collective-permute-done | bytes 1048608 | tf_op jit(solution)/shard_map/ppermute | solution.py:500
  570.3 14.2 %mlp_back.3 = (bf16[2,256,1408]{2,1,0:T(8,128)(2,1)}, bf16[256,2048]{1,0:T(8,128)(2,1)}) custom-call(s32[18]{0:T(128)S(1)} %stack.130.refs_0_, bf16[256,1408]{1,0:T(8,128)(2,1)} %get-tuple-element.285.refs_1_, bf16[256,1408]{1,0:T(8,128)(2,1)} %get-tuple-element.286.refs_2_, bf16[256,2048]{1,0:T(8,128)(2,1)S(1)} %bitcast.112, ...), custom_call_target="tpu_custom_call" | custom-call | bytes 42000000 | tf_op jit(solution)/shard_map/mlp_back/pallas_call | solution.py:185
  595.0 10.6 %mlp_grads.3 = (bf16[2,3,128,1408]{3,2,1,0:T(8,128)(2,1)}, bf16[2,3,128,1408]{3,2,1,0:T(8,128)(2,1)}, bf16[2,3,128,1408]{3,2,1,0:T(8,128)(2,1)}, bf16[3,128,1408]{2,1,0:T(8,128)(2,1)}, bf16[3,128,1408]{2,1,0:T(8,128)(2,1)}) custom-call(s32[4]{0:T(128)S(1)} %pad_add_fusion.refs_0_, bf16[256,2048]{1,0:T(8,128)(2,1)} %bitcast.123, bf16[256,2048]{1,0:T(8,128)(2,1)} %bitcast.114, ...), custom_call_target="tpu_custom_call" | custom-call | bytes 31500000 | tf_op jit(solution)/shard_map/mlp_grads/pallas_call | solution.py:645
  609.5 10.0 %all-to-all-done.11.refs_1_ = bf16[4,64,2048]{2,1,0:T(8,128)(2,1)S(1)} async-done(((bf16[4,64,2048]{2,1,0:T(8,128)(2,1)}), bf16[4,64,2048]{2,1,0:T(8,128)(2,1)S(1)}, u32[]{:S(2)}, u32[]{:S(2)}) %all-to-all-start.11) | async-done | bytes 1048608 | tf_op jit(solution)/shard_map/all_to_all | solution.py:611
  630.8 20.9 %all-to-all-done.12 = bf16[4,64,2048]{2,1,0:T(8,128)(2,1)S(1)} async-done(((bf16[4,64,2048]{2,1,0:T(8,128)(2,1)}), bf16[4,64,2048]{2,1,0:T(8,128)(2,1)S(1)}, u32[]{:S(2)}, u32[]{:S(2)}) %all-to-all-start.12) | async-done | bytes 1048608 | tf_op jit(solution)/shard_map/all_to_all | solution.py:616
  651.7 9.8 %attend_back.3 = (bf16[256,512]{1,0:T(8,128)(2,1)}, bf16[2,256,512]{2,1,0:T(8,128)(2,1)}, f32[2,256,512]{2,1,0:T(8,128)}) custom-call(s32[18]{0:T(128)S(1)} %stack.130.refs_0_, bf16[256,2048]{1,0:T(8,128)(2,1)S(1)} %bitcast.115, bf16[256,512]{1,0:T(8,128)(2,1)} %get-tuple-element.200.refs_1_.refs_2_, f32[8,256]{1,0:T(8,128)} %get-tuple-element.338.refs_3_, ...), custom_call_target="tpu_custom_call" | custom-call | bytes 30000000 | tf_op jit(solution)/shard_map/attend_back/pallas_call | solution.py:185
  667.2 9.4 %collective-permute-done.110.refs_4_ = bf16[2,256,512]{2,1,0:T(8,128)(2,1)S(1)} collective-permute-done((bf16[2,256,512]{2,1,0:T(8,128)(2,1)}, bf16[2,256,512]{2,1,0:T(8,128)(2,1)S(1)}, u32[]{:S(2)}, u32[]{:S(2)}) %collective-permute-start.110) | collective-permute-done | bytes 524320 | tf_op jit(solution)/shard_map/ppermute | solution.py:977
  677.4 9.0 %qkv_back.3 = (bf16[3,256,512]{2,1,0:T(8,128)(2,1)}, f32[3,512]{1,0:T(4,128)}, bf16[256,2048]{1,0:T(8,128)(2,1)}) custom-call(s32[18]{0:T(128)S(1)} %stack.130.refs_0_, bf16[256,512]{1,0:T(8,128)(2,1)} %get-tuple-element.339.refs_1_, f32[3,256,128]{2,1,0:T(8,128)} %pad_maximum_fusion.refs_2_.refs_4_, f32[2,256,512]{2,1,0:T(8,128)} %get-tuple-element.350.refs_3_, ...), custom_call_target="tpu_custom_call" | custom-call | bytes 27000000 | tf_op jit(solution)/shard_map/qkv_back/pallas_call | solution.py:185
  691.9 22.5 %all-to-all-done.14.refs_1_ = bf16[4,64,2048]{2,1,0:T(8,128)(2,1)S(1)} async-done(((bf16[4,64,2048]{2,1,0:T(8,128)(2,1)}), bf16[4,64,2048]{2,1,0:T(8,128)(2,1)S(1)}, u32[]{:S(2)}, u32[]{:S(2)}) %all-to-all-start.14) | async-done | bytes 1048608 | tf_op jit(solution)/shard_map/all_to_all | solution.py:611
  722.2 6.9 attn_grads.3
  734.6 9.4 %all-to-all-done.13 = bf16[4,64,2048]{2,1,0:T(8,128)(2,1)} async-done(((bf16[4,64,2048]{2,1,0:T(8,128)(2,1)}), bf16[4,64,2048]{2,1,0:T(8,128)(2,1)}, u32[]{:S(2)}, u32[]{:S(2)}) %all-to-all-start.13) | async-done | bytes 1048608 | tf_op jit(solution)/shard_map/all_to_all | solution.py:616
  748.6 7.4 collective-permute-done.119
  773.4 7.4 mlp_finish.3
  (555 shorter events, 294.4 us)
Async XLA Ops:
  2.2 22.8 %collective-permute-start.4 = (bf16[3,256,512]{2,1,0:T(8,128)(2,1)S(1)}, bf16[3,256,512]{2,1,0:T(8,128)(2,1)S(1)}, u32[]{:S(2)}, u32[]{:S(2)}) collective-permute-start(bf16[3,256,512]{2,1,0:T(8,128)(2,1)S(1)} %get-tuple-element.426.refs_6_.refs_5_), channel_id=1, source_target_pairs={{0,4},{4,0},{1,5},{5,1},{2,6},{6,2},{3,7},{7,3},{8,12},{12,8},{9,1... | collective-permute-start | bytes 2359304 | tf_op jit(solution)/shard_map/ppermute | solution.py:508
  6.8 33.7 %collective-permute-start.7 = (bf16[3,256,512]{2,1,0:T(8,128)(2,1)S(1)}, bf16[3,256,512]{2,1,0:T(8,128)(2,1)}, u32[]{:S(2)}, u32[]{:S(2)}) collective-permute-start(bf16[3,256,512]{2,1,0:T(8,128)(2,1)S(1)} %get-tuple-element.426.refs_6_.refs_5_), channel_id=1, source_target_pairs={{0,8},{8,0},{16,24},{24,16},{1,9},{9,1},{17,25},{25,17},{2,10},{10... | collective-permute-start | bytes 2359304 | tf_op jit(solution)/shard_map/ppermute | solution.py:504
  77.4 37.9 %all-to-all-start = ((bf16[4,64,2048]{2,1,0:T(8,128)(2,1)}), bf16[4,64,2048]{2,1,0:T(8,128)(2,1)S(1)}, u32[]{:S(2)}, u32[]{:S(2)}) async-start(bf16[4,64,2048]{2,1,0:T(8,128)(2,1)} %bitcast.149), calls=%async_computation | async-start | bytes 2097152 | tf_op jit(solution)/shard_map/all_to_all | solution.py:611
  102.3 23.0 %collective-permute-start.29 = (bf16[1,256,1408]{2,1,0:T(8,128)(2,1)}, bf16[1,256,1408]{2,1,0:T(8,128)(2,1)}, u32[]{:S(2)}, u32[]{:S(2)}) collective-permute-start(bf16[1,256,1408]{2,1,0:T(8,128)(2,1)} %get-tuple-element.221.refs_12_.refs_24_), channel_id=1, source_target_pairs={{0,16},{8,24},{16,0},{24,8},{1,17},{9,25},{17,1},{25,9},{2,18},{10... | collective-permute-start | bytes 2162696 | tf_op jit(solution)/shard_map/ppermute | solution.py:500
  103.5 24.4 %collective-permute-start.30 = (bf16[1,256,1408]{2,1,0:T(8,128)(2,1)}, bf16[1,256,1408]{2,1,0:T(8,128)(2,1)}, u32[]{:S(2)}, u32[]{:S(2)}) collective-permute-start(bf16[1,256,1408]{2,1,0:T(8,128)(2,1)} %get-tuple-element.221.refs_12_.refs_24_), channel_id=1, source_target_pairs={{0,4},{4,0},{1,5},{5,1},{2,6},{6,2},{3,7},{7,3},{8,12},{12,8},{9,1... | collective-permute-start | bytes 2162696 | tf_op jit(solution)/shard_map/ppermute | solution.py:508
  104.1 25.6 %collective-permute-start.42 = (bf16[1,256,1408]{2,1,0:T(8,128)(2,1)}, bf16[1,256,1408]{2,1,0:T(8,128)(2,1)}, u32[]{:S(2)}, u32[]{:S(2)}) collective-permute-start(bf16[1,256,1408]{2,1,0:T(8,128)(2,1)} %get-tuple-element.226.refs_22_.refs_4_), channel_id=1, source_target_pairs={{0,8},{8,0},{16,24},{24,16},{1,9},{9,1},{17,25},{25,17},{2,10},{10... | collective-permute-start | bytes 2162696 | tf_op jit(solution)/shard_map/ppermute | solution.py:504
  125.3 31.4 %collective-permute-start.38 = (bf16[1,256,1408]{2,1,0:T(8,128)(2,1)}, bf16[1,256,1408]{2,1,0:T(8,128)(2,1)}, u32[]{:S(2)}, u32[]{:S(2)}) collective-permute-start(bf16[1,256,1408]{2,1,0:T(8,128)(2,1)} %get-tuple-element.226.refs_22_.refs_4_), channel_id=1, source_target_pairs={{0,16},{8,24},{16,0},{24,8},{1,17},{9,25},{17,1},{25,9},{2,18},{10... | collective-permute-start | bytes 2162696 | tf_op jit(solution)/shard_map/ppermute | solution.py:500
  129.6 27.2 %collective-permute-start.39 = (bf16[1,256,1408]{2,1,0:T(8,128)(2,1)}, bf16[1,256,1408]{2,1,0:T(8,128)(2,1)}, u32[]{:S(2)}, u32[]{:S(2)}) collective-permute-start(bf16[1,256,1408]{2,1,0:T(8,128)(2,1)} %get-tuple-element.226.refs_22_.refs_4_), channel_id=1, source_target_pairs={{0,4},{4,0},{1,5},{5,1},{2,6},{6,2},{3,7},{7,3},{8,12},{12,8},{9,1... | collective-permute-start | bytes 2162696 | tf_op jit(solution)/shard_map/ppermute | solution.py:508
  131.3 24.9 %collective-permute-start.32 = (bf16[1,128,1408]{2,1,0:T(8,128)(2,1)}, bf16[1,128,1408]{2,1,0:T(8,128)(2,1)}, u32[]{:S(2)}, u32[]{:S(2)}) collective-permute-start(bf16[1,128,1408]{2,1,0:T(8,128)(2,1)} %slice.214), channel_id=1, source_target_pairs={{0,4},{4,0},{1,5},{5,1},{2,6},{6,2},{3,7},{7,3},{8,12},{12,8},{9,1... | collective-permute-start | bytes 1081352 | tf_op jit(solution)/shard_map/ppermute | solution.py:508
  131.7 24.6 %collective-permute-start.31 = (bf16[1,128,1408]{2,1,0:T(8,128)(2,1)}, bf16[1,128,1408]{2,1,0:T(8,128)(2,1)}, u32[]{:S(2)}, u32[]{:S(2)}) collective-permute-start(bf16[1,128,1408]{2,1,0:T(8,128)(2,1)} %slice.213), channel_id=1, source_target_pairs={{0,16},{8,24},{16,0},{24,8},{1,17},{9,25},{17,1},{25,9},{2,18},{10... | collective-permute-start | bytes 1081352 | tf_op jit(solution)/shard_map/ppermute | solution.py:500
  132.9 43.1 %all-to-all-start.1 = ((bf16[4,64,2048]{2,1,0:T(8,128)(2,1)}), bf16[4,64,2048]{2,1,0:T(8,128)(2,1)S(1)}, u32[]{:S(2)}, u32[]{:S(2)}) async-start(bf16[4,64,2048]{2,1,0:T(8,128)(2,1)} %get-tuple-element.207), calls=%async_computation.1 | async-start | bytes 2097152 | tf_op jit(solution)/shard_map/all_to_all | solution.py:616
  187.6 33.9 %all-to-all-start.2 = ((bf16[4,64,2048]{2,1,0:T(8,128)(2,1)}), bf16[4,64,2048]{2,1,0:T(8,128)(2,1)S(1)}, u32[]{:S(2)}, u32[]{:S(2)}) async-start(bf16[4,64,2048]{2,1,0:T(8,128)(2,1)} %bitcast.152), calls=%async_computation.2 | async-start | bytes 2097152 | tf_op jit(solution)/shard_map/all_to_all | solution.py:611
  220.7 34.2 %collective-permute-start.49 = (bf16[3,256,512]{2,1,0:T(8,128)(2,1)}, bf16[3,256,512]{2,1,0:T(8,128)(2,1)}, u32[]{:S(2)}, u32[]{:S(2)}) collective-permute-start(bf16[3,256,512]{2,1,0:T(8,128)(2,1)} %collective-permute-done.47.refs_5_.refs_6_), channel_id=1, source_target_pairs={{0,4},{4,0},{1,5},{5,1},{2,6},{6,2},{3,7},{7,3},{8,12},{12,8},{9,1... | collective-permute-start | bytes 2359304 | tf_op jit(solution)/shard_map/ppermute | solution.py:508
  224.5 34.5 %all-to-all-start.3 = ((bf16[4,64,2048]{2,1,0:T(8,128)(2,1)}), bf16[4,64,2048]{2,1,0:T(8,128)(2,1)S(1)}, u32[]{:S(2)}, u32[]{:S(2)}) async-start(bf16[4,64,2048]{2,1,0:T(8,128)(2,1)} %get-tuple-element.232), calls=%async_computation.3 | async-start | bytes 2097152 | tf_op jit(solution)/shard_map/all_to_all | solution.py:616
  229.8 25.0 %collective-permute-start.57 = (bf16[1,256,1408]{2,1,0:T(8,128)(2,1)}, bf16[1,256,1408]{2,1,0:T(8,128)(2,1)S(1)}, u32[]{:S(2)}, u32[]{:S(2)}) collective-permute-start(bf16[1,256,1408]{2,1,0:T(8,128)(2,1)} %get-tuple-element.254.refs_2_.refs_14_), channel_id=1, source_target_pairs={{0,16},{8,24},{16,0},{24,8},{1,17},{9,25},{17,1},{25,9},{2,18},{10... | collective-permute-start | bytes 2162696 | tf_op jit(solution)/shard_map/ppermute | solution.py:500
  231.0 25.0 %collective-permute-start.50 = (bf16[3,256,512]{2,1,0:T(8,128)(2,1)S(1)}, bf16[3,256,512]{2,1,0:T(8,128)(2,1)S(1)}, u32[]{:S(2)}, u32[]{:S(2)}) collective-permute-start(bf16[3,256,512]{2,1,0:T(8,128)(2,1)S(1)} %get-tuple-element.236.refs_4_.refs_5_), channel_id=1, source_target_pairs={{0,8},{8,0},{16,24},{24,16},{1,9},{9,1},{17,25},{25,17},{2,10},{10... | collective-permute-start | bytes 2359304 | tf_op jit(solution)/shard_map/ppermute | solution.py:504
  231.0 26.3 %collective-permute-start.51 = (bf16[3,256,512]{2,1,0:T(8,128)(2,1)}, bf16[3,256,512]{2,1,0:T(8,128)(2,1)S(1)}, u32[]{:S(2)}, u32[]{:S(2)}) collective-permute-start(bf16[3,256,512]{2,1,0:T(8,128)(2,1)} %collective-permute-done.47.refs_5_.refs_6_), channel_id=1, source_target_pairs={{0,8},{8,0},{16,24},{24,16},{1,9},{9,1},{17,25},{25,17},{2,10},{10... | collective-permute-start | bytes 2359304 | tf_op jit(solution)/shard_map/ppermute | solution.py:504
  278.0 26.4 %collective-permute-start.64 = (bf16[1,256,1408]{2,1,0:T(8,128)(2,1)}, bf16[1,256,1408]{2,1,0:T(8,128)(2,1)}, u32[]{:S(2)}, u32[]{:S(2)}) collective-permute-start(bf16[1,256,1408]{2,1,0:T(8,128)(2,1)} %get-tuple-element.254.refs_2_.refs_14_), channel_id=1, source_target_pairs={{0,4},{4,0},{1,5},{5,1},{2,6},{6,2},{3,7},{7,3},{8,12},{12,8},{9,1... | collective-permute-start | bytes 2162696 | tf_op jit(solution)/shard_map/ppermute | solution.py:508
  299.7 37.2 %all-to-all-start.4 = ((bf16[4,64,2048]{2,1,0:T(8,128)(2,1)}), bf16[4,64,2048]{2,1,0:T(8,128)(2,1)S(1)}, u32[]{:S(2)}, u32[]{:S(2)}) async-start(bf16[4,64,2048]{2,1,0:T(8,128)(2,1)} %bitcast.150), calls=%async_computation.4 | async-start | bytes 2097152 | tf_op jit(solution)/shard_map/all_to_all | solution.py:611
  306.4 26.0 %collective-permute-start.70 = (bf16[1,256,1408]{2,1,0:T(8,128)(2,1)}, bf16[1,256,1408]{2,1,0:T(8,128)(2,1)S(1)}, u32[]{:S(2)}, u32[]{:S(2)}) collective-permute-start(bf16[1,256,1408]{2,1,0:T(8,128)(2,1)} %get-tuple-element.260.refs_10_.refs_22_), channel_id=1, source_target_pairs={{0,4},{4,0},{1,5},{5,1},{2,6},{6,2},{3,7},{7,3},{8,12},{12,8},{9,1... | collective-permute-start | bytes 2162696 | tf_op jit(solution)/shard_map/ppermute | solution.py:508
  308.9 24.3 %collective-permute-start.68 = (bf16[1,256,1408]{2,1,0:T(8,128)(2,1)}, bf16[1,256,1408]{2,1,0:T(8,128)(2,1)S(1)}, u32[]{:S(2)}, u32[]{:S(2)}) collective-permute-start(bf16[1,256,1408]{2,1,0:T(8,128)(2,1)} %collective-permute-done.64.refs_4_.refs_16_), channel_id=1, source_target_pairs={{0,8},{8,0},{16,24},{24,16},{1,9},{9,1},{17,25},{25,17},{2,10},{10... | collective-permute-start | bytes 2162696 | tf_op jit(solution)/shard_map/ppermute | solution.py:504
  308.9 25.3 %collective-permute-start.67 = (bf16[1,256,1408]{2,1,0:T(8,128)(2,1)}, bf16[1,256,1408]{2,1,0:T(8,128)(2,1)S(1)}, u32[]{:S(2)}, u32[]{:S(2)}) collective-permute-start(bf16[1,256,1408]{2,1,0:T(8,128)(2,1)} %copy-done.25), channel_id=1, source_target_pairs={{0,8},{8,0},{16,24},{24,16},{1,9},{9,1},{17,25},{25,17},{2,10},{10... | collective-permute-start | bytes 2162696 | tf_op jit(solution)/shard_map/ppermute | solution.py:504
  321.1 23.5 %collective-permute-start.66 = (bf16[1,256,1408]{2,1,0:T(8,128)(2,1)}, bf16[1,256,1408]{2,1,0:T(8,128)(2,1)}, u32[]{:S(2)}, u32[]{:S(2)}) collective-permute-start(bf16[1,256,1408]{2,1,0:T(8,128)(2,1)} %get-tuple-element.254.refs_2_.refs_14_), channel_id=1, source_target_pairs={{0,8},{8,0},{16,24},{24,16},{1,9},{9,1},{17,25},{25,17},{2,10},{10... | collective-permute-start | bytes 2162696 | tf_op jit(solution)/shard_map/ppermute | solution.py:504
  331.3 23.6 %collective-permute-start.78 = (bf16[1,256,1408]{2,1,0:T(8,128)(2,1)}, bf16[1,256,1408]{2,1,0:T(8,128)(2,1)}, u32[]{:S(2)}, u32[]{:S(2)}) collective-permute-start(bf16[1,256,1408]{2,1,0:T(8,128)(2,1)} %get-tuple-element.269.refs_20_.refs_4_), channel_id=1, source_target_pairs={{0,16},{8,24},{16,0},{24,8},{1,17},{9,25},{17,1},{25,9},{2,18},{10... | collective-permute-start | bytes 2162696 | tf_op jit(solution)/shard_map/ppermute | solution.py:500
  339.9 33.3 %all-to-all-start.5 = ((bf16[4,64,2048]{2,1,0:T(8,128)(2,1)}), bf16[4,64,2048]{2,1,0:T(8,128)(2,1)S(1)}, u32[]{:S(2)}, u32[]{:S(2)}) async-start(bf16[4,64,2048]{2,1,0:T(8,128)(2,1)} %get-tuple-element.251), calls=%async_computation.5 | async-start | bytes 2097152 | tf_op jit(solution)/shard_map/all_to_all | solution.py:616
  399.1 30.8 %all-to-all-start.6 = ((bf16[4,64,2048]{2,1,0:T(8,128)(2,1)}), bf16[4,64,2048]{2,1,0:T(8,128)(2,1)}, u32[]{:S(2)}, u32[]{:S(2)}) async-start(bf16[4,64,2048]{2,1,0:T(8,128)(2,1)} %bitcast.147), calls=%async_computation.6 | async-start | bytes 2097152 | tf_op jit(solution)/shard_map/all_to_all | solution.py:611
  433.7 28.9 %all-to-all-start.7 = ((bf16[4,64,2048]{2,1,0:T(8,128)(2,1)}), bf16[4,64,2048]{2,1,0:T(8,128)(2,1)S(1)}, u32[]{:S(2)}, u32[]{:S(2)}) async-start(bf16[4,64,2048]{2,1,0:T(8,128)(2,1)} %get-tuple-element.283), calls=%async_computation.7 | async-start | bytes 2097152 | tf_op jit(solution)/shard_map/all_to_all | solution.py:616
  437.3 48.6 %collective-permute-start.91 = (bf16[2,3,128,1408]{3,2,1,0:T(8,128)(2,1)}, bf16[2,3,128,1408]{3,2,1,0:T(8,128)(2,1)}, u32[]{:S(2)}, u32[]{:S(2)}) collective-permute-start(bf16[2,3,128,1408]{3,2,1,0:T(8,128)(2,1)} %get-tuple-element.294), channel_id=1, source_target_pairs={{0,4},{4,0},{1,5},{5,1},{2,6},{6,2},{3,7},{7,3},{8,12},{12,8},{9,1... | collective-permute-start | bytes 6488072 | tf_op jit(solution)/shard_map/ppermute | solution.py:508
  438.1 48.2 %collective-permute-start.92 = (bf16[2,3,128,1408]{3,2,1,0:T(8,128)(2,1)}, bf16[2,3,128,1408]{3,2,1,0:T(8,128)(2,1)}, u32[]{:S(2)}, u32[]{:S(2)}) collective-permute-start(bf16[2,3,128,1408]{3,2,1,0:T(8,128)(2,1)} %get-tuple-element.295), channel_id=1, source_target_pairs={{0,16},{8,24},{16,0},{24,8},{1,17},{9,25},{17,1},{25,9},{2,18},{10... | collective-permute-start | bytes 6488072 | tf_op jit(solution)/shard_map/ppermute | solution.py:500
  462.7 47.4 %all-to-all-start.8 = ((bf16[4,64,2048]{2,1,0:T(8,128)(2,1)}), bf16[4,64,2048]{2,1,0:T(8,128)(2,1)}, u32[]{:S(2)}, u32[]{:S(2)}) async-start(bf16[4,64,2048]{2,1,0:T(8,128)(2,1)} %bitcast.145), calls=%async_computation.8 | async-start | bytes 2097152 | tf_op jit(solution)/shard_map/all_to_all | solution.py:611
  510.1 27.8 %all-to-all-start.9 = ((bf16[4,64,2048]{2,1,0:T(8,128)(2,1)}), bf16[4,64,2048]{2,1,0:T(8,128)(2,1)}, u32[]{:S(2)}, u32[]{:S(2)}) async-start(bf16[4,64,2048]{2,1,0:T(8,128)(2,1)} %bitcast.148), calls=%async_computation.9 | async-start | bytes 2097152 | tf_op jit(solution)/shard_map/all_to_all | solution.py:611
  514.7 23.2 %collective-permute-start.98 = (bf16[3,128,1408]{2,1,0:T(8,128)(2,1)}, bf16[3,128,1408]{2,1,0:T(8,128)(2,1)}, u32[]{:S(2)}, u32[]{:S(2)}) collective-permute-start(bf16[3,128,1408]{2,1,0:T(8,128)(2,1)} %get-tuple-element.296), channel_id=1, source_target_pairs={{0,16},{8,24},{16,0},{24,8},{1,17},{9,25},{17,1},{25,9},{2,18},{10... | collective-permute-start | bytes 3244040 | tf_op jit(solution)/shard_map/ppermute | solution.py:500
  515.7 22.8 %collective-permute-start.99 = (bf16[3,128,1408]{2,1,0:T(8,128)(2,1)}, bf16[3,128,1408]{2,1,0:T(8,128)(2,1)}, u32[]{:S(2)}, u32[]{:S(2)}) collective-permute-start(bf16[3,128,1408]{2,1,0:T(8,128)(2,1)} %get-tuple-element.308), channel_id=1, source_target_pairs={{0,4},{4,0},{1,5},{5,1},{2,6},{6,2},{3,7},{7,3},{8,12},{12,8},{9,1... | collective-permute-start | bytes 3244040 | tf_op jit(solution)/shard_map/ppermute | solution.py:508
  542.3 28.0 %all-to-all-start.10 = ((bf16[4,64,2048]{2,1,0:T(8,128)(2,1)}), bf16[4,64,2048]{2,1,0:T(8,128)(2,1)S(1)}, u32[]{:S(2)}, u32[]{:S(2)}) async-start(bf16[4,64,2048]{2,1,0:T(8,128)(2,1)} %get-tuple-element.311), calls=%async_computation.10 | async-start | bytes 2097152 | tf_op jit(solution)/shard_map/all_to_all | solution.py:616
  588.6 31.0 %all-to-all-start.11 = ((bf16[4,64,2048]{2,1,0:T(8,128)(2,1)}), bf16[4,64,2048]{2,1,0:T(8,128)(2,1)S(1)}, u32[]{:S(2)}, u32[]{:S(2)}) async-start(bf16[4,64,2048]{2,1,0:T(8,128)(2,1)} %bitcast.146), calls=%async_computation.11 | async-start | bytes 2097152 | tf_op jit(solution)/shard_map/all_to_all | solution.py:611
  608.3 53.3 %collective-permute-start.109 = (bf16[2,3,128,1408]{3,2,1,0:T(8,128)(2,1)}, bf16[2,3,128,1408]{3,2,1,0:T(8,128)(2,1)}, u32[]{:S(2)}, u32[]{:S(2)}) collective-permute-start(bf16[2,3,128,1408]{3,2,1,0:T(8,128)(2,1)} %get-tuple-element.348), channel_id=1, source_target_pairs={{0,16},{8,24},{16,0},{24,8},{1,17},{9,25},{17,1},{25,9},{2,18},{10... | collective-permute-start | bytes 6488072 | tf_op jit(solution)/shard_map/ppermute | solution.py:500
  609.3 52.4 %collective-permute-start.108 = (bf16[2,3,128,1408]{3,2,1,0:T(8,128)(2,1)}, bf16[2,3,128,1408]{3,2,1,0:T(8,128)(2,1)}, u32[]{:S(2)}, u32[]{:S(2)}) collective-permute-start(bf16[2,3,128,1408]{3,2,1,0:T(8,128)(2,1)} %get-tuple-element.346), channel_id=1, source_target_pairs={{0,4},{4,0},{1,5},{5,1},{2,6},{6,2},{3,7},{7,3},{8,12},{12,8},{9,1... | collective-permute-start | bytes 6488072 | tf_op jit(solution)/shard_map/ppermute | solution.py:508
  623.0 28.8 %all-to-all-start.12 = ((bf16[4,64,2048]{2,1,0:T(8,128)(2,1)}), bf16[4,64,2048]{2,1,0:T(8,128)(2,1)S(1)}, u32[]{:S(2)}, u32[]{:S(2)}) async-start(bf16[4,64,2048]{2,1,0:T(8,128)(2,1)} %get-tuple-element.332), calls=%async_computation.12 | async-start | bytes 2097152 | tf_op jit(solution)/shard_map/all_to_all | solution.py:616
  686.5 27.9 %all-to-all-start.14 = ((bf16[4,64,2048]{2,1,0:T(8,128)(2,1)}), bf16[4,64,2048]{2,1,0:T(8,128)(2,1)S(1)}, u32[]{:S(2)}, u32[]{:S(2)}) async-start(bf16[4,64,2048]{2,1,0:T(8,128)(2,1)} %bitcast.151), calls=%async_computation.14 | async-start | bytes 2097152 | tf_op jit(solution)/shard_map/all_to_all | solution.py:611
  690.2 28.6 %collective-permute-start.114 = (bf16[256,512]{1,0:T(8,128)(2,1)S(1)}, bf16[256,512]{1,0:T(8,128)(2,1)}, u32[]{:S(2)}, u32[]{:S(2)}) collective-permute-start(bf16[256,512]{1,0:T(8,128)(2,1)S(1)} %copy-done.87), channel_id=1, source_target_pairs={{0,8},{8,0},{16,24},{24,16},{1,9},{9,1},{17,25},{25,17},{2,10},{10... | collective-permute-start | bytes 786440 | tf_op jit(solution)/shard_map/ppermute | solution.py:504
  690.3 39.9 %collective-permute-start.115 = (bf16[3,128,1408]{2,1,0:T(8,128)(2,1)}, bf16[3,128,1408]{2,1,0:T(8,128)(2,1)}, u32[]{:S(2)}, u32[]{:S(2)}) collective-permute-start(bf16[3,128,1408]{2,1,0:T(8,128)(2,1)} %get-tuple-element.349), channel_id=1, source_target_pairs={{0,16},{8,24},{16,0},{24,8},{1,17},{9,25},{17,1},{25,9},{2,18},{10... | collective-permute-start | bytes 3244040 | tf_op jit(solution)/shard_map/ppermute | solution.py:500
  691.4 38.8 %collective-permute-start.116 = (bf16[3,128,1408]{2,1,0:T(8,128)(2,1)}, bf16[3,128,1408]{2,1,0:T(8,128)(2,1)}, u32[]{:S(2)}, u32[]{:S(2)}) collective-permute-start(bf16[3,128,1408]{2,1,0:T(8,128)(2,1)} %get-tuple-element.361), channel_id=1, source_target_pairs={{0,4},{4,0},{1,5},{5,1},{2,6},{6,2},{3,7},{7,3},{8,12},{12,8},{9,1... | collective-permute-start | bytes 3244040 | tf_op jit(solution)/shard_map/ppermute | solution.py:508
  691.4 29.9 %collective-permute-start.112 = (bf16[256,2048]{1,0:T(8,128)(2,1)S(1)}, bf16[256,2048]{1,0:T(8,128)(2,1)}, u32[]{:S(2)}, u32[]{:S(2)}) collective-permute-start(bf16[256,2048]{1,0:T(8,128)(2,1)S(1)} %bitcast.116), channel_id=1, source_target_pairs={{0,8},{8,0},{16,24},{24,16},{1,9},{9,1},{17,25},{25,17},{2,10},{10... | collective-permute-start | bytes 3145736 | tf_op jit(solution)/shard_map/ppermute | solution.py:504
  691.6 29.7 %collective-permute-start.111 = (bf16[256,2048]{1,0:T(8,128)(2,1)S(1)}, bf16[256,2048]{1,0:T(8,128)(2,1)}, u32[]{:S(2)}, u32[]{:S(2)}) collective-permute-start(bf16[256,2048]{1,0:T(8,128)(2,1)S(1)} %copy-done.57), channel_id=1, source_target_pairs={{0,8},{8,0},{16,24},{24,16},{1,9},{9,1},{17,25},{25,17},{2,10},{10... | collective-permute-start | bytes 3145736 | tf_op jit(solution)/shard_map/ppermute | solution.py:504
  714.4 29.6 %all-to-all-start.13 = ((bf16[4,64,2048]{2,1,0:T(8,128)(2,1)}), bf16[4,64,2048]{2,1,0:T(8,128)(2,1)}, u32[]{:S(2)}, u32[]{:S(2)}) async-start(bf16[4,64,2048]{2,1,0:T(8,128)(2,1)} %sum.1), calls=%async_computation.13 | async-start | bytes 2097152 | tf_op jit(solution)/shard_map/all_to_all | solution.py:616
  729.1 30.9 %collective-permute-start.117 = (bf16[2,4,128,512]{3,2,1,0:T(8,128)(2,1)}, bf16[2,4,128,512]{3,2,1,0:T(8,128)(2,1)S(1)}, u32[]{:S(2)}, u32[]{:S(2)}) collective-permute-start(bf16[2,4,128,512]{3,2,1,0:T(8,128)(2,1)} %get-tuple-element.368), channel_id=1, source_target_pairs={{0,16},{8,24},{16,0},{24,8},{1,17},{9,25},{17,1},{25,9},{2,18},{10... | collective-permute-start | bytes 3145736 | tf_op jit(solution)/shard_map/ppermute | solution.py:500
  730.2 29.8 %collective-permute-start.118 = (bf16[2,4,128,512]{3,2,1,0:T(8,128)(2,1)}, bf16[2,4,128,512]{3,2,1,0:T(8,128)(2,1)S(1)}, u32[]{:S(2)}, u32[]{:S(2)}) collective-permute-start(bf16[2,4,128,512]{3,2,1,0:T(8,128)(2,1)} %get-tuple-element.369), channel_id=1, source_target_pairs={{0,4},{4,0},{1,5},{5,1},{2,6},{6,2},{3,7},{7,3},{8,12},{12,8},{9,1... | collective-permute-start | bytes 3145736 | tf_op jit(solution)/shard_map/ppermute | solution.py:508
  744.0 43.4 %all-to-all-start.15 = ((bf16[4,64,2048]{2,1,0:T(8,128)(2,1)}), bf16[4,64,2048]{2,1,0:T(8,128)(2,1)S(1)}, u32[]{:S(2)}, u32[]{:S(2)}) async-start(bf16[4,64,2048]{2,1,0:T(8,128)(2,1)} %get-tuple-element.363), calls=%async_computation.15 | async-start | bytes 2097152 | tf_op jit(solution)/shard_map/all_to_all | solution.py:616
  (193 other events, 2872.3 us)

commit v3 on v2

--- a/solution.py
+++ b/solution.py
@@ -25,6 +25,7 @@
     "norm": 3.0,
     "mlp": 11.5,
     "mlp_back": 14.0,
+    "mlp_both": 18.0,
     "norm_back": 3.5,
     "attend_back": 10.0,
     "qkv_back": 9.0,
@@ -59,7 +60,7 @@
     def __init__(self, ins, loads, outs, stores, held, weights, started, extra):
         self.ins, self.loads, self.outs, self.stores = ins, loads, outs, stores
         self.held, self.weights, self.started, self.extra = held, weights, started, extra
-        self.there, self.gone = set(), []
+        self.there, self.held_there, self.gone = set(), set(), []
 
     def get(self, index):
         if index not in self.there:
@@ -68,9 +69,14 @@
         return self.ins[index]
 
     def weight(self, slot):
-        for copy in self.weights[slot]:
-            copy.wait()
-        self.begin(slot + 2)
+        if slot not in self.held_there:
+            self.held_there.add(slot)
+            copies = self.weights[slot]
+            for copy in copies[: len(copies) // 2]:
+                copy.wait()
+            self.begin(slot + 2)
+            for copy in copies[len(copies) // 2 :]:
+                copy.wait()
         return self.held[slot]
 
     def begin(self, count):
@@ -330,6 +336,29 @@
     io.put(1)
 
 
+def mlp_both_body(io):
+    hidden, part_out, d_gate_up, part = io.outs
+    second_in = io.get(0)
+    gate = mm(second_in[...], io.weight(0)[...], NN)
+    sig = jax.nn.sigmoid(gate)
+    act = gate * sig
+    slope = sig * (1.0 + gate * (1.0 - sig))
+    up = mm(second_in[...], io.weight(1)[...], NN)
+    hidden[...] = (act * up).astype(BF)
+    io.put(0)
+    down = io.weight(2)
+    d_hidden = mm(io.get(1)[...], down[...], NN)
+    d_gate_up[1] = (d_hidden * act).astype(BF)
+    d_gate_up[0] = (d_hidden * up * slope).astype(BF)
+    io.put(2)
+    total = mm(d_gate_up[0], io.weight(0)[...], NT)
+    total = total + mm(d_gate_up[1], io.weight(1)[...], NT)
+    part[...] = total.astype(BF)
+    io.put(3)
+    part_out[...] = mm(hidden[...], down[...], NT).astype(BF)
+    io.put(1)
+
+
 def norm_back_body(io):
     c = terms_sum(io.get(0))
     grad, n = norm_back(io.get(1)[...].astype(F32), c, io.get(2)[...])
@@ -404,10 +433,14 @@
 def pack_body(io):
     gate_up, down = io.get(0), io.get(1)
     for part in range(2):
-        io.outs[part][0] = gate_up[:, part, :]
-        io.put(part)
-    io.outs[2][0] = down[...].T
-    io.put(2)
+        io.outs[0][part] = gate_up[:, part, :]
+    if len(io.outs) == 1:
+        io.outs[0][2] = down[...].T
+        io.put(0)
+    else:
+        io.put(0)
+        io.outs[1][0] = down[...].T
+        io.put(1)
 
 
 def add_body(io):
@@ -545,8 +578,8 @@
                 swap_y(after(self.from_x[:, half:], *wait_y)),
             ]
 
-    def all(self):
-        far_peers = [swap_core(piece) for piece in self.pieces]
+    def all(self, *wait):
+        far_peers = [swap_core(after(piece, *wait)) for piece in self.pieces]
         return self.mine + self.pieces + self.peers + far_peers
 
 
@@ -572,37 +605,36 @@
 
 def gather_small(packed, fast):
     if not fast:
-        return lax.all_gather(packed, ("fsdp", "ctx"), axis=1, tiled=True)
+        return lax.all_gather(packed, ("fsdp", "ctx"), axis=1, tiled=True), ()
     x, core, y = place()
 
     def join(array, other, bit):
         return jnp.where(bit == 0, jnp.stack([array, other]), jnp.stack([other, array]))
 
-    held = join(packed, swap_core(packed), core)
+    from_y = swap_y(packed)
+    held = join(packed, from_y, y)
+    held = join(held, swap_core(held), core)
     held = join(held, swap_x(held), x)
-    held = join(held, swap_y(held), y)
     rows, cols = packed.shape
-    return held.transpose(3, 1, 2, 0, 4).reshape(rows, 8 * cols)
-
-
-def reduce_small(sums, fast):
+    return held.transpose(3, 0, 1, 2, 4).reshape(rows, 8 * cols), (from_y,)
+
+
+def reduce_small(sums, fast, *wait):
     if not fast:
         part = lax.psum_scatter(sums, ("fsdp", "ctx"), scatter_dimension=1, tiled=True)
-        return lax.psum(part, "tp"), part
+        return lax.psum(part, "tp")
     x, core, y = place()
     rows, width = sums.shape
     held = sums.reshape(rows, 2, 2, 2, width // 8).transpose(1, 3, 2, 0, 4)
     for bit, swap in ((x, swap_x), (y, swap_y), (core, swap_core)):
         keep = jnp.where(bit == 0, held[0], held[1])
         send = jnp.where(bit == 0, held[1], held[0])
-        held = keep + swap(send)
-        if swap is swap_y:
-            halfway = held
+        held = keep + swap(after(send, *wait) if swap is swap_y else send)
     step = 1
     while step < lax.axis_size("tp"):
         held = held + lax.ppermute(held, "tp", pairs_of("tp", step))
         step *= 2
-    return held, halfway
+    return held
 
 
 def tensor_scatter(part, *earlier):
@@ -612,15 +644,21 @@
 
 
 def tensor_gather(copies):
-    size, block, width = copies.shape
-    return lax.all_to_all(copies, "tp", 0, 0, tiled=True).reshape(size * block, width)
-
-
-def weight_grads(own, n_left, pairs, earlier, wait, name):
+    return lax.all_to_all(copies, "tp", 0, 0, tiled=True)
+
+
+def flat(blocks):
+    return blocks.reshape(-1, blocks.shape[-1])
+
+
+def weight_grads(own, peer, n_left, pairs, earlier, name):
     counts = tuple(1 if array.ndim == 2 else array.shape[0] for array in own)
     columns = own[-1].shape[-1]
     tokens, width = own[0].shape
-    peer = [swap_core(after(array, *earlier)) for array in own]
+    peer = [
+        swap_core(after(array, *earlier)) if other is None else other
+        for array, other in zip(own, peer, strict=True)
+    ]
     rows = width // 8
     half = rows // 2
     x, core, y = place()
@@ -652,23 +690,31 @@
         cost_estimate=cost(name),
         name=name,
     )(ids, *[pltpu.with_memory_space_constraint(a, pltpu.HBM) for a in list(own) + peer])
-    return (own_sum, x2, y2), (swap_x(after(x1, *wait)), swap_y(after(y1, *wait)))
-
-
-def reduce_second(spots, parts, received, earlier_add, earlier_send, name):
-    own_sum, x2, y2 = parts
+    return (own_sum, x2, y2), (x1, y1)
+
+
+def add_received(spots, parts, received, earlier, name):
+    _, x2, y2 = parts
     got_x1, got_y1 = received
     block = shape(x2.shape, BF)
-    send_x, send_y = kernel(
+    return kernel(
         add_body,
         name,
         spots,
-        [after(x2, *earlier_add), y2, (got_y1, 0), (got_x1, 0)],
+        [after(x2, *earlier), y2, (got_y1, 0), (got_x1, 0)],
         [block, block],
     )
-    far_x = swap_x(after(send_x, *earlier_send))
-    far_y = swap_y(after(send_y, *earlier_send))
-    return [own_sum, (got_x1, 1), (got_y1, 1), far_x, far_y], send_x
+
+
+def send_second(parts, received, sums, earlier):
+    far_x = swap_x(after(sums[0], *earlier))
+    far_y = swap_y(after(sums[1], *earlier))
+    return [parts[0], (received[0], 1), (received[1], 1), far_x, far_y]
+
+
+def reduce_second(spots, parts, received, earlier_add, earlier_send, name):
+    sums = add_received(spots, parts, received, earlier_add, name)
+    return send_second(parts, received, sums, earlier_send), sums[0]
 
 
 def layout(lengths, first_row, row_count):
@@ -728,7 +774,8 @@
             qkv_bias.reshape(3 * layers, -1),
         ]
     )
-    small = gather_small(small, fast).astype(F32)
+    small, sent_small = gather_small(small, fast)
+    small = small.astype(F32)
     gains = small[: 2 * layers].reshape(layers, 2, width)
     shifts = small[2 * layers : 4 * layers].reshape(layers, 2, width)
     biases = lax.dynamic_slice_in_dim(
@@ -747,17 +794,22 @@
     shards = []
     for layer in range(layers):
         if fast:
+            counts = (3,) if layer == 0 else (2, 1)
             mlp_shards = kernel(
                 pack_body,
                 "pack",
                 spots,
                 [(gate_up_weight, layer), (down_weight, layer)],
-                [shape((1, block_rows, hidden_width), BF)] * 3,
+                [shape((count, block_rows, hidden_width), BF) for count in counts],
             )
         else:
-            mlp_shards = [gate_up_weight[layer][None, :, part] for part in range(2)]
-            mlp_shards.append(down_weight[layer].T[None])
-        shards.append((qkv_weight[layer].transpose(1, 0, 2), out_weight[layer].T[None], *mlp_shards))
+            mlp_shards = [
+                jnp.concatenate(
+                    [gate_up_weight[layer].transpose(1, 0, 2), down_weight[layer].T[None]]
+                )
+            ]
+        qkv_shard, out_shard = qkv_weight[layer].transpose(1, 0, 2), out_weight[layer].T[None]
+        shards.append((jnp.concatenate([qkv_shard, out_shard]), *mlp_shards))
 
     lengths = doc_lengths[0]
     seg_query, pos_query, index_query = layout(lengths, ctx_rank * rows, rows)
@@ -789,22 +841,22 @@
     first_in = None
     saved, groups = [], []
     if fast:
-        qkv_g, out_g, gate_g, up_g, down_g = (Gather(shard) for shard in shards[0])
-        qkv_g.near()
-        qkv_g.swap()
-        qkv_g.far("both")
-        out_g.near(qkv_g.pieces, qkv_g.pieces)
+        attn_g, mlp_g = (Gather(shard) for shard in shards[0])
+        attn_g.near((), sent_small)
+        attn_g.swap()
+        attn_g.far("both")
+        mlp_g.near_x(attn_g.pieces[:1])
     for layer in range(layers):
         if fast:
-            qkv_pieces = qkv_g.all()
+            attn_pieces = attn_g.all()
         else:
-            qkv_pieces, *others = (gather_whole(shard) for shard in shards[layer])
-            out_pieces, gate_pieces, up_pieces, down_pieces = others
+            attn_pieces, mlp_pieces = (gather_whole(shard) for shard in shards[layer])
+            mlp_slots = [slot(mlp_pieces, index) for index in range(3)]
         outs = [headed, shape((2, rows, heads_width), BF)]
         if layer == 0:
             args = [biases[0], tables, gains[0, 0][None], shifts[0, 0][None], tokens[0]]
             if fast:
-                args[0] = after(args[0], gate_g.shard)
+                args[0] = after(args[0], mlp_g.shard)
             outs.append(wide)
         else:
             args = [biases[layer], tables, Free(first_in)]
@@ -814,23 +866,17 @@
             spots,
             args,
             outs,
-            [slot(qkv_pieces, index) for index in (1, 2, 0)],
+            [slot(attn_pieces, index) for index in (1, 2, 0)],
         )
         if layer == 0:
             first_in = normed[0]
         if fast:
             prev = lax.ppermute(kv, "ctx", [(0, 1)])
             kv_blocks = [prev, kv]
-            out_g.swap(queries)
             if layer == 0:
-                out_g.far("x", (queries,))
-                gate_g.near((*out_g.pieces, out_g.from_x), (prev,))
+                mlp_g.near_y((prev,))
             else:
-                out_g.far("x", (queries, up_g.from_x))
-                gate_g.swap(queries)
-                gate_g.far("x", (queries, *out_g.pieces))
-                up_g.near_y((prev,))
-            out_pieces = out_g.all()
+                down_g.near_y((prev,))
         else:
             kv_blocks = [lax.all_gather(kv, "ctx", axis=1, tiled=True)]
         mixed, log_total, part = kernel(
@@ -839,18 +885,15 @@
             spots,
             [queries] + kv_blocks + masks,
             [headed, shape((heads, rows), F32), wide],
-            [slot(out_pieces, 0)],
+            [slot(attn_pieces, 3)],
         )
         terms = tensor_scatter(part)
-        if fast:
-            if layer == 0:
-                up_g.near((part, gate_g.from_x), (part, gate_g.from_y))
-                gate_g.swap(part)
-                gate_g.far("both", (part,), (part,))
-            else:
-                down_g.near((part, *gate_g.pieces), (part, up_g.from_y))
-                up_g.swap(part)
-                up_g.far("both", (part,), (part,))
+        if fast and layer == 0:
+            terms = after(terms, mlp_g.from_x)
+        elif fast:
+            gu_g.swap(part)
+            gu_g.far("both", (part,), (part,))
+            terms = after(terms, down_g.from_x)
         mid, normed = kernel(
             norm_body,
             "norm",
@@ -861,38 +904,52 @@
         second_in = tensor_gather(normed)
         if fast:
             if layer == 0:
-                down_g.near((mid, gate_g.pieces[0]), (mid, gate_g.pieces[1]))
-                up_g.swap(mid)
-                up_g.far("both", (mid,), (mid,))
-                down_g.swap()
+                mlp_g.swap(mid)
+                mlp_g.far("both", (mid,), (mid,))
+                mlp_pieces = mlp_g.all(second_in)
+                mlp_slots = [slot(mlp_pieces, index) for index in range(3)]
+                sent = mlp_g.pieces
             else:
                 down_g.swap(mid)
-            down_g.far("both", (mid, up_g.pieces[0]), (mid, up_g.pieces[1]))
-            gate_pieces, up_pieces, down_pieces = gate_g.all(), up_g.all(), down_g.all()
-        gate, up, hidden, part = kernel(
-            mlp_body,
-            "mlp",
-            spots,
-            [Free(second_in)],
-            [inner, inner, inner, wide],
-            [slot(gate_pieces, 0), slot(up_pieces, 0), slot(down_pieces, 0)],
-        )
+                down_g.far("both", (mid,), (mid,))
+                gu_pieces, down_pieces = gu_g.all(), down_g.all(second_in)
+                mlp_slots = [slot(gu_pieces, 0), slot(gu_pieces, 1), slot(down_pieces, 0)]
+                sent = down_g.pieces
+        second_in = flat(second_in)
+        if layer < layers - 1:
+            gate, up, hidden, part = kernel(
+                mlp_body,
+                "mlp",
+                spots,
+                [Free(second_in)],
+                [inner, inner, inner, wide],
+                mlp_slots,
+            )
+        else:
+            peer = swap_core(cotangent[0]) if fast else ()
+            hidden, last_part, d_gate_up, part = kernel(
+                mlp_both_body,
+                "mlp_both",
+                spots,
+                [Free(second_in), after(cotangent[0], peer)],
+                [inner, wide, shape((2, rows, hidden_width), BF), wide],
+                mlp_slots,
+            )
+            gate, up, last_mid = None, None, mid
         saved.append((stream, first_in, queries, kv_blocks, mixed, log_total, mid))
         saved[-1] += (second_in, gate, up, hidden)
-        groups.append((qkv_pieces, out_pieces, gate_pieces, up_pieces, down_pieces))
+        groups.append((attn_pieces, mlp_slots))
         if layer == layers - 1:
             break
         terms = tensor_scatter(part)
         if fast:
-            sent = down_g.pieces
-            qkv_g, out_g, gate_g, up_g, down_g = (Gather(shard) for shard in shards[layer + 1])
-            qkv_g.near(sent[:1], sent[1:])
-            qkv_g.swap(part)
-            qkv_g.far("y", (), (part,))
-            out_g.near((qkv_g.from_x, part), (qkv_g.pieces[0],))
-            gate_g.near((out_g.from_x,), (out_g.from_y,))
-            up_g.near_x((gate_g.from_x,))
-            terms = after(terms, gate_g.shard)
+            attn_g, gu_g, down_g = (Gather(shard) for shard in shards[layer + 1])
+            attn_g.near(sent[:1], sent[1:])
+            attn_g.swap(part)
+            attn_g.far("both", (part,), (part,))
+            gu_g.near((attn_g.from_x, part), (attn_g.from_y, part))
+            down_g.near_x((gu_g.from_x,))
+            terms = after(terms, gu_g.shard, *attn_g.pieces, *attn_g.peers)
         stream, normed = kernel(
             norm_body,
             "norm",
@@ -900,10 +957,11 @@
             [Free(terms), mid, gains[layer + 1, 0][None], shifts[layer + 1, 0][None]],
             [block_f, copies_b],
         )
-        first_in = tensor_gather(normed)
-    last_part, last_mid = part, mid
-
-    attn_outs, mlp_outs, pending = None, None, None
+        first_in = flat(tensor_gather(normed))
+        if fast:
+            first_in = after(first_in, gu_g.from_x, gu_g.from_y)
+
+    attn_outs, mlp_outs, pending, mlp_pending = None, None, None, None
     sums = [None] * layers
     plain = [None] * layers
     grad = lax.dynamic_slice_in_dim(cotangent[0], tensor_rank * block, block, 0)
@@ -911,33 +969,39 @@
     for layer in reversed(range(layers)):
         (stream, first_in, queries, kv_blocks, mixed, log_total, mid) = saved[layer][:7]
         (second_in, gate, up, hidden) = saved[layer][7:]
-        qkv_pieces, out_pieces, gate_pieces, up_pieces, down_pieces = groups[layer]
-        d_gate_up, part = kernel(
-            mlp_back_body,
-            "mlp_back",
-            spots,
-            [gate, up, Free(d_mlp)],
-            [shape((2, rows, hidden_width), BF), wide],
-            [slot(down_pieces, 0), slot(gate_pieces, 0), slot(up_pieces, 0)],
-        )
+        attn_pieces, mlp_slots = groups[layer]
+        late = layer == layers - 1
+        mlp_peer = [None] * 4
+        if late:
+            mlp_peer[1] = peer
+        else:
+            if fast:
+                mlp_peer[0], mlp_peer[3] = swap_core(second_in), swap_core(hidden)
+                gate = after(gate, mlp_peer[0], mlp_peer[3])
+            d_gate_up, part = kernel(
+                mlp_back_body,
+                "mlp_back",
+                spots,
+                [gate, up, Free(d_mlp)],
+                [shape((2, rows, hidden_width), BF), wide],
+                [mlp_slots[2], mlp_slots[0], mlp_slots[1]],
+            )
         terms = tensor_scatter(part)
         pairs = ((0, 0), (0, 1), (1, 2))
         if fast:
-            ready, attn_added = [], ()
             if pending is not None:
-                attn_terms, attn_added = reduce_second(spots, *pending, (part,), (), "attn_add")
-                attn_added = (attn_added,)
-                ready += attn_terms[3:]
-            mlp_parts, mlp_sent = weight_grads(
-                [second_in, d_mlp, d_gate_up, hidden],
-                2,
-                pairs,
-                (part, *attn_added),
-                ready,
-                "mlp_grads",
+                part = after(part, *mlp_pending[3:])
+            mlp_parts, (to_x, to_y) = weight_grads(
+                [second_in, d_mlp, d_gate_up, hidden], mlp_peer, 2, pairs, (part,), "mlp_grads"
             )
-            ready.append(mlp_parts[0])
-            terms = after(terms, *ready)
+            terms = after(terms, mlp_parts[0])
+            if pending is not None:
+                mlp_pending[0] = after(mlp_pending[0], mlp_parts[0])
+                mlp_outs = mlp_finish(spots, mlp_outs, mlp_pending, layer + 1, layers)
+                attn_sums = add_received(spots, *pending, (mlp_outs[0],), "attn_add")
+                terms = after(terms, attn_sums[0])
+            got_x = swap_x(to_x)
+            got_y = None if late else swap_y(to_y)
         else:
             mlp_grad = plain_grads(
                 [second_in, d_mlp], [d_gate_up[0], d_gate_up[1], hidden], pairs
@@ -949,17 +1013,13 @@
             [Free(terms), mid, gains[layer, 1][None], grad],
             [block_f, copies_b, shape((2, width), F32)],
         )
-        d_attn = tensor_gather(normed)
-        if pending is not None:
-            attn_terms[0] = after(attn_terms[0], grad_mid)
-            attn_outs = attn_finish(spots, attn_outs, attn_terms, layer + 1, layers)
-            d_attn = after(d_attn, attn_outs[0])
+        gathered = tensor_gather(normed)
+        d_attn = flat(gathered)
         if layer == layers - 1:
-            (summed,) = kernel(
-                sum_body, "sum", spots, [tensor_scatter(last_part, d_attn), last_mid], [copies_b]
-            )
+            out_terms = tensor_scatter(last_part, gathered)
+            (summed,) = kernel(sum_body, "sum", spots, [out_terms, last_mid], [copies_b])
         elif layer == layers - 2:
-            output = tensor_gather(after(summed, d_attn))
+            out_blocks = tensor_gather(after(summed, gathered))
         kv_outs = [shape(kv.shape, BF) for kv in kv_blocks]
         if fast:
             kv_outs[-1] = shape((2, rows, heads_width), F32)
@@ -969,38 +1029,50 @@
             spots,
             [Free(d_attn), queries, log_total, tables] + kv_blocks + masks,
             [headed] + kv_outs,
-            [slot(out_pieces, 0)],
+            [slot(attn_pieces, 3)],
             extra=[pltpu.VMEM((rows, heads_width), BF)],
         )
         if fast:
             own = d_kvs[1]
-            other = [lax.ppermute(after(d_kvs[0], *mlp_sent), "ctx", [(1, 0)])]
-            mlp_terms, mlp_added = reduce_second(
-                spots, mlp_parts, mlp_sent, (d_kvs[0],), (), "mlp_add"
-            )
-            own = after(own, mlp_added)
+            other = [lax.ppermute(d_kvs[0] if late else after(d_kvs[0], got_y), "ctx", [(1, 0)])]
+            if late:
+                got_y = swap_y(after(to_y, other[0]))
+                own = after(own, got_x)
+            else:
+                mlp_sums = add_received(spots, mlp_parts, (got_x, got_y), (d_kvs[0],), "mlp_add")
+                own = after(own, mlp_sums[0])
+                if pending is not None:
+                    attn_terms = send_second(*pending, attn_sums, (other[0],))
+                mlp_terms = send_second(mlp_parts, (got_x, got_y), mlp_sums, ())
+            attn_peer = [swap_core(after(a, d_kvs[0])) for a in (first_in, d_attn)]
+            attn_peer += [None, swap_core(after(mixed, d_kvs[0]))]
+            own = after(own, attn_peer[0], attn_peer[1], attn_peer[3])
         else:
             own = lax.psum_scatter(d_kvs[0], "ctx", scatter_dimension=1, tiled=True)
             other = []
+        if layer == layers - 1:
+            own = after(own, out_terms)
+        elif layer == layers - 2:
+            own = after(own, out_blocks)
         d_qkv, bias_sums, part = kernel(
             functools.partial(qkv_back_body, len(other)),
             "qkv_back",
             spots,
             [d_query, tables, own] + other,
             [shape((3, rows, heads_width), BF), shape((3, heads_width), F32), wide],
-            [slot(qkv_pieces, index) for index in range(3)],
+            [slot(attn_pieces, index) for index in range(3)],
         )
         terms = tensor_scatter(part)
         if layer == layers - 1:
             terms = after(terms, summed)
-        elif layer == layers - 2:
-            terms = after(terms, output)
         pairs = ((0, 0), (0, 1), (0, 2), (1, 3))
         if fast:
-            pending = weight_grads(
-                [first_in, d_attn, d_qkv, mixed], 2, pairs, (part,), (), "attn_grads"
+            ready = (part,) if late else (part, *mlp_terms[3:])
+            attn_parts, (to_x, to_y) = weight_grads(
+                [first_in, d_attn, d_qkv, mixed], attn_peer, 2, pairs, ready, "attn_grads"
             )
-            terms = after(terms, pending[0][0], *mlp_terms[3:])
+            pending = (attn_parts, (swap_x(to_x), swap_y(to_y)))
+            terms = after(terms, attn_parts[0])
         else:
             rights = [d_qkv[0], d_qkv[1], d_qkv[2], mixed]
             plain[layer] = (plain_grads([first_in, d_attn], rights, pairs), mlp_grad)
@@ -1011,31 +1083,33 @@
             [Free(terms), stream, gains[layer, 0][None], grad_mid],
             [block_f, copies_b, shape((2, width), F32)],
         )
-        d_mlp = tensor_gather(normed)
+        d_mlp = flat(tensor_gather(normed))
         if fast:
-            mlp_terms[0] = after(mlp_terms[0], grad)
-            mlp_outs = kernel(
-                functools.partial(finish_body, True),
-                "mlp_finish",
-                spots,
-                mlp_terms,
-                [
-                    (shape((layers, block_rows, 2, hidden_width), F32), layer),
-                    (shape((layers, hidden_width, block_rows), F32), layer),
-                ],
-                reuse=() if mlp_outs is None else ((mlp_outs[0], 0), (mlp_outs[1], 1)),
-            )
-            d_mlp = after(d_mlp, mlp_outs[0], *pending[1])
+            if late:
+                mlp_pending, mlp_added = reduce_second(
+                    spots, mlp_parts, (got_x, got_y), (grad,), (), "mlp_add"
+                )
+                d_mlp = after(d_mlp, mlp_added)
+            else:
+                if mlp_pending is not None:
+                    attn_terms[0] = after(attn_terms[0], grad)
+                    attn_outs = attn_finish(spots, attn_outs, attn_terms, layer + 1, layers)
+                mlp_terms[0] = after(mlp_terms[0], grad)
+                mlp_outs = mlp_finish(spots, mlp_outs, mlp_terms, layer, layers)
         bias_rows = lax.dynamic_update_slice_in_dim(
             jnp.zeros((3, width), F32), bias_sums, tensor_rank * heads_width, 1
         )
         sums[layer] = jnp.concatenate(
             [sums_one[0:1], sums_two[0:1], sums_one[1:2], sums_two[1:2], bias_rows]
         )
-    totals, halfway = reduce_small(jnp.concatenate(sums), fast)
-    totals = totals.reshape(layers, 7, -1)
+    wait = ()
     if fast:
-        attn_terms, _ = reduce_second(spots, *pending, (grad,), (), "attn_add")
+        attn_terms, attn_added = reduce_second(
+            spots, *pending, (grad, mlp_outs[0], attn_outs[0]), (), "attn_add"
+        )
+        wait = (attn_added,)
+    totals = reduce_small(jnp.concatenate(sums), fast, *wait).reshape(layers, 7, -1)
+    if fast:
         attn_outs = attn_finish(spots, attn_outs, attn_terms, 0, layers)
     grad_input = d_mlp.astype(F32)
     if fast:
@@ -1050,7 +1124,7 @@
             mlp[:, 2].transpose(0, 2, 1),
         )
     return (
-        output[None],
+        flat(out_blocks)[None],
         grad_input[None],
         totals[:, 0:2],
         totals[:, 2:4],
@@ -1059,6 +1133,22 @@
         grads[1],
         grads[2],
         grads[3],
+    )
+
+
+def mlp_finish(spots, outs, terms, layer, layers):
+    _, half, columns = terms[3].shape
+    rows = 2 * half
+    return kernel(
+        functools.partial(finish_body, True),
+        "mlp_finish",
+        spots,
+        terms,
+        [
+            (shape((layers, rows, 2, columns), F32), layer),
+            (shape((layers, columns, rows), F32), layer),
+        ],
+        reuse=() if outs is None else ((outs[0], 0), (outs[1], 1)),
     )
 
 

time: 801 us -> 742 us (0.926)
  waiting for transfers between devices: 356 us -> 323 us
  starting transfers between devices: 149 us -> 132 us
  Pallas kernels: 235 us -> 223 us
    ppermute x29 -> x20, waiting for transfers between devices: 113 us -> 64 us  [swap_x(): return lax.ppermute(array, 'fsdp', pairs_of('fsdp', 2))]
    ppermute x27 -> x20, waiting for transfers between devices: 92.1 us -> 129 us  [swap_y(): return lax.ppermute(array, 'ctx', pairs_of('ctx', 1))]
    all_to_all x8, waiting for transfers between devices: 45.7 us -> 33.2 us  [tensor_scatter(): return lax.all_to_all(blocks, 'tp', 0, 0, tiled=True)]
    ppermute x29 -> x20, starting transfers between devices: 29.4 us -> 17.9 us  [swap_x(): return lax.ppermute(array, 'fsdp', pairs_of('fsdp', 2))]
    pallas_call x30 -> x29, Pallas kernels: 200 us -> 189 us  [kernel(): pl.pallas_call(run, out_shape=[pltpu.HBM(out.shape, out.dtype) for out in...]
    ppermute x2, waiting for transfers between devices: 17.7 us -> 8.28 us  [local(): lax.ppermute(d_kvs[0] if late else after(d_kvs[0], got_y), 'ctx', [(1, 0)])]
    ppermute x27 -> x20, starting transfers between devices: 26.6 us -> 23.1 us  [swap_y(): return lax.ppermute(array, 'ctx', pairs_of('ctx', 1))]
    unnamed x203 -> x137, local copies, waits for them, and re-layouts: 22.4 us -> 19.2 us
  transfers between devices with their start and end apart: 142 -> 105, of which waited for: 55 -> 56; matrix products, arithmetic and copies ran while one was open for 3% -> 4% of each run, Pallas kernels for 20% -> 22%
where the time goes in v3:
time: 742 us; the launch traced here: 732 us
  waiting for transfers between devices  323 us (44%)
  Pallas kernels  223 us (30%)
  starting transfers between devices  132 us (18%)
  local copies, waits for them, and re-layouts  43.6 us (6%)
  other arithmetic  8.56 us (1%)
    pallas_call x29, Pallas kernels, kernel(): pl.pallas_call(run, out_shape=[pltpu.HBM(out.shape, out.dtype) for out in...  189 us
    ppermute x20, waiting for transfers between devices, swap_y(): return lax.ppermute(array, 'ctx', pairs_of('ctx', 1))  129 us
    ppermute x20, waiting for transfers between devices, swap_x(): return lax.ppermute(array, 'fsdp', pairs_of('fsdp', 2))  64 us
    all_to_all x8, waiting for transfers between devices, tensor_gather(): return lax.all_to_all(copies, 'tp', 0, 0, tiled=True)  47.6 us
    all_to_all x8, starting transfers between devices, tensor_scatter(): return lax.all_to_all(blocks, 'tp', 0, 0, tiled=True)  39.7 us
    pallas_call x4, Pallas kernels, weight_grads(): pl.pallas_call(functools.partial(weight_grad_body, counts, n_left, pairs)...  34.9 us
    all_to_all x8, waiting for transfers between devices, tensor_scatter(): return lax.all_to_all(blocks, 'tp', 0, 0, tiled=True)  33.2 us
    all_to_all x8, starting transfers between devices, tensor_gather(): return lax.all_to_all(copies, 'tp', 0, 0, tiled=True)  31.6 us
  transfers between devices with their start and end apart: 105, of which 56 were waited for; matrix products, arithmetic and copies ran while one was open for 4% of the time, Pallas kernels for 22%

profile of v3, /device:TPU:0, one launch (start us, length us, event | category | flops | bytes accessed | tf_op | source)
XLA Modules:
  0.0 732.4 jit_solution(16624263259849425109)
XLA Ops:
  21.9 7.1 pack.2.refs_2_.refs_4_
  31.8 5.0 collective-permute-done.4.refs_8_.refs_11_.refs_7_
  37.4 9.5 %collective-permute-done.6.refs_10_.refs_13_.refs_9_ = bf16[4,128,512]{2,1,0:T(8,128)(2,1)} collective-permute-done((bf16[4,128,512]{2,1,0:T(8,128)(2,1)S(1)}, bf16[4,128,512]{2,1,0:T(8,128)(2,1)}, u32[]{:S(2)}, u32[]{:S(2)}) %collective-permute-start.6) | collective-permute-done | bytes 524320 | tf_op jit(solution)/shard_map/ppermute | solution.py:541
  50.6 8.6 %qkv.2 = (bf16[256,512]{1,0:T(8,128)(2,1)}, bf16[2,256,512]{2,1,0:T(8,128)(2,1)}, bf16[256,2048]{1,0:T(8,128)(2,1)}) custom-call(s32[18]{0:T(128)S(1)} %stack.130.refs_0_, f32[3,512]{1,0:T(4,128)} %get-tuple-element.179.refs_1_, f32[3,256,128]{2,1,0:T(8,128)} %pad_maximum_fusion.2.refs_2_.refs_4_, f32[1,2048]{1,0:T(1,128)} %get-tuple-element.425.refs_3_, ...), custom_call_target="tpu_custom_call" | custom-call | bytes 25500000 | tf_op jit(solution)/shard_map/qkv/pallas_call | solution.py:191
  63.4 11.0 %collective-permute-done.12.refs_2_.refs_5_ = bf16[2,256,512]{2,1,0:T(8,128)(2,1)S(1)} collective-permute-done((bf16[2,256,512]{2,1,0:T(8,128)(2,1)}, bf16[2,256,512]{2,1,0:T(8,128)(2,1)S(1)}, u32[]{:S(2)}, u32[]{:S(2)}) %collective-permute-start.12) | collective-permute-done | bytes 524320 | tf_op jit(solution)/shard_map/ppermute | solution.py:874
  77.7 8.2 %attend.2 = (bf16[256,512]{1,0:T(8,128)(2,1)}, f32[8,256]{1,0:T(8,128)}, bf16[256,2048]{1,0:T(8,128)(2,1)}) custom-call(s32[18]{0:T(128)S(1)} %stack.130.refs_0_, bf16[256,512]{1,0:T(8,128)(2,1)} %get-tuple-element.181.refs_1_.refs_2_, bf16[2,256,512]{2,1,0:T(8,128)(2,1)} %copy-done.23, bf16[2,256,512]{2,1,0:T(8,128)(2,1)} %get-tuple-element.182.refs_3_.refs_6_, ...), custom_call_target="tpu_custom_call" | custom-call | bytes 24000000 | tf_op jit(solution)/shard_map/attend/pallas_call | solution.py:191
  92.5 19.5 %collective-permute-done.13.refs_3_.refs_5_ = bf16[3,256,1408]{2,1,0:T(8,128)(2,1)} collective-permute-done((bf16[3,256,1408]{2,1,0:T(8,128)(2,1)}, bf16[3,256,1408]{2,1,0:T(8,128)(2,1)}, u32[]{:S(2)}, u32[]{:S(2)}) %collective-permute-start.13) | collective-permute-done | bytes 2162720 | tf_op jit(solution)/shard_map/ppermute | solution.py:533
  127.5 22.8 %collective-permute-done.16.refs_6_.refs_8_ = bf16[3,128,1408]{2,1,0:T(8,128)(2,1)} collective-permute-done((bf16[3,128,1408]{2,1,0:T(8,128)(2,1)S(1)}, bf16[3,128,1408]{2,1,0:T(8,128)(2,1)}, u32[]{:S(2)}, u32[]{:S(2)}) %collective-permute-start.16) | collective-permute-done | bytes 1081376 | tf_op jit(solution)/shard_map/ppermute | solution.py:541
  155.9 11.3 %mlp.1 = (bf16[256,1408]{1,0:T(8,128)(2,1)}, bf16[256,1408]{1,0:T(8,128)(2,1)}, bf16[256,1408]{1,0:T(8,128)(2,1)}, bf16[256,2048]{1,0:T(8,128)(2,1)}) custom-call(s32[18]{0:T(128)S(1)} %stack.130.refs_0_, bf16[256,2048]{1,0:T(8,128)(2,1)S(1)} %bitcast.125, bf16[3,256,1408]{2,1,0:T(8,128)(2,1)} %pack.2.refs_2_.refs_4_, ...), custom_call_target="tpu_custom_call" | custom-call | bytes 34500000 | tf_op jit(solution)/shard_map/mlp/pallas_call | solution.py:191
  167.3 5.0 all-to-all-start.2
  172.3 6.6 collective-permute-done.22.refs_6_.refs_8_.refs_11_.refs_7_
  184.0 7.1 pack.3
  191.0 5.8 collective-permute-done.25.refs_8_.refs_10_.refs_13_.refs_9_
  209.8 30.6 %collective-permute-done.30.refs_5_ = bf16[2,256,1408]{2,1,0:T(8,128)(2,1)} collective-permute-done((bf16[2,256,1408]{2,1,0:T(8,128)(2,1)}, bf16[2,256,1408]{2,1,0:T(8,128)(2,1)}, u32[]{:S(2)}, u32[]{:S(2)}) %collective-permute-start.30) | collective-permute-done | bytes 1441824 | tf_op jit(solution)/shard_map/ppermute | solution.py:541
  240.9 6.8 qkv.3
  250.9 9.5 %collective-permute-done.33.refs_2_.refs_5_ = bf16[2,256,512]{2,1,0:T(8,128)(2,1)S(1)} collective-permute-done((bf16[2,256,512]{2,1,0:T(8,128)(2,1)}, bf16[2,256,512]{2,1,0:T(8,128)(2,1)S(1)}, u32[]{:S(2)}, u32[]{:S(2)}) %collective-permute-start.33) | collective-permute-done | bytes 524320 | tf_op jit(solution)/shard_map/ppermute | solution.py:874
  261.1 8.2 %attend.3 = (bf16[256,512]{1,0:T(8,128)(2,1)}, f32[8,256]{1,0:T(8,128)}, bf16[256,2048]{1,0:T(8,128)(2,1)}) custom-call(s32[18]{0:T(128)S(1)} %stack.130.refs_0_, bf16[256,512]{1,0:T(8,128)(2,1)} %get-tuple-element.210.refs_1_.refs_2_, bf16[2,256,512]{2,1,0:T(8,128)(2,1)} %copy-done.24, bf16[2,256,512]{2,1,0:T(8,128)(2,1)} %get-tuple-element.211.refs_3_.refs_6_, ...), custom_call_target="tpu_custom_call" | custom-call | bytes 24000000 | tf_op jit(solution)/shard_map/attend/pallas_call | solution.py:191
  279.6 9.5 %collective-permute-done.34.refs_14_ = bf16[1,256,1408]{2,1,0:T(8,128)(2,1)} collective-permute-done((bf16[1,256,1408]{2,1,0:T(8,128)(2,1)}, bf16[1,256,1408]{2,1,0:T(8,128)(2,1)}, u32[]{:S(2)}, u32[]{:S(2)}) %collective-permute-start.34) | collective-permute-done | bytes 720928 | tf_op jit(solution)/shard_map/ppermute | solution.py:533
  289.1 5.4 collective-permute-done.43.refs_15_
  309.0 13.3 %collective-permute-done.36.refs_6_ = bf16[2,128,1408]{2,1,0:T(8,128)(2,1)} collective-permute-done((bf16[2,128,1408]{2,1,0:T(8,128)(2,1)S(1)}, bf16[2,128,1408]{2,1,0:T(8,128)(2,1)}, u32[]{:S(2)}, u32[]{:S(2)}) %collective-permute-start.36) | collective-permute-done | bytes 720928 | tf_op jit(solution)/shard_map/ppermute | solution.py:533
  326.5 6.9 collective-permute-done.45.refs_17_
  339.8 16.1 %mlp_both.1 = (bf16[256,1408]{1,0:T(8,128)(2,1)}, bf16[256,2048]{1,0:T(8,128)(2,1)}, bf16[2,256,1408]{2,1,0:T(8,128)(2,1)}, bf16[256,2048]{1,0:T(8,128)(2,1)}) custom-call(s32[18]{0:T(128)S(1)} %stack.130.refs_0_, bf16[256,2048]{1,0:T(8,128)(2,1)S(1)} %bitcast.113, bf16[256,2048]{1,0:T(8,128)(2,1)} %bitcast.53.refs_2_, ...), custom_call_target="tpu_custom_call" | custom-call | bytes 54000000 | tf_op jit(solution)/shard_map/mlp_both/pallas_call | solution.py:191
  355.9 5.0 all-to-all-start.6
  369.2 10.6 %mlp_grads.2 = (bf16[2,3,128,1408]{3,2,1,0:T(8,128)(2,1)}, bf16[2,3,128,1408]{3,2,1,0:T(8,128)(2,1)}, bf16[2,3,128,1408]{3,2,1,0:T(8,128)(2,1)}, bf16[3,128,1408]{2,1,0:T(8,128)(2,1)}, bf16[3,128,1408]{2,1,0:T(8,128)(2,1)}) custom-call(s32[4]{0:T(128)S(1)} %pad_add_fusion.refs_0_, bf16[256,2048]{1,0:T(8,128)(2,1)} %bitcast.115, ...), custom_call_target="tpu_custom_call" | custom-call | bytes 31500000 | tf_op jit(solution)/shard_map/mlp_grads/pallas_call | solution.py:683
  379.8 7.2 all-to-all-done.6.refs_1_
  396.1 23.5 %all-to-all-done.7 = bf16[4,64,2048]{2,1,0:T(8,128)(2,1)S(1)} async-done(((bf16[4,64,2048]{2,1,0:T(8,128)(2,1)}), bf16[4,64,2048]{2,1,0:T(8,128)(2,1)S(1)}, u32[]{:S(2)}, u32[]{:S(2)}) %all-to-all-start.7) | async-done | bytes 1048608 | tf_op jit(solution)/shard_map/all_to_all | solution.py:647
  423.8 9.9 %attend_back.2 = (bf16[256,512]{1,0:T(8,128)(2,1)}, bf16[2,256,512]{2,1,0:T(8,128)(2,1)}, f32[2,256,512]{2,1,0:T(8,128)}) custom-call(s32[18]{0:T(128)S(1)} %stack.130.refs_0_, bf16[256,2048]{1,0:T(8,128)(2,1)S(1)} %bitcast.116, bf16[256,512]{1,0:T(8,128)(2,1)} %get-tuple-element.210.refs_1_.refs_2_, f32[8,256]{1,0:T(8,128)} %get-tuple-element.248.refs_3_, ...), custom_call_target="tpu_custom_call" | custom-call | bytes 30000000 | tf_op jit(solution)/shard_map/attend_back/pallas_call | solution.py:191
  436.0 6.8 collective-permute-done.56.refs_4_.refs_2_
  450.4 8.8 %qkv_back.2 = (bf16[3,256,512]{2,1,0:T(8,128)(2,1)}, f32[3,512]{1,0:T(4,128)}, bf16[256,2048]{1,0:T(8,128)(2,1)}) custom-call(s32[18]{0:T(128)S(1)} %stack.130.refs_0_, bf16[256,512]{1,0:T(8,128)(2,1)} %get-tuple-element.249.refs_1_, f32[3,256,128]{2,1,0:T(8,128)} %pad_maximum_fusion.2.refs_2_.refs_4_, f32[2,256,512]{2,1,0:T(8,128)} %get-tuple-element.259.refs_3_, ...), custom_call_target="tpu_custom_call" | custom-call | bytes 27000000 | tf_op jit(solution)/shard_map/qkv_back/pallas_call | solution.py:191
  459.2 5.2 all-to-all-start.9
  468.4 6.9 attn_grads.2
  475.3 14.2 %all-to-all-done.9.refs_1_ = bf16[4,64,2048]{2,1,0:T(8,128)(2,1)S(1)} async-done(((bf16[4,64,2048]{2,1,0:T(8,128)(2,1)}), bf16[4,64,2048]{2,1,0:T(8,128)(2,1)S(1)}, u32[]{:S(2)}, u32[]{:S(2)}) %all-to-all-start.9) | async-done | bytes 1048608 | tf_op jit(solution)/shard_map/all_to_all | solution.py:643
  496.8 15.8 %collective-permute-done.62.refs_3_ = bf16[2,3,128,1408]{3,2,1,0:T(8,128)(2,1)} collective-permute-done((bf16[2,3,128,1408]{3,2,1,0:T(8,128)(2,1)}, bf16[2,3,128,1408]{3,2,1,0:T(8,128)(2,1)}, u32[]{:S(2)}, u32[]{:S(2)}) %collective-permute-start.62) | collective-permute-done | bytes 2162720 | tf_op jit(solution)/shard_map/ppermute | solution.py:541
  521.9 14.1 %mlp_back.1 = (bf16[2,256,1408]{2,1,0:T(8,128)(2,1)}, bf16[256,2048]{1,0:T(8,128)(2,1)}) custom-call(s32[18]{0:T(128)S(1)} %stack.130.refs_0_, bf16[256,1408]{1,0:T(8,128)(2,1)} %get-tuple-element.246.refs_1_, bf16[256,1408]{1,0:T(8,128)(2,1)} %get-tuple-element.247.refs_2_, bf16[256,2048]{1,0:T(8,128)(2,1)S(1)} %bitcast.119, ...), custom_call_target="tpu_custom_call" | custom-call | bytes 42000000 | tf_op jit(solution)/shard_map/mlp_back/pallas_call | solution.py:191
  536.0 5.2 all-to-all-start.11
  549.0 10.6 %mlp_grads.3 = (bf16[2,3,128,1408]{3,2,1,0:T(8,128)(2,1)}, bf16[2,3,128,1408]{3,2,1,0:T(8,128)(2,1)}, bf16[2,3,128,1408]{3,2,1,0:T(8,128)(2,1)}, bf16[3,128,1408]{2,1,0:T(8,128)(2,1)}, bf16[3,128,1408]{2,1,0:T(8,128)(2,1)}) custom-call(s32[4]{0:T(128)S(1)} %pad_add_fusion.refs_0_, bf16[256,2048]{1,0:T(8,128)(2,1)} %bitcast.127, bf16[256,2048]{1,0:T(8,128)(2,1)} %bitcast.121, ...), custom_call_target="tpu_custom_call" | custom-call | bytes 31500000 | tf_op jit(solution)/shard_map/mlp_grads/pallas_call | solution.py:683
  559.6 7.4 %mlp_finish.2 = (f32[2,256,2,1408]{3,2,1,0:T(2,128)}, f32[2,1408,256]{2,1,0:T(8,128)}) custom-call(s32[18]{0:T(128)S(1)} %stack.130.refs_0_, bf16[2,3,128,1408]{3,2,1,0:T(8,128)(2,1)} %get-tuple-element.285.refs_1_, bf16[2,3,128,1408]{3,2,1,0:T(8,128)(2,1)} %collective-permute-done.56.refs_4_.refs_2_, ...), custom_call_target="tpu_custom_call" | custom-call | bytes 22500000 | tf_op jit(solution)/shard_map/mlp_finish/pallas_call | solution.py:191
  576.3 5.1 all-to-all-start.12
  582.3 23.9 %all-to-all-done.12 = bf16[4,64,2048]{2,1,0:T(8,128)(2,1)S(1)} async-done(((bf16[4,64,2048]{2,1,0:T(8,128)(2,1)}), bf16[4,64,2048]{2,1,0:T(8,128)(2,1)S(1)}, u32[]{:S(2)}, u32[]{:S(2)}) %all-to-all-start.12) | async-done | bytes 1048608 | tf_op jit(solution)/shard_map/all_to_all | solution.py:647
  609.9 9.9 %attend_back.3 = (bf16[256,512]{1,0:T(8,128)(2,1)}, bf16[2,256,512]{2,1,0:T(8,128)(2,1)}, f32[2,256,512]{2,1,0:T(8,128)}) custom-call(s32[18]{0:T(128)S(1)} %stack.130.refs_0_, bf16[256,2048]{1,0:T(8,128)(2,1)S(1)} %bitcast.110, bf16[256,512]{1,0:T(8,128)(2,1)} %get-tuple-element.181.refs_1_.refs_2_, f32[8,256]{1,0:T(8,128)} %get-tuple-element.295.refs_3_, ...), custom_call_target="tpu_custom_call" | custom-call | bytes 30000000 | tf_op jit(solution)/shard_map/attend_back/pallas_call | solution.py:191
  620.5 8.8 %collective-permute-done.69.refs_3_ = bf16[2,3,128,1408]{3,2,1,0:T(8,128)(2,1)} collective-permute-done((bf16[2,3,128,1408]{3,2,1,0:T(8,128)(2,1)}, bf16[2,3,128,1408]{3,2,1,0:T(8,128)(2,1)}, u32[]{:S(2)}, u32[]{:S(2)}) %collective-permute-start.69) | collective-permute-done | bytes 2162720 | tf_op jit(solution)/shard_map/ppermute | solution.py:541
  639.4 7.0 collective-permute-done.74.refs_4_
  646.3 8.8 %qkv_back.3 = (bf16[3,256,512]{2,1,0:T(8,128)(2,1)}, f32[3,512]{1,0:T(4,128)}, bf16[256,2048]{1,0:T(8,128)(2,1)}) custom-call(s32[18]{0:T(128)S(1)} %stack.130.refs_0_, bf16[256,512]{1,0:T(8,128)(2,1)} %get-tuple-element.296.refs_1_, f32[3,256,128]{2,1,0:T(8,128)} %pad_maximum_fusion.2.refs_2_.refs_4_, f32[2,256,512]{2,1,0:T(8,128)} %get-tuple-element.312.refs_3_, ...), custom_call_target="tpu_custom_call" | custom-call | bytes 27000000 | tf_op jit(solution)/shard_map/qkv_back/pallas_call | solution.py:191
  655.2 5.2 all-to-all-start.14
  660.5 5.7 collective-permute-done.76.refs_5_
  669.4 6.9 attn_grads.3
  687.7 7.4 %mlp_finish.3 = (f32[2,256,2,1408]{3,2,1,0:T(2,128)}, f32[2,1408,256]{2,1,0:T(8,128)}) custom-call(s32[18]{0:T(128)S(1)} %stack.130.refs_0_, bf16[2,3,128,1408]{3,2,1,0:T(8,128)(2,1)} %get-tuple-element.330.refs_1_, bf16[2,3,128,1408]{3,2,1,0:T(8,128)(2,1)} %collective-permute-done.70.refs_4_.refs_2_, ...), custom_call_target="tpu_custom_call", output_to_operand_aliasing={{0}: (6, {}), {1}: (7, {})} | custom-call | bytes 22500000 | tf_op jit(solution)/shard_map/mlp_finish/pallas_call | solution.py:191
  699.4 5.4 collective-permute-done.78
  (412 shorter events, 251.4 us)
Async XLA Ops:
  3.5 26.5 %collective-permute-start.3 = (bf16[4,256,512]{2,1,0:T(8,128)(2,1)S(1)}, bf16[4,256,512]{2,1,0:T(8,128)(2,1)S(1)}, u32[]{:S(2)}, u32[]{:S(2)}) collective-permute-start(bf16[4,256,512]{2,1,0:T(8,128)(2,1)S(1)} %pad_maximum_fusion.refs_6_.refs_9_.refs_5_), channel_id=1, source_target_pairs={{0,16},{8,24},{16,0},{24,8},{1,17},{9,25},{17,1},{25,9},{2,18},{10... | collective-permute-start | bytes 3145736 | tf_op jit(solution)/shard_map/ppermute | solution.py:533
  6.5 43.3 %collective-permute-start.7 = (bf16[4,256,512]{2,1,0:T(8,128)(2,1)S(1)}, bf16[4,256,512]{2,1,0:T(8,128)(2,1)}, u32[]{:S(2)}, u32[]{:S(2)}) collective-permute-start(bf16[4,256,512]{2,1,0:T(8,128)(2,1)S(1)} %pad_maximum_fusion.refs_6_.refs_9_.refs_5_), channel_id=1, source_target_pairs={{0,8},{8,0},{16,24},{24,16},{1,9},{9,1},{17,25},{25,17},{2,10},{10... | collective-permute-start | bytes 3145736 | tf_op jit(solution)/shard_map/ppermute | solution.py:537
  10.8 26.1 %collective-permute-start.4 = (bf16[4,256,512]{2,1,0:T(8,128)(2,1)S(1)}, bf16[4,256,512]{2,1,0:T(8,128)(2,1)S(1)}, u32[]{:S(2)}, u32[]{:S(2)}) collective-permute-start(bf16[4,256,512]{2,1,0:T(8,128)(2,1)S(1)} %pad_maximum_fusion.refs_6_.refs_9_.refs_5_), channel_id=1, source_target_pairs={{0,4},{4,0},{1,5},{5,1},{2,6},{6,2},{3,7},{7,3},{8,12},{12,8},{9,1... | collective-permute-start | bytes 3145736 | tf_op jit(solution)/shard_map/ppermute | solution.py:541
  62.8 49.2 %collective-permute-start.13 = (bf16[3,256,1408]{2,1,0:T(8,128)(2,1)}, bf16[3,256,1408]{2,1,0:T(8,128)(2,1)}, u32[]{:S(2)}, u32[]{:S(2)}) collective-permute-start(bf16[3,256,1408]{2,1,0:T(8,128)(2,1)} %pack.2.refs_2_.refs_4_), channel_id=1, source_target_pairs={{0,16},{8,24},{16,0},{24,8},{1,17},{9,25},{17,1},{25,9},{2,18},{10... | collective-permute-start | bytes 6488072 | tf_op jit(solution)/shard_map/ppermute | solution.py:533
  74.4 50.3 %collective-permute-start.14 = (bf16[3,256,1408]{2,1,0:T(8,128)(2,1)}, bf16[3,256,1408]{2,1,0:T(8,128)(2,1)}, u32[]{:S(2)}, u32[]{:S(2)}) collective-permute-start(bf16[3,256,1408]{2,1,0:T(8,128)(2,1)} %pack.2.refs_2_.refs_4_), channel_id=1, source_target_pairs={{0,4},{4,0},{1,5},{5,1},{2,6},{6,2},{3,7},{7,3},{8,12},{12,8},{9,1... | collective-permute-start | bytes 6488072 | tf_op jit(solution)/shard_map/ppermute | solution.py:541
  85.9 29.9 %all-to-all-start = ((bf16[4,64,2048]{2,1,0:T(8,128)(2,1)}), bf16[4,64,2048]{2,1,0:T(8,128)(2,1)S(1)}, u32[]{:S(2)}, u32[]{:S(2)}) async-start(bf16[4,64,2048]{2,1,0:T(8,128)(2,1)} %bitcast.141), calls=%async_computation | async-start | bytes 2097152 | tf_op jit(solution)/shard_map/all_to_all | solution.py:643
  118.8 34.4 %collective-permute-start.18 = (bf16[3,256,1408]{2,1,0:T(8,128)(2,1)}, bf16[3,256,1408]{2,1,0:T(8,128)(2,1)}, u32[]{:S(2)}, u32[]{:S(2)}) collective-permute-start(bf16[3,256,1408]{2,1,0:T(8,128)(2,1)} %collective-permute-done.13.refs_3_.refs_5_), channel_id=1, source_target_pairs={{0,8},{8,0},{16,24},{24,16},{1,9},{9,1},{17,25},{25,17},{2,10},{10... | collective-permute-start | bytes 6488072 | tf_op jit(solution)/shard_map/ppermute | solution.py:537
  118.9 36.0 %collective-permute-start.17 = (bf16[3,256,1408]{2,1,0:T(8,128)(2,1)}, bf16[3,256,1408]{2,1,0:T(8,128)(2,1)}, u32[]{:S(2)}, u32[]{:S(2)}) collective-permute-start(bf16[3,256,1408]{2,1,0:T(8,128)(2,1)} %pack.2.refs_2_.refs_4_), channel_id=1, source_target_pairs={{0,8},{8,0},{16,24},{24,16},{1,9},{9,1},{17,25},{25,17},{2,10},{10... | collective-permute-start | bytes 6488072 | tf_op jit(solution)/shard_map/ppermute | solution.py:537
  119.4 30.9 %all-to-all-start.1 = ((bf16[4,64,2048]{2,1,0:T(8,128)(2,1)}), bf16[4,64,2048]{2,1,0:T(8,128)(2,1)S(1)}, u32[]{:S(2)}, u32[]{:S(2)}) async-start(bf16[4,64,2048]{2,1,0:T(8,128)(2,1)} %get-tuple-element.186), calls=%async_computation.1 | async-start | bytes 2097152 | tf_op jit(solution)/shard_map/all_to_all | solution.py:647
  124.2 26.0 %collective-permute-start.16 = (bf16[3,128,1408]{2,1,0:T(8,128)(2,1)S(1)}, bf16[3,128,1408]{2,1,0:T(8,128)(2,1)}, u32[]{:S(2)}, u32[]{:S(2)}) collective-permute-start(bf16[3,128,1408]{2,1,0:T(8,128)(2,1)S(1)} %slice.204), channel_id=1, source_target_pairs={{0,4},{4,0},{1,5},{5,1},{2,6},{6,2},{3,7},{7,3},{8,12},{12,8},{9,1... | collective-permute-start | bytes 3244040 | tf_op jit(solution)/shard_map/ppermute | solution.py:541
  126.9 25.9 %collective-permute-start.15 = (bf16[3,128,1408]{2,1,0:T(8,128)(2,1)}, bf16[3,128,1408]{2,1,0:T(8,128)(2,1)}, u32[]{:S(2)}, u32[]{:S(2)}) collective-permute-start(bf16[3,128,1408]{2,1,0:T(8,128)(2,1)} %slice.203), channel_id=1, source_target_pairs={{0,16},{8,24},{16,0},{24,8},{1,17},{9,25},{17,1},{25,9},{2,18},{10... | collective-permute-start | bytes 3244040 | tf_op jit(solution)/shard_map/ppermute | solution.py:533
  127.5 28.5 %collective-permute-start.19 = (bf16[3,256,1408]{2,1,0:T(8,128)(2,1)}, bf16[3,256,1408]{2,1,0:T(8,128)(2,1)}, u32[]{:S(2)}, u32[]{:S(2)}) collective-permute-start(bf16[3,256,1408]{2,1,0:T(8,128)(2,1)} %collective-permute-done.14.refs_4_.refs_6_), channel_id=1, source_target_pairs={{0,8},{8,0},{16,24},{24,16},{1,9},{9,1},{17,25},{25,17},{2,10},{10... | collective-permute-start | bytes 6488072 | tf_op jit(solution)/shard_map/ppermute | solution.py:537
  153.2 25.7 %collective-permute-start.22 = (bf16[4,256,512]{2,1,0:T(8,128)(2,1)S(1)}, bf16[4,256,512]{2,1,0:T(8,128)(2,1)}, u32[]{:S(2)}, u32[]{:S(2)}) collective-permute-start(bf16[4,256,512]{2,1,0:T(8,128)(2,1)S(1)} %pad_maximum_fusion.1.refs_4_.refs_6_.refs_9_.refs_5_), channel_id=1, source_target_pairs={{0,4},{4,0},{1,5},{5,1},{2,6},{6,2},{3,7},{7,3},{8,12},{12,8},{9,1... | collective-permute-start | bytes 3145736 | tf_op jit(solution)/shard_map/ppermute | solution.py:541
  154.9 25.4 %collective-permute-start.24 = (bf16[4,256,512]{2,1,0:T(8,128)(2,1)S(1)}, bf16[4,256,512]{2,1,0:T(8,128)(2,1)}, u32[]{:S(2)}, u32[]{:S(2)}) collective-permute-start(bf16[4,256,512]{2,1,0:T(8,128)(2,1)S(1)} %pad_maximum_fusion.1.refs_4_.refs_6_.refs_9_.refs_5_), channel_id=1, source_target_pairs={{0,16},{8,24},{16,0},{24,8},{1,17},{9,25},{17,1},{25,9},{2,18},{10... | collective-permute-start | bytes 3145736 | tf_op jit(solution)/shard_map/ppermute | solution.py:533
  167.3 32.2 %all-to-all-start.2 = ((bf16[4,64,2048]{2,1,0:T(8,128)(2,1)}), bf16[4,64,2048]{2,1,0:T(8,128)(2,1)S(1)}, u32[]{:S(2)}, u32[]{:S(2)}) async-start(bf16[4,64,2048]{2,1,0:T(8,128)(2,1)} %bitcast.138), calls=%async_computation.2 | async-start | bytes 2097152 | tf_op jit(solution)/shard_map/all_to_all | solution.py:643
  202.6 38.2 %all-to-all-start.3 = ((bf16[4,64,2048]{2,1,0:T(8,128)(2,1)}), bf16[4,64,2048]{2,1,0:T(8,128)(2,1)S(1)}, u32[]{:S(2)}, u32[]{:S(2)}) async-start(bf16[4,64,2048]{2,1,0:T(8,128)(2,1)} %get-tuple-element.206), calls=%async_computation.3 | async-start | bytes 2097152 | tf_op jit(solution)/shard_map/all_to_all | solution.py:647
  207.5 32.8 %collective-permute-start.30 = (bf16[2,256,1408]{2,1,0:T(8,128)(2,1)}, bf16[2,256,1408]{2,1,0:T(8,128)(2,1)}, u32[]{:S(2)}, u32[]{:S(2)}) collective-permute-start(bf16[2,256,1408]{2,1,0:T(8,128)(2,1)} %get-tuple-element.221.refs_3_), channel_id=1, source_target_pairs={{0,4},{4,0},{1,5},{5,1},{2,6},{6,2},{3,7},{7,3},{8,12},{12,8},{9,1... | collective-permute-start | bytes 4325384 | tf_op jit(solution)/shard_map/ppermute | solution.py:541
  208.7 32.1 %collective-permute-start.29 = (bf16[2,256,1408]{2,1,0:T(8,128)(2,1)}, bf16[2,256,1408]{2,1,0:T(8,128)(2,1)}, u32[]{:S(2)}, u32[]{:S(2)}) collective-permute-start(bf16[2,256,1408]{2,1,0:T(8,128)(2,1)} %get-tuple-element.221.refs_3_), channel_id=1, source_target_pairs={{0,16},{8,24},{16,0},{24,8},{1,17},{9,25},{17,1},{25,9},{2,18},{10... | collective-permute-start | bytes 4325384 | tf_op jit(solution)/shard_map/ppermute | solution.py:533
  209.3 31.6 %collective-permute-start.32 = (bf16[4,128,512]{2,1,0:T(8,128)(2,1)S(1)}, bf16[4,128,512]{2,1,0:T(8,128)(2,1)}, u32[]{:S(2)}, u32[]{:S(2)}) collective-permute-start(bf16[4,128,512]{2,1,0:T(8,128)(2,1)S(1)} %copy-done.13), channel_id=1, source_target_pairs={{0,8},{8,0},{16,24},{24,16},{1,9},{9,1},{17,25},{25,17},{2,10},{10... | collective-permute-start | bytes 1572872 | tf_op jit(solution)/shard_map/ppermute | solution.py:537
  209.3 31.6 %collective-permute-start.31 = (bf16[4,128,512]{2,1,0:T(8,128)(2,1)S(1)}, bf16[4,128,512]{2,1,0:T(8,128)(2,1)}, u32[]{:S(2)}, u32[]{:S(2)}) collective-permute-start(bf16[4,128,512]{2,1,0:T(8,128)(2,1)S(1)} %copy-done.15), channel_id=1, source_target_pairs={{0,8},{8,0},{16,24},{24,16},{1,9},{9,1},{17,25},{25,17},{2,10},{10... | collective-permute-start | bytes 1572872 | tf_op jit(solution)/shard_map/ppermute | solution.py:537
  269.4 27.5 %all-to-all-start.4 = ((bf16[4,64,2048]{2,1,0:T(8,128)(2,1)}), bf16[4,64,2048]{2,1,0:T(8,128)(2,1)S(1)}, u32[]{:S(2)}, u32[]{:S(2)}) async-start(bf16[4,64,2048]{2,1,0:T(8,128)(2,1)} %bitcast.140), calls=%async_computation.4 | async-start | bytes 2097152 | tf_op jit(solution)/shard_map/all_to_all | solution.py:643
  279.1 26.1 %collective-permute-start.37 = (bf16[2,128,1408]{2,1,0:T(8,128)(2,1)}, bf16[2,128,1408]{2,1,0:T(8,128)(2,1)}, u32[]{:S(2)}, u32[]{:S(2)}) collective-permute-start(bf16[2,128,1408]{2,1,0:T(8,128)(2,1)} %slice.212), channel_id=1, source_target_pairs={{0,4},{4,0},{1,5},{5,1},{2,6},{6,2},{3,7},{7,3},{8,12},{12,8},{9,1... | collective-permute-start | bytes 2162696 | tf_op jit(solution)/shard_map/ppermute | solution.py:541
  279.1 45.2 %collective-permute-start.40 = (bf16[2,256,1408]{2,1,0:T(8,128)(2,1)}, bf16[2,256,1408]{2,1,0:T(8,128)(2,1)}, u32[]{:S(2)}, u32[]{:S(2)}) collective-permute-start(bf16[2,256,1408]{2,1,0:T(8,128)(2,1)} %collective-permute-done.30.refs_5_), channel_id=1, source_target_pairs={{0,8},{8,0},{16,24},{24,16},{1,9},{9,1},{17,25},{25,17},{2,10},{10... | collective-permute-start | bytes 4325384 | tf_op jit(solution)/shard_map/ppermute | solution.py:537
  279.1 46.9 %collective-permute-start.39 = (bf16[2,256,1408]{2,1,0:T(8,128)(2,1)}, bf16[2,256,1408]{2,1,0:T(8,128)(2,1)}, u32[]{:S(2)}, u32[]{:S(2)}) collective-permute-start(bf16[2,256,1408]{2,1,0:T(8,128)(2,1)} %collective-permute-done.29.refs_4_), channel_id=1, source_target_pairs={{0,8},{8,0},{16,24},{24,16},{1,9},{9,1},{17,25},{25,17},{2,10},{10... | collective-permute-start | bytes 4325384 | tf_op jit(solution)/shard_map/ppermute | solution.py:537
  289.1 36.9 %collective-permute-start.38 = (bf16[2,256,1408]{2,1,0:T(8,128)(2,1)}, bf16[2,256,1408]{2,1,0:T(8,128)(2,1)}, u32[]{:S(2)}, u32[]{:S(2)}) collective-permute-start(bf16[2,256,1408]{2,1,0:T(8,128)(2,1)} %get-tuple-element.221.refs_3_), channel_id=1, source_target_pairs={{0,8},{8,0},{16,24},{24,16},{1,9},{9,1},{17,25},{25,17},{2,10},{10... | collective-permute-start | bytes 4325384 | tf_op jit(solution)/shard_map/ppermute | solution.py:537
  294.5 27.8 %collective-permute-start.35 = (bf16[256,2048]{1,0:T(8,128)(2,1)}, bf16[256,2048]{1,0:T(8,128)(2,1)}, u32[]{:S(2)}, u32[]{:S(2)}) collective-permute-start(bf16[256,2048]{1,0:T(8,128)(2,1)} %bitcast.53.refs_2_), channel_id=1, source_target_pairs={{0,8},{8,0},{16,24},{24,16},{1,9},{9,1},{17,25},{25,17},{2,10},{10... | collective-permute-start | bytes 3145736 | tf_op jit(solution)/shard_map/ppermute | solution.py:537
  299.9 35.7 %all-to-all-start.5 = ((bf16[4,64,2048]{2,1,0:T(8,128)(2,1)}), bf16[4,64,2048]{2,1,0:T(8,128)(2,1)S(1)}, u32[]{:S(2)}, u32[]{:S(2)}) async-start(bf16[4,64,2048]{2,1,0:T(8,128)(2,1)} %get-tuple-element.217), calls=%async_computation.5 | async-start | bytes 2097152 | tf_op jit(solution)/shard_map/all_to_all | solution.py:647
  355.9 31.1 %all-to-all-start.6 = ((bf16[4,64,2048]{2,1,0:T(8,128)(2,1)}), bf16[4,64,2048]{2,1,0:T(8,128)(2,1)}, u32[]{:S(2)}, u32[]{:S(2)}) async-start(bf16[4,64,2048]{2,1,0:T(8,128)(2,1)} %bitcast.137), calls=%async_computation.6 | async-start | bytes 2097152 | tf_op jit(solution)/shard_map/all_to_all | solution.py:643
  390.8 28.8 %all-to-all-start.7 = ((bf16[4,64,2048]{2,1,0:T(8,128)(2,1)}), bf16[4,64,2048]{2,1,0:T(8,128)(2,1)S(1)}, u32[]{:S(2)}, u32[]{:S(2)}) async-start(bf16[4,64,2048]{2,1,0:T(8,128)(2,1)} %get-tuple-element.242), calls=%async_computation.7 | async-start | bytes 2097152 | tf_op jit(solution)/shard_map/all_to_all | solution.py:647
  394.3 48.4 %collective-permute-start.56 = (bf16[2,3,128,1408]{3,2,1,0:T(8,128)(2,1)}, bf16[2,3,128,1408]{3,2,1,0:T(8,128)(2,1)}, u32[]{:S(2)}, u32[]{:S(2)}) collective-permute-start(bf16[2,3,128,1408]{3,2,1,0:T(8,128)(2,1)} %get-tuple-element.251), channel_id=1, source_target_pairs={{0,16},{8,24},{16,0},{24,8},{1,17},{9,25},{17,1},{25,9},{2,18},{10... | collective-permute-start | bytes 6488072 | tf_op jit(solution)/shard_map/ppermute | solution.py:533
  419.6 29.5 %all-to-all-start.8 = ((bf16[4,64,2048]{2,1,0:T(8,128)(2,1)}), bf16[4,64,2048]{2,1,0:T(8,128)(2,1)}, u32[]{:S(2)}, u32[]{:S(2)}) async-start(bf16[4,64,2048]{2,1,0:T(8,128)(2,1)} %bitcast.134), calls=%async_computation.8 | async-start | bytes 2097152 | tf_op jit(solution)/shard_map/all_to_all | solution.py:643
  459.2 30.3 %all-to-all-start.9 = ((bf16[4,64,2048]{2,1,0:T(8,128)(2,1)}), bf16[4,64,2048]{2,1,0:T(8,128)(2,1)S(1)}, u32[]{:S(2)}, u32[]{:S(2)}) async-start(bf16[4,64,2048]{2,1,0:T(8,128)(2,1)} %bitcast.139), calls=%async_computation.9 | async-start | bytes 2097152 | tf_op jit(solution)/shard_map/all_to_all | solution.py:643
  464.4 48.2 %collective-permute-start.62 = (bf16[2,3,128,1408]{3,2,1,0:T(8,128)(2,1)}, bf16[2,3,128,1408]{3,2,1,0:T(8,128)(2,1)}, u32[]{:S(2)}, u32[]{:S(2)}) collective-permute-start(bf16[2,3,128,1408]{3,2,1,0:T(8,128)(2,1)} %get-tuple-element.273), channel_id=1, source_target_pairs={{0,4},{4,0},{1,5},{5,1},{2,6},{6,2},{3,7},{7,3},{8,12},{12,8},{9,1... | collective-permute-start | bytes 6488072 | tf_op jit(solution)/shard_map/ppermute | solution.py:541
  492.9 29.0 %all-to-all-start.10 = ((bf16[4,64,2048]{2,1,0:T(8,128)(2,1)}), bf16[4,64,2048]{2,1,0:T(8,128)(2,1)S(1)}, u32[]{:S(2)}, u32[]{:S(2)}) async-start(bf16[4,64,2048]{2,1,0:T(8,128)(2,1)} %get-tuple-element.267), calls=%async_computation.10 | async-start | bytes 2097152 | tf_op jit(solution)/shard_map/all_to_all | solution.py:647
  536.0 36.8 %all-to-all-start.11 = ((bf16[4,64,2048]{2,1,0:T(8,128)(2,1)}), bf16[4,64,2048]{2,1,0:T(8,128)(2,1)S(1)}, u32[]{:S(2)}, u32[]{:S(2)}) async-start(bf16[4,64,2048]{2,1,0:T(8,128)(2,1)} %bitcast.136), calls=%async_computation.11 | async-start | bytes 2097152 | tf_op jit(solution)/shard_map/all_to_all | solution.py:643
  542.7 25.3 %collective-permute-start.67 = (bf16[2,4,128,512]{3,2,1,0:T(8,128)(2,1)}, bf16[2,4,128,512]{3,2,1,0:T(8,128)(2,1)S(1)}, u32[]{:S(2)}, u32[]{:S(2)}) collective-permute-start(bf16[2,4,128,512]{3,2,1,0:T(8,128)(2,1)} %get-tuple-element.289), channel_id=1, source_target_pairs={{0,4},{4,0},{1,5},{5,1},{2,6},{6,2},{3,7},{7,3},{8,12},{12,8},{9,1... | collective-permute-start | bytes 3145736 | tf_op jit(solution)/shard_map/ppermute | solution.py:541
  543.6 25.1 %collective-permute-start.68 = (bf16[2,4,128,512]{3,2,1,0:T(8,128)(2,1)}, bf16[2,4,128,512]{3,2,1,0:T(8,128)(2,1)S(1)}, u32[]{:S(2)}, u32[]{:S(2)}) collective-permute-start(bf16[2,4,128,512]{3,2,1,0:T(8,128)(2,1)} %get-tuple-element.290), channel_id=1, source_target_pairs={{0,16},{8,24},{16,0},{24,8},{1,17},{9,25},{17,1},{25,9},{2,18},{10... | collective-permute-start | bytes 3145736 | tf_op jit(solution)/shard_map/ppermute | solution.py:533
  576.3 29.9 %all-to-all-start.12 = ((bf16[4,64,2048]{2,1,0:T(8,128)(2,1)}), bf16[4,64,2048]{2,1,0:T(8,128)(2,1)S(1)}, u32[]{:S(2)}, u32[]{:S(2)}) async-start(bf16[4,64,2048]{2,1,0:T(8,128)(2,1)} %get-tuple-element.293), calls=%async_computation.12 | async-start | bytes 2097152 | tf_op jit(solution)/shard_map/all_to_all | solution.py:647
  581.4 47.9 %collective-permute-start.69 = (bf16[2,3,128,1408]{3,2,1,0:T(8,128)(2,1)}, bf16[2,3,128,1408]{3,2,1,0:T(8,128)(2,1)}, u32[]{:S(2)}, u32[]{:S(2)}) collective-permute-start(bf16[2,3,128,1408]{3,2,1,0:T(8,128)(2,1)} %get-tuple-element.302), channel_id=1, source_target_pairs={{0,4},{4,0},{1,5},{5,1},{2,6},{6,2},{3,7},{7,3},{8,12},{12,8},{9,1... | collective-permute-start | bytes 6488072 | tf_op jit(solution)/shard_map/ppermute | solution.py:541
  582.0 48.6 %collective-permute-start.70 = (bf16[2,3,128,1408]{3,2,1,0:T(8,128)(2,1)}, bf16[2,3,128,1408]{3,2,1,0:T(8,128)(2,1)}, u32[]{:S(2)}, u32[]{:S(2)}) collective-permute-start(bf16[2,3,128,1408]{3,2,1,0:T(8,128)(2,1)} %get-tuple-element.303), channel_id=1, source_target_pairs={{0,16},{8,24},{16,0},{24,8},{1,17},{9,25},{17,1},{25,9},{2,18},{10... | collective-permute-start | bytes 6488072 | tf_op jit(solution)/shard_map/ppermute | solution.py:533
  606.2 33.2 %all-to-all-start.13 = ((bf16[4,64,2048]{2,1,0:T(8,128)(2,1)}), bf16[4,64,2048]{2,1,0:T(8,128)(2,1)S(1)}, u32[]{:S(2)}, u32[]{:S(2)}) async-start(bf16[4,64,2048]{2,1,0:T(8,128)(2,1)} %sum.1), calls=%async_computation.13 | async-start | bytes 2097152 | tf_op jit(solution)/shard_map/all_to_all | solution.py:647
  634.6 25.9 %collective-permute-start.75 = (bf16[3,128,1408]{2,1,0:T(8,128)(2,1)}, bf16[3,128,1408]{2,1,0:T(8,128)(2,1)S(1)}, u32[]{:S(2)}, u32[]{:S(2)}) collective-permute-start(bf16[3,128,1408]{2,1,0:T(8,128)(2,1)} %get-tuple-element.304), channel_id=1, source_target_pairs={{0,16},{8,24},{16,0},{24,8},{1,17},{9,25},{17,1},{25,9},{2,18},{10... | collective-permute-start | bytes 3244040 | tf_op jit(solution)/shard_map/ppermute | solution.py:533
  635.0 31.2 %collective-permute-start.76 = (bf16[3,128,1408]{2,1,0:T(8,128)(2,1)}, bf16[3,128,1408]{2,1,0:T(8,128)(2,1)}, u32[]{:S(2)}, u32[]{:S(2)}) collective-permute-start(bf16[3,128,1408]{2,1,0:T(8,128)(2,1)} %get-tuple-element.316), channel_id=1, source_target_pairs={{0,4},{4,0},{1,5},{5,1},{2,6},{6,2},{3,7},{7,3},{8,12},{12,8},{9,1... | collective-permute-start | bytes 3244040 | tf_op jit(solution)/shard_map/ppermute | solution.py:541
  666.3 28.8 %collective-permute-start.80 = (bf16[4,128,512]{2,1,0:T(8,128)(2,1)}, bf16[4,128,512]{2,1,0:T(8,128)(2,1)}, u32[]{:S(2)}, u32[]{:S(2)}) collective-permute-start(bf16[4,128,512]{2,1,0:T(8,128)(2,1)} %get-tuple-element.336), channel_id=1, source_target_pairs={{0,4},{4,0},{1,5},{5,1},{2,6},{6,2},{3,7},{7,3},{8,12},{12,8},{9,1... | collective-permute-start | bytes 1572872 | tf_op jit(solution)/shard_map/ppermute | solution.py:541
  666.3 28.7 %collective-permute-start.79 = (bf16[4,128,512]{2,1,0:T(8,128)(2,1)}, bf16[4,128,512]{2,1,0:T(8,128)(2,1)}, u32[]{:S(2)}, u32[]{:S(2)}) collective-permute-start(bf16[4,128,512]{2,1,0:T(8,128)(2,1)} %get-tuple-element.334), channel_id=1, source_target_pairs={{0,16},{8,24},{16,0},{24,8},{1,17},{9,25},{17,1},{25,9},{2,18},{10... | collective-permute-start | bytes 1572872 | tf_op jit(solution)/shard_map/ppermute | solution.py:533
  676.3 28.6 %collective-permute-start.81 = (bf16[2,4,128,512]{3,2,1,0:T(8,128)(2,1)}, bf16[2,4,128,512]{3,2,1,0:T(8,128)(2,1)S(1)}, u32[]{:S(2)}, u32[]{:S(2)}) collective-permute-start(bf16[2,4,128,512]{3,2,1,0:T(8,128)(2,1)} %get-tuple-element.340), channel_id=1, source_target_pairs={{0,4},{4,0},{1,5},{5,1},{2,6},{6,2},{3,7},{7,3},{8,12},{12,8},{9,1... | collective-permute-start | bytes 3145736 | tf_op jit(solution)/shard_map/ppermute | solution.py:541
  676.6 28.3 %collective-permute-start.82 = (bf16[2,4,128,512]{3,2,1,0:T(8,128)(2,1)}, bf16[2,4,128,512]{3,2,1,0:T(8,128)(2,1)S(1)}, u32[]{:S(2)}, u32[]{:S(2)}) collective-permute-start(bf16[2,4,128,512]{3,2,1,0:T(8,128)(2,1)} %get-tuple-element.341), channel_id=1, source_target_pairs={{0,16},{8,24},{16,0},{24,8},{1,17},{9,25},{17,1},{25,9},{2,18},{10... | collective-permute-start | bytes 3145736 | tf_op jit(solution)/shard_map/ppermute | solution.py:533
  683.7 46.0 %all-to-all-start.15 = ((bf16[4,64,2048]{2,1,0:T(8,128)(2,1)}), bf16[4,64,2048]{2,1,0:T(8,128)(2,1)S(1)}, u32[]{:S(2)}, u32[]{:S(2)}) async-start(bf16[4,64,2048]{2,1,0:T(8,128)(2,1)} %get-tuple-element.321), calls=%async_computation.15 | async-start | bytes 2097152 | tf_op jit(solution)/shard_map/all_to_all | solution.py:647
  (123 other events, 1621.4 us)

commit v4 on v3

--- a/solution.py
+++ b/solution.py
@@ -22,6 +22,9 @@
     "pack": 7.0,
     "qkv": 8.5,
     "attend": 8.0,
+    "key_value": 6.5,
+    "attend_own": 5.5,
+    "attend_other": 5.5,
     "norm": 3.0,
     "mlp": 11.5,
     "mlp_back": 14.0,
@@ -255,6 +258,68 @@
     io.put(0)
 
 
+def key_value_body(has_norm, io):
+    kv = io.outs[0]
+    if has_norm:
+        first_in = io.outs[1]
+        n, _ = normalized(io.get(4)[...].astype(F32))
+        first_in[...] = (n * io.get(2)[...] + io.get(3)[...]).astype(BF)
+        io.put(1)
+    else:
+        first_in = io.get(2)
+    bias, tables = io.get(0), io.get(1)
+    keys = mm(first_in[...], io.weight(0)[...], NN) + bias[1:2, :]
+    kv[0] = turn_wide(keys, tables, 1.0).astype(BF)
+    kv[1] = (mm(first_in[...], io.weight(1)[...], NN) + bias[2:3, :]).astype(BF)
+    io.put(0)
+
+
+def attend_own_body(io):
+    queries, sums, stats = io.outs
+    part = mm(io.get(2)[...], io.weight(0)[...], NN) + io.get(0)[0:1, :]
+    queries[...] = turn_wide(part, io.get(1), 1.0).astype(BF)
+    io.put(0)
+    kv, mask = io.get(3), io.get(4)
+    heads = queries.shape[1] // HD
+    for head in range(heads):
+        span = slice(head * HD, (head + 1) * HD)
+        scores = mm(kv[0, :, span], queries[:, span], NT) * SCALE + mask[...]
+        top = jnp.max(scores, axis=0, keepdims=True)
+        exps = jnp.exp(scores - top)
+        stats[head : head + 1, :] = top
+        stats[heads + head : heads + head + 1, :] = jnp.sum(exps, axis=0, keepdims=True)
+        sums[span, :] = mm(kv[1, :, span], exps.astype(BF), TN)
+    io.put(1)
+    io.put(2)
+
+
+def attend_other_body(io):
+    queries, kv, mask, sums, stats = (io.get(at) for at in range(5))
+    mixed, log_total, part = io.outs
+    heads = queries.shape[1] // HD
+    pair = []
+    for head in range(heads):
+        span = slice(head * HD, (head + 1) * HD)
+        scores = mm(kv[0, :, span], queries[:, span], NT) * SCALE + mask[...]
+        own_top = stats[head : head + 1, :]
+        top = jnp.maximum(own_top, jnp.max(scores, axis=0, keepdims=True))
+        exps = jnp.exp(scores - top)
+        scale = jnp.exp(own_top - top)
+        total = stats[heads + head : heads + head + 1, :] * scale
+        total = total + jnp.sum(exps, axis=0, keepdims=True)
+        result = sums[span, :] * scale + mm(kv[1, :, span], exps.astype(BF), TN)
+        log_total[head : head + 1, :] = top + jnp.log(total)
+        pair.append(result * (1.0 / total))
+        if len(pair) == LANES // HD:
+            wide = slice((head + 1) * HD - LANES, (head + 1) * HD)
+            mixed[:, wide] = jnp.concatenate(pair, axis=0).T.astype(BF)
+            pair = []
+    io.put(0)
+    io.put(1)
+    part[...] = mm(mixed[...], io.weight(0)[...], NT).astype(BF)
+    io.put(2)
+
+
 def attend_body(n_blocks, io):
     queries = io.get(0)
     kvs = [io.get(1 + at) for at in range(n_blocks)]
@@ -852,41 +917,67 @@
         else:
             attn_pieces, mlp_pieces = (gather_whole(shard) for shard in shards[layer])
             mlp_slots = [slot(mlp_pieces, index) for index in range(3)]
-        outs = [headed, shape((2, rows, heads_width), BF)]
+        kv_shape = shape((2, rows, heads_width), BF)
         if layer == 0:
             args = [biases[0], tables, gains[0, 0][None], shifts[0, 0][None], tokens[0]]
             if fast:
                 args[0] = after(args[0], mlp_g.shard)
-            outs.append(wide)
         else:
             args = [biases[layer], tables, Free(first_in)]
-        queries, kv, *normed = kernel(
-            functools.partial(qkv_body, layer == 0),
-            "qkv",
-            spots,
-            args,
-            outs,
-            [slot(attn_pieces, index) for index in (1, 2, 0)],
-        )
+        if fast:
+            kv, *normed = kernel(
+                functools.partial(key_value_body, layer == 0),
+                "key_value",
+                spots,
+                args,
+                [kv_shape] + ([wide] if layer == 0 else []),
+                [slot(attn_pieces, index) for index in (1, 2)],
+            )
+        else:
+            queries, kv, *normed = kernel(
+                functools.partial(qkv_body, layer == 0),
+                "qkv",
+                spots,
+                args,
+                [headed, kv_shape] + ([wide] if layer == 0 else []),
+                [slot(attn_pieces, index) for index in (1, 2, 0)],
+            )
         if layer == 0:
             first_in = normed[0]
+        attended = [headed, shape((heads, rows), F32), wide]
         if fast:
             prev = lax.ppermute(kv, "ctx", [(0, 1)])
             kv_blocks = [prev, kv]
+            queries, value_sums, stats = kernel(
+                attend_own_body,
+                "attend_own",
+                spots,
+                [biases[layer], tables, Free(first_in), kv, masks[1]],
+                [headed, shape((heads_width, rows), F32), shape((2 * heads, rows), F32)],
+                [slot(attn_pieces, 0)],
+            )
             if layer == 0:
-                mlp_g.near_y((prev,))
+                mlp_g.near_y((prev, queries))
             else:
-                down_g.near_y((prev,))
+                down_g.near_y((prev, queries))
+            mixed, log_total, part = kernel(
+                attend_other_body,
+                "attend_other",
+                spots,
+                [queries, after(prev, queries), masks[0], value_sums, stats],
+                attended,
+                [slot(attn_pieces, 3)],
+            )
         else:
             kv_blocks = [lax.all_gather(kv, "ctx", axis=1, tiled=True)]
-        mixed, log_total, part = kernel(
-            functools.partial(attend_body, n_blocks),
-            "attend",
-            spots,
-            [queries] + kv_blocks + masks,
-            [headed, shape((heads, rows), F32), wide],
-            [slot(attn_pieces, 3)],
-        )
+            mixed, log_total, part = kernel(
+                functools.partial(attend_body, n_blocks),
+                "attend",
+                spots,
+                [queries] + kv_blocks + masks,
+                attended,
+                [slot(attn_pieces, 3)],
+            )
         terms = tensor_scatter(part)
         if fast and layer == 0:
             terms = after(terms, mlp_g.from_x)
@@ -947,7 +1038,7 @@
             attn_g.near(sent[:1], sent[1:])
             attn_g.swap(part)
             attn_g.far("both", (part,), (part,))
-            gu_g.near((attn_g.from_x, part), (attn_g.from_y, part))
+            gu_g.near(sent[:1], sent[1:])
             down_g.near_x((gu_g.from_x,))
             terms = after(terms, gu_g.shard, *attn_g.pieces, *attn_g.peers)
         stream, normed = kernel(
@@ -998,8 +1089,7 @@
             if pending is not None:
                 mlp_pending[0] = after(mlp_pending[0], mlp_parts[0])
                 mlp_outs = mlp_finish(spots, mlp_outs, mlp_pending, layer + 1, layers)
-                attn_sums = add_received(spots, *pending, (mlp_outs[0],), "attn_add")
-                terms = after(terms, attn_sums[0])
+                terms = after(terms, mlp_outs[0], *pending[1])
             got_x = swap_x(to_x)
             got_y = None if late else swap_y(to_y)
         else:
@@ -1042,6 +1132,8 @@
                 mlp_sums = add_received(spots, mlp_parts, (got_x, got_y), (d_kvs[0],), "mlp_add")
                 own = after(own, mlp_sums[0])
                 if pending is not None:
+                    attn_sums = add_received(spots, *pending, (mlp_sums[0],), "attn_add")
+                    own = after(own, attn_sums[0])
                     attn_terms = send_second(*pending, attn_sums, (other[0],))
                 mlp_terms = send_second(mlp_parts, (got_x, got_y), mlp_sums, ())
             attn_peer = [swap_core(after(a, d_kvs[0])) for a in (first_in, d_attn)]

time: 742 us -> 729 us (0.982)
  waiting for transfers between devices: 323 us -> 299 us
  Pallas kernels: 223 us -> 232 us
    ppermute x2, waiting for transfers between devices: 20.4 us -> 4.2 us  [local(): prev = lax.ppermute(kv, 'ctx', [(0, 1)])]
    ppermute x20, waiting for transfers between devices: 64 us -> 54.6 us  [swap_x(): return lax.ppermute(array, 'fsdp', pairs_of('fsdp', 2))]
    pallas_call x29 -> x31, Pallas kernels: 189 us -> 197 us  [kernel(): pl.pallas_call(run, out_shape=[pltpu.HBM(out.shape, out.dtype) for out in...]
    all_to_all x8, waiting for transfers between devices: 33.2 us -> 41 us  [tensor_scatter(): return lax.all_to_all(blocks, 'tp', 0, 0, tiled=True)]
    unnamed x137 -> x133, local copies, waits for them, and re-layouts: 19.2 us -> 18.8 us
  transfers between devices with their start and end apart: 105 -> 105, of which waited for: 56 -> 59; matrix products, arithmetic and copies ran while one was open for 4% -> 4% of each run, Pallas kernels for 22% -> 26%
where the time goes in v4:
time: 729 us; the launch traced here: 720 us
  waiting for transfers between devices  299 us (41%)
  Pallas kernels  232 us (32%)
  starting transfers between devices  136 us (19%)
  local copies, waits for them, and re-layouts  42.2 us (6%)
  other arithmetic  8.55 us (1%)
    pallas_call x31, Pallas kernels, kernel(): pl.pallas_call(run, out_shape=[pltpu.HBM(out.shape, out.dtype) for out in...  197 us
    ppermute x20, waiting for transfers between devices, swap_y(): return lax.ppermute(array, 'ctx', pairs_of('ctx', 1))  127 us
    ppermute x20, waiting for transfers between devices, swap_x(): return lax.ppermute(array, 'fsdp', pairs_of('fsdp', 2))  54.6 us
    all_to_all x8, waiting for transfers between devices, tensor_gather(): return lax.all_to_all(copies, 'tp', 0, 0, tiled=True)  48.9 us
    all_to_all x8, waiting for transfers between devices, tensor_scatter(): return lax.all_to_all(blocks, 'tp', 0, 0, tiled=True)  41 us
    all_to_all x8, starting transfers between devices, tensor_scatter(): return lax.all_to_all(blocks, 'tp', 0, 0, tiled=True)  38.5 us
    pallas_call x4, Pallas kernels, weight_grads(): pl.pallas_call(functools.partial(weight_grad_body, counts, n_left, pairs)...  34.9 us
    all_to_all x8, starting transfers between devices, tensor_gather(): return lax.all_to_all(copies, 'tp', 0, 0, tiled=True)  32 us
  transfers between devices with their start and end apart: 105, of which 59 were waited for; matrix products, arithmetic and copies ran while one was open for 4% of the time, Pallas kernels for 26%

profile of v4, /device:TPU:0, one launch (start us, length us, event | category | flops | bytes accessed | tf_op | source)
XLA Modules:
  0.0 719.7 jit_solution(7111751524564599123)
XLA Ops:
  21.9 7.1 pack.2.refs_2_.refs_4_
  31.8 5.0 collective-permute-done.4.refs_8_.refs_11_.refs_7_
  37.4 9.5 %collective-permute-done.6.refs_10_.refs_13_.refs_9_ = bf16[4,128,512]{2,1,0:T(8,128)(2,1)} collective-permute-done((bf16[4,128,512]{2,1,0:T(8,128)(2,1)S(1)}, bf16[4,128,512]{2,1,0:T(8,128)(2,1)}, u32[]{:S(2)}, u32[]{:S(2)}) %collective-permute-start.6) | collective-permute-done | bytes 524320 | tf_op jit(solution)/shard_map/ppermute | solution.py:606
  50.6 7.1 key_value.2
  63.5 7.1 attend_own.2
  75.2 6.9 attend_other.2
  82.1 4.9 all-to-all-start
  88.7 10.9 %collective-permute-done.13.refs_3_.refs_5_ = bf16[3,256,1408]{2,1,0:T(8,128)(2,1)} collective-permute-done((bf16[3,256,1408]{2,1,0:T(8,128)(2,1)}, bf16[3,256,1408]{2,1,0:T(8,128)(2,1)}, u32[]{:S(2)}, u32[]{:S(2)}) %collective-permute-start.13) | collective-permute-done | bytes 2162720 | tf_op jit(solution)/shard_map/ppermute | solution.py:598
  99.6 12.4 %all-to-all-done.refs_1_ = bf16[4,64,2048]{2,1,0:T(8,128)(2,1)S(1)} async-done(((bf16[4,64,2048]{2,1,0:T(8,128)(2,1)}), bf16[4,64,2048]{2,1,0:T(8,128)(2,1)S(1)}, u32[]{:S(2)}, u32[]{:S(2)}) %all-to-all-start) | async-done | bytes 1048608 | tf_op jit(solution)/shard_map/all_to_all | solution.py:708
  125.1 21.3 %collective-permute-done.16.refs_6_.refs_8_ = bf16[3,128,1408]{2,1,0:T(8,128)(2,1)} collective-permute-done((bf16[3,128,1408]{2,1,0:T(8,128)(2,1)S(1)}, bf16[3,128,1408]{2,1,0:T(8,128)(2,1)}, u32[]{:S(2)}, u32[]{:S(2)}) %collective-permute-start.16) | collective-permute-done | bytes 1081376 | tf_op jit(solution)/shard_map/ppermute | solution.py:606
  151.7 11.3 %mlp.1 = (bf16[256,1408]{1,0:T(8,128)(2,1)}, bf16[256,1408]{1,0:T(8,128)(2,1)}, bf16[256,1408]{1,0:T(8,128)(2,1)}, bf16[256,2048]{1,0:T(8,128)(2,1)}) custom-call(s32[18]{0:T(128)S(1)} %stack.130.refs_0_, bf16[256,2048]{1,0:T(8,128)(2,1)S(1)} %bitcast.126, bf16[3,256,1408]{2,1,0:T(8,128)(2,1)} %pack.2.refs_2_.refs_4_, ...), custom_call_target="tpu_custom_call" | custom-call | bytes 34500000 | tf_op jit(solution)/shard_map/mlp/pallas_call | solution.py:194
  162.9 5.1 all-to-all-start.2
  168.1 6.6 collective-permute-done.22.refs_6_.refs_8_.refs_11_.refs_7_
  180.7 7.1 pack.3
  197.9 4.9 all-to-all-start.3
  206.1 29.0 %collective-permute-done.30.refs_5_ = bf16[2,256,1408]{2,1,0:T(8,128)(2,1)} collective-permute-done((bf16[2,256,1408]{2,1,0:T(8,128)(2,1)}, bf16[2,256,1408]{2,1,0:T(8,128)(2,1)}, u32[]{:S(2)}, u32[]{:S(2)}) %collective-permute-start.30) | collective-permute-done | bytes 1441824 | tf_op jit(solution)/shard_map/ppermute | solution.py:606
  236.1 5.2 key_value.3.refs_4_.refs_6_
  244.1 7.1 attend_own.3
  253.8 6.9 attend_other.3
  260.7 4.9 all-to-all-start.4
  272.2 7.7 %collective-permute-done.34.refs_14_ = bf16[1,256,1408]{2,1,0:T(8,128)(2,1)} collective-permute-done((bf16[1,256,1408]{2,1,0:T(8,128)(2,1)}, bf16[1,256,1408]{2,1,0:T(8,128)(2,1)}, u32[]{:S(2)}, u32[]{:S(2)}) %collective-permute-start.34) | collective-permute-done | bytes 720928 | tf_op jit(solution)/shard_map/ppermute | solution.py:598
  280.0 7.1 collective-permute-done.43.refs_15_
  299.9 15.0 %collective-permute-done.36.refs_6_ = bf16[2,128,1408]{2,1,0:T(8,128)(2,1)} collective-permute-done((bf16[2,128,1408]{2,1,0:T(8,128)(2,1)S(1)}, bf16[2,128,1408]{2,1,0:T(8,128)(2,1)}, u32[]{:S(2)}, u32[]{:S(2)}) %collective-permute-start.36) | collective-permute-done | bytes 720928 | tf_op jit(solution)/shard_map/ppermute | solution.py:598
  317.9 8.1 %collective-permute-done.45.refs_17_ = bf16[1,128,1408]{2,1,0:T(8,128)(2,1)S(1)} collective-permute-done((bf16[1,128,1408]{2,1,0:T(8,128)(2,1)S(1)}, bf16[1,128,1408]{2,1,0:T(8,128)(2,1)S(1)}, u32[]{:S(2)}, u32[]{:S(2)}) %collective-permute-start.45) | collective-permute-done | bytes 360480 | tf_op jit(solution)/shard_map/ppermute | solution.py:606
  332.4 16.1 %mlp_both.1 = (bf16[256,1408]{1,0:T(8,128)(2,1)}, bf16[256,2048]{1,0:T(8,128)(2,1)}, bf16[2,256,1408]{2,1,0:T(8,128)(2,1)}, bf16[256,2048]{1,0:T(8,128)(2,1)}) custom-call(s32[18]{0:T(128)S(1)} %stack.130.refs_0_, bf16[256,2048]{1,0:T(8,128)(2,1)S(1)} %bitcast.117, bf16[256,2048]{1,0:T(8,128)(2,1)} %bitcast.53.refs_2_, ...), custom_call_target="tpu_custom_call" | custom-call | bytes 54000000 | tf_op jit(solution)/shard_map/mlp_both/pallas_call | solution.py:194
  348.5 5.0 all-to-all-start.6
  361.8 10.6 %mlp_grads.2 = (bf16[2,3,128,1408]{3,2,1,0:T(8,128)(2,1)}, bf16[2,3,128,1408]{3,2,1,0:T(8,128)(2,1)}, bf16[2,3,128,1408]{3,2,1,0:T(8,128)(2,1)}, bf16[3,128,1408]{2,1,0:T(8,128)(2,1)}, bf16[3,128,1408]{2,1,0:T(8,128)(2,1)}) custom-call(s32[4]{0:T(128)S(1)} %pad_add_fusion.refs_0_, bf16[256,2048]{1,0:T(8,128)(2,1)} %bitcast.119, ...), custom_call_target="tpu_custom_call" | custom-call | bytes 31500000 | tf_op jit(solution)/shard_map/mlp_grads/pallas_call | solution.py:748
  372.4 7.2 all-to-all-done.6.refs_1_
  387.4 24.7 %all-to-all-done.7 = bf16[4,64,2048]{2,1,0:T(8,128)(2,1)S(1)} async-done(((bf16[4,64,2048]{2,1,0:T(8,128)(2,1)}), bf16[4,64,2048]{2,1,0:T(8,128)(2,1)S(1)}, u32[]{:S(2)}, u32[]{:S(2)}) %all-to-all-start.7) | async-done | bytes 1048608 | tf_op jit(solution)/shard_map/all_to_all | solution.py:712
  416.4 9.9 %attend_back.2 = (bf16[256,512]{1,0:T(8,128)(2,1)}, bf16[2,256,512]{2,1,0:T(8,128)(2,1)}, f32[2,256,512]{2,1,0:T(8,128)}) custom-call(s32[18]{0:T(128)S(1)} %stack.130.refs_0_, bf16[256,2048]{1,0:T(8,128)(2,1)S(1)} %bitcast.120, bf16[256,512]{1,0:T(8,128)(2,1)} %get-tuple-element.220.refs_1_.refs_2_, f32[8,256]{1,0:T(8,128)} %get-tuple-element.260.refs_3_, ...), custom_call_target="tpu_custom_call" | custom-call | bytes 30000000 | tf_op jit(solution)/shard_map/attend_back/pallas_call | solution.py:194
  428.6 6.8 collective-permute-done.56.refs_4_.refs_2_
  437.0 4.7 all-to-all-done.8.refs_1_
  443.0 8.8 %qkv_back.2 = (bf16[3,256,512]{2,1,0:T(8,128)(2,1)}, f32[3,512]{1,0:T(4,128)}, bf16[256,2048]{1,0:T(8,128)(2,1)}) custom-call(s32[18]{0:T(128)S(1)} %stack.130.refs_0_, bf16[256,512]{1,0:T(8,128)(2,1)} %get-tuple-element.261.refs_1_, f32[3,256,128]{2,1,0:T(8,128)} %pad_maximum_fusion.2.refs_2_.refs_4_, f32[2,256,512]{2,1,0:T(8,128)} %get-tuple-element.271.refs_3_, ...), custom_call_target="tpu_custom_call" | custom-call | bytes 27000000 | tf_op jit(solution)/shard_map/qkv_back/pallas_call | solution.py:194
  451.8 5.2 all-to-all-start.9
  461.0 6.9 attn_grads.2
  467.9 14.2 %all-to-all-done.9.refs_1_ = bf16[4,64,2048]{2,1,0:T(8,128)(2,1)S(1)} async-done(((bf16[4,64,2048]{2,1,0:T(8,128)(2,1)}), bf16[4,64,2048]{2,1,0:T(8,128)(2,1)S(1)}, u32[]{:S(2)}, u32[]{:S(2)}) %all-to-all-start.9) | async-done | bytes 1048608 | tf_op jit(solution)/shard_map/all_to_all | solution.py:708
  489.4 15.8 %collective-permute-done.62.refs_3_ = bf16[2,3,128,1408]{3,2,1,0:T(8,128)(2,1)} collective-permute-done((bf16[2,3,128,1408]{3,2,1,0:T(8,128)(2,1)}, bf16[2,3,128,1408]{3,2,1,0:T(8,128)(2,1)}, u32[]{:S(2)}, u32[]{:S(2)}) %collective-permute-start.62) | collective-permute-done | bytes 2162720 | tf_op jit(solution)/shard_map/ppermute | solution.py:606
  514.5 14.2 %mlp_back.1 = (bf16[2,256,1408]{2,1,0:T(8,128)(2,1)}, bf16[256,2048]{1,0:T(8,128)(2,1)}) custom-call(s32[18]{0:T(128)S(1)} %stack.130.refs_0_, bf16[256,1408]{1,0:T(8,128)(2,1)} %get-tuple-element.258.refs_1_, bf16[256,1408]{1,0:T(8,128)(2,1)} %get-tuple-element.259.refs_2_, bf16[256,2048]{1,0:T(8,128)(2,1)S(1)} %bitcast.123, ...), custom_call_target="tpu_custom_call" | custom-call | bytes 42000000 | tf_op jit(solution)/shard_map/mlp_back/pallas_call | solution.py:194
  540.0 10.6 %mlp_grads.3 = (bf16[2,3,128,1408]{3,2,1,0:T(8,128)(2,1)}, bf16[2,3,128,1408]{3,2,1,0:T(8,128)(2,1)}, bf16[2,3,128,1408]{3,2,1,0:T(8,128)(2,1)}, bf16[3,128,1408]{2,1,0:T(8,128)(2,1)}, bf16[3,128,1408]{2,1,0:T(8,128)(2,1)}) custom-call(s32[4]{0:T(128)S(1)} %pad_add_fusion.refs_0_, bf16[256,2048]{1,0:T(8,128)(2,1)} %bitcast.128, bf16[256,2048]{1,0:T(8,128)(2,1)} %bitcast.125, ...), custom_call_target="tpu_custom_call" | custom-call | bytes 31500000 | tf_op jit(solution)/shard_map/mlp_grads/pallas_call | solution.py:748
  550.5 7.4 %mlp_finish.2 = (f32[2,256,2,1408]{3,2,1,0:T(2,128)}, f32[2,1408,256]{2,1,0:T(8,128)}) custom-call(s32[18]{0:T(128)S(1)} %stack.130.refs_0_, bf16[2,3,128,1408]{3,2,1,0:T(8,128)(2,1)} %get-tuple-element.296.refs_1_, bf16[2,3,128,1408]{3,2,1,0:T(8,128)(2,1)} %collective-permute-done.56.refs_4_.refs_2_, ...), custom_call_target="tpu_custom_call" | custom-call | bytes 22500000 | tf_op jit(solution)/shard_map/mlp_finish/pallas_call | solution.py:194
  570.7 22.8 %all-to-all-done.12 = bf16[4,64,2048]{2,1,0:T(8,128)(2,1)S(1)} async-done(((bf16[4,64,2048]{2,1,0:T(8,128)(2,1)}), bf16[4,64,2048]{2,1,0:T(8,128)(2,1)S(1)}, u32[]{:S(2)}, u32[]{:S(2)}) %all-to-all-start.12) | async-done | bytes 1048608 | tf_op jit(solution)/shard_map/all_to_all | solution.py:712
  597.1 9.9 %attend_back.3 = (bf16[256,512]{1,0:T(8,128)(2,1)}, bf16[2,256,512]{2,1,0:T(8,128)(2,1)}, f32[2,256,512]{2,1,0:T(8,128)}) custom-call(s32[18]{0:T(128)S(1)} %stack.130.refs_0_, bf16[256,2048]{1,0:T(8,128)(2,1)S(1)} %bitcast.114, bf16[256,512]{1,0:T(8,128)(2,1)} %get-tuple-element.189.refs_1_.refs_2_, f32[8,256]{1,0:T(8,128)} %get-tuple-element.303.refs_3_, ...), custom_call_target="tpu_custom_call" | custom-call | bytes 30000000 | tf_op jit(solution)/shard_map/attend_back/pallas_call | solution.py:194
  607.7 8.8 %collective-permute-done.69.refs_3_ = bf16[2,3,128,1408]{3,2,1,0:T(8,128)(2,1)} collective-permute-done((bf16[2,3,128,1408]{3,2,1,0:T(8,128)(2,1)}, bf16[2,3,128,1408]{3,2,1,0:T(8,128)(2,1)}, u32[]{:S(2)}, u32[]{:S(2)}) %collective-permute-start.69) | collective-permute-done | bytes 2162720 | tf_op jit(solution)/shard_map/ppermute | solution.py:606
  633.6 8.8 %qkv_back.3 = (bf16[3,256,512]{2,1,0:T(8,128)(2,1)}, f32[3,512]{1,0:T(4,128)}, bf16[256,2048]{1,0:T(8,128)(2,1)}) custom-call(s32[18]{0:T(128)S(1)} %stack.130.refs_0_, bf16[256,512]{1,0:T(8,128)(2,1)} %get-tuple-element.304.refs_1_, f32[3,256,128]{2,1,0:T(8,128)} %pad_maximum_fusion.2.refs_2_.refs_4_, f32[2,256,512]{2,1,0:T(8,128)} %get-tuple-element.324.refs_3_, ...), custom_call_target="tpu_custom_call" | custom-call | bytes 27000000 | tf_op jit(solution)/shard_map/qkv_back/pallas_call | solution.py:194
  642.4 5.2 all-to-all-start.14
  647.7 5.6 collective-permute-done.76.refs_5_
  656.5 6.9 attn_grads.3
  675.9 7.4 %mlp_finish.3 = (f32[2,256,2,1408]{3,2,1,0:T(2,128)}, f32[2,1408,256]{2,1,0:T(8,128)}) custom-call(s32[18]{0:T(128)S(1)} %stack.130.refs_0_, bf16[2,3,128,1408]{3,2,1,0:T(8,128)(2,1)} %get-tuple-element.342.refs_1_, bf16[2,3,128,1408]{3,2,1,0:T(8,128)(2,1)} %collective-permute-done.70.refs_4_.refs_2_, ...), custom_call_target="tpu_custom_call", output_to_operand_aliasing={{0}: (6, {}), {1}: (7, {})} | custom-call | bytes 22500000 | tf_op jit(solution)/shard_map/mlp_finish/pallas_call | solution.py:194
  (410 shorter events, 256.1 us)
Async XLA Ops:
  3.5 26.5 %collective-permute-start.3 = (bf16[4,256,512]{2,1,0:T(8,128)(2,1)S(1)}, bf16[4,256,512]{2,1,0:T(8,128)(2,1)S(1)}, u32[]{:S(2)}, u32[]{:S(2)}) collective-permute-start(bf16[4,256,512]{2,1,0:T(8,128)(2,1)S(1)} %pad_maximum_fusion.refs_6_.refs_9_.refs_5_), channel_id=1, source_target_pairs={{0,16},{8,24},{16,0},{24,8},{1,17},{9,25},{17,1},{25,9},{2,18},{10... | collective-permute-start | bytes 3145736 | tf_op jit(solution)/shard_map/ppermute | solution.py:598
  6.5 43.3 %collective-permute-start.7 = (bf16[4,256,512]{2,1,0:T(8,128)(2,1)S(1)}, bf16[4,256,512]{2,1,0:T(8,128)(2,1)}, u32[]{:S(2)}, u32[]{:S(2)}) collective-permute-start(bf16[4,256,512]{2,1,0:T(8,128)(2,1)S(1)} %pad_maximum_fusion.refs_6_.refs_9_.refs_5_), channel_id=1, source_target_pairs={{0,8},{8,0},{16,24},{24,16},{1,9},{9,1},{17,25},{25,17},{2,10},{10... | collective-permute-start | bytes 3145736 | tf_op jit(solution)/shard_map/ppermute | solution.py:602
  10.8 26.1 %collective-permute-start.4 = (bf16[4,256,512]{2,1,0:T(8,128)(2,1)S(1)}, bf16[4,256,512]{2,1,0:T(8,128)(2,1)S(1)}, u32[]{:S(2)}, u32[]{:S(2)}) collective-permute-start(bf16[4,256,512]{2,1,0:T(8,128)(2,1)S(1)} %pad_maximum_fusion.refs_6_.refs_9_.refs_5_), channel_id=1, source_target_pairs={{0,4},{4,0},{1,5},{5,1},{2,6},{6,2},{3,7},{7,3},{8,12},{12,8},{9,1... | collective-permute-start | bytes 3145736 | tf_op jit(solution)/shard_map/ppermute | solution.py:606
  49.8 49.8 %collective-permute-start.13 = (bf16[3,256,1408]{2,1,0:T(8,128)(2,1)}, bf16[3,256,1408]{2,1,0:T(8,128)(2,1)}, u32[]{:S(2)}, u32[]{:S(2)}) collective-permute-start(bf16[3,256,1408]{2,1,0:T(8,128)(2,1)} %pack.2.refs_2_.refs_4_), channel_id=1, source_target_pairs={{0,16},{8,24},{16,0},{24,8},{1,17},{9,25},{17,1},{25,9},{2,18},{10... | collective-permute-start | bytes 6488072 | tf_op jit(solution)/shard_map/ppermute | solution.py:598
  72.8 49.3 %collective-permute-start.14 = (bf16[3,256,1408]{2,1,0:T(8,128)(2,1)}, bf16[3,256,1408]{2,1,0:T(8,128)(2,1)}, u32[]{:S(2)}, u32[]{:S(2)}) collective-permute-start(bf16[3,256,1408]{2,1,0:T(8,128)(2,1)} %pack.2.refs_2_.refs_4_), channel_id=1, source_target_pairs={{0,4},{4,0},{1,5},{5,1},{2,6},{6,2},{3,7},{7,3},{8,12},{12,8},{9,1... | collective-permute-start | bytes 6488072 | tf_op jit(solution)/shard_map/ppermute | solution.py:606
  82.1 29.9 %all-to-all-start = ((bf16[4,64,2048]{2,1,0:T(8,128)(2,1)}), bf16[4,64,2048]{2,1,0:T(8,128)(2,1)S(1)}, u32[]{:S(2)}, u32[]{:S(2)}) async-start(bf16[4,64,2048]{2,1,0:T(8,128)(2,1)} %bitcast.142), calls=%async_computation | async-start | bytes 2097152 | tf_op jit(solution)/shard_map/all_to_all | solution.py:708
  115.0 33.9 %collective-permute-start.18 = (bf16[3,256,1408]{2,1,0:T(8,128)(2,1)}, bf16[3,256,1408]{2,1,0:T(8,128)(2,1)}, u32[]{:S(2)}, u32[]{:S(2)}) collective-permute-start(bf16[3,256,1408]{2,1,0:T(8,128)(2,1)} %collective-permute-done.13.refs_3_.refs_5_), channel_id=1, source_target_pairs={{0,8},{8,0},{16,24},{24,16},{1,9},{9,1},{17,25},{25,17},{2,10},{10... | collective-permute-start | bytes 6488072 | tf_op jit(solution)/shard_map/ppermute | solution.py:602
  115.1 34.9 %collective-permute-start.17 = (bf16[3,256,1408]{2,1,0:T(8,128)(2,1)}, bf16[3,256,1408]{2,1,0:T(8,128)(2,1)}, u32[]{:S(2)}, u32[]{:S(2)}) collective-permute-start(bf16[3,256,1408]{2,1,0:T(8,128)(2,1)} %pack.2.refs_2_.refs_4_), channel_id=1, source_target_pairs={{0,8},{8,0},{16,24},{24,16},{1,9},{9,1},{17,25},{25,17},{2,10},{10... | collective-permute-start | bytes 6488072 | tf_op jit(solution)/shard_map/ppermute | solution.py:602
  115.5 30.9 %all-to-all-start.1 = ((bf16[4,64,2048]{2,1,0:T(8,128)(2,1)}), bf16[4,64,2048]{2,1,0:T(8,128)(2,1)S(1)}, u32[]{:S(2)}, u32[]{:S(2)}) async-start(bf16[4,64,2048]{2,1,0:T(8,128)(2,1)} %get-tuple-element.196), calls=%async_computation.1 | async-start | bytes 2097152 | tf_op jit(solution)/shard_map/all_to_all | solution.py:712
  120.4 26.0 %collective-permute-start.16 = (bf16[3,128,1408]{2,1,0:T(8,128)(2,1)S(1)}, bf16[3,128,1408]{2,1,0:T(8,128)(2,1)}, u32[]{:S(2)}, u32[]{:S(2)}) collective-permute-start(bf16[3,128,1408]{2,1,0:T(8,128)(2,1)S(1)} %slice.206), channel_id=1, source_target_pairs={{0,4},{4,0},{1,5},{5,1},{2,6},{6,2},{3,7},{7,3},{8,12},{12,8},{9,1... | collective-permute-start | bytes 3244040 | tf_op jit(solution)/shard_map/ppermute | solution.py:606
  123.5 25.2 %collective-permute-start.15 = (bf16[3,128,1408]{2,1,0:T(8,128)(2,1)S(1)}, bf16[3,128,1408]{2,1,0:T(8,128)(2,1)}, u32[]{:S(2)}, u32[]{:S(2)}) collective-permute-start(bf16[3,128,1408]{2,1,0:T(8,128)(2,1)S(1)} %slice.205), channel_id=1, source_target_pairs={{0,16},{8,24},{16,0},{24,8},{1,17},{9,25},{17,1},{25,9},{2,18},{10... | collective-permute-start | bytes 3244040 | tf_op jit(solution)/shard_map/ppermute | solution.py:598
  125.1 26.6 %collective-permute-start.19 = (bf16[3,256,1408]{2,1,0:T(8,128)(2,1)}, bf16[3,256,1408]{2,1,0:T(8,128)(2,1)}, u32[]{:S(2)}, u32[]{:S(2)}) collective-permute-start(bf16[3,256,1408]{2,1,0:T(8,128)(2,1)} %collective-permute-done.14.refs_4_.refs_6_), channel_id=1, source_target_pairs={{0,8},{8,0},{16,24},{24,16},{1,9},{9,1},{17,25},{25,17},{2,10},{10... | collective-permute-start | bytes 6488072 | tf_op jit(solution)/shard_map/ppermute | solution.py:602
  148.9 25.7 %collective-permute-start.22 = (bf16[4,256,512]{2,1,0:T(8,128)(2,1)S(1)}, bf16[4,256,512]{2,1,0:T(8,128)(2,1)}, u32[]{:S(2)}, u32[]{:S(2)}) collective-permute-start(bf16[4,256,512]{2,1,0:T(8,128)(2,1)S(1)} %pad_maximum_fusion.1.refs_4_.refs_6_.refs_9_.refs_5_), channel_id=1, source_target_pairs={{0,4},{4,0},{1,5},{5,1},{2,6},{6,2},{3,7},{7,3},{8,12},{12,8},{9,1... | collective-permute-start | bytes 3145736 | tf_op jit(solution)/shard_map/ppermute | solution.py:606
  150.0 25.4 %collective-permute-start.24 = (bf16[4,256,512]{2,1,0:T(8,128)(2,1)S(1)}, bf16[4,256,512]{2,1,0:T(8,128)(2,1)}, u32[]{:S(2)}, u32[]{:S(2)}) collective-permute-start(bf16[4,256,512]{2,1,0:T(8,128)(2,1)S(1)} %pad_maximum_fusion.1.refs_4_.refs_6_.refs_9_.refs_5_), channel_id=1, source_target_pairs={{0,16},{8,24},{16,0},{24,8},{1,17},{9,25},{17,1},{25,9},{2,18},{10... | collective-permute-start | bytes 3145736 | tf_op jit(solution)/shard_map/ppermute | solution.py:598
  162.9 31.9 %all-to-all-start.2 = ((bf16[4,64,2048]{2,1,0:T(8,128)(2,1)}), bf16[4,64,2048]{2,1,0:T(8,128)(2,1)S(1)}, u32[]{:S(2)}, u32[]{:S(2)}) async-start(bf16[4,64,2048]{2,1,0:T(8,128)(2,1)} %bitcast.139), calls=%async_computation.2 | async-start | bytes 2097152 | tf_op jit(solution)/shard_map/all_to_all | solution.py:708
  197.9 38.1 %all-to-all-start.3 = ((bf16[4,64,2048]{2,1,0:T(8,128)(2,1)}), bf16[4,64,2048]{2,1,0:T(8,128)(2,1)S(1)}, u32[]{:S(2)}, u32[]{:S(2)}) async-start(bf16[4,64,2048]{2,1,0:T(8,128)(2,1)} %get-tuple-element.216), calls=%async_computation.3 | async-start | bytes 2097152 | tf_op jit(solution)/shard_map/all_to_all | solution.py:712
  202.8 32.4 %collective-permute-start.30 = (bf16[2,256,1408]{2,1,0:T(8,128)(2,1)}, bf16[2,256,1408]{2,1,0:T(8,128)(2,1)}, u32[]{:S(2)}, u32[]{:S(2)}) collective-permute-start(bf16[2,256,1408]{2,1,0:T(8,128)(2,1)} %get-tuple-element.233.refs_3_), channel_id=1, source_target_pairs={{0,4},{4,0},{1,5},{5,1},{2,6},{6,2},{3,7},{7,3},{8,12},{12,8},{9,1... | collective-permute-start | bytes 4325384 | tf_op jit(solution)/shard_map/ppermute | solution.py:606
  203.9 32.1 %collective-permute-start.29 = (bf16[2,256,1408]{2,1,0:T(8,128)(2,1)}, bf16[2,256,1408]{2,1,0:T(8,128)(2,1)}, u32[]{:S(2)}, u32[]{:S(2)}) collective-permute-start(bf16[2,256,1408]{2,1,0:T(8,128)(2,1)} %get-tuple-element.233.refs_3_), channel_id=1, source_target_pairs={{0,16},{8,24},{16,0},{24,8},{1,17},{9,25},{17,1},{25,9},{2,18},{10... | collective-permute-start | bytes 4325384 | tf_op jit(solution)/shard_map/ppermute | solution.py:598
  205.6 30.4 %collective-permute-start.32 = (bf16[4,128,512]{2,1,0:T(8,128)(2,1)S(1)}, bf16[4,128,512]{2,1,0:T(8,128)(2,1)}, u32[]{:S(2)}, u32[]{:S(2)}) collective-permute-start(bf16[4,128,512]{2,1,0:T(8,128)(2,1)S(1)} %copy-done.15), channel_id=1, source_target_pairs={{0,8},{8,0},{16,24},{24,16},{1,9},{9,1},{17,25},{25,17},{2,10},{10... | collective-permute-start | bytes 1572872 | tf_op jit(solution)/shard_map/ppermute | solution.py:602
  205.6 30.4 %collective-permute-start.31 = (bf16[4,128,512]{2,1,0:T(8,128)(2,1)S(1)}, bf16[4,128,512]{2,1,0:T(8,128)(2,1)}, u32[]{:S(2)}, u32[]{:S(2)}) collective-permute-start(bf16[4,128,512]{2,1,0:T(8,128)(2,1)S(1)} %copy-done.17), channel_id=1, source_target_pairs={{0,8},{8,0},{16,24},{24,16},{1,9},{9,1},{17,25},{25,17},{2,10},{10... | collective-permute-start | bytes 1572872 | tf_op jit(solution)/shard_map/ppermute | solution.py:602
  260.7 27.0 %all-to-all-start.4 = ((bf16[4,64,2048]{2,1,0:T(8,128)(2,1)}), bf16[4,64,2048]{2,1,0:T(8,128)(2,1)S(1)}, u32[]{:S(2)}, u32[]{:S(2)}) async-start(bf16[4,64,2048]{2,1,0:T(8,128)(2,1)} %bitcast.141), calls=%async_computation.4 | async-start | bytes 2097152 | tf_op jit(solution)/shard_map/all_to_all | solution.py:708
  271.7 25.7 %collective-permute-start.37 = (bf16[2,128,1408]{2,1,0:T(8,128)(2,1)}, bf16[2,128,1408]{2,1,0:T(8,128)(2,1)}, u32[]{:S(2)}, u32[]{:S(2)}) collective-permute-start(bf16[2,128,1408]{2,1,0:T(8,128)(2,1)} %slice.214), channel_id=1, source_target_pairs={{0,4},{4,0},{1,5},{5,1},{2,6},{6,2},{3,7},{7,3},{8,12},{12,8},{9,1... | collective-permute-start | bytes 2162696 | tf_op jit(solution)/shard_map/ppermute | solution.py:606
  271.7 45.2 %collective-permute-start.40 = (bf16[2,256,1408]{2,1,0:T(8,128)(2,1)}, bf16[2,256,1408]{2,1,0:T(8,128)(2,1)}, u32[]{:S(2)}, u32[]{:S(2)}) collective-permute-start(bf16[2,256,1408]{2,1,0:T(8,128)(2,1)} %collective-permute-done.30.refs_5_), channel_id=1, source_target_pairs={{0,8},{8,0},{16,24},{24,16},{1,9},{9,1},{17,25},{25,17},{2,10},{10... | collective-permute-start | bytes 4325384 | tf_op jit(solution)/shard_map/ppermute | solution.py:602
  271.7 45.6 %collective-permute-start.39 = (bf16[2,256,1408]{2,1,0:T(8,128)(2,1)}, bf16[2,256,1408]{2,1,0:T(8,128)(2,1)}, u32[]{:S(2)}, u32[]{:S(2)}) collective-permute-start(bf16[2,256,1408]{2,1,0:T(8,128)(2,1)} %collective-permute-done.29.refs_4_), channel_id=1, source_target_pairs={{0,8},{8,0},{16,24},{24,16},{1,9},{9,1},{17,25},{25,17},{2,10},{10... | collective-permute-start | bytes 4325384 | tf_op jit(solution)/shard_map/ppermute | solution.py:602
  280.0 37.4 %collective-permute-start.38 = (bf16[2,256,1408]{2,1,0:T(8,128)(2,1)}, bf16[2,256,1408]{2,1,0:T(8,128)(2,1)}, u32[]{:S(2)}, u32[]{:S(2)}) collective-permute-start(bf16[2,256,1408]{2,1,0:T(8,128)(2,1)} %get-tuple-element.233.refs_3_), channel_id=1, source_target_pairs={{0,8},{8,0},{16,24},{24,16},{1,9},{9,1},{17,25},{25,17},{2,10},{10... | collective-permute-start | bytes 4325384 | tf_op jit(solution)/shard_map/ppermute | solution.py:602
  287.1 27.8 %collective-permute-start.35 = (bf16[256,2048]{1,0:T(8,128)(2,1)}, bf16[256,2048]{1,0:T(8,128)(2,1)}, u32[]{:S(2)}, u32[]{:S(2)}) collective-permute-start(bf16[256,2048]{1,0:T(8,128)(2,1)} %bitcast.53.refs_2_), channel_id=1, source_target_pairs={{0,8},{8,0},{16,24},{24,16},{1,9},{9,1},{17,25},{25,17},{2,10},{10... | collective-permute-start | bytes 3145736 | tf_op jit(solution)/shard_map/ppermute | solution.py:602
  290.8 37.4 %all-to-all-start.5 = ((bf16[4,64,2048]{2,1,0:T(8,128)(2,1)}), bf16[4,64,2048]{2,1,0:T(8,128)(2,1)S(1)}, u32[]{:S(2)}, u32[]{:S(2)}) async-start(bf16[4,64,2048]{2,1,0:T(8,128)(2,1)} %get-tuple-element.229), calls=%async_computation.5 | async-start | bytes 2097152 | tf_op jit(solution)/shard_map/all_to_all | solution.py:712
  348.5 31.1 %all-to-all-start.6 = ((bf16[4,64,2048]{2,1,0:T(8,128)(2,1)}), bf16[4,64,2048]{2,1,0:T(8,128)(2,1)}, u32[]{:S(2)}, u32[]{:S(2)}) async-start(bf16[4,64,2048]{2,1,0:T(8,128)(2,1)} %bitcast.138), calls=%async_computation.6 | async-start | bytes 2097152 | tf_op jit(solution)/shard_map/all_to_all | solution.py:708
  383.4 28.8 %all-to-all-start.7 = ((bf16[4,64,2048]{2,1,0:T(8,128)(2,1)}), bf16[4,64,2048]{2,1,0:T(8,128)(2,1)S(1)}, u32[]{:S(2)}, u32[]{:S(2)}) async-start(bf16[4,64,2048]{2,1,0:T(8,128)(2,1)} %get-tuple-element.254), calls=%async_computation.7 | async-start | bytes 2097152 | tf_op jit(solution)/shard_map/all_to_all | solution.py:712
  386.9 48.4 %collective-permute-start.56 = (bf16[2,3,128,1408]{3,2,1,0:T(8,128)(2,1)}, bf16[2,3,128,1408]{3,2,1,0:T(8,128)(2,1)}, u32[]{:S(2)}, u32[]{:S(2)}) collective-permute-start(bf16[2,3,128,1408]{3,2,1,0:T(8,128)(2,1)} %get-tuple-element.263), channel_id=1, source_target_pairs={{0,16},{8,24},{16,0},{24,8},{1,17},{9,25},{17,1},{25,9},{2,18},{10... | collective-permute-start | bytes 6488072 | tf_op jit(solution)/shard_map/ppermute | solution.py:598
  412.1 29.6 %all-to-all-start.8 = ((bf16[4,64,2048]{2,1,0:T(8,128)(2,1)}), bf16[4,64,2048]{2,1,0:T(8,128)(2,1)}, u32[]{:S(2)}, u32[]{:S(2)}) async-start(bf16[4,64,2048]{2,1,0:T(8,128)(2,1)} %bitcast.135), calls=%async_computation.8 | async-start | bytes 2097152 | tf_op jit(solution)/shard_map/all_to_all | solution.py:708
  451.8 30.3 %all-to-all-start.9 = ((bf16[4,64,2048]{2,1,0:T(8,128)(2,1)}), bf16[4,64,2048]{2,1,0:T(8,128)(2,1)S(1)}, u32[]{:S(2)}, u32[]{:S(2)}) async-start(bf16[4,64,2048]{2,1,0:T(8,128)(2,1)} %bitcast.140), calls=%async_computation.9 | async-start | bytes 2097152 | tf_op jit(solution)/shard_map/all_to_all | solution.py:708
  457.0 48.2 %collective-permute-start.62 = (bf16[2,3,128,1408]{3,2,1,0:T(8,128)(2,1)}, bf16[2,3,128,1408]{3,2,1,0:T(8,128)(2,1)}, u32[]{:S(2)}, u32[]{:S(2)}) collective-permute-start(bf16[2,3,128,1408]{3,2,1,0:T(8,128)(2,1)} %get-tuple-element.285), channel_id=1, source_target_pairs={{0,4},{4,0},{1,5},{5,1},{2,6},{6,2},{3,7},{7,3},{8,12},{12,8},{9,1... | collective-permute-start | bytes 6488072 | tf_op jit(solution)/shard_map/ppermute | solution.py:606
  485.5 29.0 %all-to-all-start.10 = ((bf16[4,64,2048]{2,1,0:T(8,128)(2,1)}), bf16[4,64,2048]{2,1,0:T(8,128)(2,1)S(1)}, u32[]{:S(2)}, u32[]{:S(2)}) async-start(bf16[4,64,2048]{2,1,0:T(8,128)(2,1)} %get-tuple-element.279), calls=%async_computation.10 | async-start | bytes 2097152 | tf_op jit(solution)/shard_map/all_to_all | solution.py:712
  528.7 29.9 %all-to-all-start.11 = ((bf16[4,64,2048]{2,1,0:T(8,128)(2,1)}), bf16[4,64,2048]{2,1,0:T(8,128)(2,1)S(1)}, u32[]{:S(2)}, u32[]{:S(2)}) async-start(bf16[4,64,2048]{2,1,0:T(8,128)(2,1)} %bitcast.137), calls=%async_computation.11 | async-start | bytes 2097152 | tf_op jit(solution)/shard_map/all_to_all | solution.py:708
  534.1 25.3 %collective-permute-start.67 = (bf16[2,4,128,512]{3,2,1,0:T(8,128)(2,1)}, bf16[2,4,128,512]{3,2,1,0:T(8,128)(2,1)S(1)}, u32[]{:S(2)}, u32[]{:S(2)}) collective-permute-start(bf16[2,4,128,512]{3,2,1,0:T(8,128)(2,1)} %get-tuple-element.298), channel_id=1, source_target_pairs={{0,16},{8,24},{16,0},{24,8},{1,17},{9,25},{17,1},{25,9},{2,18},{10... | collective-permute-start | bytes 3145736 | tf_op jit(solution)/shard_map/ppermute | solution.py:598
  535.6 25.1 %collective-permute-start.68 = (bf16[2,4,128,512]{3,2,1,0:T(8,128)(2,1)}, bf16[2,4,128,512]{3,2,1,0:T(8,128)(2,1)}, u32[]{:S(2)}, u32[]{:S(2)}) collective-permute-start(bf16[2,4,128,512]{3,2,1,0:T(8,128)(2,1)} %get-tuple-element.299), channel_id=1, source_target_pairs={{0,4},{4,0},{1,5},{5,1},{2,6},{6,2},{3,7},{7,3},{8,12},{12,8},{9,1... | collective-permute-start | bytes 3145736 | tf_op jit(solution)/shard_map/ppermute | solution.py:606
  564.2 29.3 %all-to-all-start.12 = ((bf16[4,64,2048]{2,1,0:T(8,128)(2,1)}), bf16[4,64,2048]{2,1,0:T(8,128)(2,1)S(1)}, u32[]{:S(2)}, u32[]{:S(2)}) async-start(bf16[4,64,2048]{2,1,0:T(8,128)(2,1)} %get-tuple-element.301), calls=%async_computation.12 | async-start | bytes 2097152 | tf_op jit(solution)/shard_map/all_to_all | solution.py:712
  568.7 47.8 %collective-permute-start.69 = (bf16[2,3,128,1408]{3,2,1,0:T(8,128)(2,1)}, bf16[2,3,128,1408]{3,2,1,0:T(8,128)(2,1)}, u32[]{:S(2)}, u32[]{:S(2)}) collective-permute-start(bf16[2,3,128,1408]{3,2,1,0:T(8,128)(2,1)} %get-tuple-element.310), channel_id=1, source_target_pairs={{0,4},{4,0},{1,5},{5,1},{2,6},{6,2},{3,7},{7,3},{8,12},{12,8},{9,1... | collective-permute-start | bytes 6488072 | tf_op jit(solution)/shard_map/ppermute | solution.py:606
  570.2 47.6 %collective-permute-start.70 = (bf16[2,3,128,1408]{3,2,1,0:T(8,128)(2,1)}, bf16[2,3,128,1408]{3,2,1,0:T(8,128)(2,1)}, u32[]{:S(2)}, u32[]{:S(2)}) collective-permute-start(bf16[2,3,128,1408]{3,2,1,0:T(8,128)(2,1)} %get-tuple-element.311), channel_id=1, source_target_pairs={{0,16},{8,24},{16,0},{24,8},{1,17},{9,25},{17,1},{25,9},{2,18},{10... | collective-permute-start | bytes 6488072 | tf_op jit(solution)/shard_map/ppermute | solution.py:598
  593.4 36.6 %all-to-all-start.13 = ((bf16[4,64,2048]{2,1,0:T(8,128)(2,1)}), bf16[4,64,2048]{2,1,0:T(8,128)(2,1)S(1)}, u32[]{:S(2)}, u32[]{:S(2)}) async-start(bf16[4,64,2048]{2,1,0:T(8,128)(2,1)} %sum.1), calls=%async_computation.13 | async-start | bytes 2097152 | tf_op jit(solution)/shard_map/all_to_all | solution.py:712
  621.8 25.9 %collective-permute-start.75 = (bf16[3,128,1408]{2,1,0:T(8,128)(2,1)}, bf16[3,128,1408]{2,1,0:T(8,128)(2,1)}, u32[]{:S(2)}, u32[]{:S(2)}) collective-permute-start(bf16[3,128,1408]{2,1,0:T(8,128)(2,1)} %get-tuple-element.312), channel_id=1, source_target_pairs={{0,16},{8,24},{16,0},{24,8},{1,17},{9,25},{17,1},{25,9},{2,18},{10... | collective-permute-start | bytes 3244040 | tf_op jit(solution)/shard_map/ppermute | solution.py:598
  622.5 30.8 %collective-permute-start.76 = (bf16[3,128,1408]{2,1,0:T(8,128)(2,1)}, bf16[3,128,1408]{2,1,0:T(8,128)(2,1)}, u32[]{:S(2)}, u32[]{:S(2)}) collective-permute-start(bf16[3,128,1408]{2,1,0:T(8,128)(2,1)} %get-tuple-element.328), channel_id=1, source_target_pairs={{0,4},{4,0},{1,5},{5,1},{2,6},{6,2},{3,7},{7,3},{8,12},{12,8},{9,1... | collective-permute-start | bytes 3244040 | tf_op jit(solution)/shard_map/ppermute | solution.py:606
  653.4 29.9 %collective-permute-start.80 = (bf16[4,128,512]{2,1,0:T(8,128)(2,1)}, bf16[4,128,512]{2,1,0:T(8,128)(2,1)}, u32[]{:S(2)}, u32[]{:S(2)}) collective-permute-start(bf16[4,128,512]{2,1,0:T(8,128)(2,1)} %get-tuple-element.348), channel_id=1, source_target_pairs={{0,4},{4,0},{1,5},{5,1},{2,6},{6,2},{3,7},{7,3},{8,12},{12,8},{9,1... | collective-permute-start | bytes 1572872 | tf_op jit(solution)/shard_map/ppermute | solution.py:606
  653.5 29.9 %collective-permute-start.79 = (bf16[4,128,512]{2,1,0:T(8,128)(2,1)}, bf16[4,128,512]{2,1,0:T(8,128)(2,1)}, u32[]{:S(2)}, u32[]{:S(2)}) collective-permute-start(bf16[4,128,512]{2,1,0:T(8,128)(2,1)} %get-tuple-element.346), channel_id=1, source_target_pairs={{0,16},{8,24},{16,0},{24,8},{1,17},{9,25},{17,1},{25,9},{2,18},{10... | collective-permute-start | bytes 1572872 | tf_op jit(solution)/shard_map/ppermute | solution.py:598
  663.4 28.6 %collective-permute-start.81 = (bf16[2,4,128,512]{3,2,1,0:T(8,128)(2,1)}, bf16[2,4,128,512]{3,2,1,0:T(8,128)(2,1)S(1)}, u32[]{:S(2)}, u32[]{:S(2)}) collective-permute-start(bf16[2,4,128,512]{3,2,1,0:T(8,128)(2,1)} %get-tuple-element.352), channel_id=1, source_target_pairs={{0,4},{4,0},{1,5},{5,1},{2,6},{6,2},{3,7},{7,3},{8,12},{12,8},{9,1... | collective-permute-start | bytes 3145736 | tf_op jit(solution)/shard_map/ppermute | solution.py:606
  664.1 27.9 %collective-permute-start.82 = (bf16[2,4,128,512]{3,2,1,0:T(8,128)(2,1)}, bf16[2,4,128,512]{3,2,1,0:T(8,128)(2,1)S(1)}, u32[]{:S(2)}, u32[]{:S(2)}) collective-permute-start(bf16[2,4,128,512]{3,2,1,0:T(8,128)(2,1)} %get-tuple-element.353), channel_id=1, source_target_pairs={{0,16},{8,24},{16,0},{24,8},{1,17},{9,25},{17,1},{25,9},{2,18},{10... | collective-permute-start | bytes 3145736 | tf_op jit(solution)/shard_map/ppermute | solution.py:598
  671.1 45.9 %all-to-all-start.15 = ((bf16[4,64,2048]{2,1,0:T(8,128)(2,1)}), bf16[4,64,2048]{2,1,0:T(8,128)(2,1)S(1)}, u32[]{:S(2)}, u32[]{:S(2)}) async-start(bf16[4,64,2048]{2,1,0:T(8,128)(2,1)} %get-tuple-element.333), calls=%async_computation.15 | async-start | bytes 2097152 | tf_op jit(solution)/shard_map/all_to_all | solution.py:712
  (121 other events, 1586.6 us)

commit v5 on v4

--- a/solution.py
+++ b/solution.py
@@ -18,6 +18,7 @@
 BF = jnp.bfloat16
 F32 = jnp.float32
 EACH = -1
+HALVES = -2
 TIMES = {
     "pack": 7.0,
     "qkv": 8.5,
@@ -74,11 +75,8 @@
     def weight(self, slot):
         if slot not in self.held_there:
             self.held_there.add(slot)
-            copies = self.weights[slot]
-            for copy in copies[: len(copies) // 2]:
-                copy.wait()
             self.begin(slot + 2)
-            for copy in copies[len(copies) // 2 :]:
+            for copy in self.weights[slot]:
                 copy.wait()
         return self.held[slot]
 
@@ -90,6 +88,15 @@
 
     def put(self, index):
         for copy in self.stores[index]:
+            copy.start()
+            self.gone.append(copy)
+
+    def put_columns(self, index, value_of):
+        out = self.outs[index]
+        half = out.shape[1] // 2
+        for side, copy in enumerate(self.stores[index]):
+            columns = slice(side * half, (side + 1) * half)
+            out[:, columns] = value_of(columns).astype(out.dtype)
             copy.start()
             self.gone.append(copy)
 
@@ -110,7 +117,7 @@
     n_in, n_piece, n_reuse = len(loads), len(pieces), len(reuse)
 
     def part(item):
-        return tuple(item[0].shape) if item[1] is None else tuple(item[0].shape[1:])
+        return tuple(item[0].shape) if item[1] in (None, HALVES) else tuple(item[0].shape[1:])
 
     def view(ref, index):
         return ref if index is None else ref.at[index]
@@ -158,6 +165,18 @@
                         for each in range(ref.shape[0])
                     ]
                 )
+            elif index == HALVES:
+                half = ref.shape[1] // 2
+                stores.append(
+                    [
+                        pltpu.make_async_copy(
+                            results[at].at[:, pl.ds(side * half, half)],
+                            ref.at[:, pl.ds(side * half, half)],
+                            out_sems.at[at, side],
+                        )
+                        for side in range(2)
+                    ]
+                )
             else:
                 stores.append(
                     [pltpu.make_async_copy(results[at], view(ref, index), out_sems.at[at, 0])]
@@ -179,7 +198,7 @@
     aliases = {len(args) + at: out for at, (_, out) in enumerate(reuse)}
     args += [in_hbm_now(array) for array, _ in reuse]
     hbm = pl.BlockSpec(memory_space=pltpu.HBM)
-    most = max([out.shape[0] for out, index in outs if index == EACH], default=1)
+    most = max([out.shape[0] for out, index in outs if index == EACH], default=2)
     scratch = [pltpu.VMEM(part(item), item[0].dtype) for item in loads]
     scratch += [pltpu.VMEM(part(item), item[0].dtype) for item in outs]
     scratch += [
@@ -295,7 +314,7 @@
 
 def attend_other_body(io):
     queries, kv, mask, sums, stats = (io.get(at) for at in range(5))
-    mixed, log_total, part = io.outs
+    mixed, log_total, _ = io.outs
     heads = queries.shape[1] // HD
     pair = []
     for head in range(heads):
@@ -316,15 +335,15 @@
             pair = []
     io.put(0)
     io.put(1)
-    part[...] = mm(mixed[...], io.weight(0)[...], NT).astype(BF)
-    io.put(2)
+    out_weight = io.weight(0)
+    io.put_columns(2, lambda columns: mm(mixed[...], out_weight[columns, :], NT))
 
 
 def attend_body(n_blocks, io):
     queries = io.get(0)
     kvs = [io.get(1 + at) for at in range(n_blocks)]
     masks = [io.get(1 + n_blocks + at) for at in range(n_blocks)]
-    mixed, log_total, part = io.outs
+    mixed, log_total, _ = io.outs
     for head in range(queries.shape[1] // HD):
         span = slice(head * HD, (head + 1) * HD)
         query = queries[:, span]
@@ -346,8 +365,8 @@
         mixed[:, span] = result.astype(BF)
     io.put(0)
     io.put(1)
-    part[...] = mm(mixed[...], io.weight(0)[...], NT).astype(BF)
-    io.put(2)
+    out_weight = io.weight(0)
+    io.put_columns(2, lambda columns: mm(mixed[...], out_weight[columns, :], NT))
 
 
 def terms_sum(terms):
@@ -369,7 +388,7 @@
 
 
 def mlp_body(io):
-    gate_out, up_out, hidden, part = io.outs
+    gate_out, up_out, hidden, _ = io.outs
     second_in = io.get(0)
     gate = mm(second_in[...], io.weight(0)[...], NN)
     gate_out[...] = gate.astype(BF)
@@ -380,12 +399,12 @@
     io.put(1)
     hidden[...] = (act * up).astype(BF)
     io.put(2)
-    part[...] = mm(hidden[...], io.weight(2)[...], NT).astype(BF)
-    io.put(3)
+    down = io.weight(2)
+    io.put_columns(3, lambda columns: mm(hidden[...], down[columns, :], NT))
 
 
 def mlp_back_body(io):
-    d_gate_up, part = io.outs
+    d_gate_up, _ = io.outs
     d_mlp = io.get(2)
     gate = io.get(0)[...].astype(F32)
     sig = jax.nn.sigmoid(gate)
@@ -395,14 +414,16 @@
         d_hidden * io.get(1)[...].astype(F32) * (sig * (1.0 + gate * (1.0 - sig)))
     ).astype(BF)
     io.put(0)
-    total = mm(d_gate_up[0], io.weight(1)[...], NT)
-    total = total + mm(d_gate_up[1], io.weight(2)[...], NT)
-    part[...] = total.astype(BF)
-    io.put(1)
+    gates, ups = io.weight(1), io.weight(2)
+
+    def gradient(columns):
+        return mm(d_gate_up[0], gates[columns, :], NT) + mm(d_gate_up[1], ups[columns, :], NT)
+
+    io.put_columns(1, gradient)
 
 
 def mlp_both_body(io):
-    hidden, part_out, d_gate_up, part = io.outs
+    hidden, _, d_gate_up, _ = io.outs
     second_in = io.get(0)
     gate = mm(second_in[...], io.weight(0)[...], NN)
     sig = jax.nn.sigmoid(gate)
@@ -416,12 +437,13 @@
     d_gate_up[1] = (d_hidden * act).astype(BF)
     d_gate_up[0] = (d_hidden * up * slope).astype(BF)
     io.put(2)
-    total = mm(d_gate_up[0], io.weight(0)[...], NT)
-    total = total + mm(d_gate_up[1], io.weight(1)[...], NT)
-    part[...] = total.astype(BF)
-    io.put(3)
-    part_out[...] = mm(hidden[...], down[...], NT).astype(BF)
-    io.put(1)
+    gates, ups = io.weight(0), io.weight(1)
+
+    def gradient(columns):
+        return mm(d_gate_up[0], gates[columns, :], NT) + mm(d_gate_up[1], ups[columns, :], NT)
+
+    io.put_columns(3, gradient)
+    io.put_columns(1, lambda columns: mm(hidden[...], down[columns, :], NT))
 
 
 def norm_back_body(io):
@@ -477,7 +499,7 @@
 
 
 def qkv_back_body(n_other, io):
-    d_qkv, bias, part = io.outs
+    d_qkv, bias, _ = io.outs
     tables = io.get(1)
     terms = [io.get(2 + at) for at in range(1 + n_other)]
     d_qkv[0] = io.get(0)[...]
@@ -489,23 +511,25 @@
     for index in range(3):
         bias[index : index + 1, :] = jnp.sum(d_qkv[index].astype(F32), axis=0, keepdims=True)
     io.put(1)
-    part[...] = total_of(
-        [mm(d_qkv[index], io.weight(index)[...], NT) for index in range(3)]
-    ).astype(BF)
-    io.put(2)
+    weights = [io.weight(index) for index in range(3)]
+
+    def gradient(columns):
+        return total_of([mm(d_qkv[at], weights[at][columns, :], NT) for at in range(3)])
+
+    io.put_columns(2, gradient)
 
 
 def pack_body(io):
     gate_up, down = io.get(0), io.get(1)
-    for part in range(2):
-        io.outs[0][part] = gate_up[:, part, :]
     if len(io.outs) == 1:
-        io.outs[0][2] = down[...].T
-        io.put(0)
+        matrices = [io.outs[0].at[at] for at in range(3)]
     else:
-        io.put(0)
-        io.outs[1][0] = down[...].T
-        io.put(1)
+        matrices = [out.at[0] for out in io.outs]
+    matrices[0][...] = gate_up[:, 0, :]
+    matrices[1][...] = gate_up[:, 1, :]
+    matrices[2][...] = down[...].T
+    for at in range(len(io.outs)):
+        io.put(at)
 
 
 def add_body(io):
@@ -859,7 +883,7 @@
     shards = []
     for layer in range(layers):
         if fast:
-            counts = (3,) if layer == 0 else (2, 1)
+            counts = (3,) if layer == 0 else (1, 1, 1)
             mlp_shards = kernel(
                 pack_body,
                 "pack",
@@ -897,6 +921,7 @@
     n_blocks = len(masks)
 
     wide = shape((rows, width), BF)
+    wide_out = (wide, HALVES)
     inner = shape((rows, hidden_width), BF)
     headed = shape((rows, heads_width), BF)
     block_f = shape((block, width), F32)
@@ -944,7 +969,7 @@
             )
         if layer == 0:
             first_in = normed[0]
-        attended = [headed, shape((heads, rows), F32), wide]
+        attended = [headed, shape((heads, rows), F32), wide_out]
         if fast:
             prev = lax.ppermute(kv, "ctx", [(0, 1)])
             kv_blocks = [prev, kv]
@@ -959,7 +984,8 @@
             if layer == 0:
                 mlp_g.near_y((prev, queries))
             else:
-                down_g.near_y((prev, queries))
+                up_g.near_y((prev, queries))
+                down_g.near_y((up_g.from_y,))
             mixed, log_total, part = kernel(
                 attend_other_body,
                 "attend_other",
@@ -982,9 +1008,10 @@
         if fast and layer == 0:
             terms = after(terms, mlp_g.from_x)
         elif fast:
-            gu_g.swap(part)
-            gu_g.far("both", (part,), (part,))
-            terms = after(terms, down_g.from_x)
+            gate_g.swap(part)
+            gate_g.far("both", (part,), (part,))
+            up_g.swap(part)
+            terms = after(terms, down_g.from_x, up_g.from_y)
         mid, normed = kernel(
             norm_body,
             "norm",
@@ -1001,10 +1028,11 @@
                 mlp_slots = [slot(mlp_pieces, index) for index in range(3)]
                 sent = mlp_g.pieces
             else:
+                up_g.far("both", (mid,), (mid,))
                 down_g.swap(mid)
                 down_g.far("both", (mid,), (mid,))
-                gu_pieces, down_pieces = gu_g.all(), down_g.all(second_in)
-                mlp_slots = [slot(gu_pieces, 0), slot(gu_pieces, 1), slot(down_pieces, 0)]
+                mlp_groups = (gate_g.all(), up_g.all(), down_g.all(second_in))
+                mlp_slots = [slot(pieces, 0) for pieces in mlp_groups]
                 sent = down_g.pieces
         second_in = flat(second_in)
         if layer < layers - 1:
@@ -1013,7 +1041,7 @@
                 "mlp",
                 spots,
                 [Free(second_in)],
-                [inner, inner, inner, wide],
+                [inner, inner, inner, wide_out],
                 mlp_slots,
             )
         else:
@@ -1023,7 +1051,7 @@
                 "mlp_both",
                 spots,
                 [Free(second_in), after(cotangent[0], peer)],
-                [inner, wide, shape((2, rows, hidden_width), BF), wide],
+                [inner, wide_out, shape((2, rows, hidden_width), BF), wide_out],
                 mlp_slots,
             )
             gate, up, last_mid = None, None, mid
@@ -1034,13 +1062,14 @@
             break
         terms = tensor_scatter(part)
         if fast:
-            attn_g, gu_g, down_g = (Gather(shard) for shard in shards[layer + 1])
+            attn_g, gate_g, up_g, down_g = (Gather(shard) for shard in shards[layer + 1])
             attn_g.near(sent[:1], sent[1:])
             attn_g.swap(part)
             attn_g.far("both", (part,), (part,))
-            gu_g.near(sent[:1], sent[1:])
-            down_g.near_x((gu_g.from_x,))
-            terms = after(terms, gu_g.shard, *attn_g.pieces, *attn_g.peers)
+            gate_g.near(sent[:1], sent[1:])
+            up_g.near_x((gate_g.from_x,))
+            down_g.near_x((up_g.from_x,))
+            terms = after(terms, gate_g.shard, *attn_g.pieces, *attn_g.peers)
         stream, normed = kernel(
             norm_body,
             "norm",
@@ -1050,7 +1079,7 @@
         )
         first_in = flat(tensor_gather(normed))
         if fast:
-            first_in = after(first_in, gu_g.from_x, gu_g.from_y)
+            first_in = after(first_in, gate_g.from_x, gate_g.from_y)
 
     attn_outs, mlp_outs, pending, mlp_pending = None, None, None, None
     sums = [None] * layers
@@ -1074,7 +1103,7 @@
                 "mlp_back",
                 spots,
                 [gate, up, Free(d_mlp)],
-                [shape((2, rows, hidden_width), BF), wide],
+                [shape((2, rows, hidden_width), BF), wide_out],
                 [mlp_slots[2], mlp_slots[0], mlp_slots[1]],
             )
         terms = tensor_scatter(part)
@@ -1151,7 +1180,7 @@
             "qkv_back",
             spots,
             [d_query, tables, own] + other,
-            [shape((3, rows, heads_width), BF), shape((3, heads_width), F32), wide],
+            [shape((3, rows, heads_width), BF), shape((3, heads_width), F32), wide_out],
             [slot(attn_pieces, index) for index in range(3)],
         )
         terms = tensor_scatter(part)

time: 729 us -> 725 us (level)
  starting transfers between devices: 136 us -> 149 us
  waiting for transfers between devices: 299 us -> 286 us
    ppermute x20 -> x22, waiting for transfers between devices: 54.6 us -> 38.4 us  [swap_x(): return lax.ppermute(array, 'fsdp', pairs_of('fsdp', 2))]
    ppermute x20 -> x22, starting transfers between devices: 21.4 us -> 30.7 us  [swap_x(): return lax.ppermute(array, 'fsdp', pairs_of('fsdp', 2))]
    ppermute x20 -> x22, starting transfers between devices: 25 us -> 26.6 us  [swap_y(): return lax.ppermute(array, 'ctx', pairs_of('ctx', 1))]
    ppermute x43 -> x48, waiting for transfers between devices: 13.8 us -> 15.4 us  [swap_core(): return lax.ppermute(array, 'fsdp', pairs_of('fsdp', 1))]
    unnamed x133 -> x151, local copies, waits for them, and re-layouts: 18.8 us -> 19.7 us
    ppermute x20 -> x22, waiting for transfers between devices: 127 us -> 126 us  [swap_y(): return lax.ppermute(array, 'ctx', pairs_of('ctx', 1))]
  transfers between devices with their start and end apart: 105 -> 114, of which waited for: 59 -> 59; matrix products, arithmetic and copies ran while one was open for 4% -> 4% of each run, Pallas kernels for 26% -> 26%
where the time goes in v5:
time: 725 us; the launch traced here: 716 us
  waiting for transfers between devices  286 us (39%)
  Pallas kernels  227 us (31%)
  starting transfers between devices  149 us (21%)
  local copies, waits for them, and re-layouts  44.1 us (6%)
  other arithmetic  8.57 us (1%)
    pallas_call x31, Pallas kernels, kernel(): pl.pallas_call(run, out_shape=[pltpu.HBM(out.shape, out.dtype) for out in...  192 us
    ppermute x22, waiting for transfers between devices, swap_y(): return lax.ppermute(array, 'ctx', pairs_of('ctx', 1))  126 us
    all_to_all x8, waiting for transfers between devices, tensor_gather(): return lax.all_to_all(copies, 'tp', 0, 0, tiled=True)  53.2 us
    all_to_all x8, waiting for transfers between devices, tensor_scatter(): return lax.all_to_all(blocks, 'tp', 0, 0, tiled=True)  39.5 us
    all_to_all x8, starting transfers between devices, tensor_scatter(): return lax.all_to_all(blocks, 'tp', 0, 0, tiled=True)  38.6 us
    ppermute x22, waiting for transfers between devices, swap_x(): return lax.ppermute(array, 'fsdp', pairs_of('fsdp', 2))  38.4 us
    pallas_call x4, Pallas kernels, weight_grads(): pl.pallas_call(functools.partial(weight_grad_body, counts, n_left, pairs)...  34.9 us
    all_to_all x8, starting transfers between devices, tensor_gather(): return lax.all_to_all(copies, 'tp', 0, 0, tiled=True)  32.1 us
  transfers between devices with their start and end apart: 114, of which 59 were waited for; matrix products, arithmetic and copies ran while one was open for 4% of the time, Pallas kernels for 26%

profile of v5, /device:TPU:0, one launch (start us, length us, event | category | flops | bytes accessed | tf_op | source)
XLA Modules:
  0.0 716.2 jit_solution(17580171541849516321)
XLA Ops:
  21.9 7.1 pack.2.refs_2_.refs_4_
  31.8 5.0 collective-permute-done.4.refs_8_.refs_11_.refs_7_
  37.3 9.5 %collective-permute-done.6.refs_10_.refs_13_.refs_9_ = bf16[4,128,512]{2,1,0:T(8,128)(2,1)} collective-permute-done((bf16[4,128,512]{2,1,0:T(8,128)(2,1)S(1)}, bf16[4,128,512]{2,1,0:T(8,128)(2,1)}, u32[]{:S(2)}, u32[]{:S(2)}) %collective-permute-start.6) | collective-permute-done | bytes 524320 | tf_op jit(solution)/shard_map/ppermute | solution.py:630
  50.6 7.1 key_value.2
  63.5 7.1 attend_own.2
  75.2 6.7 attend_other.2
  81.9 4.9 all-to-all-start
  88.5 11.1 %collective-permute-done.13.refs_3_.refs_5_ = bf16[3,256,1408]{2,1,0:T(8,128)(2,1)} collective-permute-done((bf16[3,256,1408]{2,1,0:T(8,128)(2,1)}, bf16[3,256,1408]{2,1,0:T(8,128)(2,1)}, u32[]{:S(2)}, u32[]{:S(2)}) %collective-permute-start.13) | collective-permute-done | bytes 2162720 | tf_op jit(solution)/shard_map/ppermute | solution.py:622
  99.5 12.3 %all-to-all-done.refs_1_ = bf16[4,64,2048]{2,1,0:T(8,128)(2,1)S(1)} async-done(((bf16[4,64,2048]{2,1,0:T(8,128)(2,1)}), bf16[4,64,2048]{2,1,0:T(8,128)(2,1)S(1)}, u32[]{:S(2)}, u32[]{:S(2)}) %all-to-all-start) | async-done | bytes 1048608 | tf_op jit(solution)/shard_map/all_to_all | solution.py:732
  125.1 21.3 %collective-permute-done.16.refs_6_.refs_8_ = bf16[3,128,1408]{2,1,0:T(8,128)(2,1)} collective-permute-done((bf16[3,128,1408]{2,1,0:T(8,128)(2,1)S(1)}, bf16[3,128,1408]{2,1,0:T(8,128)(2,1)}, u32[]{:S(2)}, u32[]{:S(2)}) %collective-permute-start.16) | collective-permute-done | bytes 1081376 | tf_op jit(solution)/shard_map/ppermute | solution.py:630
  151.6 9.9 %mlp.1 = (bf16[256,1408]{1,0:T(8,128)(2,1)}, bf16[256,1408]{1,0:T(8,128)(2,1)}, bf16[256,1408]{1,0:T(8,128)(2,1)}, bf16[256,2048]{1,0:T(8,128)(2,1)}) custom-call(s32[18]{0:T(128)S(1)} %stack.130.refs_0_, bf16[256,2048]{1,0:T(8,128)(2,1)S(1)} %bitcast.126, bf16[3,256,1408]{2,1,0:T(8,128)(2,1)} %pack.2.refs_2_.refs_4_, ...), custom_call_target="tpu_custom_call" | custom-call | bytes 34500000 | tf_op jit(solution)/shard_map/mlp/pallas_call | solution.py:213
  161.6 5.1 all-to-all-start.2
  166.7 7.9 %collective-permute-done.22.refs_6_.refs_8_.refs_11_.refs_7_ = bf16[4,256,512]{2,1,0:T(8,128)(2,1)} collective-permute-done((bf16[4,256,512]{2,1,0:T(8,128)(2,1)S(1)}, bf16[4,256,512]{2,1,0:T(8,128)(2,1)}, u32[]{:S(2)}, u32[]{:S(2)}) %collective-permute-start.22) | collective-permute-done | bytes 1048608 | tf_op jit(solution)/shard_map/ppermute | solution.py:630
  180.6 6.9 pack.3
  197.9 4.8 all-to-all-start.3
  206.0 13.5 %collective-permute-done.30.refs_5_ = bf16[1,256,1408]{2,1,0:T(8,128)(2,1)} collective-permute-done((bf16[1,256,1408]{2,1,0:T(8,128)(2,1)}, bf16[1,256,1408]{2,1,0:T(8,128)(2,1)}, u32[]{:S(2)}, u32[]{:S(2)}) %collective-permute-start.30) | collective-permute-done | bytes 720928 | tf_op jit(solution)/shard_map/ppermute | solution.py:630
  220.5 6.9 all-to-all-done.3
  227.4 5.0 key_value.3.refs_4_.refs_6_
  237.3 7.1 attend_own.3
  247.0 6.7 attend_other.3
  262.9 14.5 %collective-permute-done.36.refs_15_ = bf16[1,256,1408]{2,1,0:T(8,128)(2,1)} collective-permute-done((bf16[1,256,1408]{2,1,0:T(8,128)(2,1)}, bf16[1,256,1408]{2,1,0:T(8,128)(2,1)}, u32[]{:S(2)}, u32[]{:S(2)}) %collective-permute-start.36) | collective-permute-done | bytes 720928 | tf_op jit(solution)/shard_map/ppermute | solution.py:630
  291.8 5.0 all-to-all-start.5
  306.6 5.9 collective-permute-done.54.refs_27_
  329.3 15.2 %mlp_both.1 = (bf16[256,1408]{1,0:T(8,128)(2,1)}, bf16[256,2048]{1,0:T(8,128)(2,1)}, bf16[2,256,1408]{2,1,0:T(8,128)(2,1)}, bf16[256,2048]{1,0:T(8,128)(2,1)}) custom-call(s32[18]{0:T(128)S(1)} %stack.130.refs_0_, bf16[256,2048]{1,0:T(8,128)(2,1)S(1)} %bitcast.114, bf16[256,2048]{1,0:T(8,128)(2,1)} %bitcast.130, ...), custom_call_target="tpu_custom_call" | custom-call | bytes 54000000 | tf_op jit(solution)/shard_map/mlp_both/pallas_call | solution.py:213
  344.5 4.9 all-to-all-start.6
  357.8 10.6 %mlp_grads.2 = (bf16[2,3,128,1408]{3,2,1,0:T(8,128)(2,1)}, bf16[2,3,128,1408]{3,2,1,0:T(8,128)(2,1)}, bf16[2,3,128,1408]{3,2,1,0:T(8,128)(2,1)}, bf16[3,128,1408]{2,1,0:T(8,128)(2,1)}, bf16[3,128,1408]{2,1,0:T(8,128)(2,1)}) custom-call(s32[4]{0:T(128)S(1)} %pad_add_fusion.refs_0_, bf16[256,2048]{1,0:T(8,128)(2,1)} %bitcast.116, bf16[256,2048]{1,0:T(8,128)(2,1)} %bitcast.131, ...), custom_call_target="tpu_custom_call" | custom-call | bytes 31500000 | tf_op jit(solution)/shard_map/mlp_grads/pallas_call | solution.py:772
  368.4 7.2 %all-to-all-done.6.refs_1_ = bf16[4,64,2048]{2,1,0:T(8,128)(2,1)} async-done(((bf16[4,64,2048]{2,1,0:T(8,128)(2,1)}), bf16[4,64,2048]{2,1,0:T(8,128)(2,1)}, u32[]{:S(2)}, u32[]{:S(2)}) %all-to-all-start.6) | async-done | bytes 1048608 | tf_op jit(solution)/shard_map/all_to_all | solution.py:732
  384.6 23.5 %all-to-all-done.7 = bf16[4,64,2048]{2,1,0:T(8,128)(2,1)S(1)} async-done(((bf16[4,64,2048]{2,1,0:T(8,128)(2,1)}), bf16[4,64,2048]{2,1,0:T(8,128)(2,1)S(1)}, u32[]{:S(2)}, u32[]{:S(2)}) %all-to-all-start.7) | async-done | bytes 1048608 | tf_op jit(solution)/shard_map/all_to_all | solution.py:736
  412.4 9.9 %attend_back.2 = (bf16[256,512]{1,0:T(8,128)(2,1)}, bf16[2,256,512]{2,1,0:T(8,128)(2,1)}, f32[2,256,512]{2,1,0:T(8,128)}) custom-call(s32[18]{0:T(128)S(1)} %stack.130.refs_0_, bf16[256,2048]{1,0:T(8,128)(2,1)S(1)} %bitcast.120, bf16[256,512]{1,0:T(8,128)(2,1)} %get-tuple-element.228.refs_1_.refs_2_, f32[8,256]{1,0:T(8,128)} %get-tuple-element.276.refs_3_, ...), custom_call_target="tpu_custom_call" | custom-call | bytes 30000000 | tf_op jit(solution)/shard_map/attend_back/pallas_call | solution.py:213
  424.5 6.7 collective-permute-done.65.refs_4_.refs_2_
  433.0 4.7 all-to-all-done.8.refs_1_
  439.0 8.3 %qkv_back.2 = (bf16[3,256,512]{2,1,0:T(8,128)(2,1)}, f32[3,512]{1,0:T(4,128)}, bf16[256,2048]{1,0:T(8,128)(2,1)}) custom-call(s32[18]{0:T(128)S(1)} %stack.130.refs_0_, bf16[256,512]{1,0:T(8,128)(2,1)} %get-tuple-element.277.refs_1_, f32[3,256,128]{2,1,0:T(8,128)} %pad_maximum_fusion.2.refs_2_.refs_4_, f32[2,256,512]{2,1,0:T(8,128)} %get-tuple-element.287.refs_3_, ...), custom_call_target="tpu_custom_call" | custom-call | bytes 27000000 | tf_op jit(solution)/shard_map/qkv_back/pallas_call | solution.py:213
  447.3 5.2 all-to-all-start.9
  456.6 6.9 attn_grads.2
  463.5 14.2 %all-to-all-done.9.refs_1_ = bf16[4,64,2048]{2,1,0:T(8,128)(2,1)S(1)} async-done(((bf16[4,64,2048]{2,1,0:T(8,128)(2,1)}), bf16[4,64,2048]{2,1,0:T(8,128)(2,1)S(1)}, u32[]{:S(2)}, u32[]{:S(2)}) %all-to-all-start.9) | async-done | bytes 1048608 | tf_op jit(solution)/shard_map/all_to_all | solution.py:732
  484.7 16.0 %collective-permute-done.71.refs_3_ = bf16[2,3,128,1408]{3,2,1,0:T(8,128)(2,1)} collective-permute-done((bf16[2,3,128,1408]{3,2,1,0:T(8,128)(2,1)}, bf16[2,3,128,1408]{3,2,1,0:T(8,128)(2,1)}, u32[]{:S(2)}, u32[]{:S(2)}) %collective-permute-start.71) | collective-permute-done | bytes 2162720 | tf_op jit(solution)/shard_map/ppermute | solution.py:630
  509.8 13.1 %mlp_back.1 = (bf16[2,256,1408]{2,1,0:T(8,128)(2,1)}, bf16[256,2048]{1,0:T(8,128)(2,1)}) custom-call(s32[18]{0:T(128)S(1)} %stack.130.refs_0_, bf16[256,1408]{1,0:T(8,128)(2,1)} %get-tuple-element.274.refs_1_, bf16[256,1408]{1,0:T(8,128)(2,1)} %get-tuple-element.275.refs_2_, bf16[256,2048]{1,0:T(8,128)(2,1)S(1)} %bitcast.123, ...), custom_call_target="tpu_custom_call" | custom-call | bytes 42000000 | tf_op jit(solution)/shard_map/mlp_back/pallas_call | solution.py:213
  523.0 5.2 all-to-all-start.11
  536.7 10.6 %mlp_grads.3 = (bf16[2,3,128,1408]{3,2,1,0:T(8,128)(2,1)}, bf16[2,3,128,1408]{3,2,1,0:T(8,128)(2,1)}, bf16[2,3,128,1408]{3,2,1,0:T(8,128)(2,1)}, bf16[3,128,1408]{2,1,0:T(8,128)(2,1)}, bf16[3,128,1408]{2,1,0:T(8,128)(2,1)}) custom-call(s32[4]{0:T(128)S(1)} %pad_add_fusion.refs_0_, bf16[256,2048]{1,0:T(8,128)(2,1)} %bitcast.128, bf16[256,2048]{1,0:T(8,128)(2,1)} %bitcast.125, ...), custom_call_target="tpu_custom_call" | custom-call | bytes 31500000 | tf_op jit(solution)/shard_map/mlp_grads/pallas_call | solution.py:772
  547.3 7.4 %mlp_finish.2 = (f32[2,256,2,1408]{3,2,1,0:T(2,128)}, f32[2,1408,256]{2,1,0:T(8,128)}) custom-call(s32[18]{0:T(128)S(1)} %stack.130.refs_0_, bf16[2,3,128,1408]{3,2,1,0:T(8,128)(2,1)} %get-tuple-element.312.refs_1_, bf16[2,3,128,1408]{3,2,1,0:T(8,128)(2,1)} %collective-permute-done.65.refs_4_.refs_2_, ...), custom_call_target="tpu_custom_call" | custom-call | bytes 22500000 | tf_op jit(solution)/shard_map/mlp_finish/pallas_call | solution.py:213
  566.5 22.7 %all-to-all-done.12 = bf16[4,64,2048]{2,1,0:T(8,128)(2,1)S(1)} async-done(((bf16[4,64,2048]{2,1,0:T(8,128)(2,1)}), bf16[4,64,2048]{2,1,0:T(8,128)(2,1)S(1)}, u32[]{:S(2)}, u32[]{:S(2)}) %all-to-all-start.12) | async-done | bytes 1048608 | tf_op jit(solution)/shard_map/all_to_all | solution.py:736
  593.0 9.9 %attend_back.3 = (bf16[256,512]{1,0:T(8,128)(2,1)}, bf16[2,256,512]{2,1,0:T(8,128)(2,1)}, f32[2,256,512]{2,1,0:T(8,128)}) custom-call(s32[18]{0:T(128)S(1)} %stack.130.refs_0_, bf16[256,2048]{1,0:T(8,128)(2,1)S(1)} %bitcast.117, bf16[256,512]{1,0:T(8,128)(2,1)} %get-tuple-element.197.refs_1_.refs_2_, f32[8,256]{1,0:T(8,128)} %get-tuple-element.319.refs_3_, ...), custom_call_target="tpu_custom_call" | custom-call | bytes 30000000 | tf_op jit(solution)/shard_map/attend_back/pallas_call | solution.py:213
  603.6 8.7 %collective-permute-done.78.refs_3_ = bf16[2,3,128,1408]{3,2,1,0:T(8,128)(2,1)} collective-permute-done((bf16[2,3,128,1408]{3,2,1,0:T(8,128)(2,1)}, bf16[2,3,128,1408]{3,2,1,0:T(8,128)(2,1)}, u32[]{:S(2)}, u32[]{:S(2)}) %collective-permute-start.78) | collective-permute-done | bytes 2162720 | tf_op jit(solution)/shard_map/ppermute | solution.py:630
  629.4 8.3 %qkv_back.3 = (bf16[3,256,512]{2,1,0:T(8,128)(2,1)}, f32[3,512]{1,0:T(4,128)}, bf16[256,2048]{1,0:T(8,128)(2,1)}) custom-call(s32[18]{0:T(128)S(1)} %stack.130.refs_0_, bf16[256,512]{1,0:T(8,128)(2,1)} %get-tuple-element.320.refs_1_, f32[3,256,128]{2,1,0:T(8,128)} %pad_maximum_fusion.2.refs_2_.refs_4_, f32[2,256,512]{2,1,0:T(8,128)} %get-tuple-element.340.refs_3_, ...), custom_call_target="tpu_custom_call" | custom-call | bytes 27000000 | tf_op jit(solution)/shard_map/qkv_back/pallas_call | solution.py:213
  637.8 5.2 all-to-all-start.14
  643.1 6.3 collective-permute-done.85.refs_5_
  652.6 6.9 attn_grads.3
  671.7 7.4 %mlp_finish.3 = (f32[2,256,2,1408]{3,2,1,0:T(2,128)}, f32[2,1408,256]{2,1,0:T(8,128)}) custom-call(s32[18]{0:T(128)S(1)} %stack.130.refs_0_, bf16[2,3,128,1408]{3,2,1,0:T(8,128)(2,1)} %get-tuple-element.358.refs_1_, bf16[2,3,128,1408]{3,2,1,0:T(8,128)(2,1)} %collective-permute-done.79.refs_4_.refs_2_, ...), custom_call_target="tpu_custom_call", output_to_operand_aliasing={{0}: (6, {}), {1}: (7, {})} | custom-call | bytes 22500000 | tf_op jit(solution)/shard_map/mlp_finish/pallas_call | solution.py:213
  (448 shorter events, 277.5 us)
Async XLA Ops:
  3.4 26.5 %collective-permute-start.3 = (bf16[4,256,512]{2,1,0:T(8,128)(2,1)S(1)}, bf16[4,256,512]{2,1,0:T(8,128)(2,1)S(1)}, u32[]{:S(2)}, u32[]{:S(2)}) collective-permute-start(bf16[4,256,512]{2,1,0:T(8,128)(2,1)S(1)} %pad_maximum_fusion.refs_6_.refs_9_.refs_5_), channel_id=1, source_target_pairs={{0,16},{8,24},{16,0},{24,8},{1,17},{9,25},{17,1},{25,9},{2,18},{10... | collective-permute-start | bytes 3145736 | tf_op jit(solution)/shard_map/ppermute | solution.py:622
  6.4 43.3 %collective-permute-start.7 = (bf16[4,256,512]{2,1,0:T(8,128)(2,1)S(1)}, bf16[4,256,512]{2,1,0:T(8,128)(2,1)}, u32[]{:S(2)}, u32[]{:S(2)}) collective-permute-start(bf16[4,256,512]{2,1,0:T(8,128)(2,1)S(1)} %pad_maximum_fusion.refs_6_.refs_9_.refs_5_), channel_id=1, source_target_pairs={{0,8},{8,0},{16,24},{24,16},{1,9},{9,1},{17,25},{25,17},{2,10},{10... | collective-permute-start | bytes 3145736 | tf_op jit(solution)/shard_map/ppermute | solution.py:626
  10.8 26.1 %collective-permute-start.4 = (bf16[4,256,512]{2,1,0:T(8,128)(2,1)S(1)}, bf16[4,256,512]{2,1,0:T(8,128)(2,1)S(1)}, u32[]{:S(2)}, u32[]{:S(2)}) collective-permute-start(bf16[4,256,512]{2,1,0:T(8,128)(2,1)S(1)} %pad_maximum_fusion.refs_6_.refs_9_.refs_5_), channel_id=1, source_target_pairs={{0,4},{4,0},{1,5},{5,1},{2,6},{6,2},{3,7},{7,3},{8,12},{12,8},{9,1... | collective-permute-start | bytes 3145736 | tf_op jit(solution)/shard_map/ppermute | solution.py:630
  49.7 49.8 %collective-permute-start.13 = (bf16[3,256,1408]{2,1,0:T(8,128)(2,1)}, bf16[3,256,1408]{2,1,0:T(8,128)(2,1)}, u32[]{:S(2)}, u32[]{:S(2)}) collective-permute-start(bf16[3,256,1408]{2,1,0:T(8,128)(2,1)} %pack.2.refs_2_.refs_4_), channel_id=1, source_target_pairs={{0,16},{8,24},{16,0},{24,8},{1,17},{9,25},{17,1},{25,9},{2,18},{10... | collective-permute-start | bytes 6488072 | tf_op jit(solution)/shard_map/ppermute | solution.py:622
  72.8 49.3 %collective-permute-start.14 = (bf16[3,256,1408]{2,1,0:T(8,128)(2,1)}, bf16[3,256,1408]{2,1,0:T(8,128)(2,1)}, u32[]{:S(2)}, u32[]{:S(2)}) collective-permute-start(bf16[3,256,1408]{2,1,0:T(8,128)(2,1)} %pack.2.refs_2_.refs_4_), channel_id=1, source_target_pairs={{0,4},{4,0},{1,5},{5,1},{2,6},{6,2},{3,7},{7,3},{8,12},{12,8},{9,1... | collective-permute-start | bytes 6488072 | tf_op jit(solution)/shard_map/ppermute | solution.py:630
  81.9 29.9 %all-to-all-start = ((bf16[4,64,2048]{2,1,0:T(8,128)(2,1)}), bf16[4,64,2048]{2,1,0:T(8,128)(2,1)S(1)}, u32[]{:S(2)}, u32[]{:S(2)}) async-start(bf16[4,64,2048]{2,1,0:T(8,128)(2,1)} %bitcast.145), calls=%async_computation | async-start | bytes 2097152 | tf_op jit(solution)/shard_map/all_to_all | solution.py:732
  114.8 34.0 %collective-permute-start.18 = (bf16[3,256,1408]{2,1,0:T(8,128)(2,1)}, bf16[3,256,1408]{2,1,0:T(8,128)(2,1)}, u32[]{:S(2)}, u32[]{:S(2)}) collective-permute-start(bf16[3,256,1408]{2,1,0:T(8,128)(2,1)} %collective-permute-done.13.refs_3_.refs_5_), channel_id=1, source_target_pairs={{0,8},{8,0},{16,24},{24,16},{1,9},{9,1},{17,25},{25,17},{2,10},{10... | collective-permute-start | bytes 6488072 | tf_op jit(solution)/shard_map/ppermute | solution.py:626
  114.9 35.1 %collective-permute-start.17 = (bf16[3,256,1408]{2,1,0:T(8,128)(2,1)}, bf16[3,256,1408]{2,1,0:T(8,128)(2,1)}, u32[]{:S(2)}, u32[]{:S(2)}) collective-permute-start(bf16[3,256,1408]{2,1,0:T(8,128)(2,1)} %pack.2.refs_2_.refs_4_), channel_id=1, source_target_pairs={{0,8},{8,0},{16,24},{24,16},{1,9},{9,1},{17,25},{25,17},{2,10},{10... | collective-permute-start | bytes 6488072 | tf_op jit(solution)/shard_map/ppermute | solution.py:626
  115.4 31.0 %all-to-all-start.1 = ((bf16[4,64,2048]{2,1,0:T(8,128)(2,1)}), bf16[4,64,2048]{2,1,0:T(8,128)(2,1)S(1)}, u32[]{:S(2)}, u32[]{:S(2)}) async-start(bf16[4,64,2048]{2,1,0:T(8,128)(2,1)} %get-tuple-element.204), calls=%async_computation.1 | async-start | bytes 2097152 | tf_op jit(solution)/shard_map/all_to_all | solution.py:736
  120.3 26.0 %collective-permute-start.16 = (bf16[3,128,1408]{2,1,0:T(8,128)(2,1)S(1)}, bf16[3,128,1408]{2,1,0:T(8,128)(2,1)}, u32[]{:S(2)}, u32[]{:S(2)}) collective-permute-start(bf16[3,128,1408]{2,1,0:T(8,128)(2,1)S(1)} %slice.214), channel_id=1, source_target_pairs={{0,4},{4,0},{1,5},{5,1},{2,6},{6,2},{3,7},{7,3},{8,12},{12,8},{9,1... | collective-permute-start | bytes 3244040 | tf_op jit(solution)/shard_map/ppermute | solution.py:630
  123.4 25.1 %collective-permute-start.15 = (bf16[3,128,1408]{2,1,0:T(8,128)(2,1)S(1)}, bf16[3,128,1408]{2,1,0:T(8,128)(2,1)}, u32[]{:S(2)}, u32[]{:S(2)}) collective-permute-start(bf16[3,128,1408]{2,1,0:T(8,128)(2,1)S(1)} %slice.213), channel_id=1, source_target_pairs={{0,16},{8,24},{16,0},{24,8},{1,17},{9,25},{17,1},{25,9},{2,18},{10... | collective-permute-start | bytes 3244040 | tf_op jit(solution)/shard_map/ppermute | solution.py:622
  125.1 26.6 %collective-permute-start.19 = (bf16[3,256,1408]{2,1,0:T(8,128)(2,1)}, bf16[3,256,1408]{2,1,0:T(8,128)(2,1)}, u32[]{:S(2)}, u32[]{:S(2)}) collective-permute-start(bf16[3,256,1408]{2,1,0:T(8,128)(2,1)} %collective-permute-done.14.refs_4_.refs_6_), channel_id=1, source_target_pairs={{0,8},{8,0},{16,24},{24,16},{1,9},{9,1},{17,25},{25,17},{2,10},{10... | collective-permute-start | bytes 6488072 | tf_op jit(solution)/shard_map/ppermute | solution.py:626
  148.8 25.7 %collective-permute-start.22 = (bf16[4,256,512]{2,1,0:T(8,128)(2,1)S(1)}, bf16[4,256,512]{2,1,0:T(8,128)(2,1)}, u32[]{:S(2)}, u32[]{:S(2)}) collective-permute-start(bf16[4,256,512]{2,1,0:T(8,128)(2,1)S(1)} %pad_maximum_fusion.1.refs_4_.refs_6_.refs_9_.refs_5_), channel_id=1, source_target_pairs={{0,4},{4,0},{1,5},{5,1},{2,6},{6,2},{3,7},{7,3},{8,12},{12,8},{9,1... | collective-permute-start | bytes 3145736 | tf_op jit(solution)/shard_map/ppermute | solution.py:630
  150.0 25.4 %collective-permute-start.24 = (bf16[4,256,512]{2,1,0:T(8,128)(2,1)S(1)}, bf16[4,256,512]{2,1,0:T(8,128)(2,1)}, u32[]{:S(2)}, u32[]{:S(2)}) collective-permute-start(bf16[4,256,512]{2,1,0:T(8,128)(2,1)S(1)} %pad_maximum_fusion.1.refs_4_.refs_6_.refs_9_.refs_5_), channel_id=1, source_target_pairs={{0,16},{8,24},{16,0},{24,8},{1,17},{9,25},{17,1},{25,9},{2,18},{10... | collective-permute-start | bytes 3145736 | tf_op jit(solution)/shard_map/ppermute | solution.py:622
  161.6 33.2 %all-to-all-start.2 = ((bf16[4,64,2048]{2,1,0:T(8,128)(2,1)}), bf16[4,64,2048]{2,1,0:T(8,128)(2,1)S(1)}, u32[]{:S(2)}, u32[]{:S(2)}) async-start(bf16[4,64,2048]{2,1,0:T(8,128)(2,1)} %bitcast.143), calls=%async_computation.2 | async-start | bytes 2097152 | tf_op jit(solution)/shard_map/all_to_all | solution.py:732
  197.9 29.5 %all-to-all-start.3 = ((bf16[4,64,2048]{2,1,0:T(8,128)(2,1)}), bf16[4,64,2048]{2,1,0:T(8,128)(2,1)S(1)}, u32[]{:S(2)}, u32[]{:S(2)}) async-start(bf16[4,64,2048]{2,1,0:T(8,128)(2,1)} %get-tuple-element.224), calls=%async_computation.3 | async-start | bytes 2097152 | tf_op jit(solution)/shard_map/all_to_all | solution.py:736
  235.5 24.6 %collective-permute-start.34 = (bf16[1,256,1408]{2,1,0:T(8,128)(2,1)}, bf16[1,256,1408]{2,1,0:T(8,128)(2,1)}, u32[]{:S(2)}, u32[]{:S(2)}) collective-permute-start(bf16[1,256,1408]{2,1,0:T(8,128)(2,1)} %get-tuple-element.250.refs_13_), channel_id=1, source_target_pairs={{0,16},{8,24},{16,0},{24,8},{1,17},{9,25},{17,1},{25,9},{2,18},{10... | collective-permute-start | bytes 2162696 | tf_op jit(solution)/shard_map/ppermute | solution.py:622
  253.7 35.0 %all-to-all-start.4 = ((bf16[4,64,2048]{2,1,0:T(8,128)(2,1)}), bf16[4,64,2048]{2,1,0:T(8,128)(2,1)S(1)}, u32[]{:S(2)}, u32[]{:S(2)}) async-start(bf16[4,64,2048]{2,1,0:T(8,128)(2,1)} %bitcast.142), calls=%async_computation.4 | async-start | bytes 2097152 | tf_op jit(solution)/shard_map/all_to_all | solution.py:732
  260.1 25.0 %collective-permute-start.35 = (bf16[1,256,1408]{2,1,0:T(8,128)(2,1)}, bf16[1,256,1408]{2,1,0:T(8,128)(2,1)}, u32[]{:S(2)}, u32[]{:S(2)}) collective-permute-start(bf16[1,256,1408]{2,1,0:T(8,128)(2,1)} %get-tuple-element.256.refs_23_), channel_id=1, source_target_pairs={{0,16},{8,24},{16,0},{24,8},{1,17},{9,25},{17,1},{25,9},{2,18},{10... | collective-permute-start | bytes 2162696 | tf_op jit(solution)/shard_map/ppermute | solution.py:622
  261.8 35.1 %collective-permute-start.37 = (bf16[256,2048]{1,0:T(8,128)(2,1)}, bf16[256,2048]{1,0:T(8,128)(2,1)}, u32[]{:S(2)}, u32[]{:S(2)}) collective-permute-start(bf16[256,2048]{1,0:T(8,128)(2,1)} %bitcast.129), channel_id=1, source_target_pairs={{0,8},{8,0},{16,24},{24,16},{1,9},{9,1},{17,25},{25,17},{2,10},{10... | collective-permute-start | bytes 3145736 | tf_op jit(solution)/shard_map/ppermute | solution.py:626
  262.8 22.3 %collective-permute-start.39 = (bf16[1,128,1408]{2,1,0:T(8,128)(2,1)S(1)}, bf16[1,128,1408]{2,1,0:T(8,128)(2,1)S(1)}, u32[]{:S(2)}, u32[]{:S(2)}) collective-permute-start(bf16[1,128,1408]{2,1,0:T(8,128)(2,1)S(1)} %slice.222), channel_id=1, source_target_pairs={{0,4},{4,0},{1,5},{5,1},{2,6},{6,2},{3,7},{7,3},{8,12},{12,8},{9,1... | collective-permute-start | bytes 1081352 | tf_op jit(solution)/shard_map/ppermute | solution.py:630
  291.8 32.3 %all-to-all-start.5 = ((bf16[4,64,2048]{2,1,0:T(8,128)(2,1)}), bf16[4,64,2048]{2,1,0:T(8,128)(2,1)S(1)}, u32[]{:S(2)}, u32[]{:S(2)}) async-start(bf16[4,64,2048]{2,1,0:T(8,128)(2,1)} %get-tuple-element.240), calls=%async_computation.5 | async-start | bytes 2097152 | tf_op jit(solution)/shard_map/all_to_all | solution.py:736
  344.5 31.0 %all-to-all-start.6 = ((bf16[4,64,2048]{2,1,0:T(8,128)(2,1)}), bf16[4,64,2048]{2,1,0:T(8,128)(2,1)}, u32[]{:S(2)}, u32[]{:S(2)}) async-start(bf16[4,64,2048]{2,1,0:T(8,128)(2,1)} %bitcast.140), calls=%async_computation.6 | async-start | bytes 2097152 | tf_op jit(solution)/shard_map/all_to_all | solution.py:732
  379.3 28.8 %all-to-all-start.7 = ((bf16[4,64,2048]{2,1,0:T(8,128)(2,1)}), bf16[4,64,2048]{2,1,0:T(8,128)(2,1)S(1)}, u32[]{:S(2)}, u32[]{:S(2)}) async-start(bf16[4,64,2048]{2,1,0:T(8,128)(2,1)} %get-tuple-element.270), calls=%async_computation.7 | async-start | bytes 2097152 | tf_op jit(solution)/shard_map/all_to_all | solution.py:736
  382.9 48.4 %collective-permute-start.65 = (bf16[2,3,128,1408]{3,2,1,0:T(8,128)(2,1)}, bf16[2,3,128,1408]{3,2,1,0:T(8,128)(2,1)}, u32[]{:S(2)}, u32[]{:S(2)}) collective-permute-start(bf16[2,3,128,1408]{3,2,1,0:T(8,128)(2,1)} %get-tuple-element.279), channel_id=1, source_target_pairs={{0,16},{8,24},{16,0},{24,8},{1,17},{9,25},{17,1},{25,9},{2,18},{10... | collective-permute-start | bytes 6488072 | tf_op jit(solution)/shard_map/ppermute | solution.py:622
  408.1 29.5 %all-to-all-start.8 = ((bf16[4,64,2048]{2,1,0:T(8,128)(2,1)}), bf16[4,64,2048]{2,1,0:T(8,128)(2,1)}, u32[]{:S(2)}, u32[]{:S(2)}) async-start(bf16[4,64,2048]{2,1,0:T(8,128)(2,1)} %bitcast.138), calls=%async_computation.8 | async-start | bytes 2097152 | tf_op jit(solution)/shard_map/all_to_all | solution.py:732
  447.3 30.3 %all-to-all-start.9 = ((bf16[4,64,2048]{2,1,0:T(8,128)(2,1)}), bf16[4,64,2048]{2,1,0:T(8,128)(2,1)S(1)}, u32[]{:S(2)}, u32[]{:S(2)}) async-start(bf16[4,64,2048]{2,1,0:T(8,128)(2,1)} %bitcast.144), calls=%async_computation.9 | async-start | bytes 2097152 | tf_op jit(solution)/shard_map/all_to_all | solution.py:732
  452.5 48.2 %collective-permute-start.71 = (bf16[2,3,128,1408]{3,2,1,0:T(8,128)(2,1)}, bf16[2,3,128,1408]{3,2,1,0:T(8,128)(2,1)}, u32[]{:S(2)}, u32[]{:S(2)}) collective-permute-start(bf16[2,3,128,1408]{3,2,1,0:T(8,128)(2,1)} %get-tuple-element.301), channel_id=1, source_target_pairs={{0,4},{4,0},{1,5},{5,1},{2,6},{6,2},{3,7},{7,3},{8,12},{12,8},{9,1... | collective-permute-start | bytes 6488072 | tf_op jit(solution)/shard_map/ppermute | solution.py:630
  481.0 28.8 %all-to-all-start.10 = ((bf16[4,64,2048]{2,1,0:T(8,128)(2,1)}), bf16[4,64,2048]{2,1,0:T(8,128)(2,1)S(1)}, u32[]{:S(2)}, u32[]{:S(2)}) async-start(bf16[4,64,2048]{2,1,0:T(8,128)(2,1)} %get-tuple-element.295), calls=%async_computation.10 | async-start | bytes 2097152 | tf_op jit(solution)/shard_map/all_to_all | solution.py:736
  504.7 24.2 %collective-permute-start.72 = (bf16[3,128,1408]{2,1,0:T(8,128)(2,1)}, bf16[3,128,1408]{2,1,0:T(8,128)(2,1)}, u32[]{:S(2)}, u32[]{:S(2)}) collective-permute-start(bf16[3,128,1408]{2,1,0:T(8,128)(2,1)} %get-tuple-element.302), channel_id=1, source_target_pairs={{0,16},{8,24},{16,0},{24,8},{1,17},{9,25},{17,1},{25,9},{2,18},{10... | collective-permute-start | bytes 3244040 | tf_op jit(solution)/shard_map/ppermute | solution.py:622
  506.5 23.8 %collective-permute-start.73 = (bf16[3,128,1408]{2,1,0:T(8,128)(2,1)}, bf16[3,128,1408]{2,1,0:T(8,128)(2,1)}, u32[]{:S(2)}, u32[]{:S(2)}) collective-permute-start(bf16[3,128,1408]{2,1,0:T(8,128)(2,1)} %get-tuple-element.306), channel_id=1, source_target_pairs={{0,4},{4,0},{1,5},{5,1},{2,6},{6,2},{3,7},{7,3},{8,12},{12,8},{9,1... | collective-permute-start | bytes 3244040 | tf_op jit(solution)/shard_map/ppermute | solution.py:630
  523.0 31.8 %all-to-all-start.11 = ((bf16[4,64,2048]{2,1,0:T(8,128)(2,1)}), bf16[4,64,2048]{2,1,0:T(8,128)(2,1)S(1)}, u32[]{:S(2)}, u32[]{:S(2)}) async-start(bf16[4,64,2048]{2,1,0:T(8,128)(2,1)} %bitcast.141), calls=%async_computation.11 | async-start | bytes 2097152 | tf_op jit(solution)/shard_map/all_to_all | solution.py:732
  530.8 25.3 %collective-permute-start.76 = (bf16[2,4,128,512]{3,2,1,0:T(8,128)(2,1)}, bf16[2,4,128,512]{3,2,1,0:T(8,128)(2,1)S(1)}, u32[]{:S(2)}, u32[]{:S(2)}) collective-permute-start(bf16[2,4,128,512]{3,2,1,0:T(8,128)(2,1)} %get-tuple-element.314), channel_id=1, source_target_pairs={{0,16},{8,24},{16,0},{24,8},{1,17},{9,25},{17,1},{25,9},{2,18},{10... | collective-permute-start | bytes 3145736 | tf_op jit(solution)/shard_map/ppermute | solution.py:622
  531.2 25.1 %collective-permute-start.77 = (bf16[2,4,128,512]{3,2,1,0:T(8,128)(2,1)}, bf16[2,4,128,512]{3,2,1,0:T(8,128)(2,1)}, u32[]{:S(2)}, u32[]{:S(2)}) collective-permute-start(bf16[2,4,128,512]{3,2,1,0:T(8,128)(2,1)} %get-tuple-element.315), channel_id=1, source_target_pairs={{0,4},{4,0},{1,5},{5,1},{2,6},{6,2},{3,7},{7,3},{8,12},{12,8},{9,1... | collective-permute-start | bytes 3145736 | tf_op jit(solution)/shard_map/ppermute | solution.py:630
  559.7 29.5 %all-to-all-start.12 = ((bf16[4,64,2048]{2,1,0:T(8,128)(2,1)}), bf16[4,64,2048]{2,1,0:T(8,128)(2,1)S(1)}, u32[]{:S(2)}, u32[]{:S(2)}) async-start(bf16[4,64,2048]{2,1,0:T(8,128)(2,1)} %get-tuple-element.317), calls=%async_computation.12 | async-start | bytes 2097152 | tf_op jit(solution)/shard_map/all_to_all | solution.py:736
  564.3 48.0 %collective-permute-start.78 = (bf16[2,3,128,1408]{3,2,1,0:T(8,128)(2,1)}, bf16[2,3,128,1408]{3,2,1,0:T(8,128)(2,1)}, u32[]{:S(2)}, u32[]{:S(2)}) collective-permute-start(bf16[2,3,128,1408]{3,2,1,0:T(8,128)(2,1)} %get-tuple-element.326), channel_id=1, source_target_pairs={{0,4},{4,0},{1,5},{5,1},{2,6},{6,2},{3,7},{7,3},{8,12},{12,8},{9,1... | collective-permute-start | bytes 6488072 | tf_op jit(solution)/shard_map/ppermute | solution.py:630
  564.8 48.8 %collective-permute-start.79 = (bf16[2,3,128,1408]{3,2,1,0:T(8,128)(2,1)}, bf16[2,3,128,1408]{3,2,1,0:T(8,128)(2,1)}, u32[]{:S(2)}, u32[]{:S(2)}) collective-permute-start(bf16[2,3,128,1408]{3,2,1,0:T(8,128)(2,1)} %get-tuple-element.327), channel_id=1, source_target_pairs={{0,16},{8,24},{16,0},{24,8},{1,17},{9,25},{17,1},{25,9},{2,18},{10... | collective-permute-start | bytes 6488072 | tf_op jit(solution)/shard_map/ppermute | solution.py:622
  589.2 37.4 %all-to-all-start.13 = ((bf16[4,64,2048]{2,1,0:T(8,128)(2,1)}), bf16[4,64,2048]{2,1,0:T(8,128)(2,1)S(1)}, u32[]{:S(2)}, u32[]{:S(2)}) async-start(bf16[4,64,2048]{2,1,0:T(8,128)(2,1)} %sum.1), calls=%async_computation.13 | async-start | bytes 2097152 | tf_op jit(solution)/shard_map/all_to_all | solution.py:736
  602.9 22.7 %collective-permute-start.81 = (bf16[256,2048]{1,0:T(8,128)(2,1)S(1)}, bf16[256,2048]{1,0:T(8,128)(2,1)S(1)}, u32[]{:S(2)}, u32[]{:S(2)}) collective-permute-start(bf16[256,2048]{1,0:T(8,128)(2,1)S(1)} %bitcast.118), channel_id=1, source_target_pairs={{0,8},{8,0},{16,24},{24,16},{1,9},{9,1},{17,25},{25,17},{2,10},{10... | collective-permute-start | bytes 3145736 | tf_op jit(solution)/shard_map/ppermute | solution.py:626
  603.0 23.7 %collective-permute-start.80 = (bf16[256,2048]{1,0:T(8,128)(2,1)S(1)}, bf16[256,2048]{1,0:T(8,128)(2,1)}, u32[]{:S(2)}, u32[]{:S(2)}) collective-permute-start(bf16[256,2048]{1,0:T(8,128)(2,1)S(1)} %copy-done.7), channel_id=1, source_target_pairs={{0,8},{8,0},{16,24},{24,16},{1,9},{9,1},{17,25},{25,17},{2,10},{10... | collective-permute-start | bytes 3145736 | tf_op jit(solution)/shard_map/ppermute | solution.py:626
  617.6 25.4 %collective-permute-start.84 = (bf16[3,128,1408]{2,1,0:T(8,128)(2,1)}, bf16[3,128,1408]{2,1,0:T(8,128)(2,1)}, u32[]{:S(2)}, u32[]{:S(2)}) collective-permute-start(bf16[3,128,1408]{2,1,0:T(8,128)(2,1)} %get-tuple-element.328), channel_id=1, source_target_pairs={{0,16},{8,24},{16,0},{24,8},{1,17},{9,25},{17,1},{25,9},{2,18},{10... | collective-permute-start | bytes 3244040 | tf_op jit(solution)/shard_map/ppermute | solution.py:622
  619.1 30.3 %collective-permute-start.85 = (bf16[3,128,1408]{2,1,0:T(8,128)(2,1)}, bf16[3,128,1408]{2,1,0:T(8,128)(2,1)}, u32[]{:S(2)}, u32[]{:S(2)}) collective-permute-start(bf16[3,128,1408]{2,1,0:T(8,128)(2,1)} %get-tuple-element.344), channel_id=1, source_target_pairs={{0,4},{4,0},{1,5},{5,1},{2,6},{6,2},{3,7},{7,3},{8,12},{12,8},{9,1... | collective-permute-start | bytes 3244040 | tf_op jit(solution)/shard_map/ppermute | solution.py:630
  637.8 24.9 %all-to-all-start.14 = ((bf16[4,64,2048]{2,1,0:T(8,128)(2,1)}), bf16[4,64,2048]{2,1,0:T(8,128)(2,1)S(1)}, u32[]{:S(2)}, u32[]{:S(2)}) async-start(bf16[4,64,2048]{2,1,0:T(8,128)(2,1)} %bitcast.139), calls=%async_computation.14 | async-start | bytes 2097152 | tf_op jit(solution)/shard_map/all_to_all | solution.py:732
  649.5 29.6 %collective-permute-start.89 = (bf16[4,128,512]{2,1,0:T(8,128)(2,1)}, bf16[4,128,512]{2,1,0:T(8,128)(2,1)}, u32[]{:S(2)}, u32[]{:S(2)}) collective-permute-start(bf16[4,128,512]{2,1,0:T(8,128)(2,1)} %get-tuple-element.364), channel_id=1, source_target_pairs={{0,4},{4,0},{1,5},{5,1},{2,6},{6,2},{3,7},{7,3},{8,12},{12,8},{9,1... | collective-permute-start | bytes 1572872 | tf_op jit(solution)/shard_map/ppermute | solution.py:630
  649.5 29.6 %collective-permute-start.88 = (bf16[4,128,512]{2,1,0:T(8,128)(2,1)}, bf16[4,128,512]{2,1,0:T(8,128)(2,1)}, u32[]{:S(2)}, u32[]{:S(2)}) collective-permute-start(bf16[4,128,512]{2,1,0:T(8,128)(2,1)} %get-tuple-element.362), channel_id=1, source_target_pairs={{0,16},{8,24},{16,0},{24,8},{1,17},{9,25},{17,1},{25,9},{2,18},{10... | collective-permute-start | bytes 1572872 | tf_op jit(solution)/shard_map/ppermute | solution.py:622
  659.4 28.6 %collective-permute-start.90 = (bf16[2,4,128,512]{3,2,1,0:T(8,128)(2,1)}, bf16[2,4,128,512]{3,2,1,0:T(8,128)(2,1)S(1)}, u32[]{:S(2)}, u32[]{:S(2)}) collective-permute-start(bf16[2,4,128,512]{3,2,1,0:T(8,128)(2,1)} %get-tuple-element.368), channel_id=1, source_target_pairs={{0,4},{4,0},{1,5},{5,1},{2,6},{6,2},{3,7},{7,3},{8,12},{12,8},{9,1... | collective-permute-start | bytes 3145736 | tf_op jit(solution)/shard_map/ppermute | solution.py:630
  660.6 27.5 %collective-permute-start.91 = (bf16[2,4,128,512]{3,2,1,0:T(8,128)(2,1)}, bf16[2,4,128,512]{3,2,1,0:T(8,128)(2,1)S(1)}, u32[]{:S(2)}, u32[]{:S(2)}) collective-permute-start(bf16[2,4,128,512]{3,2,1,0:T(8,128)(2,1)} %get-tuple-element.369), channel_id=1, source_target_pairs={{0,16},{8,24},{16,0},{24,8},{1,17},{9,25},{17,1},{25,9},{2,18},{10... | collective-permute-start | bytes 3145736 | tf_op jit(solution)/shard_map/ppermute | solution.py:622
  667.1 46.3 %all-to-all-start.15 = ((bf16[4,64,2048]{2,1,0:T(8,128)(2,1)}), bf16[4,64,2048]{2,1,0:T(8,128)(2,1)S(1)}, u32[]{:S(2)}, u32[]{:S(2)}) async-start(bf16[4,64,2048]{2,1,0:T(8,128)(2,1)} %get-tuple-element.349), calls=%async_computation.15 | async-start | bytes 2097152 | tf_op jit(solution)/shard_map/all_to_all | solution.py:736
  (139 other events, 1752.6 us)

commit v6 on v5

--- a/solution.py
+++ b/solution.py
@@ -302,7 +302,7 @@
     heads = queries.shape[1] // HD
     for head in range(heads):
         span = slice(head * HD, (head + 1) * HD)
-        scores = mm(kv[0, :, span], queries[:, span], NT) * SCALE + mask[...]
+        scores = mm(kv[0, :, span], queries[:, span] * SCALE, NT) + mask[...]
         top = jnp.max(scores, axis=0, keepdims=True)
         exps = jnp.exp(scores - top)
         stats[head : head + 1, :] = top
@@ -319,7 +319,7 @@
     pair = []
     for head in range(heads):
         span = slice(head * HD, (head + 1) * HD)
-        scores = mm(kv[0, :, span], queries[:, span], NT) * SCALE + mask[...]
+        scores = mm(kv[0, :, span], queries[:, span] * SCALE, NT) + mask[...]
         own_top = stats[head : head + 1, :]
         top = jnp.maximum(own_top, jnp.max(scores, axis=0, keepdims=True))
         exps = jnp.exp(scores - top)
@@ -346,9 +346,9 @@
     mixed, log_total, _ = io.outs
     for head in range(queries.shape[1] // HD):
         span = slice(head * HD, (head + 1) * HD)
-        query = queries[:, span]
+        query = queries[:, span] * SCALE
         scores = [
-            mm(kv[0, :, span], query, NT) * SCALE + mask[...]
+            mm(kv[0, :, span], query, NT) + mask[...]
             for kv, mask in zip(kvs, masks, strict=True)
         ]
         top = functools.reduce(jnp.maximum, [jnp.max(s, axis=0, keepdims=True) for s in scores])
@@ -469,11 +469,11 @@
     pair = []
     for head in range(queries.shape[1] // HD):
         span = slice(head * HD, (head + 1) * HD)
-        query = queries[:, span]
+        query = queries[:, span] * SCALE
         d_out = d_mixed[:, span]
         row_log = log_total[head : head + 1, :]
         probs = [
-            jnp.exp(mm(kv[0, :, span], query, NT) * SCALE + mask[...] - row_log)
+            jnp.exp(mm(kv[0, :, span], query, NT) + mask[...] - row_log)
             for kv, mask in zip(kvs, masks, strict=True)
         ]
         d_probs = [mm(kv[1, :, span], d_out, NT) for kv in kvs]
@@ -492,7 +492,7 @@
             d_query[:, wide] = turn_wide(jnp.concatenate(pair, axis=1), tables, -1.0).astype(BF)
             pair = []
         for ds, p, d_kv in zip(d_scores, probs, d_kvs, strict=True):
-            d_kv[0, :, span] = (mm(ds, query, NN) * SCALE).astype(d_kv.dtype)
+            d_kv[0, :, span] = mm(ds, query, NN).astype(d_kv.dtype)
             d_kv[1, :, span] = mm(p.astype(BF), d_out, NN).astype(d_kv.dtype)
     for at in range(1 + n_blocks):
         io.put(at)

time: 725 us -> 725 us (level)
  no operation moved by 1% of the time
where the time goes in v6:
time: 725 us; the launch traced here: 716 us
  waiting for transfers between devices  286 us (39%)
  Pallas kernels  227 us (31%)
  starting transfers between devices  149 us (21%)
  local copies, waits for them, and re-layouts  44.1 us (6%)
  other arithmetic  8.57 us (1%)
    pallas_call x31, Pallas kernels, kernel(): pl.pallas_call(run, out_shape=[pltpu.HBM(out.shape, out.dtype) for out in...  192 us
    ppermute x22, waiting for transfers between devices, swap_y(): return lax.ppermute(array, 'ctx', pairs_of('ctx', 1))  126 us
    all_to_all x8, waiting for transfers between devices, tensor_gather(): return lax.all_to_all(copies, 'tp', 0, 0, tiled=True)  53.1 us
    all_to_all x8, waiting for transfers between devices, tensor_scatter(): return lax.all_to_all(blocks, 'tp', 0, 0, tiled=True)  39.5 us
    all_to_all x8, starting transfers between devices, tensor_scatter(): return lax.all_to_all(blocks, 'tp', 0, 0, tiled=True)  38.6 us
    ppermute x22, waiting for transfers between devices, swap_x(): return lax.ppermute(array, 'fsdp', pairs_of('fsdp', 2))  38.4 us
    pallas_call x4, Pallas kernels, weight_grads(): pl.pallas_call(functools.partial(weight_grad_body, counts, n_left, pairs)...  34.9 us
    all_to_all x8, starting transfers between devices, tensor_gather(): return lax.all_to_all(copies, 'tp', 0, 0, tiled=True)  32.1 us
  transfers between devices with their start and end apart: 114, of which 59 were waited for; matrix products, arithmetic and copies ran while one was open for 4% of the time, Pallas kernels for 26%

profile of v6, /device:TPU:0, one launch (start us, length us, event | category | flops | bytes accessed | tf_op | source)
XLA Modules:
  0.0 716.1 jit_solution(5726434554527977250)
XLA Ops:
  21.9 7.1 pack.2.refs_2_.refs_4_
  31.8 5.0 collective-permute-done.4.refs_8_.refs_11_.refs_7_
  37.3 9.5 %collective-permute-done.6.refs_10_.refs_13_.refs_9_ = bf16[4,128,512]{2,1,0:T(8,128)(2,1)} collective-permute-done((bf16[4,128,512]{2,1,0:T(8,128)(2,1)S(1)}, bf16[4,128,512]{2,1,0:T(8,128)(2,1)}, u32[]{:S(2)}, u32[]{:S(2)}) %collective-permute-start.6) | collective-permute-done | bytes 524320 | tf_op jit(solution)/shard_map/ppermute | solution.py:630
  50.6 7.1 key_value.2
  63.5 7.1 attend_own.2
  75.2 6.7 attend_other.2
  81.9 4.9 all-to-all-start
  88.5 11.1 %collective-permute-done.13.refs_3_.refs_5_ = bf16[3,256,1408]{2,1,0:T(8,128)(2,1)} collective-permute-done((bf16[3,256,1408]{2,1,0:T(8,128)(2,1)}, bf16[3,256,1408]{2,1,0:T(8,128)(2,1)}, u32[]{:S(2)}, u32[]{:S(2)}) %collective-permute-start.13) | collective-permute-done | bytes 2162720 | tf_op jit(solution)/shard_map/ppermute | solution.py:622
  99.5 12.3 %all-to-all-done.refs_1_ = bf16[4,64,2048]{2,1,0:T(8,128)(2,1)S(1)} async-done(((bf16[4,64,2048]{2,1,0:T(8,128)(2,1)}), bf16[4,64,2048]{2,1,0:T(8,128)(2,1)S(1)}, u32[]{:S(2)}, u32[]{:S(2)}) %all-to-all-start) | async-done | bytes 1048608 | tf_op jit(solution)/shard_map/all_to_all | solution.py:732
  125.1 21.3 %collective-permute-done.16.refs_6_.refs_8_ = bf16[3,128,1408]{2,1,0:T(8,128)(2,1)} collective-permute-done((bf16[3,128,1408]{2,1,0:T(8,128)(2,1)S(1)}, bf16[3,128,1408]{2,1,0:T(8,128)(2,1)}, u32[]{:S(2)}, u32[]{:S(2)}) %collective-permute-start.16) | collective-permute-done | bytes 1081376 | tf_op jit(solution)/shard_map/ppermute | solution.py:630
  151.6 9.9 %mlp.1 = (bf16[256,1408]{1,0:T(8,128)(2,1)}, bf16[256,1408]{1,0:T(8,128)(2,1)}, bf16[256,1408]{1,0:T(8,128)(2,1)}, bf16[256,2048]{1,0:T(8,128)(2,1)}) custom-call(s32[18]{0:T(128)S(1)} %stack.130.refs_0_, bf16[256,2048]{1,0:T(8,128)(2,1)S(1)} %bitcast.126, bf16[3,256,1408]{2,1,0:T(8,128)(2,1)} %pack.2.refs_2_.refs_4_, ...), custom_call_target="tpu_custom_call" | custom-call | bytes 34500000 | tf_op jit(solution)/shard_map/mlp/pallas_call | solution.py:213
  161.6 5.1 all-to-all-start.2
  166.7 7.8 %collective-permute-done.22.refs_6_.refs_8_.refs_11_.refs_7_ = bf16[4,256,512]{2,1,0:T(8,128)(2,1)} collective-permute-done((bf16[4,256,512]{2,1,0:T(8,128)(2,1)S(1)}, bf16[4,256,512]{2,1,0:T(8,128)(2,1)}, u32[]{:S(2)}, u32[]{:S(2)}) %collective-permute-start.22) | collective-permute-done | bytes 1048608 | tf_op jit(solution)/shard_map/ppermute | solution.py:630
  180.6 6.9 pack.3
  197.9 4.8 all-to-all-start.3
  206.0 13.5 %collective-permute-done.30.refs_5_ = bf16[1,256,1408]{2,1,0:T(8,128)(2,1)} collective-permute-done((bf16[1,256,1408]{2,1,0:T(8,128)(2,1)}, bf16[1,256,1408]{2,1,0:T(8,128)(2,1)}, u32[]{:S(2)}, u32[]{:S(2)}) %collective-permute-start.30) | collective-permute-done | bytes 720928 | tf_op jit(solution)/shard_map/ppermute | solution.py:630
  220.5 6.9 all-to-all-done.3
  227.4 5.0 key_value.3.refs_4_.refs_6_
  237.3 7.1 attend_own.3
  247.0 6.7 attend_other.3
  262.9 14.5 %collective-permute-done.36.refs_15_ = bf16[1,256,1408]{2,1,0:T(8,128)(2,1)} collective-permute-done((bf16[1,256,1408]{2,1,0:T(8,128)(2,1)}, bf16[1,256,1408]{2,1,0:T(8,128)(2,1)}, u32[]{:S(2)}, u32[]{:S(2)}) %collective-permute-start.36) | collective-permute-done | bytes 720928 | tf_op jit(solution)/shard_map/ppermute | solution.py:630
  291.8 5.0 all-to-all-start.5
  306.6 5.9 collective-permute-done.54.refs_27_
  329.3 15.2 %mlp_both.1 = (bf16[256,1408]{1,0:T(8,128)(2,1)}, bf16[256,2048]{1,0:T(8,128)(2,1)}, bf16[2,256,1408]{2,1,0:T(8,128)(2,1)}, bf16[256,2048]{1,0:T(8,128)(2,1)}) custom-call(s32[18]{0:T(128)S(1)} %stack.130.refs_0_, bf16[256,2048]{1,0:T(8,128)(2,1)S(1)} %bitcast.114, bf16[256,2048]{1,0:T(8,128)(2,1)} %bitcast.130, ...), custom_call_target="tpu_custom_call" | custom-call | bytes 54000000 | tf_op jit(solution)/shard_map/mlp_both/pallas_call | solution.py:213
  344.5 4.9 all-to-all-start.6
  357.8 10.6 %mlp_grads.2 = (bf16[2,3,128,1408]{3,2,1,0:T(8,128)(2,1)}, bf16[2,3,128,1408]{3,2,1,0:T(8,128)(2,1)}, bf16[2,3,128,1408]{3,2,1,0:T(8,128)(2,1)}, bf16[3,128,1408]{2,1,0:T(8,128)(2,1)}, bf16[3,128,1408]{2,1,0:T(8,128)(2,1)}) custom-call(s32[4]{0:T(128)S(1)} %pad_add_fusion.refs_0_, bf16[256,2048]{1,0:T(8,128)(2,1)} %bitcast.116, bf16[256,2048]{1,0:T(8,128)(2,1)} %bitcast.131, ...), custom_call_target="tpu_custom_call" | custom-call | bytes 31500000 | tf_op jit(solution)/shard_map/mlp_grads/pallas_call | solution.py:772
  368.4 7.2 %all-to-all-done.6.refs_1_ = bf16[4,64,2048]{2,1,0:T(8,128)(2,1)} async-done(((bf16[4,64,2048]{2,1,0:T(8,128)(2,1)}), bf16[4,64,2048]{2,1,0:T(8,128)(2,1)}, u32[]{:S(2)}, u32[]{:S(2)}) %all-to-all-start.6) | async-done | bytes 1048608 | tf_op jit(solution)/shard_map/all_to_all | solution.py:732
  384.6 23.5 %all-to-all-done.7 = bf16[4,64,2048]{2,1,0:T(8,128)(2,1)S(1)} async-done(((bf16[4,64,2048]{2,1,0:T(8,128)(2,1)}), bf16[4,64,2048]{2,1,0:T(8,128)(2,1)S(1)}, u32[]{:S(2)}, u32[]{:S(2)}) %all-to-all-start.7) | async-done | bytes 1048608 | tf_op jit(solution)/shard_map/all_to_all | solution.py:736
  412.4 9.9 %attend_back.2 = (bf16[256,512]{1,0:T(8,128)(2,1)}, bf16[2,256,512]{2,1,0:T(8,128)(2,1)}, f32[2,256,512]{2,1,0:T(8,128)}) custom-call(s32[18]{0:T(128)S(1)} %stack.130.refs_0_, bf16[256,2048]{1,0:T(8,128)(2,1)S(1)} %bitcast.120, bf16[256,512]{1,0:T(8,128)(2,1)} %get-tuple-element.228.refs_1_.refs_2_, f32[8,256]{1,0:T(8,128)} %get-tuple-element.276.refs_3_, ...), custom_call_target="tpu_custom_call" | custom-call | bytes 30000000 | tf_op jit(solution)/shard_map/attend_back/pallas_call | solution.py:213
  424.5 6.8 collective-permute-done.65.refs_4_.refs_2_
  433.0 4.7 all-to-all-done.8.refs_1_
  438.9 8.3 %qkv_back.2 = (bf16[3,256,512]{2,1,0:T(8,128)(2,1)}, f32[3,512]{1,0:T(4,128)}, bf16[256,2048]{1,0:T(8,128)(2,1)}) custom-call(s32[18]{0:T(128)S(1)} %stack.130.refs_0_, bf16[256,512]{1,0:T(8,128)(2,1)} %get-tuple-element.277.refs_1_, f32[3,256,128]{2,1,0:T(8,128)} %pad_maximum_fusion.2.refs_2_.refs_4_, f32[2,256,512]{2,1,0:T(8,128)} %get-tuple-element.287.refs_3_, ...), custom_call_target="tpu_custom_call" | custom-call | bytes 27000000 | tf_op jit(solution)/shard_map/qkv_back/pallas_call | solution.py:213
  447.3 5.2 all-to-all-start.9
  456.5 6.9 attn_grads.2
  463.4 14.2 %all-to-all-done.9.refs_1_ = bf16[4,64,2048]{2,1,0:T(8,128)(2,1)S(1)} async-done(((bf16[4,64,2048]{2,1,0:T(8,128)(2,1)}), bf16[4,64,2048]{2,1,0:T(8,128)(2,1)S(1)}, u32[]{:S(2)}, u32[]{:S(2)}) %all-to-all-start.9) | async-done | bytes 1048608 | tf_op jit(solution)/shard_map/all_to_all | solution.py:732
  484.6 16.0 %collective-permute-done.71.refs_3_ = bf16[2,3,128,1408]{3,2,1,0:T(8,128)(2,1)} collective-permute-done((bf16[2,3,128,1408]{3,2,1,0:T(8,128)(2,1)}, bf16[2,3,128,1408]{3,2,1,0:T(8,128)(2,1)}, u32[]{:S(2)}, u32[]{:S(2)}) %collective-permute-start.71) | collective-permute-done | bytes 2162720 | tf_op jit(solution)/shard_map/ppermute | solution.py:630
  509.8 13.1 %mlp_back.1 = (bf16[2,256,1408]{2,1,0:T(8,128)(2,1)}, bf16[256,2048]{1,0:T(8,128)(2,1)}) custom-call(s32[18]{0:T(128)S(1)} %stack.130.refs_0_, bf16[256,1408]{1,0:T(8,128)(2,1)} %get-tuple-element.274.refs_1_, bf16[256,1408]{1,0:T(8,128)(2,1)} %get-tuple-element.275.refs_2_, bf16[256,2048]{1,0:T(8,128)(2,1)S(1)} %bitcast.123, ...), custom_call_target="tpu_custom_call" | custom-call | bytes 42000000 | tf_op jit(solution)/shard_map/mlp_back/pallas_call | solution.py:213
  522.9 5.2 all-to-all-start.11
  536.7 10.6 %mlp_grads.3 = (bf16[2,3,128,1408]{3,2,1,0:T(8,128)(2,1)}, bf16[2,3,128,1408]{3,2,1,0:T(8,128)(2,1)}, bf16[2,3,128,1408]{3,2,1,0:T(8,128)(2,1)}, bf16[3,128,1408]{2,1,0:T(8,128)(2,1)}, bf16[3,128,1408]{2,1,0:T(8,128)(2,1)}) custom-call(s32[4]{0:T(128)S(1)} %pad_add_fusion.refs_0_, bf16[256,2048]{1,0:T(8,128)(2,1)} %bitcast.128, bf16[256,2048]{1,0:T(8,128)(2,1)} %bitcast.125, ...), custom_call_target="tpu_custom_call" | custom-call | bytes 31500000 | tf_op jit(solution)/shard_map/mlp_grads/pallas_call | solution.py:772
  547.3 7.4 %mlp_finish.2 = (f32[2,256,2,1408]{3,2,1,0:T(2,128)}, f32[2,1408,256]{2,1,0:T(8,128)}) custom-call(s32[18]{0:T(128)S(1)} %stack.130.refs_0_, bf16[2,3,128,1408]{3,2,1,0:T(8,128)(2,1)} %get-tuple-element.312.refs_1_, bf16[2,3,128,1408]{3,2,1,0:T(8,128)(2,1)} %collective-permute-done.65.refs_4_.refs_2_, ...), custom_call_target="tpu_custom_call" | custom-call | bytes 22500000 | tf_op jit(solution)/shard_map/mlp_finish/pallas_call | solution.py:213
  566.4 22.7 %all-to-all-done.12 = bf16[4,64,2048]{2,1,0:T(8,128)(2,1)S(1)} async-done(((bf16[4,64,2048]{2,1,0:T(8,128)(2,1)}), bf16[4,64,2048]{2,1,0:T(8,128)(2,1)S(1)}, u32[]{:S(2)}, u32[]{:S(2)}) %all-to-all-start.12) | async-done | bytes 1048608 | tf_op jit(solution)/shard_map/all_to_all | solution.py:736
  592.9 9.9 %attend_back.3 = (bf16[256,512]{1,0:T(8,128)(2,1)}, bf16[2,256,512]{2,1,0:T(8,128)(2,1)}, f32[2,256,512]{2,1,0:T(8,128)}) custom-call(s32[18]{0:T(128)S(1)} %stack.130.refs_0_, bf16[256,2048]{1,0:T(8,128)(2,1)S(1)} %bitcast.117, bf16[256,512]{1,0:T(8,128)(2,1)} %get-tuple-element.197.refs_1_.refs_2_, f32[8,256]{1,0:T(8,128)} %get-tuple-element.319.refs_3_, ...), custom_call_target="tpu_custom_call" | custom-call | bytes 30000000 | tf_op jit(solution)/shard_map/attend_back/pallas_call | solution.py:213
  603.5 8.8 %collective-permute-done.78.refs_3_ = bf16[2,3,128,1408]{3,2,1,0:T(8,128)(2,1)} collective-permute-done((bf16[2,3,128,1408]{3,2,1,0:T(8,128)(2,1)}, bf16[2,3,128,1408]{3,2,1,0:T(8,128)(2,1)}, u32[]{:S(2)}, u32[]{:S(2)}) %collective-permute-start.78) | collective-permute-done | bytes 2162720 | tf_op jit(solution)/shard_map/ppermute | solution.py:630
  629.3 8.3 %qkv_back.3 = (bf16[3,256,512]{2,1,0:T(8,128)(2,1)}, f32[3,512]{1,0:T(4,128)}, bf16[256,2048]{1,0:T(8,128)(2,1)}) custom-call(s32[18]{0:T(128)S(1)} %stack.130.refs_0_, bf16[256,512]{1,0:T(8,128)(2,1)} %get-tuple-element.320.refs_1_, f32[3,256,128]{2,1,0:T(8,128)} %pad_maximum_fusion.2.refs_2_.refs_4_, f32[2,256,512]{2,1,0:T(8,128)} %get-tuple-element.340.refs_3_, ...), custom_call_target="tpu_custom_call" | custom-call | bytes 27000000 | tf_op jit(solution)/shard_map/qkv_back/pallas_call | solution.py:213
  637.8 5.2 all-to-all-start.14
  643.0 6.3 collective-permute-done.85.refs_5_
  652.5 6.9 attn_grads.3
  671.6 7.4 %mlp_finish.3 = (f32[2,256,2,1408]{3,2,1,0:T(2,128)}, f32[2,1408,256]{2,1,0:T(8,128)}) custom-call(s32[18]{0:T(128)S(1)} %stack.130.refs_0_, bf16[2,3,128,1408]{3,2,1,0:T(8,128)(2,1)} %get-tuple-element.358.refs_1_, bf16[2,3,128,1408]{3,2,1,0:T(8,128)(2,1)} %collective-permute-done.79.refs_4_.refs_2_, ...), custom_call_target="tpu_custom_call", output_to_operand_aliasing={{0}: (6, {}), {1}: (7, {})} | custom-call | bytes 22500000 | tf_op jit(solution)/shard_map/mlp_finish/pallas_call | solution.py:213
  (448 shorter events, 277.5 us)
Async XLA Ops:
  3.4 26.5 %collective-permute-start.3 = (bf16[4,256,512]{2,1,0:T(8,128)(2,1)S(1)}, bf16[4,256,512]{2,1,0:T(8,128)(2,1)S(1)}, u32[]{:S(2)}, u32[]{:S(2)}) collective-permute-start(bf16[4,256,512]{2,1,0:T(8,128)(2,1)S(1)} %pad_maximum_fusion.refs_6_.refs_9_.refs_5_), channel_id=1, source_target_pairs={{0,16},{8,24},{16,0},{24,8},{1,17},{9,25},{17,1},{25,9},{2,18},{10... | collective-permute-start | bytes 3145736 | tf_op jit(solution)/shard_map/ppermute | solution.py:622
  6.4 43.3 %collective-permute-start.7 = (bf16[4,256,512]{2,1,0:T(8,128)(2,1)S(1)}, bf16[4,256,512]{2,1,0:T(8,128)(2,1)}, u32[]{:S(2)}, u32[]{:S(2)}) collective-permute-start(bf16[4,256,512]{2,1,0:T(8,128)(2,1)S(1)} %pad_maximum_fusion.refs_6_.refs_9_.refs_5_), channel_id=1, source_target_pairs={{0,8},{8,0},{16,24},{24,16},{1,9},{9,1},{17,25},{25,17},{2,10},{10... | collective-permute-start | bytes 3145736 | tf_op jit(solution)/shard_map/ppermute | solution.py:626
  10.8 26.1 %collective-permute-start.4 = (bf16[4,256,512]{2,1,0:T(8,128)(2,1)S(1)}, bf16[4,256,512]{2,1,0:T(8,128)(2,1)S(1)}, u32[]{:S(2)}, u32[]{:S(2)}) collective-permute-start(bf16[4,256,512]{2,1,0:T(8,128)(2,1)S(1)} %pad_maximum_fusion.refs_6_.refs_9_.refs_5_), channel_id=1, source_target_pairs={{0,4},{4,0},{1,5},{5,1},{2,6},{6,2},{3,7},{7,3},{8,12},{12,8},{9,1... | collective-permute-start | bytes 3145736 | tf_op jit(solution)/shard_map/ppermute | solution.py:630
  49.7 49.8 %collective-permute-start.13 = (bf16[3,256,1408]{2,1,0:T(8,128)(2,1)}, bf16[3,256,1408]{2,1,0:T(8,128)(2,1)}, u32[]{:S(2)}, u32[]{:S(2)}) collective-permute-start(bf16[3,256,1408]{2,1,0:T(8,128)(2,1)} %pack.2.refs_2_.refs_4_), channel_id=1, source_target_pairs={{0,16},{8,24},{16,0},{24,8},{1,17},{9,25},{17,1},{25,9},{2,18},{10... | collective-permute-start | bytes 6488072 | tf_op jit(solution)/shard_map/ppermute | solution.py:622
  72.8 49.3 %collective-permute-start.14 = (bf16[3,256,1408]{2,1,0:T(8,128)(2,1)}, bf16[3,256,1408]{2,1,0:T(8,128)(2,1)}, u32[]{:S(2)}, u32[]{:S(2)}) collective-permute-start(bf16[3,256,1408]{2,1,0:T(8,128)(2,1)} %pack.2.refs_2_.refs_4_), channel_id=1, source_target_pairs={{0,4},{4,0},{1,5},{5,1},{2,6},{6,2},{3,7},{7,3},{8,12},{12,8},{9,1... | collective-permute-start | bytes 6488072 | tf_op jit(solution)/shard_map/ppermute | solution.py:630
  81.9 29.9 %all-to-all-start = ((bf16[4,64,2048]{2,1,0:T(8,128)(2,1)}), bf16[4,64,2048]{2,1,0:T(8,128)(2,1)S(1)}, u32[]{:S(2)}, u32[]{:S(2)}) async-start(bf16[4,64,2048]{2,1,0:T(8,128)(2,1)} %bitcast.145), calls=%async_computation | async-start | bytes 2097152 | tf_op jit(solution)/shard_map/all_to_all | solution.py:732
  114.8 34.0 %collective-permute-start.18 = (bf16[3,256,1408]{2,1,0:T(8,128)(2,1)}, bf16[3,256,1408]{2,1,0:T(8,128)(2,1)}, u32[]{:S(2)}, u32[]{:S(2)}) collective-permute-start(bf16[3,256,1408]{2,1,0:T(8,128)(2,1)} %collective-permute-done.13.refs_3_.refs_5_), channel_id=1, source_target_pairs={{0,8},{8,0},{16,24},{24,16},{1,9},{9,1},{17,25},{25,17},{2,10},{10... | collective-permute-start | bytes 6488072 | tf_op jit(solution)/shard_map/ppermute | solution.py:626
  114.9 35.1 %collective-permute-start.17 = (bf16[3,256,1408]{2,1,0:T(8,128)(2,1)}, bf16[3,256,1408]{2,1,0:T(8,128)(2,1)}, u32[]{:S(2)}, u32[]{:S(2)}) collective-permute-start(bf16[3,256,1408]{2,1,0:T(8,128)(2,1)} %pack.2.refs_2_.refs_4_), channel_id=1, source_target_pairs={{0,8},{8,0},{16,24},{24,16},{1,9},{9,1},{17,25},{25,17},{2,10},{10... | collective-permute-start | bytes 6488072 | tf_op jit(solution)/shard_map/ppermute | solution.py:626
  115.4 31.0 %all-to-all-start.1 = ((bf16[4,64,2048]{2,1,0:T(8,128)(2,1)}), bf16[4,64,2048]{2,1,0:T(8,128)(2,1)S(1)}, u32[]{:S(2)}, u32[]{:S(2)}) async-start(bf16[4,64,2048]{2,1,0:T(8,128)(2,1)} %get-tuple-element.204), calls=%async_computation.1 | async-start | bytes 2097152 | tf_op jit(solution)/shard_map/all_to_all | solution.py:736
  120.3 26.0 %collective-permute-start.16 = (bf16[3,128,1408]{2,1,0:T(8,128)(2,1)S(1)}, bf16[3,128,1408]{2,1,0:T(8,128)(2,1)}, u32[]{:S(2)}, u32[]{:S(2)}) collective-permute-start(bf16[3,128,1408]{2,1,0:T(8,128)(2,1)S(1)} %slice.214), channel_id=1, source_target_pairs={{0,4},{4,0},{1,5},{5,1},{2,6},{6,2},{3,7},{7,3},{8,12},{12,8},{9,1... | collective-permute-start | bytes 3244040 | tf_op jit(solution)/shard_map/ppermute | solution.py:630
  123.4 25.1 %collective-permute-start.15 = (bf16[3,128,1408]{2,1,0:T(8,128)(2,1)S(1)}, bf16[3,128,1408]{2,1,0:T(8,128)(2,1)}, u32[]{:S(2)}, u32[]{:S(2)}) collective-permute-start(bf16[3,128,1408]{2,1,0:T(8,128)(2,1)S(1)} %slice.213), channel_id=1, source_target_pairs={{0,16},{8,24},{16,0},{24,8},{1,17},{9,25},{17,1},{25,9},{2,18},{10... | collective-permute-start | bytes 3244040 | tf_op jit(solution)/shard_map/ppermute | solution.py:622
  125.1 26.6 %collective-permute-start.19 = (bf16[3,256,1408]{2,1,0:T(8,128)(2,1)}, bf16[3,256,1408]{2,1,0:T(8,128)(2,1)}, u32[]{:S(2)}, u32[]{:S(2)}) collective-permute-start(bf16[3,256,1408]{2,1,0:T(8,128)(2,1)} %collective-permute-done.14.refs_4_.refs_6_), channel_id=1, source_target_pairs={{0,8},{8,0},{16,24},{24,16},{1,9},{9,1},{17,25},{25,17},{2,10},{10... | collective-permute-start | bytes 6488072 | tf_op jit(solution)/shard_map/ppermute | solution.py:626
  148.8 25.7 %collective-permute-start.22 = (bf16[4,256,512]{2,1,0:T(8,128)(2,1)S(1)}, bf16[4,256,512]{2,1,0:T(8,128)(2,1)}, u32[]{:S(2)}, u32[]{:S(2)}) collective-permute-start(bf16[4,256,512]{2,1,0:T(8,128)(2,1)S(1)} %pad_maximum_fusion.1.refs_4_.refs_6_.refs_9_.refs_5_), channel_id=1, source_target_pairs={{0,4},{4,0},{1,5},{5,1},{2,6},{6,2},{3,7},{7,3},{8,12},{12,8},{9,1... | collective-permute-start | bytes 3145736 | tf_op jit(solution)/shard_map/ppermute | solution.py:630
  150.0 25.4 %collective-permute-start.24 = (bf16[4,256,512]{2,1,0:T(8,128)(2,1)S(1)}, bf16[4,256,512]{2,1,0:T(8,128)(2,1)}, u32[]{:S(2)}, u32[]{:S(2)}) collective-permute-start(bf16[4,256,512]{2,1,0:T(8,128)(2,1)S(1)} %pad_maximum_fusion.1.refs_4_.refs_6_.refs_9_.refs_5_), channel_id=1, source_target_pairs={{0,16},{8,24},{16,0},{24,8},{1,17},{9,25},{17,1},{25,9},{2,18},{10... | collective-permute-start | bytes 3145736 | tf_op jit(solution)/shard_map/ppermute | solution.py:622
  161.6 33.2 %all-to-all-start.2 = ((bf16[4,64,2048]{2,1,0:T(8,128)(2,1)}), bf16[4,64,2048]{2,1,0:T(8,128)(2,1)S(1)}, u32[]{:S(2)}, u32[]{:S(2)}) async-start(bf16[4,64,2048]{2,1,0:T(8,128)(2,1)} %bitcast.143), calls=%async_computation.2 | async-start | bytes 2097152 | tf_op jit(solution)/shard_map/all_to_all | solution.py:732
  197.9 29.5 %all-to-all-start.3 = ((bf16[4,64,2048]{2,1,0:T(8,128)(2,1)}), bf16[4,64,2048]{2,1,0:T(8,128)(2,1)S(1)}, u32[]{:S(2)}, u32[]{:S(2)}) async-start(bf16[4,64,2048]{2,1,0:T(8,128)(2,1)} %get-tuple-element.224), calls=%async_computation.3 | async-start | bytes 2097152 | tf_op jit(solution)/shard_map/all_to_all | solution.py:736
  235.5 24.6 %collective-permute-start.34 = (bf16[1,256,1408]{2,1,0:T(8,128)(2,1)}, bf16[1,256,1408]{2,1,0:T(8,128)(2,1)}, u32[]{:S(2)}, u32[]{:S(2)}) collective-permute-start(bf16[1,256,1408]{2,1,0:T(8,128)(2,1)} %get-tuple-element.250.refs_13_), channel_id=1, source_target_pairs={{0,16},{8,24},{16,0},{24,8},{1,17},{9,25},{17,1},{25,9},{2,18},{10... | collective-permute-start | bytes 2162696 | tf_op jit(solution)/shard_map/ppermute | solution.py:622
  253.7 35.0 %all-to-all-start.4 = ((bf16[4,64,2048]{2,1,0:T(8,128)(2,1)}), bf16[4,64,2048]{2,1,0:T(8,128)(2,1)S(1)}, u32[]{:S(2)}, u32[]{:S(2)}) async-start(bf16[4,64,2048]{2,1,0:T(8,128)(2,1)} %bitcast.142), calls=%async_computation.4 | async-start | bytes 2097152 | tf_op jit(solution)/shard_map/all_to_all | solution.py:732
  260.1 25.0 %collective-permute-start.35 = (bf16[1,256,1408]{2,1,0:T(8,128)(2,1)}, bf16[1,256,1408]{2,1,0:T(8,128)(2,1)}, u32[]{:S(2)}, u32[]{:S(2)}) collective-permute-start(bf16[1,256,1408]{2,1,0:T(8,128)(2,1)} %get-tuple-element.256.refs_23_), channel_id=1, source_target_pairs={{0,16},{8,24},{16,0},{24,8},{1,17},{9,25},{17,1},{25,9},{2,18},{10... | collective-permute-start | bytes 2162696 | tf_op jit(solution)/shard_map/ppermute | solution.py:622
  261.8 35.0 %collective-permute-start.37 = (bf16[256,2048]{1,0:T(8,128)(2,1)}, bf16[256,2048]{1,0:T(8,128)(2,1)}, u32[]{:S(2)}, u32[]{:S(2)}) collective-permute-start(bf16[256,2048]{1,0:T(8,128)(2,1)} %bitcast.129), channel_id=1, source_target_pairs={{0,8},{8,0},{16,24},{24,16},{1,9},{9,1},{17,25},{25,17},{2,10},{10... | collective-permute-start | bytes 3145736 | tf_op jit(solution)/shard_map/ppermute | solution.py:626
  262.8 22.3 %collective-permute-start.39 = (bf16[1,128,1408]{2,1,0:T(8,128)(2,1)S(1)}, bf16[1,128,1408]{2,1,0:T(8,128)(2,1)S(1)}, u32[]{:S(2)}, u32[]{:S(2)}) collective-permute-start(bf16[1,128,1408]{2,1,0:T(8,128)(2,1)S(1)} %slice.222), channel_id=1, source_target_pairs={{0,4},{4,0},{1,5},{5,1},{2,6},{6,2},{3,7},{7,3},{8,12},{12,8},{9,1... | collective-permute-start | bytes 1081352 | tf_op jit(solution)/shard_map/ppermute | solution.py:630
  291.8 32.3 %all-to-all-start.5 = ((bf16[4,64,2048]{2,1,0:T(8,128)(2,1)}), bf16[4,64,2048]{2,1,0:T(8,128)(2,1)S(1)}, u32[]{:S(2)}, u32[]{:S(2)}) async-start(bf16[4,64,2048]{2,1,0:T(8,128)(2,1)} %get-tuple-element.240), calls=%async_computation.5 | async-start | bytes 2097152 | tf_op jit(solution)/shard_map/all_to_all | solution.py:736
  344.5 31.0 %all-to-all-start.6 = ((bf16[4,64,2048]{2,1,0:T(8,128)(2,1)}), bf16[4,64,2048]{2,1,0:T(8,128)(2,1)}, u32[]{:S(2)}, u32[]{:S(2)}) async-start(bf16[4,64,2048]{2,1,0:T(8,128)(2,1)} %bitcast.140), calls=%async_computation.6 | async-start | bytes 2097152 | tf_op jit(solution)/shard_map/all_to_all | solution.py:732
  379.3 28.8 %all-to-all-start.7 = ((bf16[4,64,2048]{2,1,0:T(8,128)(2,1)}), bf16[4,64,2048]{2,1,0:T(8,128)(2,1)S(1)}, u32[]{:S(2)}, u32[]{:S(2)}) async-start(bf16[4,64,2048]{2,1,0:T(8,128)(2,1)} %get-tuple-element.270), calls=%async_computation.7 | async-start | bytes 2097152 | tf_op jit(solution)/shard_map/all_to_all | solution.py:736
  382.9 48.4 %collective-permute-start.65 = (bf16[2,3,128,1408]{3,2,1,0:T(8,128)(2,1)}, bf16[2,3,128,1408]{3,2,1,0:T(8,128)(2,1)}, u32[]{:S(2)}, u32[]{:S(2)}) collective-permute-start(bf16[2,3,128,1408]{3,2,1,0:T(8,128)(2,1)} %get-tuple-element.279), channel_id=1, source_target_pairs={{0,16},{8,24},{16,0},{24,8},{1,17},{9,25},{17,1},{25,9},{2,18},{10... | collective-permute-start | bytes 6488072 | tf_op jit(solution)/shard_map/ppermute | solution.py:622
  408.1 29.5 %all-to-all-start.8 = ((bf16[4,64,2048]{2,1,0:T(8,128)(2,1)}), bf16[4,64,2048]{2,1,0:T(8,128)(2,1)}, u32[]{:S(2)}, u32[]{:S(2)}) async-start(bf16[4,64,2048]{2,1,0:T(8,128)(2,1)} %bitcast.138), calls=%async_computation.8 | async-start | bytes 2097152 | tf_op jit(solution)/shard_map/all_to_all | solution.py:732
  447.3 30.3 %all-to-all-start.9 = ((bf16[4,64,2048]{2,1,0:T(8,128)(2,1)}), bf16[4,64,2048]{2,1,0:T(8,128)(2,1)S(1)}, u32[]{:S(2)}, u32[]{:S(2)}) async-start(bf16[4,64,2048]{2,1,0:T(8,128)(2,1)} %bitcast.144), calls=%async_computation.9 | async-start | bytes 2097152 | tf_op jit(solution)/shard_map/all_to_all | solution.py:732
  452.4 48.2 %collective-permute-start.71 = (bf16[2,3,128,1408]{3,2,1,0:T(8,128)(2,1)}, bf16[2,3,128,1408]{3,2,1,0:T(8,128)(2,1)}, u32[]{:S(2)}, u32[]{:S(2)}) collective-permute-start(bf16[2,3,128,1408]{3,2,1,0:T(8,128)(2,1)} %get-tuple-element.301), channel_id=1, source_target_pairs={{0,4},{4,0},{1,5},{5,1},{2,6},{6,2},{3,7},{7,3},{8,12},{12,8},{9,1... | collective-permute-start | bytes 6488072 | tf_op jit(solution)/shard_map/ppermute | solution.py:630
  481.0 28.8 %all-to-all-start.10 = ((bf16[4,64,2048]{2,1,0:T(8,128)(2,1)}), bf16[4,64,2048]{2,1,0:T(8,128)(2,1)S(1)}, u32[]{:S(2)}, u32[]{:S(2)}) async-start(bf16[4,64,2048]{2,1,0:T(8,128)(2,1)} %get-tuple-element.295), calls=%async_computation.10 | async-start | bytes 2097152 | tf_op jit(solution)/shard_map/all_to_all | solution.py:736
  504.7 24.2 %collective-permute-start.72 = (bf16[3,128,1408]{2,1,0:T(8,128)(2,1)}, bf16[3,128,1408]{2,1,0:T(8,128)(2,1)}, u32[]{:S(2)}, u32[]{:S(2)}) collective-permute-start(bf16[3,128,1408]{2,1,0:T(8,128)(2,1)} %get-tuple-element.302), channel_id=1, source_target_pairs={{0,16},{8,24},{16,0},{24,8},{1,17},{9,25},{17,1},{25,9},{2,18},{10... | collective-permute-start | bytes 3244040 | tf_op jit(solution)/shard_map/ppermute | solution.py:622
  506.4 23.8 %collective-permute-start.73 = (bf16[3,128,1408]{2,1,0:T(8,128)(2,1)}, bf16[3,128,1408]{2,1,0:T(8,128)(2,1)}, u32[]{:S(2)}, u32[]{:S(2)}) collective-permute-start(bf16[3,128,1408]{2,1,0:T(8,128)(2,1)} %get-tuple-element.306), channel_id=1, source_target_pairs={{0,4},{4,0},{1,5},{5,1},{2,6},{6,2},{3,7},{7,3},{8,12},{12,8},{9,1... | collective-permute-start | bytes 3244040 | tf_op jit(solution)/shard_map/ppermute | solution.py:630
  522.9 31.8 %all-to-all-start.11 = ((bf16[4,64,2048]{2,1,0:T(8,128)(2,1)}), bf16[4,64,2048]{2,1,0:T(8,128)(2,1)S(1)}, u32[]{:S(2)}, u32[]{:S(2)}) async-start(bf16[4,64,2048]{2,1,0:T(8,128)(2,1)} %bitcast.141), calls=%async_computation.11 | async-start | bytes 2097152 | tf_op jit(solution)/shard_map/all_to_all | solution.py:732
  530.8 25.3 %collective-permute-start.76 = (bf16[2,4,128,512]{3,2,1,0:T(8,128)(2,1)}, bf16[2,4,128,512]{3,2,1,0:T(8,128)(2,1)S(1)}, u32[]{:S(2)}, u32[]{:S(2)}) collective-permute-start(bf16[2,4,128,512]{3,2,1,0:T(8,128)(2,1)} %get-tuple-element.314), channel_id=1, source_target_pairs={{0,16},{8,24},{16,0},{24,8},{1,17},{9,25},{17,1},{25,9},{2,18},{10... | collective-permute-start | bytes 3145736 | tf_op jit(solution)/shard_map/ppermute | solution.py:622
  531.1 25.1 %collective-permute-start.77 = (bf16[2,4,128,512]{3,2,1,0:T(8,128)(2,1)}, bf16[2,4,128,512]{3,2,1,0:T(8,128)(2,1)}, u32[]{:S(2)}, u32[]{:S(2)}) collective-permute-start(bf16[2,4,128,512]{3,2,1,0:T(8,128)(2,1)} %get-tuple-element.315), channel_id=1, source_target_pairs={{0,4},{4,0},{1,5},{5,1},{2,6},{6,2},{3,7},{7,3},{8,12},{12,8},{9,1... | collective-permute-start | bytes 3145736 | tf_op jit(solution)/shard_map/ppermute | solution.py:630
  559.7 29.5 %all-to-all-start.12 = ((bf16[4,64,2048]{2,1,0:T(8,128)(2,1)}), bf16[4,64,2048]{2,1,0:T(8,128)(2,1)S(1)}, u32[]{:S(2)}, u32[]{:S(2)}) async-start(bf16[4,64,2048]{2,1,0:T(8,128)(2,1)} %get-tuple-element.317), calls=%async_computation.12 | async-start | bytes 2097152 | tf_op jit(solution)/shard_map/all_to_all | solution.py:736
  564.2 48.0 %collective-permute-start.78 = (bf16[2,3,128,1408]{3,2,1,0:T(8,128)(2,1)}, bf16[2,3,128,1408]{3,2,1,0:T(8,128)(2,1)}, u32[]{:S(2)}, u32[]{:S(2)}) collective-permute-start(bf16[2,3,128,1408]{3,2,1,0:T(8,128)(2,1)} %get-tuple-element.326), channel_id=1, source_target_pairs={{0,4},{4,0},{1,5},{5,1},{2,6},{6,2},{3,7},{7,3},{8,12},{12,8},{9,1... | collective-permute-start | bytes 6488072 | tf_op jit(solution)/shard_map/ppermute | solution.py:630
  564.8 48.8 %collective-permute-start.79 = (bf16[2,3,128,1408]{3,2,1,0:T(8,128)(2,1)}, bf16[2,3,128,1408]{3,2,1,0:T(8,128)(2,1)}, u32[]{:S(2)}, u32[]{:S(2)}) collective-permute-start(bf16[2,3,128,1408]{3,2,1,0:T(8,128)(2,1)} %get-tuple-element.327), channel_id=1, source_target_pairs={{0,16},{8,24},{16,0},{24,8},{1,17},{9,25},{17,1},{25,9},{2,18},{10... | collective-permute-start | bytes 6488072 | tf_op jit(solution)/shard_map/ppermute | solution.py:622
  589.2 37.4 %all-to-all-start.13 = ((bf16[4,64,2048]{2,1,0:T(8,128)(2,1)}), bf16[4,64,2048]{2,1,0:T(8,128)(2,1)S(1)}, u32[]{:S(2)}, u32[]{:S(2)}) async-start(bf16[4,64,2048]{2,1,0:T(8,128)(2,1)} %sum.1), calls=%async_computation.13 | async-start | bytes 2097152 | tf_op jit(solution)/shard_map/all_to_all | solution.py:736
  602.8 22.7 %collective-permute-start.81 = (bf16[256,2048]{1,0:T(8,128)(2,1)S(1)}, bf16[256,2048]{1,0:T(8,128)(2,1)S(1)}, u32[]{:S(2)}, u32[]{:S(2)}) collective-permute-start(bf16[256,2048]{1,0:T(8,128)(2,1)S(1)} %bitcast.118), channel_id=1, source_target_pairs={{0,8},{8,0},{16,24},{24,16},{1,9},{9,1},{17,25},{25,17},{2,10},{10... | collective-permute-start | bytes 3145736 | tf_op jit(solution)/shard_map/ppermute | solution.py:626
  602.9 23.7 %collective-permute-start.80 = (bf16[256,2048]{1,0:T(8,128)(2,1)S(1)}, bf16[256,2048]{1,0:T(8,128)(2,1)}, u32[]{:S(2)}, u32[]{:S(2)}) collective-permute-start(bf16[256,2048]{1,0:T(8,128)(2,1)S(1)} %copy-done.7), channel_id=1, source_target_pairs={{0,8},{8,0},{16,24},{24,16},{1,9},{9,1},{17,25},{25,17},{2,10},{10... | collective-permute-start | bytes 3145736 | tf_op jit(solution)/shard_map/ppermute | solution.py:626
  617.6 25.4 %collective-permute-start.84 = (bf16[3,128,1408]{2,1,0:T(8,128)(2,1)}, bf16[3,128,1408]{2,1,0:T(8,128)(2,1)}, u32[]{:S(2)}, u32[]{:S(2)}) collective-permute-start(bf16[3,128,1408]{2,1,0:T(8,128)(2,1)} %get-tuple-element.328), channel_id=1, source_target_pairs={{0,16},{8,24},{16,0},{24,8},{1,17},{9,25},{17,1},{25,9},{2,18},{10... | collective-permute-start | bytes 3244040 | tf_op jit(solution)/shard_map/ppermute | solution.py:622
  619.1 30.3 %collective-permute-start.85 = (bf16[3,128,1408]{2,1,0:T(8,128)(2,1)}, bf16[3,128,1408]{2,1,0:T(8,128)(2,1)}, u32[]{:S(2)}, u32[]{:S(2)}) collective-permute-start(bf16[3,128,1408]{2,1,0:T(8,128)(2,1)} %get-tuple-element.344), channel_id=1, source_target_pairs={{0,4},{4,0},{1,5},{5,1},{2,6},{6,2},{3,7},{7,3},{8,12},{12,8},{9,1... | collective-permute-start | bytes 3244040 | tf_op jit(solution)/shard_map/ppermute | solution.py:630
  637.8 24.9 %all-to-all-start.14 = ((bf16[4,64,2048]{2,1,0:T(8,128)(2,1)}), bf16[4,64,2048]{2,1,0:T(8,128)(2,1)S(1)}, u32[]{:S(2)}, u32[]{:S(2)}) async-start(bf16[4,64,2048]{2,1,0:T(8,128)(2,1)} %bitcast.139), calls=%async_computation.14 | async-start | bytes 2097152 | tf_op jit(solution)/shard_map/all_to_all | solution.py:732
  649.4 29.6 %collective-permute-start.89 = (bf16[4,128,512]{2,1,0:T(8,128)(2,1)}, bf16[4,128,512]{2,1,0:T(8,128)(2,1)}, u32[]{:S(2)}, u32[]{:S(2)}) collective-permute-start(bf16[4,128,512]{2,1,0:T(8,128)(2,1)} %get-tuple-element.364), channel_id=1, source_target_pairs={{0,4},{4,0},{1,5},{5,1},{2,6},{6,2},{3,7},{7,3},{8,12},{12,8},{9,1... | collective-permute-start | bytes 1572872 | tf_op jit(solution)/shard_map/ppermute | solution.py:630
  649.5 29.6 %collective-permute-start.88 = (bf16[4,128,512]{2,1,0:T(8,128)(2,1)}, bf16[4,128,512]{2,1,0:T(8,128)(2,1)}, u32[]{:S(2)}, u32[]{:S(2)}) collective-permute-start(bf16[4,128,512]{2,1,0:T(8,128)(2,1)} %get-tuple-element.362), channel_id=1, source_target_pairs={{0,16},{8,24},{16,0},{24,8},{1,17},{9,25},{17,1},{25,9},{2,18},{10... | collective-permute-start | bytes 1572872 | tf_op jit(solution)/shard_map/ppermute | solution.py:622
  659.4 28.6 %collective-permute-start.90 = (bf16[2,4,128,512]{3,2,1,0:T(8,128)(2,1)}, bf16[2,4,128,512]{3,2,1,0:T(8,128)(2,1)S(1)}, u32[]{:S(2)}, u32[]{:S(2)}) collective-permute-start(bf16[2,4,128,512]{3,2,1,0:T(8,128)(2,1)} %get-tuple-element.368), channel_id=1, source_target_pairs={{0,4},{4,0},{1,5},{5,1},{2,6},{6,2},{3,7},{7,3},{8,12},{12,8},{9,1... | collective-permute-start | bytes 3145736 | tf_op jit(solution)/shard_map/ppermute | solution.py:630
  660.5 27.5 %collective-permute-start.91 = (bf16[2,4,128,512]{3,2,1,0:T(8,128)(2,1)}, bf16[2,4,128,512]{3,2,1,0:T(8,128)(2,1)S(1)}, u32[]{:S(2)}, u32[]{:S(2)}) collective-permute-start(bf16[2,4,128,512]{3,2,1,0:T(8,128)(2,1)} %get-tuple-element.369), channel_id=1, source_target_pairs={{0,16},{8,24},{16,0},{24,8},{1,17},{9,25},{17,1},{25,9},{2,18},{10... | collective-permute-start | bytes 3145736 | tf_op jit(solution)/shard_map/ppermute | solution.py:622
  667.1 46.3 %all-to-all-start.15 = ((bf16[4,64,2048]{2,1,0:T(8,128)(2,1)}), bf16[4,64,2048]{2,1,0:T(8,128)(2,1)S(1)}, u32[]{:S(2)}, u32[]{:S(2)}) async-start(bf16[4,64,2048]{2,1,0:T(8,128)(2,1)} %get-tuple-element.349), calls=%async_computation.15 | async-start | bytes 2097152 | tf_op jit(solution)/shard_map/all_to_all | solution.py:736
  (139 other events, 1752.5 us)
